TPU v7x, 32 devices: a whole 2x2x4 slice. The times are simulated.
32 devices in a mesh: dp: 16 (over z, x, core), tensor: 2 (over y).
Axes of the slice: x: 2, y: 2, z: 4, core: 2. Of those that a mesh axis runs over, the one named last changes fastest.
Arguments:
- rows_in: bfloat16 [532, 16, 768], P('tensor', 'dp'), may hold values from -6 to 6
- d_out: bfloat16 [532, 16, 768], P('tensor', 'dp'), may hold values from -6 to 6
- starts: int32 [16, 8], P('dp'), may hold values from 0 to 511, as said below
- lengths: int32 [16], P('dp'), may hold values from 257 to 512, as said below
- resets: int32 [16], P('dp'), may hold values 0 or 1
- qkv_weight: bfloat16 [768, 2304], P(('dp', 'tensor')), may hold values from -0.21875 to 0.21875
- out_weight: bfloat16 [768, 768], P(('dp', 'tensor')), may hold values from -0.875 to 0.875
- bias_vec: bfloat16 [6, 768], P(None, ('dp', 'tensor')), may hold values from -2 to 2
- gains: bfloat16 [2, 768], P(None, ('dp', 'tensor')), may hold values from 0.5 to 1.5
- mem_init: bfloat16 [20, 768], P(None, ('dp', 'tensor')), may hold values from -6 to 6
- ffn_up: bfloat16 [768, 3072], P('dp', 'tensor'), may hold values from -0.21875 to 0.21875
- up_bias: bfloat16 [3072], P(('dp', 'tensor')), may hold values from -2 to 2
- ffn_down: bfloat16 [3072, 768], P('tensor', 'dp'), may hold values from -0.109375 to 0.109375
Outputs:
- layer_out: bfloat16 [532, 16, 768], P('tensor', 'dp')
- grad_rows: float32 [532, 16, 768], P('tensor', 'dp')
- grad_qkv: float32 [768, 2304], P(('dp', 'tensor'))
- grad_out_weight: float32 [768, 768], P(('dp', 'tensor'))
- grad_bias_vec: float32 [6, 768], P(None, ('dp', 'tensor'))
- grad_gains: float32 [2, 768], P(None, ('dp', 'tensor'))
- grad_mem_init: float32 [20, 768], P(None, ('dp', 'tensor'))
- grad_ffn_up: float32 [768, 3072], P('dp', 'tensor')
- grad_up_bias: float32 [3072], P(('dp', 'tensor'))
- grad_ffn_down: float32 [3072, 768], P('tensor', 'dp')
Inputs may be any that keep to these rules, and one draw needn't show every extreme that they name: `starts`: each row begins with 0 and rises strictly. `lengths`: every fourth segment, counted from the first, is full.
All inputs are finite; a program needn't handle non-finite values. No bound on the sum of `resets` on one device may be relied on, other than what follows from the above.
Results may differ from a plain program's by a relative error of at most 0.015.
Values may be sent and summed in bfloat16 or wider, within the bound.
No kernel may reach another device: no remote copies, remote signals or barrier semaphores. Data moves between devices by JAX's collectives and lax.ppermute only.
A program may use at most 128 MiB of HBM per device.

v0:
```python
import functools

import jax
import jax.numpy as jnp
import numpy as np
from jax import lax
from jax.experimental import pallas as pl
from jax.experimental.pallas import tpu as pltpu
from jax.sharding import PartitionSpec as P

HEADS = 12
HEAD = 64
NORM_EPSILON = 1e-06
LOW = jnp.bfloat16
WIDE = jnp.float32
CHUNK = 32
ROWS = 16
PAIR = 2 * HEAD
QUICK = pl.CostEstimate(flops=1, bytes_accessed=1, transcendentals=0)
T, X, CORE, OUTER, DP, FRESH, LENGTH, STARTS = range(8)


def ceil_to(count, unit):
    return -(-count // unit) * unit


def nn(a, b):
    return lax.dot_general(a, b, (((1,), (0,)), ((), ())), preferred_element_type=WIDE)


def nt(a, b):
    return lax.dot_general(a, b, (((1,), (1,)), ((), ())), preferred_element_type=WIDE)


def tn(a, b):
    return lax.dot_general(a, b, (((0,), (0,)), ((), ())), preferred_element_type=WIDE)


def low_of(*shape):
    return jax.ShapeDtypeStruct(shape, LOW)


def wide_of(*shape):
    return jax.ShapeDtypeStruct(shape, WIDE)


def held_bytes(array):
    rows, cols = ((1,) + tuple(array.shape))[-2:]
    lead = int(np.prod(array.shape[:-2])) if len(array.shape) > 2 else 1
    return lead * ceil_to(rows, 16) * ceil_to(cols, 128) * jnp.dtype(array.dtype).itemsize


def call(kernel, outs, at, *arrays, scratch=(), room=0):
    room += sum(held_bytes(array) for array in (*arrays, *outs))
    room += sum(held_bytes(ref) for ref in scratch)
    return pl.pallas_call(
        kernel,
        in_specs=[pl.BlockSpec(memory_space=pltpu.SMEM)]
        + [pl.BlockSpec(memory_space=pltpu.VMEM)] * len(arrays),
        out_specs=[pl.BlockSpec(memory_space=pltpu.VMEM)] * len(outs),
        out_shape=list(outs),
        scratch_shapes=list(scratch),
        compiler_params=pltpu.CompilerParams(vmem_limit_bytes=room + (3 << 20)),
        cost_estimate=QUICK,
    )(at, *arrays)


def digits_of(dp_count):
    assert dp_count % 4 == 0
    sizes = [2, 2]
    left = dp_count // 4
    while left > 1:
        size = next((s for s in (4, 2, 3) if left % s == 0), left)
        sizes.append(size)
        left //= size
    if len(sizes) == 2:
        sizes.append(1)
    digits, stride = [], 1
    for size in sizes:
        digits.append((stride, size))
        stride *= size
    return digits[::-1]


def digit_at(digit):
    stride, size = digit
    return (lax.axis_index("dp") // stride) % size


def rotate(value, digit, step):
    stride, size = digit
    pairs = []
    for at in range(lax.axis_size("dp")):
        mine = (at // stride) % size
        pairs.append((at, at + ((mine + step) % size - mine) * stride))
    return lax.ppermute(value, "dp", pairs)


def swap_tensor(value):
    return lax.ppermute(value, "tensor", [(0, 1), (1, 0)])


def tie(value, *others):
    return lax.optimization_barrier((value,) + others)[0]


join = lambda *values: lax.optimization_barrier(values)


def spread_outer(value, digits):
    for digit in reversed(digits[:-2]):
        got = [value] + [rotate(value, digit, step) for step in range(1, digit[1])]
        value = jnp.stack(got)
    return value.reshape((-1,) + value.shape[-2:])


def assemble_kernel(sizes, cuts, at, *refs):
    parts, wholes = refs[:4], refs[4:]
    outer = sizes[:-2]
    me, digits = at[DP], []
    for size in reversed(sizes):
        digits.append(lax.rem(me, size))
        me = lax.div(me, size)
    digits = digits[::-1]
    for swap_core in range(2):
        for swap_x in range(2):
            source = parts[2 * swap_core + swap_x]
            for slot in range(source.shape[0]):
                left, steps = slot, []
                for size in reversed(outer):
                    steps.append(left % size)
                    left //= size
                place = 0
                for size, digit, step in zip(outer, digits, steps[::-1]):
                    place = place * size + lax.rem(digit + (size - step), size)
                x, core = digits[-2], digits[-1]
                place = place * 2 + (1 - x if swap_x else x)
                place = place * 2 + (1 - core if swap_core else core)
                for whole, low, high in zip(wholes, cuts[:-1], cuts[1:]):
                    whole[place] = source[slot, :, low:high]


def assemble(at, mine, x_got, digits, *cuts):
    core = digits[-1]
    parts = [mine, x_got, rotate(mine, core, 1), rotate(x_got, core, 1)]
    slots, rows, cols = mine.shape
    cuts = (0, *cuts, cols)
    outs = [low_of(4 * slots, rows, b - a) for a, b in zip(cuts[:-1], cuts[1:])]
    sizes = tuple(size for _, size in digits)
    wholes = call(functools.partial(assemble_kernel, sizes, cuts), outs, at, *parts)
    wholes = [whole.reshape(4 * slots * rows, -1) for whole in wholes]
    return wholes if len(wholes) > 1 else wholes[0]


def columns_kernel(part, small_rows, at, weight, vectors, gains, memory, up, out, kept, sent, turn):
    lines, width = weight.shape[0], weight.shape[1] // 3
    first = at[T] == 0
    for pair in range(part // PAIR):
        for kind in range(3):
            low = kind * width + pair * PAIR
            a, b = weight[:, low : low + PAIR], weight[:, low + part : low + part + PAIR]
            here = (3 * pair + kind) * PAIR
            kept[:, here : here + PAIR] = jnp.where(first, a, b)
            sent[:, here : here + PAIR] = jnp.where(first, b, a)
    turn[...] = jnp.zeros_like(turn)
    for source, (low, high) in zip((memory, vectors, gains, up), small_rows):
        turn[low:high, :lines] = source[...].astype(WIDE)
    columns = turn[...].T[:lines].astype(LOW)
    for target in (kept, sent):
        target[:, 3 * part : 3 * part + PAIR] = columns
        target[:, 3 * part + PAIR :] = out[...]


def pair_kernel(at, kept, got, pair):
    lines = kept.shape[0]
    first = at[T] == 0
    pair[:lines] = jnp.where(first, kept[...], got[...])
    pair[lines:] = jnp.where(first, got[...], kept[...])


def put_blocks(total, kept, sent, core, at):
    groups, rows, _ = kept.shape
    cols = total.shape[1]
    total = total.astype(LOW).reshape(2 * groups, rows, cols)
    second = core == 1
    for group in range(groups):
        even, odd = total[2 * group], total[2 * group + 1]
        kept[group, :, at : at + cols] = jnp.where(second, odd, even)
        sent[group, :, at : at + cols] = jnp.where(second, even, odd)


def put_gradient(a, b, outs, core, tile=384, own=None):
    for low in range(0, b.shape[1], tile):
        total = tn(a[...], b[:, low : low + tile])
        if own is not None:
            total = total + own[:, low : low + tile]
        if len(outs) == 1:
            outs[0][:, low : low + tile] = total.astype(LOW)
        else:
            put_blocks(total, *outs, core, low)


def gradient_outs(width, cols, dp_count):
    rows = width // dp_count
    if rows % 16:
        return [low_of(width, cols)]
    return [low_of(dp_count // 2, rows, cols)] * 2


def split_cores(outs, dp_count, core):
    if len(outs) == 2:
        return outs
    whole = outs[0].reshape(dp_count // 2, 2, -1, outs[0].shape[1])
    take = lambda which: lax.dynamic_index_in_dim(whole, which, 1, keepdims=False)
    return take(core), take(1 - core)


def gradient_kernel(at, a, b, *outs):
    put_gradient(a, b, outs, at[CORE])


def own_kernel(at, a_down, b_down, a_up, b_up, down, up, sums):
    tile = 384
    for low in range(0, b_down.shape[1], tile):
        here = slice(low, low + tile)
        down[:, here] = tn(a_down[...], b_down[:, here])
        up[:, here] = tn(a_up[...], b_up[:, here])
    sums[...] = jnp.sum(b_up[...].astype(WIDE), axis=0, keepdims=True)


def rest_kernel(at, own, a, b, *outs):
    put_gradient(a, b, outs, at[CORE], own=own)


def rest_sums_kernel(spots, at, own, own_sums, a, b, target, sums, *outs):
    put_gradient(a, b, outs, at[CORE], own=own)
    total = (own_sums[...] + jnp.sum(b[...].astype(WIDE), axis=0, keepdims=True)).astype(LOW)
    total = jnp.broadcast_to(total, (8, total.shape[1]))
    for spot in range(spots):
        sums[spot : spot + 1, :] = nt(total, one_hot(target, spot, total.shape[1]))[:1]


def one_hot(target, spot, count):
    at = lax.broadcasted_iota(jnp.int32, (target.shape[0], count), 1)
    return (at == target[:, :1] + spot * target[0, 1]).astype(WIDE).astype(LOW)


def up_row_kernel(first_row, spots, at, small, target, row):
    part = target.shape[0]
    total = jnp.zeros((8, row.shape[1]), WIDE)
    for spot in range(spots):
        line = small[first_row + spot : first_row + spot + 1, :]
        line = jnp.where(at[T] == 0, line[:, :part], line[:, part:]).astype(LOW)
        line = jnp.broadcast_to(line, (8, part))
        total = total + nn(line, one_hot(target, spot, row.shape[1]))
    row[...] = jnp.broadcast_to(total[:1], row.shape)


def halve_kernel(at, mine, got, kept, sent):
    x = at[X]
    for group in range(kept.shape[0]):
        for other, out in ((0, kept), (1, sent)):
            place = 2 * group + (1 - x if other else x)
            out[group] = (mine[place].astype(WIDE) + got[place].astype(WIDE)).astype(LOW)


def halve(at, mine, got):
    groups, rows, cols = mine.shape
    return call(halve_kernel, [low_of(groups // 2, rows, cols)] * 2, at, mine, got)


def parts_kernel(size, count, at, *refs):
    mine, got, outs = refs[:count], refs[count : 2 * count], refs[2 * count :]
    me = at[OUTER]
    for group in range(outs[0].shape[0]):
        low = 0
        for a, b in zip(mine, got):
            high = low + a.shape[2]
            for step, out in enumerate(outs):
                place = group * size + lax.rem(me + step, size)
                total = a[place].astype(WIDE) + b[place].astype(WIDE)
                out[group, :, low:high] = total.astype(out.dtype)
            low = high


def outer_parts(at, mine, got, digits):
    size = digits[-3][1]
    blocks, rows, _ = mine[0].shape
    cols = sum(array.shape[2] for array in mine)
    shape = (blocks // size, rows, cols)
    outs = [wide_of(*shape)] + [low_of(*shape)] * (size - 1)
    kept, *sent = call(
        functools.partial(parts_kernel, size, len(mine)), outs, at, *mine, *got
    )
    return kept, sent


def outer_send(sent, digits):
    return [rotate(part, digits[-3], step + 1) for step, part in enumerate(sent)]


def outer_sum(kept, got, digits):
    for part in got:
        kept = kept + part.astype(WIDE)
    for digit in reversed(digits[:-3]):
        size = digit[1]
        kept = kept.reshape((-1, size) + kept.shape[1:])
        at = digit_at(digit)
        take = lambda step: lax.dynamic_index_in_dim(kept, (at + step) % size, 1, keepdims=False)
        total = take(0)
        for step in range(1, size):
            total = total + rotate(take(step).astype(LOW), digit, step).astype(WIDE)
        kept = total
    return kept[0]


def fill_mask(mask, at, half_rows, mem_count, starts):
    rows = mask.shape[0]
    padded = rows // 2

    def places(shape, axis):
        spot = lax.broadcasted_iota(jnp.int32, shape, axis)
        second = spot >= padded
        within = jnp.where(second, spot - padded, spot)
        pos = within + jnp.where(second, half_rows, 0) - mem_count
        doc = jnp.zeros(shape, jnp.int32)
        for i in range(starts):
            doc = doc + (at[STARTS + i] <= pos).astype(jnp.int32)
        return within < half_rows, pos, doc

    _, q_pos, q_doc = places((rows, 1), 0)
    real, k_pos, k_doc = places((1, rows), 1)
    key_ok = real & (k_pos < at[LENGTH])
    for low in range(0, rows, CHUNK):
        qp, qd = q_pos[low : low + CHUNK], q_doc[low : low + CHUNK]
        same = (qd == k_doc) | (qp < 0) | (k_pos < 0)
        mask[low : low + CHUNK, :] = jnp.where(same & key_ok, 0.0, -1e9)


def lanes(pair, count):
    return pl.ds(pl.multiple_of(pair * count, PAIR), count)


def forward_kernel(
    half_rows, mem_count, starts, first_bias,
    at, own, other, w, qkv, mix_own, mix_sent, lse, x, small, mask, s, p, mixed,
):
    rows, padded = x.shape[0], own.shape[0]
    t = at[T]
    part = mix_own.shape[1]
    fill_mask(mask, at, half_rows, mem_count, starts)
    lse[...] = jnp.zeros_like(lse)
    small[...] = w[:, 3 * part :].astype(WIDE).T[: small.shape[0]]
    x[pl.ds(pl.multiple_of(t * padded, 16), padded), :] = own[...]
    x[pl.ds(pl.multiple_of((1 - t) * padded, 16), padded), :] = other[...]
    row = lax.broadcasted_iota(jnp.int32, (32, 1), 0)
    fresh = (row < mem_count) & (at[FRESH] == 1)
    x[:32, :] = jnp.where(fresh, small[:32, :], x[:32, :].astype(WIDE)).astype(LOW)
    lane = lax.broadcasted_iota(jnp.int32, (1, PAIR), 1)
    scale = jnp.where(lax.broadcasted_iota(jnp.int32, (1, 3 * PAIR), 1) < PAIR, 0.125, 1.0)

    def one_pair(pair, _):
        here = pl.ds(pl.multiple_of(t * part + pair * PAIR, PAIR), PAIR)
        q_bias = small[first_bias : first_bias + 1, here]
        v_bias = small[first_bias + 1 : first_bias + 2, here]
        bias = jnp.concatenate([q_bias, jnp.zeros_like(q_bias), v_bias], axis=1)
        got = (nn(x[...], w[:, lanes(pair, 3 * PAIR)]) + bias).astype(LOW)
        got = (got.astype(WIDE) * scale).astype(LOW)
        qkv[:, lanes(pair, 3 * PAIR)] = got
        keys, values = got[:, PAIR : 2 * PAIR], got[:, 2 * PAIR :]
        for h in range(2):
            mine = (lane < HEAD) if h == 0 else (lane >= HEAD)
            s[...] = nt(jnp.where(mine, got[:, :PAIR], jnp.zeros((), LOW)), keys)

            def body(i, _):
                here = pl.ds(pl.multiple_of(i * CHUNK, CHUNK), CHUNK)
                v = s[here, :] + mask[here, :]
                top = jnp.max(v, axis=-1, keepdims=True)
                e = jnp.exp(v - top)
                total = jnp.sum(e, axis=-1, keepdims=True)
                p[here, :] = (e * (1.0 / total)).astype(LOW)
                spot = lane == 2 * pair + h
                lse[here, :] = jnp.where(spot, top + jnp.log(total), lse[here, :])
                return 0

            lax.fori_loop(0, rows // CHUNK, body, 0, unroll=True)
            out = nn(p[...], values).astype(LOW)
            if h == 0:
                mixed[...] = out
            else:
                mixed[...] = jnp.where(mine, out, mixed[...])
        mix_own[:, lanes(pair, PAIR)] = mixed[pl.ds(pl.multiple_of(t * padded, 16), padded), :]
        mix_sent[:, lanes(pair, PAIR)] = mixed[
            pl.ds(pl.multiple_of((1 - t) * padded, 16), padded), :
        ]
        return 0

    lax.fori_loop(0, part // PAIR, one_pair, 0)


def backward_kernel(
    half_rows, mem_count, starts, at, qkv, own, got, lse, dproj, sums, mask, s, dp, p, ds, dmix
):
    rows, padded = qkv.shape[0], own.shape[0]
    part = own.shape[1]
    t = at[T]
    fill_mask(mask, at, half_rows, mem_count, starts)
    dmix[pl.ds(pl.multiple_of(t * padded, 16), padded), :] = own[...]
    dmix[pl.ds(pl.multiple_of((1 - t) * padded, 16), padded), :] = got[...]
    lane = lax.broadcasted_iota(jnp.int32, (1, PAIR), 1)
    zero = jnp.zeros((), LOW)

    def one_pair(pair, _):
        here = lanes(pair, 3 * PAIR)
        whole = qkv[:, here]
        keys, values = whole[:, PAIR : 2 * PAIR], whole[:, 2 * PAIR :]
        dm_pair = dmix[:, lanes(pair, PAIR)]
        parts = []
        for h in range(2):
            mine = (lane < HEAD) if h == 0 else (lane >= HEAD)
            q = jnp.where(mine, whole[:, :PAIR], zero)
            dm = jnp.where(mine, dm_pair, zero)
            s[...] = nt(q, keys)
            dp[...] = nt(dm, values)

            def body(i, _):
                here = pl.ds(pl.multiple_of(i * CHUNK, CHUNK), CHUNK)
                spot = lane == 2 * pair + h
                stat = jnp.sum(jnp.where(spot, lse[here, :], 0.0), axis=-1, keepdims=True)
                e = jnp.exp(s[here, :] + mask[here, :] - stat)
                d = dp[here, :]
                dot = jnp.sum(e * d, axis=-1, keepdims=True)
                p[here, :] = e.astype(LOW)
                ds[here, :] = (e * (d - dot)).astype(LOW)
                return 0

            lax.fori_loop(0, rows // CHUNK, body, 0, unroll=True)
            parts.append((nn(ds[...], keys) * 0.125, tn(ds[...], q), tn(p[...], dm)))
        dq = jnp.where(lane < HEAD, parts[0][0], parts[1][0])
        dk, dv = parts[0][1] + parts[1][1], parts[0][2] + parts[1][2]
        out = jnp.concatenate([dq, dk, dv], axis=1).astype(LOW)
        dproj[:, here] = out
        sums[:, here] = jnp.sum(out.astype(WIDE), axis=0, keepdims=True)
        return 0

    lax.fori_loop(0, part // PAIR, one_pair, 0)


def projection_back_kernel(
    small_rows, at, layer_in, d_projected, proj_sums, sums_one, sums_two, up_sums, wqkv, d_attn,
    *outs,
):
    d_own, d_sent = outs[:2]
    grads, turn = outs[2:-1], outs[-1]
    padded, part = d_own.shape[0], up_sums.shape[1]
    cols = d_projected.shape[1]
    t = at[T]
    first = t == 0
    half = lambda which: d_projected[pl.ds(pl.multiple_of(which * padded, 16), padded), :]
    weights = wqkv[:, :cols]
    own = nt(half(t), weights)
    other = nt(half(1 - t), weights)
    d_own[...] = d_attn[...] + own
    d_sent[...] = other.astype(LOW)
    turn[...] = jnp.zeros_like(turn)
    (m0, m1), (v0, _), (g0, _), (u0, _) = small_rows
    count = m1 - m0
    memory = jnp.where(first, own[:count] + d_attn[:count, :], other[:count])
    turn[m0:m1, :] = jnp.where(at[FRESH] == 1, memory, 0.0)
    sums = [
        jnp.concatenate(
            [proj_sums[:, (3 * p + k) * PAIR : (3 * p + k + 1) * PAIR] for p in range(part // PAIR)],
            axis=1,
        )
        for k in (0, 2)
    ]
    for value, low in zip(sums + [up_sums[...]], (v0, v0 + 1, u0)):
        high = low + value.shape[0]
        turn[low:high, :part] = jnp.where(first, value, 0.0)
        turn[low:high, part:] = jnp.where(first, 0.0, value)
    turn[v0 + 2 : v0 + 4, :] = sums_one[0:2, :]
    turn[v0 + 4 : v0 + 6, :] = sums_two[0:2, :]
    turn[g0 : g0 + 1, :] = sums_one[2:3, :]
    turn[g0 + 1 : g0 + 2, :] = sums_two[2:3, :]
    small = turn[...].T
    put_gradient(layer_in, d_projected, grads, at[CORE])
    if len(grads) == 1:
        grads[0][:, cols:] = small.astype(LOW)
    else:
        put_blocks(small, *grads, at[CORE], cols)


def halves_kernel(count, at, *refs):
    parts, (mine, give) = refs[:count], refs[count:]
    lines = mine.shape[0]
    total = parts[0][...]
    for part in parts[1:]:
        total = total + part[...].astype(WIDE)
    first = at[T] == 0
    mine[...] = jnp.where(first, total[:lines], total[lines:])
    give[...] = jnp.where(first, total[lines:], total[:lines]).astype(LOW)


def finish_kernel(part, small_rows, at, mine, got, qkv, out, memory, vectors, gains, up, turn):
    lines = mine.shape[0]
    cols, width = 3 * part, 2 * part
    first = at[T] == 0
    for pair in range(part // PAIR):
        for kind in range(3):
            here = (3 * pair + kind) * PAIR
            a = mine[:, here : here + PAIR]
            b = got[:, here : here + PAIR].astype(WIDE)
            low = kind * width + pair * PAIR
            qkv[:, low : low + PAIR] = jnp.where(first, a, b)
            qkv[:, low + part : low + part + PAIR] = jnp.where(first, b, a)
    turn[...] = jnp.zeros_like(turn)
    turn[:lines, :] = mine[:, cols : cols + PAIR] + got[:, cols : cols + PAIR].astype(WIDE)
    out[...] = mine[:, cols + PAIR :] + got[:, cols + PAIR :].astype(WIDE)
    small = turn[...].T
    for target, (low, high) in zip((memory, vectors, gains, up), small_rows):
        target[...] = small[low:high, :lines]


def spread_of(v):
    return jnp.mean(v, axis=-1, keepdims=True)


def first_norm_kernel(bias, gain, at, own, got, wout, layer_in, small, mixed, unit, scale, normed, s):
    padded, part = own.shape
    first = at[T] == 0
    mixed[:, :part] = jnp.where(first, own[...], got[...])
    mixed[:, part:] = jnp.where(first, got[...], own[...])
    s[...] = nn(mixed[...], wout[...])
    for low in range(0, padded, ROWS):
        here = slice(low, low + ROWS)
        rows = layer_in[pl.ds(pl.multiple_of(at[T] * padded + low, ROWS), ROWS), :]
        total = rows.astype(WIDE) + (s[here, :] + small[bias + 2 : bias + 3, :])
        centered = total - spread_of(total)
        factor = lax.rsqrt(spread_of(centered * centered) + NORM_EPSILON)
        value = centered * factor
        unit[here, :] = value
        scale[here, :] = jnp.broadcast_to(factor, (ROWS, PAIR))
        value = value * small[gain : gain + 1, :] + small[bias + 3 : bias + 4, :]
        normed[here, :] = value.astype(LOW)


def add_sums(sums, values):
    sums[...] = jnp.zeros_like(sums)
    for n, value in enumerate(values):
        sums[n : n + 1, :] = jnp.sum(value, axis=0, keepdims=True)


def second_norm_kernel(
    bias, gain, at, unit, small, own, got, d_out, layer_out, d_second, d_ffn, sums
):
    padded, width = unit.shape
    real = d_out.shape[0]
    totals = [jnp.zeros((ROWS, width), WIDE)] * 3
    for low in range(0, padded, ROWS):
        here = slice(low, low + ROWS)
        count = min(ROWS, real - low)
        first = unit[here, :] * small[gain : gain + 1, :] + small[bias + 3 : bias + 4, :]
        ffn = own[here, :] + got[here, :].astype(WIDE) + small[bias + 4 : bias + 5, :]
        total = first + ffn
        centered = total - spread_of(total)
        factor = lax.rsqrt(spread_of(centered * centered) + NORM_EPSILON)
        value = centered * factor
        out = value * small[gain + 1 : gain + 2, :] + small[bias + 5 : bias + 6, :]
        layer_out[low : low + count, :] = out[:count].astype(LOW)
        cotangent = d_out[low : low + count, :].astype(WIDE)
        if count < ROWS:
            cotangent = jnp.concatenate(
                [cotangent, jnp.zeros((ROWS - count, width), WIDE)], axis=0
            )
        d_unit = cotangent * small[gain + 1 : gain + 2, :]
        back = factor * (d_unit - spread_of(d_unit) - value * spread_of(d_unit * value))
        d_second[here, :] = back
        rounded = back.astype(LOW)
        d_ffn[here, :] = rounded
        terms = (rounded.astype(WIDE), cotangent, cotangent * value)
        totals = [a + b for a, b in zip(totals, terms)]
    add_sums(sums, totals)


def first_back_kernel(
    gain, at, d_second, own, got, unit, scale, small, wout, d_attn_in, d_attn, mix_own, mix_sent, sums
):
    padded, width = unit.shape
    part = mix_own.shape[1]
    totals = [jnp.zeros((ROWS, width), WIDE)] * 3
    for low in range(0, padded, ROWS):
        here = slice(low, low + ROWS)
        cotangent = d_second[here, :] + own[here, :] + got[here, :].astype(WIDE)
        value = unit[here, :]
        d_unit = cotangent * small[gain : gain + 1, :]
        back = d_unit - spread_of(d_unit) - value * spread_of(d_unit * value)
        back = scale[here, :1] * back
        d_attn_in[here, :] = back
        rounded = back.astype(LOW)
        d_attn[here, :] = rounded
        terms = (rounded.astype(WIDE), cotangent, cotangent * value)
        totals = [a + b for a, b in zip(totals, terms)]
    add_sums(sums, totals)
    mixed = nt(d_attn[...], wout[...]).astype(LOW)
    first = at[T] == 0
    mix_own[...] = jnp.where(first, mixed[:, :part], mixed[:, part:])
    mix_sent[...] = jnp.where(first, mixed[:, part:], mixed[:, :part])


def rows_kernel(mem_count, at, own, got, out):
    real = out.shape[0]
    row = lax.broadcasted_iota(jnp.int32, (32, 1), 0)
    fresh = (row < mem_count) & (at[FRESH] == 1) & (at[T] == 0)
    out[:32, :] = jnp.where(fresh, 0.0, own[:32, :] + got[:32, :].astype(WIDE))
    out[32:, :] = own[32:real, :] + got[32:real, :].astype(WIDE)


def gelu_parts(pre):
    cdf = 0.5 * (1.0 + lax.erf(pre * 0.7071067811865476))
    density = jnp.exp(-0.5 * pre * pre) * 0.3989422804014327
    return pre * cdf, cdf + pre * density


def shards(
    rows_in,
    d_out,
    starts,
    lengths,
    resets,
    qkv_weight,
    out_weight,
    bias_vec,
    gains,
    mem_init,
    ffn_up,
    up_bias,
    ffn_down,
):
    half_rows, seg_count, width = rows_in.shape
    assert seg_count == 1
    dp_count, t_count = lax.axis_size("dp"), lax.axis_size("tensor")
    assert t_count == 2
    digits = digits_of(dp_count)
    x_digit, core_digit = digits[-2:]
    padded = ceil_to(half_rows, 16)
    rows = 2 * padded
    mem_count = mem_init.shape[0]
    part = HEADS // t_count * HEAD
    cols = 3 * part
    hidden_mine = ffn_up.shape[1]
    feat = bias_vec.shape[1]
    lines = qkv_weight.shape[0]
    spots = up_bias.shape[0] // feat
    doc_count = starts.shape[1]
    counts = (mem_count, bias_vec.shape[0], gains.shape[0], spots)
    edges = [sum(counts[:n]) for n in range(len(counts) + 1)]
    small_rows = tuple(zip(edges[:-1], edges[1:]))
    bias, gain = edges[1], edges[2]
    target = np.arange(part)
    target = (target // feat) * (spots * feat) + target % feat
    target = np.stack([target, np.full(part, feat)], axis=1).astype(np.int32)

    integers = [
        lax.axis_index("tensor"),
        digit_at(x_digit),
        digit_at(core_digit),
        digit_at(digits[-3]),
        lax.axis_index("dp"),
        resets[0],
        lengths[0],
    ]
    at = jnp.concatenate([jnp.stack(integers).astype(jnp.int32), starts[0]])

    kept, sent = call(
        functools.partial(columns_kernel, part, small_rows),
        [low_of(lines, cols + PAIR + width)] * 2,
        lax.axis_index("tensor").astype(jnp.int32).reshape(1),
        qkv_weight, bias_vec, gains, mem_init, up_bias.reshape(spots, feat), out_weight,
        scratch=[pltpu.VMEM((PAIR, PAIR), WIDE)],
        room=48 << 20,
    )
    got = swap_tensor(sent)
    (first_pair,) = call(pair_kernel, [low_of(2 * lines, kept.shape[1])], at, kept, got)
    rows_low = jnp.pad(rows_in[:, 0, :], ((0, padded - half_rows), (0, 0)))
    rows_other = swap_tensor(tie(rows_low, first_pair))
    first_z = spread_outer(first_pair, digits)
    first_z, rows_other = join(first_z, rows_other)
    first_x = rotate(first_z, x_digit, 1)
    up_z = spread_outer(tie(ffn_up, first_z), digits)
    first_z, first_x, up_z = join(first_z, first_x, up_z)
    wqkv, wout = assemble(at, first_z, first_x, digits, cols + PAIR)
    up_x = rotate(up_z, x_digit, 1)
    down_z = spread_outer(tie(ffn_down.T, up_z), digits)

    projected, mix_own, mix_sent, log_total, layer_in, small = call(
        functools.partial(forward_kernel, half_rows, mem_count, doc_count, bias),
        [
            low_of(rows, cols),
            low_of(padded, part),
            low_of(padded, part),
            wide_of(rows, PAIR),
            low_of(rows, width),
            wide_of(edges[-1], width),
        ],
        at, rows_low, rows_other, wqkv,
        scratch=[
            pltpu.VMEM((rows, rows), WIDE),
            pltpu.VMEM((rows, rows), WIDE),
            pltpu.VMEM((rows, rows), LOW),
            pltpu.VMEM((rows, PAIR), LOW),
        ],
    )
    mix_got = swap_tensor(mix_sent)
    mixed, unit, scale, normed_own = call(
        functools.partial(first_norm_kernel, bias, gain),
        [low_of(padded, width), wide_of(padded, width), wide_of(padded, PAIR), low_of(padded, width)],
        at, mix_own, mix_got, wout, layer_in, small,
        scratch=[pltpu.VMEM((padded, width), WIDE)],
    )

    normed_got = swap_tensor(normed_own)
    up_x, up_z, down_z = tie(up_x, mix_sent), tie(up_z, mix_sent), tie(down_z, mix_sent)
    up = assemble(at, up_z, up_x, digits)
    (up_b,) = call(
        functools.partial(up_row_kernel, edges[3], spots),
        [wide_of(ROWS, hidden_mine)], at, small, jnp.asarray(target),
    )
    down_x = rotate(down_z, x_digit, 1)
    normed_got, down_x, up_b, up = join(normed_got, down_x, up_b, up)
    down_t = assemble(at, down_z, down_x, digits)

    def feed_forward(rows):
        pre_act = nn(rows, up).reshape(-1, *up_b.shape) + up_b
        hidden, slope = (part.reshape(rows.shape[0], -1) for part in gelu_parts(pre_act))
        hidden = hidden.astype(LOW)
        return hidden, slope, nt(hidden, down_t)

    hidden_got, slope_got, ffn_sent = feed_forward(normed_got)
    ffn_sent = ffn_sent.astype(LOW)
    ffn_got = swap_tensor(ffn_sent)
    hidden_own, slope_own, ffn_own = feed_forward(tie(normed_own, ffn_sent))
    layer_out, d_second, d_ffn_own, sums_two = call(
        functools.partial(second_norm_kernel, bias, gain),
        [low_of(half_rows, width), wide_of(padded, width), low_of(padded, width), wide_of(8, width)],
        at, unit, small, ffn_own, ffn_got, d_out.reshape(half_rows, width),
    )

    d_ffn_got = swap_tensor(d_ffn_own)

    def feed_back(rows, slope):
        d_pre = (slope * nn(rows, down_t)).astype(LOW)
        return d_pre, nt(d_pre, up)

    d_pre_own, d_first_own = feed_back(d_ffn_own, slope_own)
    down_own, up_own, sums_own = call(
        own_kernel,
        [wide_of(width, hidden_mine), wide_of(width, hidden_mine), wide_of(1, hidden_mine)],
        at, d_ffn_own, hidden_own, normed_own, d_pre_own,
    )
    d_ffn_got, d_first_own, down_own, up_own = join(d_ffn_got, d_first_own, down_own, up_own)
    d_pre_got, d_first_sent = feed_back(d_ffn_got, slope_got)
    d_first_sent = d_first_sent.astype(LOW)
    d_first_got = swap_tensor(d_first_sent)

    core = lax.axis_index("dp") % 2
    outs = gradient_outs(width, hidden_mine, dp_count)
    down_grads = call(
        rest_kernel, outs, at, down_own, tie(d_ffn_got, d_first_sent), hidden_got
    )
    down_kept, down_sent = split_cores(down_grads, dp_count, core)
    down_kept, down_sent = halve(at, down_kept, rotate(down_sent, core_digit, 1))
    down_got = rotate(down_sent, x_digit, 1)
    up_sums, *up_grads = call(
        functools.partial(rest_sums_kernel, spots), [wide_of(spots, part)] + outs, at,
        up_own, sums_own, normed_got, tie(d_pre_got, d_first_sent), jnp.asarray(target),
    )
    up_kept, up_sent = split_cores(up_grads, dp_count, core)
    up_kept, up_sent = halve(at, up_kept, rotate(up_sent, core_digit, 1))
    up_got = rotate(tie(up_sent, down_got), x_digit, 1)

    d_attn_in, d_attn, d_mix_own, d_mix_sent, sums_one = call(
        functools.partial(first_back_kernel, gain),
        [
            wide_of(padded, width),
            low_of(padded, width),
            low_of(padded, part),
            low_of(padded, part),
            wide_of(8, width),
        ],
        at, d_second, d_first_own, d_first_got, unit, scale, small, wout,
    )
    d_mix_got = swap_tensor(d_mix_sent)
    out_grads = call(
        gradient_kernel, gradient_outs(width, width, dp_count), at, mixed, tie(d_attn, d_mix_sent)
    )
    out_kept, out_sent = split_cores(out_grads, dp_count, core)
    out_kept, out_sent = halve(at, out_kept, rotate(out_sent, core_digit, 1))
    out_got = rotate(tie(out_sent, up_got), x_digit, 1)
    down_kept, down_sent = outer_parts(at, [down_kept], [down_got], digits)
    d_mix_got, *down_sent = join(d_mix_got, *down_sent)
    down_got = outer_send(down_sent, digits)

    d_projected, proj_sums = call(
        functools.partial(backward_kernel, half_rows, mem_count, doc_count),
        [low_of(rows, cols), wide_of(1, cols)],
        at, projected, d_mix_own, d_mix_got, log_total,
        scratch=[
            pltpu.VMEM((rows, rows), WIDE),
            pltpu.VMEM((rows, rows), WIDE),
            pltpu.VMEM((rows, rows), WIDE),
            pltpu.VMEM((rows, rows), LOW),
            pltpu.VMEM((rows, rows), LOW),
            pltpu.VMEM((rows, part), LOW),
        ],
    )
    up_kept, up_sent = outer_parts(at, [up_kept], [up_got], digits)
    d_in_own, d_in_sent, *qkv_grads = call(
        functools.partial(projection_back_kernel, small_rows),
        [wide_of(padded, width), low_of(padded, width)]
        + gradient_outs(width, cols + PAIR, dp_count),
        at, layer_in, d_projected, proj_sums, sums_one, sums_two, up_sums, wqkv, d_attn_in,
        scratch=[pltpu.VMEM((PAIR, width), WIDE)],
    )
    qkv_kept, qkv_sent = split_cores(qkv_grads, dp_count, core)
    qkv_sent, *up_sent = join(qkv_sent, *up_sent, *down_got)[: 1 + len(up_sent)]
    qkv_kept, qkv_sent = halve(at, qkv_kept, rotate(qkv_sent, core_digit, 1))

    qkv_got = rotate(qkv_sent, x_digit, 1)
    up_got = outer_send(up_sent, digits)
    qkv_got, d_in_sent, out_got, *up_got = join(qkv_got, d_in_sent, out_got, *up_got)
    d_in_got = swap_tensor(d_in_sent)
    both_kept, both_sent = outer_parts(at, [qkv_kept, out_kept], [qkv_got, out_got], digits)
    both_got = outer_send(both_sent, digits)
    grad_ffn_down = outer_sum(down_kept, down_got, digits)
    grad_ffn_up = outer_sum(up_kept, up_got, digits)
    (grad_rows,) = call(
        functools.partial(rows_kernel, mem_count), [wide_of(half_rows, width)], at, d_in_own, d_in_got
    )
    grad_ffn_down, grad_ffn_up, grad_rows, *both_got = join(
        grad_ffn_down, grad_ffn_up, grad_rows, *both_got
    )

    if len(digits) == 3:
        parts = [both_kept[0], *[part[0] for part in both_got]]
    else:
        parts = [outer_sum(both_kept, both_got, digits)]
    mine, give = call(
        functools.partial(halves_kernel, len(parts)),
        [wide_of(lines, kept.shape[1]), low_of(lines, kept.shape[1])],
        at, *parts,
    )
    grad_qkv, grad_out_weight, grad_mem, grad_vec, grad_gains, grad_up_bias = call(
        functools.partial(finish_kernel, part, small_rows),
        [wide_of(lines, 3 * width), wide_of(lines, width)] + [wide_of(n, feat) for n in counts],
        at, mine, swap_tensor(give),
        scratch=[pltpu.VMEM((PAIR, PAIR), WIDE)],
    )
    return (
        layer_out.reshape(half_rows, 1, width),
        grad_rows.reshape(half_rows, 1, width),
        grad_qkv,
        grad_out_weight,
        grad_vec,
        grad_gains,
        grad_mem,
        grad_ffn_up,
        grad_up_bias.reshape(up_bias.shape),
        grad_ffn_down.T,
    )


def solution(mesh):
    both = ("dp", "tensor")
    in_specs = (
        P("tensor", "dp", None),
        P("tensor", "dp", None),
        P("dp", None),
        P("dp"),
        P("dp"),
        P(both, None),
        P(both, None),
        P(None, both),
        P(None, both),
        P(None, both),
        P("dp", "tensor"),
        P(both),
        P("tensor", "dp"),
    )
    out_specs = (
        P("tensor", "dp", None),
        P("tensor", "dp", None),
        P(both, None),
        P(both, None),
        P(None, both),
        P(None, both),
        P(None, both),
        P("dp", "tensor"),
        P(both),
        P("tensor", "dp"),
    )
    return jax.shard_map(shards, mesh=mesh, in_specs=in_specs, out_specs=out_specs, check_vma=False)
```

profile of v0, /device:TPU:0, one launch (start us, length us, event | category | flops | bytes accessed | tf_op | source)
XLA Modules:
  0.0 211.4 jit_solution(17848225999491701858)
XLA Ops:
  1.4 0.9 copy-done.2
  5.2 3.0 %collective-permute-start = (bf16[24,2048]{1,0:T(8,128)(2,1)S(1)}, bf16[24,2048]{1,0:T(8,128)(2,1)S(1)}, u32[]{:S(2)}, u32[]{:S(2)}) collective-permute-start(bf16[24,2048]{1,0:T(8,128)(2,1)S(1)} %get-tuple-element.123), channel_id=1, source_target_pairs={{0,1},{1,0},{2,3},{3,2},{4,5},{5,4},{6,7},{7,6},{8,9},{9,8},{10,11... | collective-permute-start | bytes 294920 | tf_op jit(solution)/shard_map/ppermute | solution.py:100
  11.5 4.0 %collective-permute-start.3 = (bf16[48,2048]{1,0:T(8,128)(2,1)S(1)}, bf16[48,2048]{1,0:T(8,128)(2,1)S(1)}, u32[]{:S(2)}, u32[]{:S(2)}) collective-permute-start(bf16[48,2048]{1,0:T(8,128)(2,1)S(1)} %shard_map.214), channel_id=1, source_target_pairs={{0,24},{2,26},{4,28},{6,30},{8,0},{10,2},{12,4},{14,6},{16,8},{18,... | collective-permute-start | bytes 589832 | tf_op jit(solution)/shard_map/ppermute | solution.py:96
  15.5 1.0 collective-permute-start.2
  16.5 1.1 pad.4.own
  17.6 1.6 collective-permute-start.4
  19.2 1.7 collective-permute-done.3
  20.8 4.3 %collective-permute-done.1 = bf16[48,2048]{1,0:T(8,128)(2,1)S(1)} collective-permute-done((bf16[48,2048]{1,0:T(8,128)(2,1)S(1)}, bf16[48,2048]{1,0:T(8,128)(2,1)S(1)}, u32[]{:S(2)}, u32[]{:S(2)}) %collective-permute-start.1) | collective-permute-done | bytes 196640 | tf_op jit(solution)/shard_map/ppermute | solution.py:96
  25.1 6.1 %collective-permute-done.2 = bf16[48,2048]{1,0:T(8,128)(2,1)S(1)} collective-permute-done((bf16[48,2048]{1,0:T(8,128)(2,1)S(1)}, bf16[48,2048]{1,0:T(8,128)(2,1)S(1)}, u32[]{:S(2)}, u32[]{:S(2)}) %collective-permute-start.2) | collective-permute-done | bytes 196640 | tf_op jit(solution)/shard_map/ppermute | solution.py:96
  31.3 1.6 collective-permute-start.5
  32.9 3.0 %collective-permute-start.7 = (bf16[48,1536]{1,0:T(8,128)(2,1)S(1)}, bf16[48,1536]{1,0:T(8,128)(2,1)S(1)}, u32[]{:S(2)}, u32[]{:S(2)}) collective-permute-start(bf16[48,1536]{1,0:T(8,128)(2,1)S(1)} %copy-done.7), channel_id=1, source_target_pairs={{0,16},{2,18},{4,20},{6,22},{8,24},{10,26},{12,28},{14,30},{16,0},... | collective-permute-start | bytes 442376 | tf_op jit(solution)/shard_map/ppermute | solution.py:96
  36.7 4.8 %collective-permute-done.6 = bf16[48,1536]{1,0:T(8,128)(2,1)S(1)} collective-permute-done((bf16[48,1536]{1,0:T(8,128)(2,1)S(1)}, bf16[48,1536]{1,0:T(8,128)(2,1)S(1)}, u32[]{:S(2)}, u32[]{:S(2)}) %collective-permute-start.6) | collective-permute-done | bytes 147488 | tf_op jit(solution)/shard_map/ppermute | solution.py:96
  41.5 4.1 %collective-permute-done.7 = bf16[48,1536]{1,0:T(8,128)(2,1)S(1)} collective-permute-done((bf16[48,1536]{1,0:T(8,128)(2,1)S(1)}, bf16[48,1536]{1,0:T(8,128)(2,1)S(1)}, u32[]{:S(2)}, u32[]{:S(2)}) %collective-permute-start.7) | collective-permute-done | bytes 147488 | tf_op jit(solution)/shard_map/ppermute | solution.py:96
  45.7 4.1 %collective-permute-done.5.refs_1_ = bf16[4,48,2048]{2,1,0:T(8,128)(2,1)S(1)} collective-permute-done((bf16[4,48,2048]{2,1,0:T(8,128)(2,1)S(1)}, bf16[4,48,2048]{2,1,0:T(8,128)(2,1)S(1)}, u32[]{:S(2)}, u32[]{:S(2)}) %collective-permute-start.5) | collective-permute-done | bytes 786464 | tf_op jit(solution)/shard_map/ppermute | solution.py:96
  50.3 1.5 collective-permute-start.17
  51.8 2.3 %collective-permute-start.14 = (bf16[48,1536]{1,0:T(8,128)(2,1)S(1)}, bf16[48,1536]{1,0:T(8,128)(2,1)S(1)}, u32[]{:S(2)}, u32[]{:S(2)}) collective-permute-start(bf16[48,1536]{1,0:T(8,128)(2,1)S(1)} %bitcast.81), channel_id=1, source_target_pairs={{0,16},{2,18},{4,20},{6,22},{8,24},{10,26},{12,28},{14,30},{16,0},... | collective-permute-start | bytes 442376 | tf_op jit(solution)/shard_map/ppermute | solution.py:96
  54.1 1.5 collective-permute-start.15
  56.4 9.1 %shard_map.216 = (bf16[544,1152]{1,0:T(8,128)(2,1)S(1)}, bf16[272,384]{1,0:T(8,128)(2,1)S(1)}, bf16[272,384]{1,0:T(8,128)(2,1)S(1)}, f32[544,128]{1,0:T(8,128)S(...) custom-call(s32[15]{0:T(128)S(1)} %concatenate.3.at, bf16[272,768]{1,0:T(8,128)(2,1)S(1)} %pad.4.own, ...), custom_call_target="tpu_custom_call" | custom-call | flops 1 | bytes 1 | tf_op jit(solution)/shard_map/pallas_call | solution.py:56
  65.4 1.6 collective-permute-start.11
  68.2 3.5 %collective-permute-done.11.got = bf16[272,384]{1,0:T(8,128)(2,1)S(1)} collective-permute-done((bf16[272,384]{1,0:T(8,128)(2,1)S(1)}, bf16[272,384]{1,0:T(8,128)(2,1)S(1)}, u32[]{:S(2)}, u32[]{:S(2)}) %collective-permute-start.11) | collective-permute-done | bytes 208928 | tf_op jit(solution)/shard_map/ppermute | solution.py:100
  71.7 1.3 shard_map.217
  73.0 1.6 collective-permute-start.12
  74.6 1.4 shard_map.218
  76.8 6.2 %collective-permute-done.16.refs_1_ = bf16[4,48,1536]{2,1,0:T(8,128)(2,1)S(1)} collective-permute-done((bf16[4,48,1536]{2,1,0:T(8,128)(2,1)S(1)}, bf16[4,48,1536]{2,1,0:T(8,128)(2,1)S(1)}, u32[]{:S(2)}, u32[]{:S(2)}) %collective-permute-start.16) | collective-permute-done | bytes 589856 | tf_op jit(solution)/shard_map/ppermute | solution.py:96
  83.2 0.9 multiply_convert_fusion.1
  84.1 0.9 collective-permute-done.21.refs_3_
  86.6 1.4 collective-permute-start.22
  88.0 0.9 multiply_convert_fusion
  89.8 8.5 %collective-permute-done.22.got = bf16[272,768]{1,0:T(8,128)(2,1)S(1)} collective-permute-done((bf16[272,768]{1,0:T(8,128)(2,1)S(1)}, bf16[272,768]{1,0:T(8,128)(2,1)S(1)}, u32[]{:S(2)}, u32[]{:S(2)}) %collective-permute-start.22) | collective-permute-done | bytes 417824 | tf_op jit(solution)/shard_map/ppermute | solution.py:100
  98.3 2.0 shard_map.221
  100.3 1.4 collective-permute-start.23
  101.7 1.0 fusion.b_up
  102.7 3.7 %shard_map.222 = (f32[768,1536]{1,0:T(8,128)S(1)}, f32[768,1536]{1,0:T(8,128)S(1)}, f32[1,1536]{1,0:T(1,128)S(1)}) custom-call(s32[15]{0:T(128)S(1)} %concatenate.3.at, bf16[272,768]{1,0:T(8,128)(2,1)S(1)} %get-tuple-element.149.a_down, bf16[272,1536]{1,0:T(8,128)(2,1)S(1)} %get-tuple-element.246.b_down, bf16[272,768]{1,0:T(8,128)(2,1)S(1)} %get-tuple-element.147.a_up, ...), custom_call_target="tpu_custom_call" | custom-call | flops 1 | bytes 1 | tf_op jit(solution)/shard_map/pallas_call | solution.py:56
  107.2 3.9 %collective-permute-done.23.a = bf16[272,768]{1,0:T(8,128)(2,1)S(1)} collective-permute-done((bf16[272,768]{1,0:T(8,128)(2,1)S(1)}, bf16[272,768]{1,0:T(8,128)(2,1)S(1)}, u32[]{:S(2)}, u32[]{:S(2)}) %collective-permute-start.23) | collective-permute-done | bytes 417824 | tf_op jit(solution)/shard_map/ppermute | solution.py:100
  111.2 1.0 fusion.1.b
  113.0 2.4 %shard_map.223 = (bf16[8,48,1536]{2,1,0:T(8,128)(2,1)S(1)}, bf16[8,48,1536]{2,1,0:T(8,128)(2,1)S(1)}) custom-call(s32[15]{0:T(128)S(1)} %concatenate.3.at, f32[768,1536]{1,0:T(8,128)S(1)} %get-tuple-element.152.own, bf16[272,768]{1,0:T(8,128)(2,1)S(1)} %collective-permute-done.23.a, bf16[272,1536]{1,0:T(8,128)(2,1)S(1)} %get-tuple-element.244.b), custom_call_target="tpu_custom_call" | custom-call | flops 1 | bytes 1 | tf_op jit(solution)/shard_map/pallas_call | solution.py:56
  115.5 3.6 %shard_map.227 = (f32[4,384]{1,0:T(4,128)S(1)}, bf16[8,48,1536]{2,1,0:T(8,128)(2,1)S(1)}, bf16[8,48,1536]{2,1,0:T(8,128)(2,1)S(1)}) custom-call(s32[15]{0:T(128)S(1)} %concatenate.3.at, f32[768,1536]{1,0:T(8,128)S(1)} %get-tuple-element.170.own, f32[1,1536]{1,0:T(1,128)S(1)} %get-tuple-element.171.own_sums, bf16[272,768]{1,0:T(8,128)(2,1)S(1)} %collective-permute-done.12.a, ...), custom_call_target="tpu_custom_call" | custom-call | flops 1 | bytes 1 | tf_op jit(solution)/shard_map/pallas_call | solution.py:56
  121.1 1.4 collective-permute-start.26
  123.3 12.5 %collective-permute-done.25.refs_1_ = bf16[4,48,1536]{2,1,0:T(8,128)(2,1)S(1)} collective-permute-done((bf16[4,48,1536]{2,1,0:T(8,128)(2,1)S(1)}, bf16[4,48,1536]{2,1,0:T(8,128)(2,1)S(1)}, u32[]{:S(2)}, u32[]{:S(2)}) %collective-permute-start.25) | collective-permute-done | bytes 589856 | tf_op jit(solution)/shard_map/ppermute | solution.py:96
  136.4 1.6 shard_map.226
  138.0 1.4 collective-permute-start.27
  140.1 3.9 %collective-permute-done.27.got = bf16[272,384]{1,0:T(8,128)(2,1)S(1)} collective-permute-done((bf16[272,384]{1,0:T(8,128)(2,1)S(1)}, bf16[272,384]{1,0:T(8,128)(2,1)S(1)}, u32[]{:S(2)}, u32[]{:S(2)}) %collective-permute-start.27) | collective-permute-done | bytes 208928 | tf_op jit(solution)/shard_map/ppermute | solution.py:100
  144.0 1.1 collective-permute-start.28
  145.2 1.3 collective-permute-start.29
  146.4 2.6 %collective-permute-start.30 = (bf16[1,48,1536]{2,1,0:T(8,128)(2,1)S(1)}, bf16[1,48,1536]{2,1,0:T(8,128)(2,1)S(1)}, u32[]{:S(2)}, u32[]{:S(2)}) collective-permute-start(bf16[1,48,1536]{2,1,0:T(8,128)(2,1)S(1)} %get-tuple-element.169), channel_id=1, source_target_pairs={{0,24},{2,26},{4,28},{6,30},{8,0},{10,2},{12,4},{14,6},{16,8},{18,... | collective-permute-start | bytes 442376 | tf_op jit(solution)/shard_map/ppermute | solution.py:96
  149.0 10.5 %shard_map.230 = (bf16[544,1152]{1,0:T(8,128)(2,1)S(1)}, f32[1,1152]{1,0:T(1,128)S(1)}) custom-call(s32[15]{0:T(128)S(1)} %concatenate.3.at, bf16[544,1152]{1,0:T(8,128)(2,1)S(1)} %get-tuple-element.179.qkv, bf16[272,384]{1,0:T(8,128)(2,1)S(1)} %get-tuple-element.180.own, bf16[272,384]{1,0:T(8,128)(2,1)S(1)} %collective-permute-done.27.got, ...), custom_call_target="tpu_custom_call" | custom-call | flops 1 | bytes 1 | tf_op jit(solution)/shard_map/pallas_call | solution.py:56
  159.5 3.6 %shard_map.231 = (f32[272,768]{1,0:T(8,128)S(1)}, bf16[272,768]{1,0:T(8,128)(2,1)S(1)}, bf16[8,48,1280]{2,1,0:T(8,128)(2,1)S(1)}, bf16[8,48,1280]{2,1,0:T(8,128)(2,1)S(1)}) custom-call(s32[15]{0:T(128)S(1)} %concatenate.3.at, bf16[544,768]{1,0:T(8,128)(2,1)S(1)} %get-tuple-element.134.layer_in, bf16[544,1152]{1,0:T(8,128)(2,1)S(1)} %get-tuple-element.183.d_projected, ...), custom_call_target="tpu_custom_call" | custom-call | flops 1 | bytes 1 | tf_op jit(solution)/shard_map/pallas_call | solution.py:56
  163.9 1.5 shard_map.233
  167.2 1.6 collective-permute-start.34
  170.1 1.1 collective-permute-start.38
  171.2 2.7 %collective-permute-start.39 = (bf16[1,48,1536]{2,1,0:T(8,128)(2,1)S(1)}, bf16[1,48,1536]{2,1,0:T(8,128)(2,1)S(1)}, u32[]{:S(2)}, u32[]{:S(2)}) collective-permute-start(bf16[1,48,1536]{2,1,0:T(8,128)(2,1)S(1)} %get-tuple-element.206), channel_id=1, source_target_pairs={{0,24},{2,26},{4,28},{6,30},{8,0},{10,2},{12,4},{14,6},{16,8},{18,... | collective-permute-start | bytes 442376 | tf_op jit(solution)/shard_map/ppermute | solution.py:96
  173.9 4.8 %collective-permute-done.37 = bf16[1,48,1536]{2,1,0:T(8,128)(2,1)S(1)} collective-permute-done((bf16[1,48,1536]{2,1,0:T(8,128)(2,1)S(1)}, bf16[1,48,1536]{2,1,0:T(8,128)(2,1)S(1)}, u32[]{:S(2)}, u32[]{:S(2)}) %collective-permute-start.37) | collective-permute-done | bytes 147488 | tf_op jit(solution)/shard_map/ppermute | solution.py:96
  178.7 5.2 %collective-permute-done.38 = bf16[1,48,1536]{2,1,0:T(8,128)(2,1)S(1)} collective-permute-done((bf16[1,48,1536]{2,1,0:T(8,128)(2,1)S(1)}, bf16[1,48,1536]{2,1,0:T(8,128)(2,1)S(1)}, u32[]{:S(2)}, u32[]{:S(2)}) %collective-permute-start.38) | collective-permute-done | bytes 147488 | tf_op jit(solution)/shard_map/ppermute | solution.py:96
  183.9 3.0 %collective-permute-done.36.refs_3_ = bf16[4,48,768]{2,1,0:T(8,128)(2,1)S(1)} collective-permute-done((bf16[4,48,768]{2,1,0:T(8,128)(2,1)S(1)}, bf16[4,48,768]{2,1,0:T(8,128)(2,1)S(1)}, u32[]{:S(2)}, u32[]{:S(2)}) %collective-permute-start.36) | collective-permute-done | bytes 294944 | tf_op jit(solution)/shard_map/ppermute | solution.py:96
  187.7 1.1 collective-permute-start.42
  188.8 2.7 %collective-permute-start.43 = (bf16[1,48,2048]{2,1,0:T(8,128)(2,1)S(1)}, bf16[1,48,2048]{2,1,0:T(8,128)(2,1)S(1)}, u32[]{:S(2)}, u32[]{:S(2)}) collective-permute-start(bf16[1,48,2048]{2,1,0:T(8,128)(2,1)S(1)} %get-tuple-element.218), channel_id=1, source_target_pairs={{0,24},{2,26},{4,28},{6,30},{8,0},{10,2},{12,4},{14,6},{16,8},{18,... | collective-permute-start | bytes 589832 | tf_op jit(solution)/shard_map/ppermute | solution.py:96
  191.5 1.4 collective-permute-start.40
  192.8 0.9 add_bitcast_fusion
  193.8 8.0 %collective-permute-done.40.got = bf16[272,768]{1,0:T(8,128)(2,1)S(1)} collective-permute-done((bf16[272,768]{1,0:T(8,128)(2,1)S(1)}, bf16[272,768]{1,0:T(8,128)(2,1)S(1)}, u32[]{:S(2)}, u32[]{:S(2)}) %collective-permute-start.40) | collective-permute-done | bytes 417824 | tf_op jit(solution)/shard_map/ppermute | solution.py:100
  202.4 1.8 collective-permute-done.42
  204.8 0.9 collective-permute-start.44
  205.7 1.7 copy.24
  207.4 2.1 collective-permute-done.44.got
  209.5 1.3 shard_map.238
  (88 shorter events, 24.7 us)
Async XLA Ops:
  1.4 0.9 copy-start.2
  2.3 0.8 copy-start.3
  3.1 0.7 copy-start.4
  3.7 0.7 copy-start.5
  4.4 0.7 copy-start.6
  5.1 27.8 %copy-start.7 = (bf16[48,1536]{1,0:T(8,128)(2,1)S(1)}, bf16[48,1536]{1,0:T(8,128)(2,1)}, u32[]{:S(2)}) copy-start(bf16[48,1536]{1,0:T(8,128)(2,1)} %param.24) | copy-start | bytes 442372
  5.2 5.8 %collective-permute-start = (bf16[24,2048]{1,0:T(8,128)(2,1)S(1)}, bf16[24,2048]{1,0:T(8,128)(2,1)S(1)}, u32[]{:S(2)}, u32[]{:S(2)}) collective-permute-start(bf16[24,2048]{1,0:T(8,128)(2,1)S(1)} %get-tuple-element.123), channel_id=1, source_target_pairs={{0,1},{1,0},{2,3},{3,2},{4,5},{5,4},{6,7},{7,6},{8,9},{9,8},{10,11... | collective-permute-start | bytes 294920 | tf_op jit(solution)/shard_map/ppermute | solution.py:100
  11.5 9.3 %collective-permute-start.3 = (bf16[48,2048]{1,0:T(8,128)(2,1)S(1)}, bf16[48,2048]{1,0:T(8,128)(2,1)S(1)}, u32[]{:S(2)}, u32[]{:S(2)}) collective-permute-start(bf16[48,2048]{1,0:T(8,128)(2,1)S(1)} %shard_map.214), channel_id=1, source_target_pairs={{0,24},{2,26},{4,28},{6,30},{8,0},{10,2},{12,4},{14,6},{16,8},{18,... | collective-permute-start | bytes 589832 | tf_op jit(solution)/shard_map/ppermute | solution.py:96
  15.5 9.6 %collective-permute-start.1 = (bf16[48,2048]{1,0:T(8,128)(2,1)S(1)}, bf16[48,2048]{1,0:T(8,128)(2,1)S(1)}, u32[]{:S(2)}, u32[]{:S(2)}) collective-permute-start(bf16[48,2048]{1,0:T(8,128)(2,1)S(1)} %shard_map.214), channel_id=1, source_target_pairs={{0,8},{2,10},{4,12},{6,14},{8,16},{10,18},{12,20},{14,22},{16,24},... | collective-permute-start | bytes 589832 | tf_op jit(solution)/shard_map/ppermute | solution.py:96
  15.5 15.7 %collective-permute-start.2 = (bf16[48,2048]{1,0:T(8,128)(2,1)S(1)}, bf16[48,2048]{1,0:T(8,128)(2,1)S(1)}, u32[]{:S(2)}, u32[]{:S(2)}) collective-permute-start(bf16[48,2048]{1,0:T(8,128)(2,1)S(1)} %shard_map.214), channel_id=1, source_target_pairs={{0,16},{2,18},{4,20},{6,22},{8,24},{10,26},{12,28},{14,30},{16,0},... | collective-permute-start | bytes 589832 | tf_op jit(solution)/shard_map/ppermute | solution.py:96
  16.5 35.3 %copy-start.8 = (bf16[1536,48]{0,1:T(8,128)(2,1)S(1)}, bf16[1536,48]{0,1:T(8,128)(2,1)}, u32[]{:S(2)}) copy-start(bf16[1536,48]{0,1:T(8,128)(2,1)} %param.26) | copy-start | bytes 442372
  17.6 13.7 %collective-permute-start.4 = (bf16[272,768]{1,0:T(8,128)(2,1)S(1)}, bf16[272,768]{1,0:T(8,128)(2,1)S(1)}, u32[]{:S(2)}, u32[]{:S(2)}) collective-permute-start(bf16[272,768]{1,0:T(8,128)(2,1)S(1)} %pad.4.own), channel_id=1, source_target_pairs={{0,1},{1,0},{2,3},{3,2},{4,5},{5,4},{6,7},{7,6},{8,9},{9,8},{10,11... | collective-permute-start | bytes 1253384 | tf_op jit(solution)/shard_map/ppermute | solution.py:100
  31.3 18.4 %collective-permute-start.5 = (bf16[4,48,2048]{2,1,0:T(8,128)(2,1)S(1)}, bf16[4,48,2048]{2,1,0:T(8,128)(2,1)S(1)}, u32[]{:S(2)}, u32[]{:S(2)}) collective-permute-start(bf16[4,48,2048]{2,1,0:T(8,128)(2,1)S(1)} %pad_maximum_fusion.refs_0_), channel_id=1, source_target_pairs={{0,4},{2,6},{4,0},{6,2},{8,12},{10,14},{12,8},{14,10},{16,20},{18,... | collective-permute-start | bytes 2359304 | tf_op jit(solution)/shard_map/ppermute | solution.py:96
  32.9 8.6 %collective-permute-start.6 = (bf16[48,1536]{1,0:T(8,128)(2,1)S(1)}, bf16[48,1536]{1,0:T(8,128)(2,1)S(1)}, u32[]{:S(2)}, u32[]{:S(2)}) collective-permute-start(bf16[48,1536]{1,0:T(8,128)(2,1)S(1)} %copy-done.7), channel_id=1, source_target_pairs={{0,8},{2,10},{4,12},{6,14},{8,16},{10,18},{12,20},{14,22},{16,24},... | collective-permute-start | bytes 442376 | tf_op jit(solution)/shard_map/ppermute | solution.py:96
  32.9 12.7 %collective-permute-start.7 = (bf16[48,1536]{1,0:T(8,128)(2,1)S(1)}, bf16[48,1536]{1,0:T(8,128)(2,1)S(1)}, u32[]{:S(2)}, u32[]{:S(2)}) collective-permute-start(bf16[48,1536]{1,0:T(8,128)(2,1)S(1)} %copy-done.7), channel_id=1, source_target_pairs={{0,16},{2,18},{4,20},{6,22},{8,24},{10,26},{12,28},{14,30},{16,0},... | collective-permute-start | bytes 442376 | tf_op jit(solution)/shard_map/ppermute | solution.py:96
  35.9 9.7 %collective-permute-start.8 = (bf16[48,1536]{1,0:T(8,128)(2,1)S(1)}, bf16[48,1536]{1,0:T(8,128)(2,1)S(1)}, u32[]{:S(2)}, u32[]{:S(2)}) collective-permute-start(bf16[48,1536]{1,0:T(8,128)(2,1)S(1)} %copy-done.7), channel_id=1, source_target_pairs={{0,24},{2,26},{4,28},{6,30},{8,0},{10,2},{12,4},{14,6},{16,8},{18,... | collective-permute-start | bytes 442376 | tf_op jit(solution)/shard_map/ppermute | solution.py:96
  49.7 4.3 %collective-permute-start.10 = (bf16[4,48,2048]{2,1,0:T(8,128)(2,1)S(1)}, bf16[4,48,2048]{2,1,0:T(8,128)(2,1)S(1)}, u32[]{:S(2)}, u32[]{:S(2)}) collective-permute-start(bf16[4,48,2048]{2,1,0:T(8,128)(2,1)S(1)} %collective-permute-done.5.refs_1_), channel_id=1, source_target_pairs={{0,2},{2,0},{4,6},{6,4},{8,10},{10,8},{12,14},{14,12},{16,18},{18,... | collective-permute-start | bytes 2359304 | tf_op jit(solution)/shard_map/ppermute | solution.py:96
  49.7 5.8 %collective-permute-start.9 = (bf16[4,48,2048]{2,1,0:T(8,128)(2,1)S(1)}, bf16[4,48,2048]{2,1,0:T(8,128)(2,1)S(1)}, u32[]{:S(2)}, u32[]{:S(2)}) collective-permute-start(bf16[4,48,2048]{2,1,0:T(8,128)(2,1)S(1)} %pad_maximum_fusion.refs_0_), channel_id=1, source_target_pairs={{0,2},{2,0},{4,6},{6,4},{8,10},{10,8},{12,14},{14,12},{16,18},{18,... | collective-permute-start | bytes 2359304 | tf_op jit(solution)/shard_map/ppermute | solution.py:96
  50.3 16.9 %collective-permute-start.17 = (bf16[4,48,1536]{2,1,0:T(8,128)(2,1)S(1)}, bf16[4,48,1536]{2,1,0:T(8,128)(2,1)S(1)}, u32[]{:S(2)}, u32[]{:S(2)}) collective-permute-start(bf16[4,48,1536]{2,1,0:T(8,128)(2,1)S(1)} %pad_maximum_fusion.1.refs_0_), channel_id=1, source_target_pairs={{0,4},{2,6},{4,0},{6,2},{8,12},{10,14},{12,8},{14,10},{16,20},{18,... | collective-permute-start | bytes 1769480 | tf_op jit(solution)/shard_map/ppermute | solution.py:96
  51.8 15.3 %collective-permute-start.13 = (bf16[48,1536]{1,0:T(8,128)(2,1)S(1)}, bf16[48,1536]{1,0:T(8,128)(2,1)S(1)}, u32[]{:S(2)}, u32[]{:S(2)}) collective-permute-start(bf16[48,1536]{1,0:T(8,128)(2,1)S(1)} %bitcast.80), channel_id=1, source_target_pairs={{0,8},{2,10},{4,12},{6,14},{8,16},{10,18},{12,20},{14,22},{16,24},... | collective-permute-start | bytes 442376 | tf_op jit(solution)/shard_map/ppermute | solution.py:96
  51.8 15.3 %collective-permute-start.14 = (bf16[48,1536]{1,0:T(8,128)(2,1)S(1)}, bf16[48,1536]{1,0:T(8,128)(2,1)S(1)}, u32[]{:S(2)}, u32[]{:S(2)}) collective-permute-start(bf16[48,1536]{1,0:T(8,128)(2,1)S(1)} %bitcast.81), channel_id=1, source_target_pairs={{0,16},{2,18},{4,20},{6,22},{8,24},{10,26},{12,28},{14,30},{16,0},... | collective-permute-start | bytes 442376 | tf_op jit(solution)/shard_map/ppermute | solution.py:96
  54.1 12.9 %collective-permute-start.15 = (bf16[48,1536]{1,0:T(8,128)(2,1)S(1)}, bf16[48,1536]{1,0:T(8,128)(2,1)S(1)}, u32[]{:S(2)}, u32[]{:S(2)}) collective-permute-start(bf16[48,1536]{1,0:T(8,128)(2,1)S(1)} %bitcast.82), channel_id=1, source_target_pairs={{0,24},{2,26},{4,28},{6,30},{8,0},{10,2},{12,4},{14,6},{16,8},{18,... | collective-permute-start | bytes 442376 | tf_op jit(solution)/shard_map/ppermute | solution.py:96
  65.4 6.3 %collective-permute-start.11 = (bf16[272,384]{1,0:T(8,128)(2,1)S(1)}, bf16[272,384]{1,0:T(8,128)(2,1)S(1)}, u32[]{:S(2)}, u32[]{:S(2)}) collective-permute-start(bf16[272,384]{1,0:T(8,128)(2,1)S(1)} %get-tuple-element.132), channel_id=1, source_target_pairs={{0,1},{1,0},{2,3},{3,2},{4,5},{5,4},{6,7},{7,6},{8,9},{9,8},{10,11... | collective-permute-start | bytes 626696 | tf_op jit(solution)/shard_map/ppermute | solution.py:100
  67.0 7.6 %copy-start = (s32[384,2]{1,0:T(8,128)S(1)}, s32[384,2]{1,0:T(8,128)}, u32[]{:S(2)}) copy-start(s32[384,2]{1,0:T(8,128)} %constant.78.clone.target) | copy-start | bytes 9220
  67.1 8.9 %collective-permute-start.19 = (bf16[4,48,1536]{2,1,0:T(8,128)(2,1)S(1)}, bf16[4,48,1536]{2,1,0:T(8,128)(2,1)S(1)}, u32[]{:S(2)}, u32[]{:S(2)}) collective-permute-start(bf16[4,48,1536]{2,1,0:T(8,128)(2,1)S(1)} %collective-permute-done.17.refs_1_), channel_id=1, source_target_pairs={{0,2},{2,0},{4,6},{6,4},{8,10},{10,8},{12,14},{14,12},{16,18},{18,... | collective-permute-start | bytes 1769480 | tf_op jit(solution)/shard_map/ppermute | solution.py:96
  67.2 8.9 %collective-permute-start.18 = (bf16[4,48,1536]{2,1,0:T(8,128)(2,1)S(1)}, bf16[4,48,1536]{2,1,0:T(8,128)(2,1)S(1)}, u32[]{:S(2)}, u32[]{:S(2)}) collective-permute-start(bf16[4,48,1536]{2,1,0:T(8,128)(2,1)S(1)} %pad_maximum_fusion.1.refs_0_), channel_id=1, source_target_pairs={{0,2},{2,0},{4,6},{6,4},{8,10},{10,8},{12,14},{14,12},{16,18},{18,... | collective-permute-start | bytes 1769480 | tf_op jit(solution)/shard_map/ppermute | solution.py:96
  67.7 15.3 %collective-permute-start.16 = (bf16[4,48,1536]{2,1,0:T(8,128)(2,1)S(1)}, bf16[4,48,1536]{2,1,0:T(8,128)(2,1)S(1)}, u32[]{:S(2)}, u32[]{:S(2)}) collective-permute-start(bf16[4,48,1536]{2,1,0:T(8,128)(2,1)S(1)} %pad_maximum_fusion.2.refs_0_), channel_id=1, source_target_pairs={{0,4},{2,6},{4,0},{6,2},{8,12},{10,14},{12,8},{14,10},{16,20},{18,... | collective-permute-start | bytes 1769480 | tf_op jit(solution)/shard_map/ppermute | solution.py:96
  73.0 10.0 %collective-permute-start.12 = (bf16[272,768]{1,0:T(8,128)(2,1)S(1)}, bf16[272,768]{1,0:T(8,128)(2,1)S(1)}, u32[]{:S(2)}, u32[]{:S(2)}) collective-permute-start(bf16[272,768]{1,0:T(8,128)(2,1)S(1)} %get-tuple-element.147.a_up), channel_id=1, source_target_pairs={{0,1},{1,0},{2,3},{3,2},{4,5},{5,4},{6,7},{7,6},{8,9},{9,8},{10,11... | collective-permute-start | bytes 1253384 | tf_op jit(solution)/shard_map/ppermute | solution.py:100
  74.6 9.5 %collective-permute-start.20 = (bf16[4,48,1536]{2,1,0:T(8,128)(2,1)S(1)}, bf16[4,48,1536]{2,1,0:T(8,128)(2,1)S(1)}, u32[]{:S(2)}, u32[]{:S(2)}) collective-permute-start(bf16[4,48,1536]{2,1,0:T(8,128)(2,1)S(1)} %pad_maximum_fusion.2.refs_0_), channel_id=1, source_target_pairs={{0,2},{2,0},{4,6},{6,4},{8,10},{10,8},{12,14},{14,12},{16,18},{18,... | collective-permute-start | bytes 1769480 | tf_op jit(solution)/shard_map/ppermute | solution.py:96
  83.0 2.0 collective-permute-start.21
  86.6 11.7 %collective-permute-start.22 = (bf16[272,768]{1,0:T(8,128)(2,1)S(1)}, bf16[272,768]{1,0:T(8,128)(2,1)S(1)}, u32[]{:S(2)}, u32[]{:S(2)}) collective-permute-start(bf16[272,768]{1,0:T(8,128)(2,1)S(1)} %convolution_convert_fusion.1), channel_id=1, source_target_pairs={{0,1},{1,0},{2,3},{3,2},{4,5},{5,4},{6,7},{7,6},{8,9},{9,8},{10,11... | collective-permute-start | bytes 1253384 | tf_op jit(solution)/shard_map/ppermute | solution.py:100
  88.9 9.4 %copy-start.1 = (bf16[266,1,768]{2,0,1:T(8,128)(2,1)S(1)}, bf16[266,1,768]{2,0,1:T(8,128)(2,1)}, u32[]{:S(2)}) copy-start(bf16[266,1,768]{2,0,1:T(8,128)(2,1)} %param.15) | copy-start | bytes 1225732
  100.3 10.8 %collective-permute-start.23 = (bf16[272,768]{1,0:T(8,128)(2,1)S(1)}, bf16[272,768]{1,0:T(8,128)(2,1)S(1)}, u32[]{:S(2)}, u32[]{:S(2)}) collective-permute-start(bf16[272,768]{1,0:T(8,128)(2,1)S(1)} %get-tuple-element.149.a_down), channel_id=1, source_target_pairs={{0,1},{1,0},{2,3},{3,2},{4,5},{5,4},{6,7},{7,6},{8,9},{9,8},{10,11... | collective-permute-start | bytes 1253384 | tf_op jit(solution)/shard_map/ppermute | solution.py:100
  115.4 4.2 %collective-permute-start.24 = (bf16[8,48,1536]{2,1,0:T(8,128)(2,1)S(1)}, bf16[8,48,1536]{2,1,0:T(8,128)(2,1)S(1)}, u32[]{:S(2)}, u32[]{:S(2)}) collective-permute-start(bf16[8,48,1536]{2,1,0:T(8,128)(2,1)S(1)} %get-tuple-element.156), channel_id=1, source_target_pairs={{0,2},{2,0},{4,6},{6,4},{8,10},{10,8},{12,14},{14,12},{16,18},{18,... | collective-permute-start | bytes 3538952 | tf_op jit(solution)/shard_map/ppermute | solution.py:96
  119.2 3.3 %collective-permute-start.31 = (bf16[8,48,1536]{2,1,0:T(8,128)(2,1)S(1)}, bf16[8,48,1536]{2,1,0:T(8,128)(2,1)S(1)}, u32[]{:S(2)}, u32[]{:S(2)}) collective-permute-start(bf16[8,48,1536]{2,1,0:T(8,128)(2,1)S(1)} %get-tuple-element.174), channel_id=1, source_target_pairs={{0,2},{2,0},{4,6},{6,4},{8,10},{10,8},{12,14},{14,12},{16,18},{18,... | collective-permute-start | bytes 3538952 | tf_op jit(solution)/shard_map/ppermute | solution.py:96
  120.5 15.3 %collective-permute-start.25 = (bf16[4,48,1536]{2,1,0:T(8,128)(2,1)S(1)}, bf16[4,48,1536]{2,1,0:T(8,128)(2,1)S(1)}, u32[]{:S(2)}, u32[]{:S(2)}) collective-permute-start(bf16[4,48,1536]{2,1,0:T(8,128)(2,1)S(1)} %get-tuple-element.158), channel_id=1, source_target_pairs={{0,4},{2,6},{4,0},{6,2},{8,12},{10,14},{12,8},{14,10},{16,20},{18,... | collective-permute-start | bytes 1769480 | tf_op jit(solution)/shard_map/ppermute | solution.py:96
  121.1 15.3 %collective-permute-start.26 = (bf16[272,768]{1,0:T(8,128)(2,1)S(1)}, bf16[272,768]{1,0:T(8,128)(2,1)S(1)}, u32[]{:S(2)}, u32[]{:S(2)}) collective-permute-start(bf16[272,768]{1,0:T(8,128)(2,1)S(1)} %convolution_convert_fusion), channel_id=1, source_target_pairs={{0,1},{1,0},{2,3},{3,2},{4,5},{5,4},{6,7},{7,6},{8,9},{9,8},{10,11... | collective-permute-start | bytes 1253384 | tf_op jit(solution)/shard_map/ppermute | solution.py:100
  135.8 27.3 %collective-permute-start.32 = (bf16[4,48,1536]{2,1,0:T(8,128)(2,1)S(1)}, bf16[4,48,1536]{2,1,0:T(8,128)(2,1)S(1)}, u32[]{:S(2)}, u32[]{:S(2)}) collective-permute-start(bf16[4,48,1536]{2,1,0:T(8,128)(2,1)S(1)} %get-tuple-element.177), channel_id=1, source_target_pairs={{0,4},{2,6},{4,0},{6,2},{8,12},{10,14},{12,8},{14,10},{16,20},{18,... | collective-permute-start | bytes 1769480 | tf_op jit(solution)/shard_map/ppermute | solution.py:96
  138.0 6.0 %collective-permute-start.27 = (bf16[272,384]{1,0:T(8,128)(2,1)S(1)}, bf16[272,384]{1,0:T(8,128)(2,1)S(1)}, u32[]{:S(2)}, u32[]{:S(2)}) collective-permute-start(bf16[272,384]{1,0:T(8,128)(2,1)S(1)} %get-tuple-element.163), channel_id=1, source_target_pairs={{0,1},{1,0},{2,3},{3,2},{4,5},{5,4},{6,7},{7,6},{8,9},{9,8},{10,11... | collective-permute-start | bytes 626696 | tf_op jit(solution)/shard_map/ppermute | solution.py:100
  144.0 19.7 %collective-permute-start.28 = (bf16[1,48,1536]{2,1,0:T(8,128)(2,1)S(1)}, bf16[1,48,1536]{2,1,0:T(8,128)(2,1)S(1)}, u32[]{:S(2)}, u32[]{:S(2)}) collective-permute-start(bf16[1,48,1536]{2,1,0:T(8,128)(2,1)S(1)} %get-tuple-element.167), channel_id=1, source_target_pairs={{0,8},{2,10},{4,12},{6,14},{8,16},{10,18},{12,20},{14,22},{16,24},... | collective-permute-start | bytes 442376 | tf_op jit(solution)/shard_map/ppermute | solution.py:96
  145.2 18.6 %collective-permute-start.29 = (bf16[1,48,1536]{2,1,0:T(8,128)(2,1)S(1)}, bf16[1,48,1536]{2,1,0:T(8,128)(2,1)S(1)}, u32[]{:S(2)}, u32[]{:S(2)}) collective-permute-start(bf16[1,48,1536]{2,1,0:T(8,128)(2,1)S(1)} %get-tuple-element.168), channel_id=1, source_target_pairs={{0,16},{2,18},{4,20},{6,22},{8,24},{10,26},{12,28},{14,30},{16,0},... | collective-permute-start | bytes 442376 | tf_op jit(solution)/shard_map/ppermute | solution.py:96
  146.4 17.4 %collective-permute-start.30 = (bf16[1,48,1536]{2,1,0:T(8,128)(2,1)S(1)}, bf16[1,48,1536]{2,1,0:T(8,128)(2,1)S(1)}, u32[]{:S(2)}, u32[]{:S(2)}) collective-permute-start(bf16[1,48,1536]{2,1,0:T(8,128)(2,1)S(1)} %get-tuple-element.169), channel_id=1, source_target_pairs={{0,24},{2,26},{4,28},{6,30},{8,0},{10,2},{12,4},{14,6},{16,8},{18,... | collective-permute-start | bytes 442376 | tf_op jit(solution)/shard_map/ppermute | solution.py:96
  163.8 2.6 %collective-permute-start.33 = (bf16[8,48,1280]{2,1,0:T(8,128)(2,1)S(1)}, bf16[8,48,1280]{2,1,0:T(8,128)(2,1)S(1)}, u32[]{:S(2)}, u32[]{:S(2)}) collective-permute-start(bf16[8,48,1280]{2,1,0:T(8,128)(2,1)S(1)} %get-tuple-element.194), channel_id=1, source_target_pairs={{0,2},{2,0},{4,6},{6,4},{8,10},{10,8},{12,14},{14,12},{16,18},{18,... | collective-permute-start | bytes 2949128 | tf_op jit(solution)/shard_map/ppermute | solution.py:96
  165.3 3.4 %collective-permute-start.35 = (bf16[8,48,768]{2,1,0:T(8,128)(2,1)S(1)}, bf16[8,48,768]{2,1,0:T(8,128)(2,1)S(1)}, u32[]{:S(2)}, u32[]{:S(2)}) collective-permute-start(bf16[8,48,768]{2,1,0:T(8,128)(2,1)S(1)} %get-tuple-element.201), channel_id=1, source_target_pairs={{0,2},{2,0},{4,6},{6,4},{8,10},{10,8},{12,14},{14,12},{16,18},{18,... | collective-permute-start | bytes 1769480 | tf_op jit(solution)/shard_map/ppermute | solution.py:96
  167.2 19.7 %collective-permute-start.34 = (bf16[4,48,1280]{2,1,0:T(8,128)(2,1)S(1)}, bf16[4,48,1280]{2,1,0:T(8,128)(2,1)S(1)}, u32[]{:S(2)}, u32[]{:S(2)}) collective-permute-start(bf16[4,48,1280]{2,1,0:T(8,128)(2,1)S(1)} %get-tuple-element.195), channel_id=1, source_target_pairs={{0,4},{2,6},{4,0},{6,2},{8,12},{10,14},{12,8},{14,10},{16,20},{18,... | collective-permute-start | bytes 1474568 | tf_op jit(solution)/shard_map/ppermute | solution.py:96
  169.5 17.4 %collective-permute-start.36 = (bf16[4,48,768]{2,1,0:T(8,128)(2,1)S(1)}, bf16[4,48,768]{2,1,0:T(8,128)(2,1)S(1)}, u32[]{:S(2)}, u32[]{:S(2)}) collective-permute-start(bf16[4,48,768]{2,1,0:T(8,128)(2,1)S(1)} %get-tuple-element.203), channel_id=1, source_target_pairs={{0,4},{2,6},{4,0},{6,2},{8,12},{10,14},{12,8},{14,10},{16,20},{18,... | collective-permute-start | bytes 884744 | tf_op jit(solution)/shard_map/ppermute | solution.py:96
  170.1 8.6 %collective-permute-start.37 = (bf16[1,48,1536]{2,1,0:T(8,128)(2,1)S(1)}, bf16[1,48,1536]{2,1,0:T(8,128)(2,1)S(1)}, u32[]{:S(2)}, u32[]{:S(2)}) collective-permute-start(bf16[1,48,1536]{2,1,0:T(8,128)(2,1)S(1)} %get-tuple-element.204), channel_id=1, source_target_pairs={{0,8},{2,10},{4,12},{6,14},{8,16},{10,18},{12,20},{14,22},{16,24},... | collective-permute-start | bytes 442376 | tf_op jit(solution)/shard_map/ppermute | solution.py:96
  170.1 13.8 %collective-permute-start.38 = (bf16[1,48,1536]{2,1,0:T(8,128)(2,1)S(1)}, bf16[1,48,1536]{2,1,0:T(8,128)(2,1)S(1)}, u32[]{:S(2)}, u32[]{:S(2)}) collective-permute-start(bf16[1,48,1536]{2,1,0:T(8,128)(2,1)S(1)} %get-tuple-element.205), channel_id=1, source_target_pairs={{0,16},{2,18},{4,20},{6,22},{8,24},{10,26},{12,28},{14,30},{16,0},... | collective-permute-start | bytes 442376 | tf_op jit(solution)/shard_map/ppermute | solution.py:96
  171.2 12.7 %collective-permute-start.39 = (bf16[1,48,1536]{2,1,0:T(8,128)(2,1)S(1)}, bf16[1,48,1536]{2,1,0:T(8,128)(2,1)S(1)}, u32[]{:S(2)}, u32[]{:S(2)}) collective-permute-start(bf16[1,48,1536]{2,1,0:T(8,128)(2,1)S(1)} %get-tuple-element.206), channel_id=1, source_target_pairs={{0,24},{2,26},{4,28},{6,30},{8,0},{10,2},{12,4},{14,6},{16,8},{18,... | collective-permute-start | bytes 442376 | tf_op jit(solution)/shard_map/ppermute | solution.py:96
  187.6 14.8 %collective-permute-start.41 = (bf16[1,48,2048]{2,1,0:T(8,128)(2,1)S(1)}, bf16[1,48,2048]{2,1,0:T(8,128)(2,1)S(1)}, u32[]{:S(2)}, u32[]{:S(2)}) collective-permute-start(bf16[1,48,2048]{2,1,0:T(8,128)(2,1)S(1)} %get-tuple-element.216), channel_id=1, source_target_pairs={{0,8},{2,10},{4,12},{6,14},{8,16},{10,18},{12,20},{14,22},{16,24},... | collective-permute-start | bytes 589832 | tf_op jit(solution)/shard_map/ppermute | solution.py:96
  187.7 16.5 %collective-permute-start.42 = (bf16[1,48,2048]{2,1,0:T(8,128)(2,1)S(1)}, bf16[1,48,2048]{2,1,0:T(8,128)(2,1)S(1)}, u32[]{:S(2)}, u32[]{:S(2)}) collective-permute-start(bf16[1,48,2048]{2,1,0:T(8,128)(2,1)S(1)} %get-tuple-element.217), channel_id=1, source_target_pairs={{0,16},{2,18},{4,20},{6,22},{8,24},{10,26},{12,28},{14,30},{16,0},... | collective-permute-start | bytes 589832 | tf_op jit(solution)/shard_map/ppermute | solution.py:96
  188.8 15.4 %collective-permute-start.43 = (bf16[1,48,2048]{2,1,0:T(8,128)(2,1)S(1)}, bf16[1,48,2048]{2,1,0:T(8,128)(2,1)S(1)}, u32[]{:S(2)}, u32[]{:S(2)}) collective-permute-start(bf16[1,48,2048]{2,1,0:T(8,128)(2,1)S(1)} %get-tuple-element.218), channel_id=1, source_target_pairs={{0,24},{2,26},{4,28},{6,30},{8,0},{10,2},{12,4},{14,6},{16,8},{18,... | collective-permute-start | bytes 589832 | tf_op jit(solution)/shard_map/ppermute | solution.py:96
  191.5 10.3 %collective-permute-start.40 = (bf16[272,768]{1,0:T(8,128)(2,1)S(1)}, bf16[272,768]{1,0:T(8,128)(2,1)S(1)}, u32[]{:S(2)}, u32[]{:S(2)}) collective-permute-start(bf16[272,768]{1,0:T(8,128)(2,1)S(1)} %get-tuple-element.211), channel_id=1, source_target_pairs={{0,1},{1,0},{2,3},{3,2},{4,5},{5,4},{6,7},{7,6},{8,9},{9,8},{10,11... | collective-permute-start | bytes 1253384 | tf_op jit(solution)/shard_map/ppermute | solution.py:100
  204.8 4.7 %collective-permute-start.44 = (bf16[24,2048]{1,0:T(8,128)(2,1)S(1)}, bf16[24,2048]{1,0:T(8,128)(2,1)S(1)}, u32[]{:S(2)}, u32[]{:S(2)}) collective-permute-start(bf16[24,2048]{1,0:T(8,128)(2,1)S(1)} %get-tuple-element.225), channel_id=1, source_target_pairs={{0,1},{1,0},{2,3},{3,2},{4,5},{5,4},{6,7},{7,6},{8,9},{9,8},{10,11... | collective-permute-start | bytes 294920 | tf_op jit(solution)/shard_map/ppermute | solution.py:100
where the time goes:
time: 212 us; the launch traced here: 211 us
  waiting for transfers between devices  90.6 us (43%)
  Pallas kernels  51.2 us (24%)
  starting transfers between devices  50.1 us (24%)
  local copies, waits for them, and re-layouts  8.76 us (4%)
  matrix products  7.13 us (3%)
  between operations  2.36 us (1%)
    ppermute x35, waiting for transfers between devices, rotate(): return lax.ppermute(value, 'dp', pairs)  60 us
    pallas_call x26, Pallas kernels, call(): pl.pallas_call(kernel, in_specs=[pl.BlockSpec(memory_space=pltpu.SMEM)] +...  51.2 us
    ppermute x35, starting transfers between devices, rotate(): return lax.ppermute(value, 'dp', pairs)  34.5 us
    ppermute x10, waiting for transfers between devices, swap_tensor(): return lax.ppermute(value, 'tensor', [(0, 1), (1, 0)])  30.7 us
    ppermute x10, starting transfers between devices, swap_tensor(): return lax.ppermute(value, 'tensor', [(0, 1), (1, 0)])  15.6 us
    unnamed x19, local copies, waits for them, and re-layouts  5.44 us
  transfers between devices with their start and end apart: 45, of which 21 were waited for; matrix products, arithmetic and copies ran while one was open for 4% of the time, Pallas kernels for 20%

commit v1 on v0

--- a/solution.py
+++ b/solution.py
@@ -14,6 +14,8 @@
 LOW = jnp.bfloat16
 WIDE = jnp.float32
 CHUNK = 32
+TILE = 384
+OUT_TILE = 256
 ROWS = 16
 PAIR = 2 * HEAD
 QUICK = pl.CostEstimate(flops=1, bytes_accessed=1, transcendentals=0)
@@ -114,45 +116,73 @@
     return value.reshape((-1,) + value.shape[-2:])
 
 
-def assemble_kernel(sizes, cuts, at, *refs):
-    parts, wholes = refs[:4], refs[4:]
-    outer = sizes[:-2]
-    me, digits = at[DP], []
+def placer(sizes, me):
+    outer, digits = sizes[:-2], []
     for size in reversed(sizes):
         digits.append(lax.rem(me, size))
         me = lax.div(me, size)
     digits = digits[::-1]
+
+    def place_of(swap_core, swap_x, slot):
+        steps = []
+        for size in reversed(outer):
+            steps.append(slot % size)
+            slot //= size
+        place = 0
+        for size, digit, step in zip(outer, digits, steps[::-1]):
+            place = place * size + lax.rem(digit + (size - step), size)
+        x, core = digits[-2], digits[-1]
+        place = place * 2 + (1 - x if swap_x else x)
+        return place * 2 + (1 - core if swap_core else core)
+
+    return place_of
+
+
+def assemble_kernel(sizes, at, *refs):
+    parts, whole = refs[:4], refs[4]
+    cols = whole.shape[2]
+    place_of = placer(sizes, at[DP])
     for swap_core in range(2):
         for swap_x in range(2):
             source = parts[2 * swap_core + swap_x]
             for slot in range(source.shape[0]):
-                left, steps = slot, []
-                for size in reversed(outer):
-                    steps.append(left % size)
-                    left //= size
-                place = 0
-                for size, digit, step in zip(outer, digits, steps[::-1]):
-                    place = place * size + lax.rem(digit + (size - step), size)
-                x, core = digits[-2], digits[-1]
-                place = place * 2 + (1 - x if swap_x else x)
-                place = place * 2 + (1 - core if swap_core else core)
-                for whole, low, high in zip(wholes, cuts[:-1], cuts[1:]):
-                    whole[place] = source[slot, :, low:high]
-
-
-def assemble(at, mine, x_got, digits, *cuts):
+                whole[place_of(swap_core, swap_x, slot)] = source[slot, :, :cols]
+
+
+def swap_blocks(mine, x_got, digits):
     core = digits[-1]
-    parts = [mine, x_got, rotate(mine, core, 1), rotate(x_got, core, 1)]
-    slots, rows, cols = mine.shape
-    cuts = (0, *cuts, cols)
-    outs = [low_of(4 * slots, rows, b - a) for a, b in zip(cuts[:-1], cuts[1:])]
+    return [mine, x_got, rotate(mine, core, 1), rotate(x_got, core, 1)]
+
+
+def assemble(at, parts, digits, cols):
+    slots, rows, _ = parts[0].shape
     sizes = tuple(size for _, size in digits)
-    wholes = call(functools.partial(assemble_kernel, sizes, cuts), outs, at, *parts)
-    wholes = [whole.reshape(4 * slots * rows, -1) for whole in wholes]
-    return wholes if len(wholes) > 1 else wholes[0]
-
-
-def columns_kernel(part, small_rows, at, weight, vectors, gains, memory, up, out, kept, sent, turn):
+    (whole,) = call(
+        functools.partial(assemble_kernel, sizes), [low_of(4 * slots, rows, cols)], at, *parts
+    )
+    return whole.reshape(4 * slots * rows, cols)
+
+
+def assemble_out_kernel(sizes, cols, at, *refs):
+    parts, gots, whole = refs[:4], refs[4:6], refs[6]
+    place_of = placer(sizes, at[DP])
+    first = at[T] == 0
+    lines = whole.shape[1] // 2
+    for swap_core in range(2):
+        for swap_x in range(2):
+            source, got = parts[2 * swap_core + swap_x], gots[swap_core]
+            slots = source.shape[0]
+            for slot in range(slots):
+                mine = jnp.concatenate(
+                    [source[slot, :lines, cols:], source[slot, lines:, cols:]], axis=1
+                )
+                other = got[swap_x * slots + slot]
+                place = place_of(swap_core, swap_x, slot)
+                whole[place, :lines] = jnp.where(first, mine, other)
+                whole[place, lines:] = jnp.where(first, other, mine)
+
+
+def columns_kernel(part, small_rows, at, weight, vectors, gains, memory, up, kept, sent, turn):
     lines, width = weight.shape[0], weight.shape[1] // 3
     first = at[T] == 0
     for pair in range(part // PAIR):
@@ -166,16 +196,26 @@
     for source, (low, high) in zip((memory, vectors, gains, up), small_rows):
         turn[low:high, :lines] = source[...].astype(WIDE)
     columns = turn[...].T[:lines].astype(LOW)
-    for target in (kept, sent):
-        target[:, 3 * part : 3 * part + PAIR] = columns
-        target[:, 3 * part + PAIR :] = out[...]
-
-
-def pair_kernel(at, kept, got, pair):
-    lines = kept.shape[0]
+    kept[:, 3 * part :] = columns
+    sent[:, 3 * part :] = columns
+
+
+def pair_kernel(at, kept, got, out, pair):
+    lines, cols = kept.shape
+    fold = out.shape[1] // 2
     first = at[T] == 0
-    pair[:lines] = jnp.where(first, kept[...], got[...])
-    pair[lines:] = jnp.where(first, got[...], kept[...])
+    pair[:lines, :cols] = jnp.where(first, kept[...], got[...])
+    pair[lines:, :cols] = jnp.where(first, got[...], kept[...])
+    pair[:lines, cols:] = out[:, :fold]
+    pair[lines:, cols:] = out[:, fold:]
+
+
+def unfold_kernel(cols, at, mine, x_got, out):
+    slots, lines, fold = mine.shape[0], out.shape[1], out.shape[2] // 2
+    for n, source in enumerate((mine, x_got)):
+        for slot in range(slots):
+            out[n * slots + slot, :, :fold] = source[slot, :lines, cols:]
+            out[n * slots + slot, :, fold:] = source[slot, lines:, cols:]
 
 
 def put_blocks(total, kept, sent, core, at):
@@ -186,37 +226,54 @@
     for group in range(groups):
         even, odd = total[2 * group], total[2 * group + 1]
         kept[group, :, at : at + cols] = jnp.where(second, odd, even)
-        sent[group, :, at : at + cols] = jnp.where(second, even, odd)
-
-
-def put_gradient(a, b, outs, core, tile=384, own=None):
-    for low in range(0, b.shape[1], tile):
+        sent[group] = jnp.where(second, even, odd)
+
+
+def put_gradient(a, b, outs, core, own=None, tile=TILE):
+    for n, low in enumerate(range(0, b.shape[1], tile)):
         total = tn(a[...], b[:, low : low + tile])
         if own is not None:
             total = total + own[:, low : low + tile]
         if len(outs) == 1:
             outs[0][:, low : low + tile] = total.astype(LOW)
         else:
-            put_blocks(total, *outs, core, low)
-
-
-def gradient_outs(width, cols, dp_count):
+            put_blocks(total, outs[0], outs[1 + n], core, low)
+
+
+def gradient_outs(width, cols, dp_count, tile=TILE):
     rows = width // dp_count
     if rows % 16:
         return [low_of(width, cols)]
-    return [low_of(dp_count // 2, rows, cols)] * 2
-
-
-def split_cores(outs, dp_count, core):
-    if len(outs) == 2:
-        return outs
-    whole = outs[0].reshape(dp_count // 2, 2, -1, outs[0].shape[1])
-    take = lambda which: lax.dynamic_index_in_dim(whole, which, 1, keepdims=False)
-    return take(core), take(1 - core)
-
-
-def gradient_kernel(at, a, b, *outs):
-    put_gradient(a, b, outs, at[CORE])
+    tiles = [min(tile, cols - low) for low in range(0, cols, tile)]
+    return [low_of(dp_count // 2, rows, n) for n in [cols] + tiles]
+
+
+def swap_cores(outs, dp_count, digit):
+    if len(outs) == 1:
+        whole = outs[0].reshape(dp_count // 2, 2, -1, outs[0].shape[1])
+        core = digit_at(digit)
+        take = lambda which: lax.dynamic_index_in_dim(whole, which, 1, keepdims=False)
+        outs = [take(core), take(1 - core)]
+    return outs[0], [rotate(part, digit, 1) for part in outs[1:]]
+
+
+def out_gradient_kernel(at, a, b, *outs):
+    put_gradient(a, b, outs, at[CORE], tile=OUT_TILE)
+
+
+def rows_halves_kernel(at, mine, *refs):
+    got, (kept, sent) = refs[:-2], refs[-2:]
+    lines = kept.shape[1]
+    first = at[T] == 0
+    for group in range(mine.shape[0]):
+        low = 0
+        for part in got:
+            high = low + part.shape[2]
+            total = mine[group, :, low:high].astype(WIDE) + part[group].astype(WIDE)
+            a, b = total[:lines], total[lines:]
+            kept[group, :, low:high] = jnp.where(first, a, b).astype(LOW)
+            sent[group, :, low:high] = jnp.where(first, b, a).astype(LOW)
+            low = high
 
 
 def own_kernel(at, a_down, b_down, a_up, b_up, down, up, sums):
@@ -256,42 +313,49 @@
     row[...] = jnp.broadcast_to(total[:1], row.shape)
 
 
-def halve_kernel(at, mine, got, kept, sent):
+def halve_kernel(at, mine, *refs):
+    got, (kept, sent) = refs[:-2], refs[-2:]
     x = at[X]
     for group in range(kept.shape[0]):
         for other, out in ((0, kept), (1, sent)):
             place = 2 * group + (1 - x if other else x)
-            out[group] = (mine[place].astype(WIDE) + got[place].astype(WIDE)).astype(LOW)
+            low = 0
+            for part in got:
+                high = low + part.shape[2]
+                total = mine[place, :, low:high].astype(WIDE) + part[place].astype(WIDE)
+                out[group, :, low:high] = total.astype(LOW)
+                low = high
 
 
 def halve(at, mine, got):
     groups, rows, cols = mine.shape
-    return call(halve_kernel, [low_of(groups // 2, rows, cols)] * 2, at, mine, got)
-
-
-def parts_kernel(size, count, at, *refs):
-    mine, got, outs = refs[:count], refs[count : 2 * count], refs[2 * count :]
+    return call(halve_kernel, [low_of(groups // 2, rows, cols)] * 2, at, mine, *got)
+
+
+def parts_kernel(size, at, mine, got, *refs):
+    folded, outs = refs[: len(refs) - size], refs[len(refs) - size :]
     me = at[OUTER]
+    cols = mine.shape[2]
     for group in range(outs[0].shape[0]):
-        low = 0
-        for a, b in zip(mine, got):
-            high = low + a.shape[2]
-            for step, out in enumerate(outs):
-                place = group * size + lax.rem(me + step, size)
-                total = a[place].astype(WIDE) + b[place].astype(WIDE)
-                out[group, :, low:high] = total.astype(out.dtype)
-            low = high
-
-
-def outer_parts(at, mine, got, digits):
+        for step, out in enumerate(outs):
+            place = group * size + lax.rem(me + step, size)
+            total = mine[place].astype(WIDE) + got[place].astype(WIDE)
+            out[group, :, :cols] = total.astype(out.dtype)
+            if folded:
+                total = folded[0][place].astype(WIDE) + folded[1][place].astype(WIDE)
+                lines, fold = total.shape[0], total.shape[1] // 2
+                out[group, :lines, cols:] = total[:, :fold].astype(out.dtype)
+                out[group, lines:, cols:] = total[:, fold:].astype(out.dtype)
+
+
+def outer_parts(at, mine, got, digits, *folded):
     size = digits[-3][1]
-    blocks, rows, _ = mine[0].shape
-    cols = sum(array.shape[2] for array in mine)
+    blocks, rows, cols = mine.shape
+    if folded:
+        cols += folded[0].shape[2] // 2
     shape = (blocks // size, rows, cols)
     outs = [wide_of(*shape)] + [low_of(*shape)] * (size - 1)
-    kept, *sent = call(
-        functools.partial(parts_kernel, size, len(mine)), outs, at, *mine, *got
-    )
+    kept, *sent = call(functools.partial(parts_kernel, size), outs, at, mine, got, *folded)
     return kept, sent
 
 
@@ -487,21 +551,25 @@
     if len(grads) == 1:
         grads[0][:, cols:] = small.astype(LOW)
     else:
-        put_blocks(small, *grads, at[CORE], cols)
+        put_blocks(small, grads[0], grads[-1], at[CORE], cols)
 
 
 def halves_kernel(count, at, *refs):
-    parts, (mine, give) = refs[:count], refs[count:]
-    lines = mine.shape[0]
+    parts, (mine, give, out) = refs[:count], refs[count:]
+    lines, cols = mine.shape
+    fold = out.shape[1] // 2
     total = parts[0][...]
     for part in parts[1:]:
         total = total + part[...].astype(WIDE)
     first = at[T] == 0
-    mine[...] = jnp.where(first, total[:lines], total[lines:])
-    give[...] = jnp.where(first, total[lines:], total[:lines]).astype(LOW)
-
-
-def finish_kernel(part, small_rows, at, mine, got, qkv, out, memory, vectors, gains, up, turn):
+    low, high = total[:lines, :cols], total[lines:, :cols]
+    mine[...] = jnp.where(first, low, high)
+    give[...] = jnp.where(first, high, low).astype(LOW)
+    out[:, :fold] = total[:lines, cols:]
+    out[:, fold:] = total[lines:, cols:]
+
+
+def finish_kernel(part, small_rows, at, mine, got, qkv, memory, vectors, gains, up, turn):
     lines = mine.shape[0]
     cols, width = 3 * part, 2 * part
     first = at[T] == 0
@@ -515,7 +583,6 @@
             qkv[:, low + part : low + part + PAIR] = jnp.where(first, b, a)
     turn[...] = jnp.zeros_like(turn)
     turn[:lines, :] = mine[:, cols : cols + PAIR] + got[:, cols : cols + PAIR].astype(WIDE)
-    out[...] = mine[:, cols + PAIR :] + got[:, cols + PAIR :].astype(WIDE)
     small = turn[...].T
     for target, (low, high) in zip((memory, vectors, gains, up), small_rows):
         target[...] = small[low:high, :lines]
@@ -673,24 +740,33 @@
 
     kept, sent = call(
         functools.partial(columns_kernel, part, small_rows),
-        [low_of(lines, cols + PAIR + width)] * 2,
+        [low_of(lines, cols + PAIR)] * 2,
         lax.axis_index("tensor").astype(jnp.int32).reshape(1),
-        qkv_weight, bias_vec, gains, mem_init, up_bias.reshape(spots, feat), out_weight,
+        qkv_weight, bias_vec, gains, mem_init, up_bias.reshape(spots, feat),
         scratch=[pltpu.VMEM((PAIR, PAIR), WIDE)],
         room=48 << 20,
     )
-    got = swap_tensor(sent)
-    (first_pair,) = call(pair_kernel, [low_of(2 * lines, kept.shape[1])], at, kept, got)
+    first_cols = cols + PAIR + part
+    (first_pair,) = call(
+        pair_kernel, [low_of(2 * lines, first_cols)], at, kept, swap_tensor(sent), out_weight
+    )
     rows_low = jnp.pad(rows_in[:, 0, :], ((0, padded - half_rows), (0, 0)))
     rows_other = swap_tensor(tie(rows_low, first_pair))
     first_z = spread_outer(first_pair, digits)
     first_z, rows_other = join(first_z, rows_other)
     first_x = rotate(first_z, x_digit, 1)
     up_z = spread_outer(tie(ffn_up, first_z), digits)
+    down_in = tie(ffn_down.T, up_z)
     first_z, first_x, up_z = join(first_z, first_x, up_z)
-    wqkv, wout = assemble(at, first_z, first_x, digits, cols + PAIR)
+    first_parts = swap_blocks(first_z, first_x, digits)
+    wqkv = assemble(at, first_parts, digits, cols + PAIR)
+    (out_sent,) = call(
+        functools.partial(unfold_kernel, cols + PAIR),
+        [low_of(dp_count // 2, lines, width)], at, first_z, first_x,
+    )
+    out_got = swap_tensor(out_sent)
     up_x = rotate(up_z, x_digit, 1)
-    down_z = spread_outer(tie(ffn_down.T, up_z), digits)
+    down_z = spread_outer(down_in, digits)
 
     projected, mix_own, mix_sent, log_total, layer_in, small = call(
         functools.partial(forward_kernel, half_rows, mem_count, doc_count, bias),
@@ -711,6 +787,15 @@
         ],
     )
     mix_got = swap_tensor(mix_sent)
+    out_got = tie(out_got, mix_sent)
+    (wout,) = call(
+        functools.partial(
+            assemble_out_kernel, tuple(size for _, size in digits), cols + PAIR
+        ),
+        [low_of(dp_count, 2 * lines, width)],
+        at, *first_parts, out_got, rotate(out_got, core_digit, 1),
+    )
+    wout = wout.reshape(width, width)
     mixed, unit, scale, normed_own = call(
         functools.partial(first_norm_kernel, bias, gain),
         [low_of(padded, width), wide_of(padded, width), wide_of(padded, PAIR), low_of(padded, width)],
@@ -720,14 +805,14 @@
 
     normed_got = swap_tensor(normed_own)
     up_x, up_z, down_z = tie(up_x, mix_sent), tie(up_z, mix_sent), tie(down_z, mix_sent)
-    up = assemble(at, up_z, up_x, digits)
+    up = assemble(at, swap_blocks(up_z, up_x, digits), digits, hidden_mine)
     (up_b,) = call(
         functools.partial(up_row_kernel, edges[3], spots),
         [wide_of(ROWS, hidden_mine)], at, small, jnp.asarray(target),
     )
     down_x = rotate(down_z, x_digit, 1)
     normed_got, down_x, up_b, up = join(normed_got, down_x, up_b, up)
-    down_t = assemble(at, down_z, down_x, digits)
+    down_t = assemble(at, swap_blocks(down_z, down_x, digits), digits, hidden_mine)
 
     def feed_forward(rows):
         pre_act = nn(rows, up).reshape(-1, *up_b.shape) + up_b
@@ -762,21 +847,17 @@
     d_first_sent = d_first_sent.astype(LOW)
     d_first_got = swap_tensor(d_first_sent)
 
-    core = lax.axis_index("dp") % 2
     outs = gradient_outs(width, hidden_mine, dp_count)
     down_grads = call(
         rest_kernel, outs, at, down_own, tie(d_ffn_got, d_first_sent), hidden_got
     )
-    down_kept, down_sent = split_cores(down_grads, dp_count, core)
-    down_kept, down_sent = halve(at, down_kept, rotate(down_sent, core_digit, 1))
+    down_kept, down_sent = halve(at, *swap_cores(down_grads, dp_count, core_digit))
     down_got = rotate(down_sent, x_digit, 1)
     up_sums, *up_grads = call(
         functools.partial(rest_sums_kernel, spots), [wide_of(spots, part)] + outs, at,
-        up_own, sums_own, normed_got, tie(d_pre_got, d_first_sent), jnp.asarray(target),
-    )
-    up_kept, up_sent = split_cores(up_grads, dp_count, core)
-    up_kept, up_sent = halve(at, up_kept, rotate(up_sent, core_digit, 1))
-    up_got = rotate(tie(up_sent, down_got), x_digit, 1)
+        up_own, sums_own, normed_got, tie(d_pre_got, down_sent), jnp.asarray(target),
+    )
+    up_kept, up_sent = halve(at, *swap_cores(up_grads, dp_count, core_digit))
 
     d_attn_in, d_attn, d_mix_own, d_mix_sent, sums_one = call(
         functools.partial(first_back_kernel, gain),
@@ -791,14 +872,18 @@
     )
     d_mix_got = swap_tensor(d_mix_sent)
     out_grads = call(
-        gradient_kernel, gradient_outs(width, width, dp_count), at, mixed, tie(d_attn, d_mix_sent)
-    )
-    out_kept, out_sent = split_cores(out_grads, dp_count, core)
-    out_kept, out_sent = halve(at, out_kept, rotate(out_sent, core_digit, 1))
-    out_got = rotate(tie(out_sent, up_got), x_digit, 1)
-    down_kept, down_sent = outer_parts(at, [down_kept], [down_got], digits)
-    d_mix_got, *down_sent = join(d_mix_got, *down_sent)
+        out_gradient_kernel, gradient_outs(width, width, dp_count, OUT_TILE),
+        at, mixed, tie(d_attn, d_mix_sent),
+    )
+    out_kept, out_parts = swap_cores(out_grads, dp_count, core_digit)
+    out_kept, out_sent = call(
+        rows_halves_kernel, [low_of(dp_count // 2, lines, width)] * 2, at, out_kept, *out_parts
+    )
+    down_kept, down_sent = outer_parts(at, down_kept, down_got, digits)
+    d_mix_got, out_sent, up_sent, *down_sent = join(d_mix_got, out_sent, up_sent, *down_sent)
     down_got = outer_send(down_sent, digits)
+    out_got = swap_tensor(out_sent)
+    up_got = rotate(up_sent, x_digit, 1)
 
     d_projected, proj_sums = call(
         functools.partial(backward_kernel, half_rows, mem_count, doc_count),
@@ -813,7 +898,7 @@
             pltpu.VMEM((rows, part), LOW),
         ],
     )
-    up_kept, up_sent = outer_parts(at, [up_kept], [up_got], digits)
+    up_kept, up_sent = outer_parts(at, up_kept, up_got, digits)
     d_in_own, d_in_sent, *qkv_grads = call(
         functools.partial(projection_back_kernel, small_rows),
         [wide_of(padded, width), low_of(padded, width)]
@@ -821,37 +906,39 @@
         at, layer_in, d_projected, proj_sums, sums_one, sums_two, up_sums, wqkv, d_attn_in,
         scratch=[pltpu.VMEM((PAIR, width), WIDE)],
     )
-    qkv_kept, qkv_sent = split_cores(qkv_grads, dp_count, core)
-    qkv_sent, *up_sent = join(qkv_sent, *up_sent, *down_got)[: 1 + len(up_sent)]
-    qkv_kept, qkv_sent = halve(at, qkv_kept, rotate(qkv_sent, core_digit, 1))
-
+    out_got, *qkv_grads = join(out_got, *qkv_grads, *down_got)[: 1 + len(qkv_grads)]
+    out_kept, out_sent = halve(at, out_kept, [out_got])
+    out_got = rotate(out_sent, x_digit, 1)
+    qkv_kept, qkv_sent = halve(at, *swap_cores(qkv_grads, dp_count, core_digit))
+
+    qkv_sent, *up_sent = join(qkv_sent, *up_sent)
     qkv_got = rotate(qkv_sent, x_digit, 1)
     up_got = outer_send(up_sent, digits)
     qkv_got, d_in_sent, out_got, *up_got = join(qkv_got, d_in_sent, out_got, *up_got)
     d_in_got = swap_tensor(d_in_sent)
-    both_kept, both_sent = outer_parts(at, [qkv_kept, out_kept], [qkv_got, out_got], digits)
+    both_kept, both_sent = outer_parts(
+        at, qkv_kept, qkv_got, digits, out_kept, out_got
+    )
     both_got = outer_send(both_sent, digits)
     grad_ffn_down = outer_sum(down_kept, down_got, digits)
     grad_ffn_up = outer_sum(up_kept, up_got, digits)
     (grad_rows,) = call(
         functools.partial(rows_kernel, mem_count), [wide_of(half_rows, width)], at, d_in_own, d_in_got
     )
-    grad_ffn_down, grad_ffn_up, grad_rows, *both_got = join(
-        grad_ffn_down, grad_ffn_up, grad_rows, *both_got
-    )
+    grad_rows, *both_got = join(grad_rows, *both_got)
 
     if len(digits) == 3:
         parts = [both_kept[0], *[part[0] for part in both_got]]
     else:
         parts = [outer_sum(both_kept, both_got, digits)]
-    mine, give = call(
+    mine, give, grad_out_weight = call(
         functools.partial(halves_kernel, len(parts)),
-        [wide_of(lines, kept.shape[1]), low_of(lines, kept.shape[1])],
+        [wide_of(lines, cols + PAIR), low_of(lines, cols + PAIR), wide_of(lines, width)],
         at, *parts,
     )
-    grad_qkv, grad_out_weight, grad_mem, grad_vec, grad_gains, grad_up_bias = call(
+    grad_qkv, grad_mem, grad_vec, grad_gains, grad_up_bias = call(
         functools.partial(finish_kernel, part, small_rows),
-        [wide_of(lines, 3 * width), wide_of(lines, width)] + [wide_of(n, feat) for n in counts],
+        [wide_of(lines, 3 * width)] + [wide_of(n, feat) for n in counts],
         at, mine, swap_tensor(give),
         scratch=[pltpu.VMEM((PAIR, PAIR), WIDE)],
     )

time: 212 us -> 198 us (0.934)
  waiting for transfers between devices: 90.6 us -> 70.7 us
  starting transfers between devices: 50.1 us -> 53.4 us
  Pallas kernels: 51.2 us -> 53.6 us
    ppermute x35 -> x47, waiting for transfers between devices: 60 us -> 45.1 us  [rotate(): return lax.ppermute(value, 'dp', pairs)]
    ppermute x10 -> x12, waiting for transfers between devices: 30.7 us -> 25.6 us  [swap_tensor(): return lax.ppermute(value, 'tensor', [(0, 1), (1, 0)])]
    ppermute x35 -> x47, starting transfers between devices: 34.5 us -> 39.4 us  [rotate(): return lax.ppermute(value, 'dp', pairs)]
    pallas_call x26 -> x29, Pallas kernels: 51.2 us -> 53.6 us  [call(): pl.pallas_call(kernel, in_specs=[pl.BlockSpec(memory_space=pltpu.SMEM)] +...]
    ppermute x10 -> x12, starting transfers between devices: 15.6 us -> 14 us  [swap_tensor(): return lax.ppermute(value, 'tensor', [(0, 1), (1, 0)])]
  transfers between devices with their start and end apart: 45 -> 59, of which waited for: 21 -> 22; matrix products, arithmetic and copies ran while one was open for 4% -> 5% of each run, Pallas kernels for 20% -> 23%
where the time goes in v1:
time: 198 us
  waiting for transfers between devices  70.7 us (36%)
  Pallas kernels  53.6 us (27%)
  starting transfers between devices  53.4 us (27%)
  local copies, waits for them, and re-layouts  8.73 us (4%)
  matrix products  7.12 us (4%)
  between operations  2.46 us (1%)
    pallas_call x29, Pallas kernels, call(): pl.pallas_call(kernel, in_specs=[pl.BlockSpec(memory_space=pltpu.SMEM)] +...  53.6 us
    ppermute x47, waiting for transfers between devices, rotate(): return lax.ppermute(value, 'dp', pairs)  45.1 us
    ppermute x47, starting transfers between devices, rotate(): return lax.ppermute(value, 'dp', pairs)  39.4 us
    ppermute x12, waiting for transfers between devices, swap_tensor(): return lax.ppermute(value, 'tensor', [(0, 1), (1, 0)])  25.6 us
    ppermute x12, starting transfers between devices, swap_tensor(): return lax.ppermute(value, 'tensor', [(0, 1), (1, 0)])  14 us
    unnamed x19, local copies, waits for them, and re-layouts  5.44 us
  transfers between devices with their start and end apart: 59, of which 22 were waited for; matrix products, arithmetic and copies ran while one was open for 5% of the time, Pallas kernels for 23%

profile of v1, /device:TPU:0, one launch (start us, length us, event | category | flops | bytes accessed | tf_op | source)
XLA Modules:
  0.0 197.8 jit_solution(12603481967984667394)
XLA Ops:
  1.4 0.9 copy-done.2
  4.4 3.0 %collective-permute-start = (bf16[24,1280]{1,0:T(8,128)(2,1)S(1)}, bf16[24,1280]{1,0:T(8,128)(2,1)S(1)}, u32[]{:S(2)}, u32[]{:S(2)}) collective-permute-start(bf16[24,1280]{1,0:T(8,128)(2,1)S(1)} %get-tuple-element.139), channel_id=1, source_target_pairs={{0,1},{1,0},{2,3},{3,2},{4,5},{5,4},{6,7},{7,6},{8,9},{9,8},{10,11... | collective-permute-start | bytes 184328 | tf_op jit(solution)/shard_map/ppermute | solution.py:102
  8.7 1.0 pad.4.own
  11.8 1.2 collective-permute-start.4
  13.0 3.6 %collective-permute-start.3 = (bf16[48,1664]{1,0:T(8,128)(2,1)S(1)}, bf16[48,1664]{1,0:T(8,128)(2,1)S(1)}, u32[]{:S(2)}, u32[]{:S(2)}) collective-permute-start(bf16[48,1664]{1,0:T(8,128)(2,1)S(1)} %shard_map.214), channel_id=1, source_target_pairs={{0,24},{2,26},{4,28},{6,30},{8,0},{10,2},{12,4},{14,6},{16,8},{18,... | collective-permute-start | bytes 479240 | tf_op jit(solution)/shard_map/ppermute | solution.py:98
  16.6 1.0 collective-permute-start.2
  17.6 3.6 %collective-permute-done.3 = bf16[48,1664]{1,0:T(8,128)(2,1)S(1)} collective-permute-done((bf16[48,1664]{1,0:T(8,128)(2,1)S(1)}, bf16[48,1664]{1,0:T(8,128)(2,1)S(1)}, u32[]{:S(2)}, u32[]{:S(2)}) %collective-permute-start.3) | collective-permute-done | bytes 159776 | tf_op jit(solution)/shard_map/ppermute | solution.py:98
  21.2 4.2 %collective-permute-done.1 = bf16[48,1664]{1,0:T(8,128)(2,1)S(1)} collective-permute-done((bf16[48,1664]{1,0:T(8,128)(2,1)S(1)}, bf16[48,1664]{1,0:T(8,128)(2,1)S(1)}, u32[]{:S(2)}, u32[]{:S(2)}) %collective-permute-start.1) | collective-permute-done | bytes 159776 | tf_op jit(solution)/shard_map/ppermute | solution.py:98
  25.5 4.1 %collective-permute-done.2 = bf16[48,1664]{1,0:T(8,128)(2,1)S(1)} collective-permute-done((bf16[48,1664]{1,0:T(8,128)(2,1)S(1)}, bf16[48,1664]{1,0:T(8,128)(2,1)S(1)}, u32[]{:S(2)}, u32[]{:S(2)}) %collective-permute-start.2) | collective-permute-done | bytes 159776 | tf_op jit(solution)/shard_map/ppermute | solution.py:98
  29.7 1.6 collective-permute-start.5
  31.3 2.6 %collective-permute-start.7 = (bf16[48,1536]{1,0:T(8,128)(2,1)S(1)}, bf16[48,1536]{1,0:T(8,128)(2,1)S(1)}, u32[]{:S(2)}, u32[]{:S(2)}) collective-permute-start(bf16[48,1536]{1,0:T(8,128)(2,1)S(1)} %copy-done.7), channel_id=1, source_target_pairs={{0,16},{2,18},{4,20},{6,22},{8,24},{10,26},{12,28},{14,30},{16,0},... | collective-permute-start | bytes 442376 | tf_op jit(solution)/shard_map/ppermute | solution.py:98
  33.9 1.2 collective-permute-start.8
  35.1 4.8 %collective-permute-done.6 = bf16[48,1536]{1,0:T(8,128)(2,1)S(1)} collective-permute-done((bf16[48,1536]{1,0:T(8,128)(2,1)S(1)}, bf16[48,1536]{1,0:T(8,128)(2,1)S(1)}, u32[]{:S(2)}, u32[]{:S(2)}) %collective-permute-start.6) | collective-permute-done | bytes 147488 | tf_op jit(solution)/shard_map/ppermute | solution.py:98
  39.9 4.3 %collective-permute-done.7 = bf16[48,1536]{1,0:T(8,128)(2,1)S(1)} collective-permute-done((bf16[48,1536]{1,0:T(8,128)(2,1)S(1)}, bf16[48,1536]{1,0:T(8,128)(2,1)S(1)}, u32[]{:S(2)}, u32[]{:S(2)}) %collective-permute-start.7) | collective-permute-done | bytes 147488 | tf_op jit(solution)/shard_map/ppermute | solution.py:98
  44.3 0.9 collective-permute-done.5.refs_1_.x_got
  45.7 1.5 collective-permute-start.19
  48.5 1.1 collective-permute-start.15
  49.6 2.1 %collective-permute-start.16 = (bf16[48,1536]{1,0:T(8,128)(2,1)S(1)}, bf16[48,1536]{1,0:T(8,128)(2,1)S(1)}, u32[]{:S(2)}, u32[]{:S(2)}) collective-permute-start(bf16[48,1536]{1,0:T(8,128)(2,1)S(1)} %bitcast.81), channel_id=1, source_target_pairs={{0,16},{2,18},{4,20},{6,22},{8,24},{10,26},{12,28},{14,30},{16,0},... | collective-permute-start | bytes 442376 | tf_op jit(solution)/shard_map/ppermute | solution.py:98
  53.1 9.1 %shard_map.216 = (bf16[544,1152]{1,0:T(8,128)(2,1)S(1)}, bf16[272,384]{1,0:T(8,128)(2,1)S(1)}, bf16[272,384]{1,0:T(8,128)(2,1)S(1)}, f32[544,128]{1,0:T(8,128)S(...) custom-call(s32[15]{0:T(128)S(1)} %concatenate.3.at, bf16[272,768]{1,0:T(8,128)(2,1)S(1)} %pad.4.own, ...), custom_call_target="tpu_custom_call" | custom-call | flops 1 | bytes 1 | tf_op jit(solution)/shard_map/pallas_call | solution.py:58
  62.2 1.4 collective-permute-start.11
  64.3 0.9 collective-permute-start.18
  66.0 2.3 %collective-permute-done.11.got = bf16[272,384]{1,0:T(8,128)(2,1)S(1)} collective-permute-done((bf16[272,384]{1,0:T(8,128)(2,1)S(1)}, bf16[272,384]{1,0:T(8,128)(2,1)S(1)}, u32[]{:S(2)}, u32[]{:S(2)}) %collective-permute-start.11) | collective-permute-done | bytes 208928 | tf_op jit(solution)/shard_map/ppermute | solution.py:102
  68.2 1.3 shard_map.219
  69.5 1.4 collective-permute-start.14
  70.9 1.4 shard_map.220
  73.1 6.9 %collective-permute-done.18.refs_1_ = bf16[4,48,1536]{2,1,0:T(8,128)(2,1)S(1)} collective-permute-done((bf16[4,48,1536]{2,1,0:T(8,128)(2,1)S(1)}, bf16[4,48,1536]{2,1,0:T(8,128)(2,1)S(1)}, u32[]{:S(2)}, u32[]{:S(2)}) %collective-permute-start.18) | collective-permute-done | bytes 589856 | tf_op jit(solution)/shard_map/ppermute | solution.py:98
  80.2 0.9 multiply_convert_fusion.1
  81.1 0.9 collective-permute-done.23.refs_3_
  82.7 0.8 convolution_convert_fusion.1
  84.4 0.9 multiply_convert_fusion
  86.1 9.2 %collective-permute-done.24.got = bf16[272,768]{1,0:T(8,128)(2,1)S(1)} collective-permute-done((bf16[272,768]{1,0:T(8,128)(2,1)S(1)}, bf16[272,768]{1,0:T(8,128)(2,1)S(1)}, u32[]{:S(2)}, u32[]{:S(2)}) %collective-permute-start.24) | collective-permute-done | bytes 417824 | tf_op jit(solution)/shard_map/ppermute | solution.py:102
  95.3 2.0 %shard_map.223 = (bf16[266,768]{1,0:T(8,128)(2,1)}, f32[272,768]{1,0:T(8,128)S(1)}, bf16[272,768]{1,0:T(8,128)(2,1)S(1)}, f32[8,768]{1,0:T(8,128)S(1)}) custom-call(s32[15]{0:T(128)S(1)} %concatenate.3.at, f32[272,768]{1,0:T(8,128)S(1)} %get-tuple-element.151.unit, f32[32,768]{1,0:T(8,128)S(1)} %get-tuple-element.150.small, f32[272,768]{1,0:T(8,128)S(1)} %fusion.10.own, ...), custom_call_target="tpu_custom_call" | custom-call | flops 1 | bytes 1 | tf_op jit(solution)/shard_map/pallas_call | solution.py:58
  98.0 1.0 fusion.b_up
  99.0 3.7 %shard_map.224 = (f32[768,1536]{1,0:T(8,128)S(1)}, f32[768,1536]{1,0:T(8,128)S(1)}, f32[1,1536]{1,0:T(1,128)S(1)}) custom-call(s32[15]{0:T(128)S(1)} %concatenate.3.at, bf16[272,768]{1,0:T(8,128)(2,1)S(1)} %get-tuple-element.166.a_down, bf16[272,1536]{1,0:T(8,128)(2,1)S(1)} %get-tuple-element.278.b_down, bf16[272,768]{1,0:T(8,128)(2,1)S(1)} %get-tuple-element.162.a_up, ...), custom_call_target="tpu_custom_call" | custom-call | flops 1 | bytes 1 | tf_op jit(solution)/shard_map/pallas_call | solution.py:58
  103.6 4.6 %collective-permute-done.25.a = bf16[272,768]{1,0:T(8,128)(2,1)S(1)} collective-permute-done((bf16[272,768]{1,0:T(8,128)(2,1)S(1)}, bf16[272,768]{1,0:T(8,128)(2,1)S(1)}, u32[]{:S(2)}, u32[]{:S(2)}) %collective-permute-start.25) | collective-permute-done | bytes 417824 | tf_op jit(solution)/shard_map/ppermute | solution.py:102
  108.1 1.0 fusion.1.b
  110.8 2.4 %shard_map.228 = (bf16[8,48,1536]{2,1,0:T(8,128)(2,1)S(1)}, bf16[8,48,384]{2,1,0:T(8,128)(2,1)S(1)}, bf16[8,48,384]{2,1,0:T(8,128)(2,1)S(1)}, bf16[8,48,384]{2,1,0:T(8,128)(2,1)S(1)}, bf16[8,48,384]{2,1,0:T(8,128)(2,1)S(1)}) custom-call(s32[15]{0:T(128)S(1)} %concatenate.3.at, f32[768,1536]{1,0:T(8,128)S(1)} %get-tuple-element.184.own, ...), custom_call_target="tpu_custom_call" | custom-call | flops 1 | bytes 1 | tf_op jit(solution)/shard_map/pallas_call | solution.py:58
  116.2 0.8 shard_map.229
  117.0 1.2 collective-permute-start.39
  118.2 3.6 %shard_map.230 = (f32[4,384]{1,0:T(4,128)S(1)}, bf16[8,48,1536]{2,1,0:T(8,128)(2,1)S(1)}, bf16[8,48,384]{2,1,0:T(8,128)(2,1)S(1)}, bf16[8,48,384]{2,1,0:T(8,128)...) custom-call(s32[15]{0:T(128)S(1)} %concatenate.3.at, ...), custom_call_target="tpu_custom_call" | custom-call | flops 1 | bytes 1 | tf_op jit(solution)/shard_map/pallas_call | solution.py:58
  122.9 1.6 shard_map.225
  124.5 1.2 collective-permute-start.27
  125.7 1.4 shard_map.226
  129.9 2.6 %collective-permute-done.39.got = bf16[4,48,1536]{2,1,0:T(8,128)(2,1)S(1)} collective-permute-done((bf16[4,48,1536]{2,1,0:T(8,128)(2,1)S(1)}, bf16[4,48,1536]{2,1,0:T(8,128)(2,1)S(1)}, u32[]{:S(2)}, u32[]{:S(2)}) %collective-permute-start.39) | collective-permute-done | bytes 589856 | tf_op jit(solution)/shard_map/ppermute | solution.py:98
  133.1 1.3 collective-permute-start.40
  134.5 1.0 collective-permute-start.48
  135.4 1.2 collective-permute-start.41
  136.6 1.3 collective-permute-start.42
  137.9 2.0 %collective-permute-start.43 = (bf16[1,48,1536]{2,1,0:T(8,128)(2,1)S(1)}, bf16[1,48,1536]{2,1,0:T(8,128)(2,1)S(1)}, u32[]{:S(2)}, u32[]{:S(2)}) collective-permute-start(bf16[1,48,1536]{2,1,0:T(8,128)(2,1)S(1)} %get-tuple-element.220), channel_id=1, source_target_pairs={{0,24},{2,26},{4,28},{6,30},{8,0},{10,2},{12,4},{14,6},{16,8},{18,... | collective-permute-start | bytes 442376 | tf_op jit(solution)/shard_map/ppermute | solution.py:98
  139.9 10.5 %shard_map.233 = (bf16[544,1152]{1,0:T(8,128)(2,1)S(1)}, f32[1,1152]{1,0:T(1,128)S(1)}) custom-call(s32[15]{0:T(128)S(1)} %concatenate.3.at, bf16[544,1152]{1,0:T(8,128)(2,1)S(1)} %get-tuple-element.164.qkv, bf16[272,384]{1,0:T(8,128)(2,1)S(1)} %get-tuple-element.172.own, bf16[272,384]{1,0:T(8,128)(2,1)S(1)} %collective-permute-done.27.got, ...), custom_call_target="tpu_custom_call" | custom-call | flops 1 | bytes 1 | tf_op jit(solution)/shard_map/pallas_call | solution.py:58
  150.5 3.6 %shard_map.234 = (f32[272,768]{1,0:T(8,128)S(1)}, bf16[272,768]{1,0:T(8,128)(2,1)S(1)}, bf16[8,48,1280]{2,1,0:T(8,128)(2,1)S(1)}, bf16[8,48,384]{2,1,0:T(8,128)(...) custom-call(s32[15]{0:T(128)S(1)} %concatenate.3.at, ...), custom_call_target="tpu_custom_call" | custom-call | flops 1 | bytes 1 | tf_op jit(solution)/shard_map/pallas_call | solution.py:58
  155.8 0.9 collective-permute-done.47.refs_3_
  157.5 1.5 collective-permute-start.49
  160.3 1.6 collective-permute-start.52
  161.9 2.7 %collective-permute-start.53 = (bf16[1,48,1536]{2,1,0:T(8,128)(2,1)S(1)}, bf16[1,48,1536]{2,1,0:T(8,128)(2,1)S(1)}, u32[]{:S(2)}, u32[]{:S(2)}) collective-permute-start(bf16[1,48,1536]{2,1,0:T(8,128)(2,1)S(1)} %get-tuple-element.239), channel_id=1, source_target_pairs={{0,24},{2,26},{4,28},{6,30},{8,0},{10,2},{12,4},{14,6},{16,8},{18,... | collective-permute-start | bytes 442376 | tf_op jit(solution)/shard_map/ppermute | solution.py:98
  164.6 9.5 %collective-permute-done.50.refs_1_ = bf16[4,24,768]{2,1,0:T(8,128)(2,1)S(1)} collective-permute-done((bf16[4,24,768]{2,1,0:T(8,128)(2,1)S(1)}, bf16[4,24,768]{2,1,0:T(8,128)(2,1)S(1)}, u32[]{:S(2)}, u32[]{:S(2)}) %collective-permute-start.50) | collective-permute-done | bytes 147488 | tf_op jit(solution)/shard_map/ppermute | solution.py:98
  174.7 2.6 %collective-permute-start.55 = (bf16[1,48,1664]{2,1,0:T(8,128)(2,1)S(1)}, bf16[1,48,1664]{2,1,0:T(8,128)(2,1)S(1)}, u32[]{:S(2)}, u32[]{:S(2)}) collective-permute-start(bf16[1,48,1664]{2,1,0:T(8,128)(2,1)S(1)} %get-tuple-element.245), channel_id=1, source_target_pairs={{0,8},{2,10},{4,12},{6,14},{8,16},{10,18},{12,20},{14,22},{16,24},... | collective-permute-start | bytes 479240 | tf_op jit(solution)/shard_map/ppermute | solution.py:98
  177.3 1.3 collective-permute-start.56
  178.7 1.1 collective-permute-start.57
  181.3 8.5 %collective-permute-done.54.got = bf16[272,768]{1,0:T(8,128)(2,1)S(1)} collective-permute-done((bf16[272,768]{1,0:T(8,128)(2,1)S(1)}, bf16[272,768]{1,0:T(8,128)(2,1)S(1)}, u32[]{:S(2)}, u32[]{:S(2)}) %collective-permute-start.54) | collective-permute-done | bytes 417824 | tf_op jit(solution)/shard_map/ppermute | solution.py:102
  190.5 1.2 shard_map.240
  193.2 1.7 copy.24
  194.9 1.0 collective-permute-done.58.got
  195.9 1.3 shard_map.241
  (120 shorter events, 32.5 us)
Async XLA Ops:
  1.4 0.9 copy-start.2
  4.3 26.9 %copy-start.7 = (bf16[48,1536]{1,0:T(8,128)(2,1)S(1)}, bf16[48,1536]{1,0:T(8,128)(2,1)}, u32[]{:S(2)}) copy-start(bf16[48,1536]{1,0:T(8,128)(2,1)} %param.24) | copy-start | bytes 442372
  4.4 6.1 %collective-permute-start = (bf16[24,1280]{1,0:T(8,128)(2,1)S(1)}, bf16[24,1280]{1,0:T(8,128)(2,1)S(1)}, u32[]{:S(2)}, u32[]{:S(2)}) collective-permute-start(bf16[24,1280]{1,0:T(8,128)(2,1)S(1)} %get-tuple-element.139), channel_id=1, source_target_pairs={{0,1},{1,0},{2,3},{3,2},{4,5},{5,4},{6,7},{7,6},{8,9},{9,8},{10,11... | collective-permute-start | bytes 184328 | tf_op jit(solution)/shard_map/ppermute | solution.py:102
  11.8 17.9 %collective-permute-start.4 = (bf16[272,768]{1,0:T(8,128)(2,1)S(1)}, bf16[272,768]{1,0:T(8,128)(2,1)S(1)}, u32[]{:S(2)}, u32[]{:S(2)}) collective-permute-start(bf16[272,768]{1,0:T(8,128)(2,1)S(1)} %pad.4.own), channel_id=1, source_target_pairs={{0,1},{1,0},{2,3},{3,2},{4,5},{5,4},{6,7},{7,6},{8,9},{9,8},{10,11... | collective-permute-start | bytes 1253384 | tf_op jit(solution)/shard_map/ppermute | solution.py:102
  13.0 8.2 %collective-permute-start.3 = (bf16[48,1664]{1,0:T(8,128)(2,1)S(1)}, bf16[48,1664]{1,0:T(8,128)(2,1)S(1)}, u32[]{:S(2)}, u32[]{:S(2)}) collective-permute-start(bf16[48,1664]{1,0:T(8,128)(2,1)S(1)} %shard_map.214), channel_id=1, source_target_pairs={{0,24},{2,26},{4,28},{6,30},{8,0},{10,2},{12,4},{14,6},{16,8},{18,... | collective-permute-start | bytes 479240 | tf_op jit(solution)/shard_map/ppermute | solution.py:98
  16.6 8.8 %collective-permute-start.1 = (bf16[48,1664]{1,0:T(8,128)(2,1)S(1)}, bf16[48,1664]{1,0:T(8,128)(2,1)S(1)}, u32[]{:S(2)}, u32[]{:S(2)}) collective-permute-start(bf16[48,1664]{1,0:T(8,128)(2,1)S(1)} %shard_map.214), channel_id=1, source_target_pairs={{0,8},{2,10},{4,12},{6,14},{8,16},{10,18},{12,20},{14,22},{16,24},... | collective-permute-start | bytes 479240 | tf_op jit(solution)/shard_map/ppermute | solution.py:98
  16.6 13.0 %collective-permute-start.2 = (bf16[48,1664]{1,0:T(8,128)(2,1)S(1)}, bf16[48,1664]{1,0:T(8,128)(2,1)S(1)}, u32[]{:S(2)}, u32[]{:S(2)}) collective-permute-start(bf16[48,1664]{1,0:T(8,128)(2,1)S(1)} %shard_map.214), channel_id=1, source_target_pairs={{0,16},{2,18},{4,20},{6,22},{8,24},{10,26},{12,28},{14,30},{16,0},... | collective-permute-start | bytes 479240 | tf_op jit(solution)/shard_map/ppermute | solution.py:98
  29.7 18.9 %copy-start.8 = (bf16[1536,48]{0,1:T(8,128)(2,1)S(1)}, bf16[1536,48]{0,1:T(8,128)(2,1)}, u32[]{:S(2)}) copy-start(bf16[1536,48]{0,1:T(8,128)(2,1)} %param.26) | copy-start | bytes 442372
  29.7 15.5 %collective-permute-start.5 = (bf16[4,48,1664]{2,1,0:T(8,128)(2,1)S(1)}, bf16[4,48,1664]{2,1,0:T(8,128)(2,1)S(1)}, u32[]{:S(2)}, u32[]{:S(2)}) collective-permute-start(bf16[4,48,1664]{2,1,0:T(8,128)(2,1)S(1)} %pad_maximum_fusion.refs_0_.mine), channel_id=1, source_target_pairs={{0,4},{2,6},{4,0},{6,2},{8,12},{10,14},{12,8},{14,10},{16,20},{18,... | collective-permute-start | bytes 1916936 | tf_op jit(solution)/shard_map/ppermute | solution.py:98
  31.3 8.6 %collective-permute-start.6 = (bf16[48,1536]{1,0:T(8,128)(2,1)S(1)}, bf16[48,1536]{1,0:T(8,128)(2,1)S(1)}, u32[]{:S(2)}, u32[]{:S(2)}) collective-permute-start(bf16[48,1536]{1,0:T(8,128)(2,1)S(1)} %copy-done.7), channel_id=1, source_target_pairs={{0,8},{2,10},{4,12},{6,14},{8,16},{10,18},{12,20},{14,22},{16,24},... | collective-permute-start | bytes 442376 | tf_op jit(solution)/shard_map/ppermute | solution.py:98
  31.3 12.9 %collective-permute-start.7 = (bf16[48,1536]{1,0:T(8,128)(2,1)S(1)}, bf16[48,1536]{1,0:T(8,128)(2,1)S(1)}, u32[]{:S(2)}, u32[]{:S(2)}) collective-permute-start(bf16[48,1536]{1,0:T(8,128)(2,1)S(1)} %copy-done.7), channel_id=1, source_target_pairs={{0,16},{2,18},{4,20},{6,22},{8,24},{10,26},{12,28},{14,30},{16,0},... | collective-permute-start | bytes 442376 | tf_op jit(solution)/shard_map/ppermute | solution.py:98
  33.9 10.3 %collective-permute-start.8 = (bf16[48,1536]{1,0:T(8,128)(2,1)S(1)}, bf16[48,1536]{1,0:T(8,128)(2,1)S(1)}, u32[]{:S(2)}, u32[]{:S(2)}) collective-permute-start(bf16[48,1536]{1,0:T(8,128)(2,1)S(1)} %copy-done.7), channel_id=1, source_target_pairs={{0,24},{2,26},{4,28},{6,30},{8,0},{10,2},{12,4},{14,6},{16,8},{18,... | collective-permute-start | bytes 442376 | tf_op jit(solution)/shard_map/ppermute | solution.py:98
  45.2 4.4 %collective-permute-start.10 = (bf16[4,48,1664]{2,1,0:T(8,128)(2,1)S(1)}, bf16[4,48,1664]{2,1,0:T(8,128)(2,1)S(1)}, u32[]{:S(2)}, u32[]{:S(2)}) collective-permute-start(bf16[4,48,1664]{2,1,0:T(8,128)(2,1)S(1)} %collective-permute-done.5.refs_1_.x_got), channel_id=1, source_target_pairs={{0,2},{2,0},{4,6},{6,4},{8,10},{10,8},{12,14},{14,12},{16,18},{18,... | collective-permute-start | bytes 1916936 | tf_op jit(solution)/shard_map/ppermute | solution.py:98
  45.2 6.5 %collective-permute-start.9 = (bf16[4,48,1664]{2,1,0:T(8,128)(2,1)S(1)}, bf16[4,48,1664]{2,1,0:T(8,128)(2,1)S(1)}, u32[]{:S(2)}, u32[]{:S(2)}) collective-permute-start(bf16[4,48,1664]{2,1,0:T(8,128)(2,1)S(1)} %pad_maximum_fusion.refs_0_.mine), channel_id=1, source_target_pairs={{0,2},{2,0},{4,6},{6,4},{8,10},{10,8},{12,14},{14,12},{16,18},{18,... | collective-permute-start | bytes 1916936 | tf_op jit(solution)/shard_map/ppermute | solution.py:98
  45.7 18.0 %collective-permute-start.19 = (bf16[4,48,1536]{2,1,0:T(8,128)(2,1)S(1)}, bf16[4,48,1536]{2,1,0:T(8,128)(2,1)S(1)}, u32[]{:S(2)}, u32[]{:S(2)}) collective-permute-start(bf16[4,48,1536]{2,1,0:T(8,128)(2,1)S(1)} %pad_maximum_fusion.1.refs_0_), channel_id=1, source_target_pairs={{0,4},{2,6},{4,0},{6,2},{8,12},{10,14},{12,8},{14,10},{16,20},{18,... | collective-permute-start | bytes 1769480 | tf_op jit(solution)/shard_map/ppermute | solution.py:98
  47.8 14.4 %collective-permute-start.12 = (bf16[8,24,768]{2,1,0:T(8,128)(2,1)S(1)}, bf16[8,24,768]{2,1,0:T(8,128)(2,1)S(1)}, u32[]{:S(2)}, u32[]{:S(2)}) collective-permute-start(bf16[8,24,768]{2,1,0:T(8,128)(2,1)S(1)} %shard_map.217), channel_id=1, source_target_pairs={{0,1},{1,0},{2,3},{3,2},{4,5},{5,4},{6,7},{7,6},{8,9},{9,8},{10,11... | collective-permute-start | bytes 884744 | tf_op jit(solution)/shard_map/ppermute | solution.py:102
  48.5 15.0 %collective-permute-start.15 = (bf16[48,1536]{1,0:T(8,128)(2,1)S(1)}, bf16[48,1536]{1,0:T(8,128)(2,1)S(1)}, u32[]{:S(2)}, u32[]{:S(2)}) collective-permute-start(bf16[48,1536]{1,0:T(8,128)(2,1)S(1)} %bitcast.80), channel_id=1, source_target_pairs={{0,8},{2,10},{4,12},{6,14},{8,16},{10,18},{12,20},{14,22},{16,24},... | collective-permute-start | bytes 442376 | tf_op jit(solution)/shard_map/ppermute | solution.py:98
  49.6 14.0 %collective-permute-start.16 = (bf16[48,1536]{1,0:T(8,128)(2,1)S(1)}, bf16[48,1536]{1,0:T(8,128)(2,1)S(1)}, u32[]{:S(2)}, u32[]{:S(2)}) collective-permute-start(bf16[48,1536]{1,0:T(8,128)(2,1)S(1)} %bitcast.81), channel_id=1, source_target_pairs={{0,16},{2,18},{4,20},{6,22},{8,24},{10,26},{12,28},{14,30},{16,0},... | collective-permute-start | bytes 442376 | tf_op jit(solution)/shard_map/ppermute | solution.py:98
  51.7 11.9 %collective-permute-start.17 = (bf16[48,1536]{1,0:T(8,128)(2,1)S(1)}, bf16[48,1536]{1,0:T(8,128)(2,1)S(1)}, u32[]{:S(2)}, u32[]{:S(2)}) collective-permute-start(bf16[48,1536]{1,0:T(8,128)(2,1)S(1)} %bitcast.82), channel_id=1, source_target_pairs={{0,24},{2,26},{4,28},{6,30},{8,0},{10,2},{12,4},{14,6},{16,8},{18,... | collective-permute-start | bytes 442376 | tf_op jit(solution)/shard_map/ppermute | solution.py:98
  62.2 6.0 %collective-permute-start.11 = (bf16[272,384]{1,0:T(8,128)(2,1)S(1)}, bf16[272,384]{1,0:T(8,128)(2,1)S(1)}, u32[]{:S(2)}, u32[]{:S(2)}) collective-permute-start(bf16[272,384]{1,0:T(8,128)(2,1)S(1)} %get-tuple-element.147), channel_id=1, source_target_pairs={{0,1},{1,0},{2,3},{3,2},{4,5},{5,4},{6,7},{7,6},{8,9},{9,8},{10,11... | collective-permute-start | bytes 626696 | tf_op jit(solution)/shard_map/ppermute | solution.py:102
  63.6 1.7 collective-permute-start.13
  63.7 8.7 %collective-permute-start.21 = (bf16[4,48,1536]{2,1,0:T(8,128)(2,1)S(1)}, bf16[4,48,1536]{2,1,0:T(8,128)(2,1)S(1)}, u32[]{:S(2)}, u32[]{:S(2)}) collective-permute-start(bf16[4,48,1536]{2,1,0:T(8,128)(2,1)S(1)} %collective-permute-done.19.refs_1_), channel_id=1, source_target_pairs={{0,2},{2,0},{4,6},{6,4},{8,10},{10,8},{12,14},{14,12},{16,18},{18,... | collective-permute-start | bytes 1769480 | tf_op jit(solution)/shard_map/ppermute | solution.py:98
  64.3 8.1 %collective-permute-start.20 = (bf16[4,48,1536]{2,1,0:T(8,128)(2,1)S(1)}, bf16[4,48,1536]{2,1,0:T(8,128)(2,1)S(1)}, u32[]{:S(2)}, u32[]{:S(2)}) collective-permute-start(bf16[4,48,1536]{2,1,0:T(8,128)(2,1)S(1)} %pad_maximum_fusion.1.refs_0_), channel_id=1, source_target_pairs={{0,2},{2,0},{4,6},{6,4},{8,10},{10,8},{12,14},{14,12},{16,18},{18,... | collective-permute-start | bytes 1769480 | tf_op jit(solution)/shard_map/ppermute | solution.py:98
  64.3 15.7 %collective-permute-start.18 = (bf16[4,48,1536]{2,1,0:T(8,128)(2,1)S(1)}, bf16[4,48,1536]{2,1,0:T(8,128)(2,1)S(1)}, u32[]{:S(2)}, u32[]{:S(2)}) collective-permute-start(bf16[4,48,1536]{2,1,0:T(8,128)(2,1)S(1)} %pad_maximum_fusion.2.refs_0_), channel_id=1, source_target_pairs={{0,4},{2,6},{4,0},{6,2},{8,12},{10,14},{12,8},{14,10},{16,20},{18,... | collective-permute-start | bytes 1769480 | tf_op jit(solution)/shard_map/ppermute | solution.py:98
  65.9 5.0 %copy-start = (s32[384,2]{1,0:T(8,128)S(1)}, s32[384,2]{1,0:T(8,128)}, u32[]{:S(2)}) copy-start(s32[384,2]{1,0:T(8,128)} %constant.78.clone.target) | copy-start | bytes 9220
  69.5 10.5 %collective-permute-start.14 = (bf16[272,768]{1,0:T(8,128)(2,1)S(1)}, bf16[272,768]{1,0:T(8,128)(2,1)S(1)}, u32[]{:S(2)}, u32[]{:S(2)}) collective-permute-start(bf16[272,768]{1,0:T(8,128)(2,1)S(1)} %get-tuple-element.162.a_up), channel_id=1, source_target_pairs={{0,1},{1,0},{2,3},{3,2},{4,5},{5,4},{6,7},{7,6},{8,9},{9,8},{10,11... | collective-permute-start | bytes 1253384 | tf_op jit(solution)/shard_map/ppermute | solution.py:102
  70.9 10.2 %collective-permute-start.22 = (bf16[4,48,1536]{2,1,0:T(8,128)(2,1)S(1)}, bf16[4,48,1536]{2,1,0:T(8,128)(2,1)S(1)}, u32[]{:S(2)}, u32[]{:S(2)}) collective-permute-start(bf16[4,48,1536]{2,1,0:T(8,128)(2,1)S(1)} %pad_maximum_fusion.2.refs_0_), channel_id=1, source_target_pairs={{0,2},{2,0},{4,6},{6,4},{8,10},{10,8},{12,14},{14,12},{16,18},{18,... | collective-permute-start | bytes 1769480 | tf_op jit(solution)/shard_map/ppermute | solution.py:98
  80.0 2.0 %collective-permute-start.23 = (bf16[4,48,1536]{2,1,0:T(8,128)(2,1)S(1)}, bf16[4,48,1536]{2,1,0:T(8,128)(2,1)S(1)}, u32[]{:S(2)}, u32[]{:S(2)}) collective-permute-start(bf16[4,48,1536]{2,1,0:T(8,128)(2,1)S(1)} %collective-permute-done.18.refs_1_), channel_id=1, source_target_pairs={{0,2},{2,0},{4,6},{6,4},{8,10},{10,8},{12,14},{14,12},{16,18},{18,... | collective-permute-start | bytes 1769480 | tf_op jit(solution)/shard_map/ppermute | solution.py:98
  83.6 11.7 %collective-permute-start.24 = (bf16[272,768]{1,0:T(8,128)(2,1)S(1)}, bf16[272,768]{1,0:T(8,128)(2,1)S(1)}, u32[]{:S(2)}, u32[]{:S(2)}) collective-permute-start(bf16[272,768]{1,0:T(8,128)(2,1)S(1)} %convolution_convert_fusion.1), channel_id=1, source_target_pairs={{0,1},{1,0},{2,3},{3,2},{4,5},{5,4},{6,7},{7,6},{8,9},{9,8},{10,11... | collective-permute-start | bytes 1253384 | tf_op jit(solution)/shard_map/ppermute | solution.py:102
  85.3 10.0 %copy-start.1 = (bf16[266,1,768]{2,0,1:T(8,128)(2,1)S(1)}, bf16[266,1,768]{2,0,1:T(8,128)(2,1)}, u32[]{:S(2)}) copy-start(bf16[266,1,768]{2,0,1:T(8,128)(2,1)} %param.15) | copy-start | bytes 1225732
  97.3 10.8 %collective-permute-start.25 = (bf16[272,768]{1,0:T(8,128)(2,1)S(1)}, bf16[272,768]{1,0:T(8,128)(2,1)S(1)}, u32[]{:S(2)}, u32[]{:S(2)}) collective-permute-start(bf16[272,768]{1,0:T(8,128)(2,1)S(1)} %get-tuple-element.166.a_down), channel_id=1, source_target_pairs={{0,1},{1,0},{2,3},{3,2},{4,5},{5,4},{6,7},{7,6},{8,9},{9,8},{10,11... | collective-permute-start | bytes 1253384 | tf_op jit(solution)/shard_map/ppermute | solution.py:102
  110.0 12.4 %collective-permute-start.26 = (bf16[272,768]{1,0:T(8,128)(2,1)S(1)}, bf16[272,768]{1,0:T(8,128)(2,1)S(1)}, u32[]{:S(2)}, u32[]{:S(2)}) collective-permute-start(bf16[272,768]{1,0:T(8,128)(2,1)S(1)} %convolution_convert_fusion), channel_id=1, source_target_pairs={{0,1},{1,0},{2,3},{3,2},{4,5},{5,4},{6,7},{7,6},{8,9},{9,8},{10,11... | collective-permute-start | bytes 1253384 | tf_op jit(solution)/shard_map/ppermute | solution.py:102
  113.2 1.6 collective-permute-start.31
  113.3 2.0 %collective-permute-start.32 = (bf16[8,48,384]{2,1,0:T(8,128)(2,1)S(1)}, bf16[8,48,384]{2,1,0:T(8,128)(2,1)S(1)}, u32[]{:S(2)}, u32[]{:S(2)}) collective-permute-start(bf16[8,48,384]{2,1,0:T(8,128)(2,1)S(1)} %get-tuple-element.188), channel_id=1, source_target_pairs={{0,2},{2,0},{4,6},{6,4},{8,10},{10,8},{12,14},{14,12},{16,18},{18,... | collective-permute-start | bytes 884744 | tf_op jit(solution)/shard_map/ppermute | solution.py:98
  113.8 1.9 collective-permute-start.33
  113.9 2.3 %collective-permute-start.34 = (bf16[8,48,384]{2,1,0:T(8,128)(2,1)S(1)}, bf16[8,48,384]{2,1,0:T(8,128)(2,1)S(1)}, u32[]{:S(2)}, u32[]{:S(2)}) collective-permute-start(bf16[8,48,384]{2,1,0:T(8,128)(2,1)S(1)} %get-tuple-element.190), channel_id=1, source_target_pairs={{0,2},{2,0},{4,6},{6,4},{8,10},{10,8},{12,14},{14,12},{16,18},{18,... | collective-permute-start | bytes 884744 | tf_op jit(solution)/shard_map/ppermute | solution.py:98
  117.0 15.4 %collective-permute-start.39 = (bf16[4,48,1536]{2,1,0:T(8,128)(2,1)S(1)}, bf16[4,48,1536]{2,1,0:T(8,128)(2,1)S(1)}, u32[]{:S(2)}, u32[]{:S(2)}) collective-permute-start(bf16[4,48,1536]{2,1,0:T(8,128)(2,1)S(1)} %get-tuple-element.191), channel_id=1, source_target_pairs={{0,4},{2,6},{4,0},{6,2},{8,12},{10,14},{12,8},{14,10},{16,20},{18,... | collective-permute-start | bytes 1769480 | tf_op jit(solution)/shard_map/ppermute | solution.py:98
  121.8 2.7 %collective-permute-start.35 = (bf16[8,48,384]{2,1,0:T(8,128)(2,1)S(1)}, bf16[8,48,384]{2,1,0:T(8,128)(2,1)S(1)}, u32[]{:S(2)}, u32[]{:S(2)}) collective-permute-start(bf16[8,48,384]{2,1,0:T(8,128)(2,1)S(1)} %get-tuple-element.194), channel_id=1, source_target_pairs={{0,2},{2,0},{4,6},{6,4},{8,10},{10,8},{12,14},{14,12},{16,18},{18,... | collective-permute-start | bytes 884744 | tf_op jit(solution)/shard_map/ppermute | solution.py:98
  121.8 5.2 %collective-permute-start.36 = (bf16[8,48,384]{2,1,0:T(8,128)(2,1)S(1)}, bf16[8,48,384]{2,1,0:T(8,128)(2,1)S(1)}, u32[]{:S(2)}, u32[]{:S(2)}) collective-permute-start(bf16[8,48,384]{2,1,0:T(8,128)(2,1)S(1)} %get-tuple-element.195), channel_id=1, source_target_pairs={{0,2},{2,0},{4,6},{6,4},{8,10},{10,8},{12,14},{14,12},{16,18},{18,... | collective-permute-start | bytes 884744 | tf_op jit(solution)/shard_map/ppermute | solution.py:98
  122.4 4.8 %collective-permute-start.37 = (bf16[8,48,384]{2,1,0:T(8,128)(2,1)S(1)}, bf16[8,48,384]{2,1,0:T(8,128)(2,1)S(1)}, u32[]{:S(2)}, u32[]{:S(2)}) collective-permute-start(bf16[8,48,384]{2,1,0:T(8,128)(2,1)S(1)} %get-tuple-element.196), channel_id=1, source_target_pairs={{0,2},{2,0},{4,6},{6,4},{8,10},{10,8},{12,14},{14,12},{16,18},{18,... | collective-permute-start | bytes 884744 | tf_op jit(solution)/shard_map/ppermute | solution.py:98
  122.4 5.3 %collective-permute-start.38 = (bf16[8,48,384]{2,1,0:T(8,128)(2,1)S(1)}, bf16[8,48,384]{2,1,0:T(8,128)(2,1)S(1)}, u32[]{:S(2)}, u32[]{:S(2)}) collective-permute-start(bf16[8,48,384]{2,1,0:T(8,128)(2,1)S(1)} %get-tuple-element.197), channel_id=1, source_target_pairs={{0,2},{2,0},{4,6},{6,4},{8,10},{10,8},{12,14},{14,12},{16,18},{18,... | collective-permute-start | bytes 884744 | tf_op jit(solution)/shard_map/ppermute | solution.py:98
  124.5 8.6 %collective-permute-start.27 = (bf16[272,384]{1,0:T(8,128)(2,1)S(1)}, bf16[272,384]{1,0:T(8,128)(2,1)S(1)}, u32[]{:S(2)}, u32[]{:S(2)}) collective-permute-start(bf16[272,384]{1,0:T(8,128)(2,1)S(1)} %get-tuple-element.173), channel_id=1, source_target_pairs={{0,1},{1,0},{2,3},{3,2},{4,5},{5,4},{6,7},{7,6},{8,9},{9,8},{10,11... | collective-permute-start | bytes 626696 | tf_op jit(solution)/shard_map/ppermute | solution.py:102
  127.1 1.5 collective-permute-start.28
  127.2 1.7 collective-permute-start.29
  127.7 1.5 collective-permute-start.30
  133.1 20.9 %collective-permute-start.40 = (bf16[8,24,768]{2,1,0:T(8,128)(2,1)S(1)}, bf16[8,24,768]{2,1,0:T(8,128)(2,1)S(1)}, u32[]{:S(2)}, u32[]{:S(2)}) collective-permute-start(bf16[8,24,768]{2,1,0:T(8,128)(2,1)S(1)} %get-tuple-element.212), channel_id=1, source_target_pairs={{0,1},{1,0},{2,3},{3,2},{4,5},{5,4},{6,7},{7,6},{8,9},{9,8},{10,11... | collective-permute-start | bytes 884744 | tf_op jit(solution)/shard_map/ppermute | solution.py:102
  134.5 20.7 %collective-permute-start.48 = (bf16[4,48,1536]{2,1,0:T(8,128)(2,1)S(1)}, bf16[4,48,1536]{2,1,0:T(8,128)(2,1)S(1)}, u32[]{:S(2)}, u32[]{:S(2)}) collective-permute-start(bf16[4,48,1536]{2,1,0:T(8,128)(2,1)S(1)} %get-tuple-element.228), channel_id=1, source_target_pairs={{0,4},{2,6},{4,0},{6,2},{8,12},{10,14},{12,8},{14,10},{16,20},{18,... | collective-permute-start | bytes 1769480 | tf_op jit(solution)/shard_map/ppermute | solution.py:98
  135.4 18.6 %collective-permute-start.41 = (bf16[1,48,1536]{2,1,0:T(8,128)(2,1)S(1)}, bf16[1,48,1536]{2,1,0:T(8,128)(2,1)S(1)}, u32[]{:S(2)}, u32[]{:S(2)}) collective-permute-start(bf16[1,48,1536]{2,1,0:T(8,128)(2,1)S(1)} %get-tuple-element.218), channel_id=1, source_target_pairs={{0,8},{2,10},{4,12},{6,14},{8,16},{10,18},{12,20},{14,22},{16,24},... | collective-permute-start | bytes 442376 | tf_op jit(solution)/shard_map/ppermute | solution.py:98
  136.6 17.5 %collective-permute-start.42 = (bf16[1,48,1536]{2,1,0:T(8,128)(2,1)S(1)}, bf16[1,48,1536]{2,1,0:T(8,128)(2,1)S(1)}, u32[]{:S(2)}, u32[]{:S(2)}) collective-permute-start(bf16[1,48,1536]{2,1,0:T(8,128)(2,1)S(1)} %get-tuple-element.219), channel_id=1, source_target_pairs={{0,16},{2,18},{4,20},{6,22},{8,24},{10,26},{12,28},{14,30},{16,0},... | collective-permute-start | bytes 442376 | tf_op jit(solution)/shard_map/ppermute | solution.py:98
  137.9 16.1 %collective-permute-start.43 = (bf16[1,48,1536]{2,1,0:T(8,128)(2,1)S(1)}, bf16[1,48,1536]{2,1,0:T(8,128)(2,1)S(1)}, u32[]{:S(2)}, u32[]{:S(2)}) collective-permute-start(bf16[1,48,1536]{2,1,0:T(8,128)(2,1)S(1)} %get-tuple-element.220), channel_id=1, source_target_pairs={{0,24},{2,26},{4,28},{6,30},{8,0},{10,2},{12,4},{14,6},{16,8},{18,... | collective-permute-start | bytes 442376 | tf_op jit(solution)/shard_map/ppermute | solution.py:98
  154.1 2.6 %collective-permute-start.44 = (bf16[8,48,384]{2,1,0:T(8,128)(2,1)S(1)}, bf16[8,48,384]{2,1,0:T(8,128)(2,1)S(1)}, u32[]{:S(2)}, u32[]{:S(2)}) collective-permute-start(bf16[8,48,384]{2,1,0:T(8,128)(2,1)S(1)} %get-tuple-element.222), channel_id=1, source_target_pairs={{0,2},{2,0},{4,6},{6,4},{8,10},{10,8},{12,14},{14,12},{16,18},{18,... | collective-permute-start | bytes 884744 | tf_op jit(solution)/shard_map/ppermute | solution.py:98
  154.2 2.6 %collective-permute-start.45 = (bf16[8,48,384]{2,1,0:T(8,128)(2,1)S(1)}, bf16[8,48,384]{2,1,0:T(8,128)(2,1)S(1)}, u32[]{:S(2)}, u32[]{:S(2)}) collective-permute-start(bf16[8,48,384]{2,1,0:T(8,128)(2,1)S(1)} %get-tuple-element.223), channel_id=1, source_target_pairs={{0,2},{2,0},{4,6},{6,4},{8,10},{10,8},{12,14},{14,12},{16,18},{18,... | collective-permute-start | bytes 884744 | tf_op jit(solution)/shard_map/ppermute | solution.py:98
  154.7 2.1 %collective-permute-start.46 = (bf16[8,48,384]{2,1,0:T(8,128)(2,1)S(1)}, bf16[8,48,384]{2,1,0:T(8,128)(2,1)S(1)}, u32[]{:S(2)}, u32[]{:S(2)}) collective-permute-start(bf16[8,48,384]{2,1,0:T(8,128)(2,1)S(1)} %get-tuple-element.224), channel_id=1, source_target_pairs={{0,2},{2,0},{4,6},{6,4},{8,10},{10,8},{12,14},{14,12},{16,18},{18,... | collective-permute-start | bytes 884744 | tf_op jit(solution)/shard_map/ppermute | solution.py:98
  154.7 2.0 collective-permute-start.47
  157.5 16.5 %collective-permute-start.49 = (bf16[4,48,1280]{2,1,0:T(8,128)(2,1)S(1)}, bf16[4,48,1280]{2,1,0:T(8,128)(2,1)S(1)}, u32[]{:S(2)}, u32[]{:S(2)}) collective-permute-start(bf16[4,48,1280]{2,1,0:T(8,128)(2,1)S(1)} %get-tuple-element.232), channel_id=1, source_target_pairs={{0,4},{2,6},{4,0},{6,2},{8,12},{10,14},{12,8},{14,10},{16,20},{18,... | collective-permute-start | bytes 1474568 | tf_op jit(solution)/shard_map/ppermute | solution.py:98
  159.7 14.4 %collective-permute-start.50 = (bf16[4,24,768]{2,1,0:T(8,128)(2,1)S(1)}, bf16[4,24,768]{2,1,0:T(8,128)(2,1)S(1)}, u32[]{:S(2)}, u32[]{:S(2)}) collective-permute-start(bf16[4,24,768]{2,1,0:T(8,128)(2,1)S(1)} %get-tuple-element.236), channel_id=1, source_target_pairs={{0,4},{2,6},{4,0},{6,2},{8,12},{10,14},{12,8},{14,10},{16,20},{18,... | collective-permute-start | bytes 442376 | tf_op jit(solution)/shard_map/ppermute | solution.py:98
  160.3 13.7 %collective-permute-start.51 = (bf16[1,48,1536]{2,1,0:T(8,128)(2,1)S(1)}, bf16[1,48,1536]{2,1,0:T(8,128)(2,1)S(1)}, u32[]{:S(2)}, u32[]{:S(2)}) collective-permute-start(bf16[1,48,1536]{2,1,0:T(8,128)(2,1)S(1)} %get-tuple-element.237), channel_id=1, source_target_pairs={{0,8},{2,10},{4,12},{6,14},{8,16},{10,18},{12,20},{14,22},{16,24},... | collective-permute-start | bytes 442376 | tf_op jit(solution)/shard_map/ppermute | solution.py:98
  160.3 13.7 %collective-permute-start.52 = (bf16[1,48,1536]{2,1,0:T(8,128)(2,1)S(1)}, bf16[1,48,1536]{2,1,0:T(8,128)(2,1)S(1)}, u32[]{:S(2)}, u32[]{:S(2)}) collective-permute-start(bf16[1,48,1536]{2,1,0:T(8,128)(2,1)S(1)} %get-tuple-element.238), channel_id=1, source_target_pairs={{0,16},{2,18},{4,20},{6,22},{8,24},{10,26},{12,28},{14,30},{16,0},... | collective-permute-start | bytes 442376 | tf_op jit(solution)/shard_map/ppermute | solution.py:98
  161.9 12.1 %collective-permute-start.53 = (bf16[1,48,1536]{2,1,0:T(8,128)(2,1)S(1)}, bf16[1,48,1536]{2,1,0:T(8,128)(2,1)S(1)}, u32[]{:S(2)}, u32[]{:S(2)}) collective-permute-start(bf16[1,48,1536]{2,1,0:T(8,128)(2,1)S(1)} %get-tuple-element.239), channel_id=1, source_target_pairs={{0,24},{2,26},{4,28},{6,30},{8,0},{10,2},{12,4},{14,6},{16,8},{18,... | collective-permute-start | bytes 442376 | tf_op jit(solution)/shard_map/ppermute | solution.py:98
  174.7 15.7 %collective-permute-start.55 = (bf16[1,48,1664]{2,1,0:T(8,128)(2,1)S(1)}, bf16[1,48,1664]{2,1,0:T(8,128)(2,1)S(1)}, u32[]{:S(2)}, u32[]{:S(2)}) collective-permute-start(bf16[1,48,1664]{2,1,0:T(8,128)(2,1)S(1)} %get-tuple-element.245), channel_id=1, source_target_pairs={{0,8},{2,10},{4,12},{6,14},{8,16},{10,18},{12,20},{14,22},{16,24},... | collective-permute-start | bytes 479240 | tf_op jit(solution)/shard_map/ppermute | solution.py:98
  177.3 13.1 %collective-permute-start.56 = (bf16[1,48,1664]{2,1,0:T(8,128)(2,1)S(1)}, bf16[1,48,1664]{2,1,0:T(8,128)(2,1)S(1)}, u32[]{:S(2)}, u32[]{:S(2)}) collective-permute-start(bf16[1,48,1664]{2,1,0:T(8,128)(2,1)S(1)} %get-tuple-element.246), channel_id=1, source_target_pairs={{0,16},{2,18},{4,20},{6,22},{8,24},{10,26},{12,28},{14,30},{16,0},... | collective-permute-start | bytes 479240 | tf_op jit(solution)/shard_map/ppermute | solution.py:98
  178.7 11.8 %collective-permute-start.57 = (bf16[1,48,1664]{2,1,0:T(8,128)(2,1)S(1)}, bf16[1,48,1664]{2,1,0:T(8,128)(2,1)S(1)}, u32[]{:S(2)}, u32[]{:S(2)}) collective-permute-start(bf16[1,48,1664]{2,1,0:T(8,128)(2,1)S(1)} %get-tuple-element.247), channel_id=1, source_target_pairs={{0,24},{2,26},{4,28},{6,30},{8,0},{10,2},{12,4},{14,6},{16,8},{18,... | collective-permute-start | bytes 479240 | tf_op jit(solution)/shard_map/ppermute | solution.py:98
  179.8 10.0 %collective-permute-start.54 = (bf16[272,768]{1,0:T(8,128)(2,1)S(1)}, bf16[272,768]{1,0:T(8,128)(2,1)S(1)}, u32[]{:S(2)}, u32[]{:S(2)}) collective-permute-start(bf16[272,768]{1,0:T(8,128)(2,1)S(1)} %get-tuple-element.240), channel_id=1, source_target_pairs={{0,1},{1,0},{2,3},{3,2},{4,5},{5,4},{6,7},{7,6},{8,9},{9,8},{10,11... | collective-permute-start | bytes 1253384 | tf_op jit(solution)/shard_map/ppermute | solution.py:102
  191.7 4.2 %collective-permute-start.58 = (bf16[24,1280]{1,0:T(8,128)(2,1)S(1)}, bf16[24,1280]{1,0:T(8,128)(2,1)S(1)}, u32[]{:S(2)}, u32[]{:S(2)}) collective-permute-start(bf16[24,1280]{1,0:T(8,128)(2,1)S(1)} %get-tuple-element.254), channel_id=1, source_target_pairs={{0,1},{1,0},{2,3},{3,2},{4,5},{5,4},{6,7},{7,6},{8,9},{9,8},{10,11... | collective-permute-start | bytes 184328 | tf_op jit(solution)/shard_map/ppermute | solution.py:102
  (4 other events, 2.8 us)

commit v2 on v1

--- a/solution.py
+++ b/solution.py
@@ -14,6 +14,8 @@
 LOW = jnp.bfloat16
 WIDE = jnp.float32
 CHUNK = 32
+FORWARD_BLOCK = 272
+BACKWARD_BLOCK = 544
 TILE = 384
 OUT_TILE = 256
 ROWS = 16
@@ -359,6 +361,47 @@
     return kept, sent
 
 
+def far_kernel(at, mine, got, kept, sent):
+    me = at[OUTER]
+    pair = lax.bitwise_xor(me, 1)
+    for group in range(kept.shape[0] // 2):
+        for n, block in enumerate((me, pair)):
+            for out, place in ((kept, block), (sent, lax.bitwise_xor(block, 2))):
+                spot = 4 * group + place
+                total = mine[spot].astype(WIDE) + got[spot].astype(WIDE)
+                out[2 * group + n] = total.astype(out.dtype)
+
+
+def near_kernel(at, mine, got, kept, sent):
+    for group in range(kept.shape[0]):
+        kept[group] = mine[2 * group] + got[2 * group].astype(WIDE)
+        total = mine[2 * group + 1] + got[2 * group + 1].astype(WIDE)
+        sent[group] = total.astype(LOW)
+
+
+def far_parts(at, mine, got, digits):
+    assert digits[-3][1] == 4
+    blocks, rows, cols = mine.shape
+    return call(
+        far_kernel, [wide_of(blocks // 2, rows, cols), low_of(blocks // 2, rows, cols)], at, mine, got
+    )
+
+
+def near_parts(at, mine, got):
+    blocks, rows, cols = mine.shape
+    return call(
+        near_kernel, [wide_of(blocks // 2, rows, cols), low_of(blocks // 2, rows, cols)], at, mine, got
+    )
+
+
+def swap_near(value, digit):
+    stride, _ = digit
+    pairs = []
+    for at in range(lax.axis_size("dp")):
+        pairs.append((at, at + stride if (at // stride) % 2 == 0 else at - stride))
+    return lax.ppermute(value, "dp", pairs)
+
+
 def outer_send(sent, digits):
     return [rotate(part, digits[-3], step + 1) for step, part in enumerate(sent)]
 
@@ -401,13 +444,21 @@
         mask[low : low + CHUNK, :] = jnp.where(same & key_ok, 0.0, -1e9)
 
 
+def heads_apart(pair):
+    lane = lax.broadcasted_iota(jnp.int32, (1, PAIR), 1)
+    zero = jnp.zeros((), LOW)
+    return jnp.concatenate(
+        [jnp.where(lane < HEAD, pair, zero), jnp.where(lane < HEAD, zero, pair)], axis=0
+    )
+
+
 def lanes(pair, count):
     return pl.ds(pl.multiple_of(pair * count, PAIR), count)
 
 
 def forward_kernel(
     half_rows, mem_count, starts, first_bias,
-    at, own, other, w, qkv, mix_own, mix_sent, lse, x, small, mask, s, p, mixed,
+    at, own, other, w, qkv, mix_own, mix_sent, lse, x, small, mask, s, mixed,
 ):
     rows, padded = x.shape[0], own.shape[0]
     t = at[T]
@@ -432,27 +483,20 @@
         got = (got.astype(WIDE) * scale).astype(LOW)
         qkv[:, lanes(pair, 3 * PAIR)] = got
         keys, values = got[:, PAIR : 2 * PAIR], got[:, 2 * PAIR :]
-        for h in range(2):
-            mine = (lane < HEAD) if h == 0 else (lane >= HEAD)
-            s[...] = nt(jnp.where(mine, got[:, :PAIR], jnp.zeros((), LOW)), keys)
-
-            def body(i, _):
-                here = pl.ds(pl.multiple_of(i * CHUNK, CHUNK), CHUNK)
-                v = s[here, :] + mask[here, :]
-                top = jnp.max(v, axis=-1, keepdims=True)
-                e = jnp.exp(v - top)
-                total = jnp.sum(e, axis=-1, keepdims=True)
-                p[here, :] = (e * (1.0 / total)).astype(LOW)
-                spot = lane == 2 * pair + h
-                lse[here, :] = jnp.where(spot, top + jnp.log(total), lse[here, :])
-                return 0
-
-            lax.fori_loop(0, rows // CHUNK, body, 0, unroll=True)
-            out = nn(p[...], values).astype(LOW)
-            if h == 0:
-                mixed[...] = out
+        q = heads_apart(got[:, :PAIR])
+        for low in range(0, 2 * rows, FORWARD_BLOCK):
+            here, there = slice(low, low + FORWARD_BLOCK), slice(low % rows, low % rows + FORWARD_BLOCK)
+            v = nt(q[here], keys) + mask[there, :]
+            top = jnp.max(v, axis=-1, keepdims=True)
+            e = jnp.exp(v - top)
+            total = jnp.sum(e, axis=-1, keepdims=True)
+            out = nn((e * (1.0 / total)).astype(LOW), values)
+            spot = lane == 2 * pair + low // rows
+            lse[there, :] = jnp.where(spot, top + jnp.log(total), lse[there, :])
+            if low < rows:
+                s[there, :] = out
             else:
-                mixed[...] = jnp.where(mine, out, mixed[...])
+                mixed[there, :] = jnp.where(lane < HEAD, s[there, :], out).astype(LOW)
         mix_own[:, lanes(pair, PAIR)] = mixed[pl.ds(pl.multiple_of(t * padded, 16), padded), :]
         mix_sent[:, lanes(pair, PAIR)] = mixed[
             pl.ds(pl.multiple_of((1 - t) * padded, 16), padded), :
@@ -463,7 +507,7 @@
 
 
 def backward_kernel(
-    half_rows, mem_count, starts, at, qkv, own, got, lse, dproj, sums, mask, s, dp, p, ds, dmix
+    half_rows, mem_count, starts, at, qkv, own, got, lse, dproj, sums, mask, s, p, ds, dmix
 ):
     rows, padded = qkv.shape[0], own.shape[0]
     part = own.shape[1]
@@ -479,29 +523,20 @@
         whole = qkv[:, here]
         keys, values = whole[:, PAIR : 2 * PAIR], whole[:, 2 * PAIR :]
         dm_pair = dmix[:, lanes(pair, PAIR)]
-        parts = []
-        for h in range(2):
-            mine = (lane < HEAD) if h == 0 else (lane >= HEAD)
-            q = jnp.where(mine, whole[:, :PAIR], zero)
-            dm = jnp.where(mine, dm_pair, zero)
-            s[...] = nt(q, keys)
-            dp[...] = nt(dm, values)
-
-            def body(i, _):
-                here = pl.ds(pl.multiple_of(i * CHUNK, CHUNK), CHUNK)
-                spot = lane == 2 * pair + h
-                stat = jnp.sum(jnp.where(spot, lse[here, :], 0.0), axis=-1, keepdims=True)
-                e = jnp.exp(s[here, :] + mask[here, :] - stat)
-                d = dp[here, :]
-                dot = jnp.sum(e * d, axis=-1, keepdims=True)
-                p[here, :] = e.astype(LOW)
-                ds[here, :] = (e * (d - dot)).astype(LOW)
-                return 0
-
-            lax.fori_loop(0, rows // CHUNK, body, 0, unroll=True)
-            parts.append((nn(ds[...], keys) * 0.125, tn(ds[...], q), tn(p[...], dm)))
-        dq = jnp.where(lane < HEAD, parts[0][0], parts[1][0])
-        dk, dv = parts[0][1] + parts[1][1], parts[0][2] + parts[1][2]
+        q, dm = heads_apart(whole[:, :PAIR]), heads_apart(dm_pair)
+        for low in range(0, 2 * rows, BACKWARD_BLOCK):
+            block, there = slice(low, low + BACKWARD_BLOCK), slice(low % rows, low % rows + BACKWARD_BLOCK)
+            spot = lane == 2 * pair + low // rows
+            stat = jnp.sum(jnp.where(spot, lse[there, :], 0.0), axis=-1, keepdims=True)
+            e = jnp.exp(nt(q[block], keys) + mask[there, :] - stat)
+            d = nt(dm[block], values)
+            dot = jnp.sum(e * d, axis=-1, keepdims=True)
+            p[block, :] = e.astype(LOW)
+            d = (e * (d - dot)).astype(LOW)
+            ds[block, :] = d
+            s[block, :] = nn(d, keys)
+        dq = jnp.where(lane < HEAD, s[:rows, :], s[rows:, :]) * 0.125
+        dk, dv = tn(ds[...], q), tn(p[...], dm)
         out = jnp.concatenate([dq, dk, dv], axis=1).astype(LOW)
         dproj[:, here] = out
         sums[:, here] = jnp.sum(out.astype(WIDE), axis=0, keepdims=True)
@@ -510,26 +545,23 @@
     lax.fori_loop(0, part // PAIR, one_pair, 0)
 
 
-def projection_back_kernel(
-    small_rows, at, layer_in, d_projected, proj_sums, sums_one, sums_two, up_sums, wqkv, d_attn,
-    *outs,
+def half_rows_of(ref, which, padded):
+    return ref[pl.ds(pl.multiple_of(which * padded, 16), padded), :]
+
+
+def projection_gradient_kernel(
+    small_rows, at, layer_in, d_projected, proj_sums, sums_one, two0, two1, up_sums, wqkv, d_attn,
+    *refs,
 ):
-    d_own, d_sent = outs[:2]
-    grads, turn = outs[2:-1], outs[-1]
-    padded, part = d_own.shape[0], up_sums.shape[1]
+    grads, turn = refs[:-1], refs[-1]
+    part = up_sums.shape[1]
     cols = d_projected.shape[1]
-    t = at[T]
-    first = t == 0
-    half = lambda which: d_projected[pl.ds(pl.multiple_of(which * padded, 16), padded), :]
-    weights = wqkv[:, :cols]
-    own = nt(half(t), weights)
-    other = nt(half(1 - t), weights)
-    d_own[...] = d_attn[...] + own
-    d_sent[...] = other.astype(LOW)
+    first = at[T] == 0
     turn[...] = jnp.zeros_like(turn)
     (m0, m1), (v0, _), (g0, _), (u0, _) = small_rows
     count = m1 - m0
-    memory = jnp.where(first, own[:count] + d_attn[:count, :], other[:count])
+    memory = nt(d_projected[:32, :], wqkv[:, :cols])[:count]
+    memory = memory + jnp.where(first, d_attn[:count, :], 0.0)
     turn[m0:m1, :] = jnp.where(at[FRESH] == 1, memory, 0.0)
     sums = [
         jnp.concatenate(
@@ -542,6 +574,7 @@
         high = low + value.shape[0]
         turn[low:high, :part] = jnp.where(first, value, 0.0)
         turn[low:high, part:] = jnp.where(first, 0.0, value)
+    sums_two = two0[...] + two1[...]
     turn[v0 + 2 : v0 + 4, :] = sums_one[0:2, :]
     turn[v0 + 4 : v0 + 6, :] = sums_two[0:2, :]
     turn[g0 : g0 + 1, :] = sums_one[2:3, :]
@@ -552,6 +585,13 @@
         grads[0][:, cols:] = small.astype(LOW)
     else:
         put_blocks(small, grads[0], grads[-1], at[CORE], cols)
+
+
+def projection_back_kernel(at, d_projected, wqkv, d_attn, d_own, d_sent):
+    padded, cols = d_own.shape[0], d_projected.shape[1]
+    t = at[T]
+    d_own[...] = d_attn[...] + nt(half_rows_of(d_projected, t, padded), wqkv[:, :cols])
+    d_sent[...] = nt(half_rows_of(d_projected, 1 - t, padded), wqkv[:, :cols]).astype(LOW)
 
 
 def halves_kernel(count, at, *refs):
@@ -618,23 +658,23 @@
 
 
 def second_norm_kernel(
-    bias, gain, at, unit, small, own, got, d_out, layer_out, d_second, d_ffn, sums
+    bias, gain, start, at, unit, small, own, got, d_out, _, layer_out, d_second, d_ffn, sums
 ):
-    padded, width = unit.shape
-    real = d_out.shape[0]
+    width = unit.shape[1]
+    real = d_out.shape[0] - start
     totals = [jnp.zeros((ROWS, width), WIDE)] * 3
-    for low in range(0, padded, ROWS):
-        here = slice(low, low + ROWS)
+    for low in range(0, got.shape[0], ROWS):
+        here, there = slice(low, low + ROWS), slice(start + low, start + low + ROWS)
         count = min(ROWS, real - low)
-        first = unit[here, :] * small[gain : gain + 1, :] + small[bias + 3 : bias + 4, :]
-        ffn = own[here, :] + got[here, :].astype(WIDE) + small[bias + 4 : bias + 5, :]
+        first = unit[there, :] * small[gain : gain + 1, :] + small[bias + 3 : bias + 4, :]
+        ffn = own[there, :] + got[here, :].astype(WIDE) + small[bias + 4 : bias + 5, :]
         total = first + ffn
         centered = total - spread_of(total)
         factor = lax.rsqrt(spread_of(centered * centered) + NORM_EPSILON)
         value = centered * factor
         out = value * small[gain + 1 : gain + 2, :] + small[bias + 5 : bias + 6, :]
         layer_out[low : low + count, :] = out[:count].astype(LOW)
-        cotangent = d_out[low : low + count, :].astype(WIDE)
+        cotangent = d_out[start + low : start + low + count, :].astype(WIDE)
         if count < ROWS:
             cotangent = jnp.concatenate(
                 [cotangent, jnp.zeros((ROWS - count, width), WIDE)], axis=0
@@ -650,14 +690,16 @@
 
 
 def first_back_kernel(
-    gain, at, d_second, own, got, unit, scale, small, wout, d_attn_in, d_attn, mix_own, mix_sent, sums
+    gain, at, second0, second1, own, got, unit, scale, small, wout, d_attn_in, d_attn, mix_own, mix_sent, sums
 ):
     padded, width = unit.shape
     part = mix_own.shape[1]
     totals = [jnp.zeros((ROWS, width), WIDE)] * 3
     for low in range(0, padded, ROWS):
         here = slice(low, low + ROWS)
-        cotangent = d_second[here, :] + own[here, :] + got[here, :].astype(WIDE)
+        cut = second0.shape[0]
+        second = second0[here, :] if low < cut else second1[low - cut : low - cut + ROWS, :]
+        cotangent = second + own[here, :] + got[here, :].astype(WIDE)
         value = unit[here, :]
         d_unit = cotangent * small[gain : gain + 1, :]
         back = d_unit - spread_of(d_unit) - value * spread_of(d_unit * value)
@@ -781,8 +823,7 @@
         at, rows_low, rows_other, wqkv,
         scratch=[
             pltpu.VMEM((rows, rows), WIDE),
-            pltpu.VMEM((rows, rows), WIDE),
-            pltpu.VMEM((rows, rows), LOW),
+            pltpu.VMEM((rows, PAIR), WIDE),
             pltpu.VMEM((rows, PAIR), LOW),
         ],
     )
@@ -820,17 +861,29 @@
         hidden = hidden.astype(LOW)
         return hidden, slope, nt(hidden, down_t)
 
+    cut = ceil_to(padded // 2, ROWS)
+    pieces = ((0, cut), (cut, padded))
     hidden_got, slope_got, ffn_sent = feed_forward(normed_got)
     ffn_sent = ffn_sent.astype(LOW)
-    ffn_got = swap_tensor(ffn_sent)
+    ffn_got = [swap_tensor(ffn_sent[low:high]) for low, high in pieces]
     hidden_own, slope_own, ffn_own = feed_forward(tie(normed_own, ffn_sent))
-    layer_out, d_second, d_ffn_own, sums_two = call(
-        functools.partial(second_norm_kernel, bias, gain),
-        [low_of(half_rows, width), wide_of(padded, width), low_of(padded, width), wide_of(8, width)],
-        at, unit, small, ffn_own, ffn_got, d_out.reshape(half_rows, width),
-    )
-
-    d_ffn_got = swap_tensor(d_ffn_own)
+    d_out_rows = d_out.reshape(half_rows, width)
+    second, ahead = [], small
+    for (low, high), got in zip(pieces, ffn_got):
+        if second:
+            ahead = rotate(second[-1][2][:ROWS, :PAIR], core_digit, 1)
+        outs = [
+            low_of(min(high, half_rows) - low, width),
+            wide_of(high - low, width),
+            low_of(high - low, width),
+            wide_of(8, width),
+        ]
+        kernel = functools.partial(second_norm_kernel, bias, gain, low)
+        second.append(call(kernel, outs, at, unit, small, ffn_own, got, d_out_rows, ahead))
+    layer_out, d_second, d_ffn_sent, sums_two = zip(*second)
+
+    d_ffn_got = jnp.concatenate([swap_tensor(piece) for piece in d_ffn_sent], axis=0)
+    d_ffn_own = jnp.concatenate(d_ffn_sent, axis=0)
 
     def feed_back(rows, slope):
         d_pre = (slope * nn(rows, down_t)).astype(LOW)
@@ -868,7 +921,7 @@
             low_of(padded, part),
             wide_of(8, width),
         ],
-        at, d_second, d_first_own, d_first_got, unit, scale, small, wout,
+        at, *d_second, d_first_own, d_first_got, unit, scale, small, wout,
     )
     d_mix_got = swap_tensor(d_mix_sent)
     out_grads = call(
@@ -879,9 +932,9 @@
     out_kept, out_sent = call(
         rows_halves_kernel, [low_of(dp_count // 2, lines, width)] * 2, at, out_kept, *out_parts
     )
-    down_kept, down_sent = outer_parts(at, down_kept, down_got, digits)
-    d_mix_got, out_sent, up_sent, *down_sent = join(d_mix_got, out_sent, up_sent, *down_sent)
-    down_got = outer_send(down_sent, digits)
+    down_kept, down_sent = far_parts(at, down_kept, down_got, digits)
+    d_mix_got, out_sent, up_sent, down_sent = join(d_mix_got, out_sent, up_sent, down_sent)
+    down_got = rotate(down_sent, digits[-3], 2)
     out_got = swap_tensor(out_sent)
     up_got = rotate(up_sent, x_digit, 1)
 
@@ -891,37 +944,46 @@
         at, projected, d_mix_own, d_mix_got, log_total,
         scratch=[
             pltpu.VMEM((rows, rows), WIDE),
-            pltpu.VMEM((rows, rows), WIDE),
-            pltpu.VMEM((rows, rows), WIDE),
-            pltpu.VMEM((rows, rows), LOW),
-            pltpu.VMEM((rows, rows), LOW),
+            pltpu.VMEM((2 * rows, PAIR), WIDE),
+            pltpu.VMEM((2 * rows, rows), LOW),
+            pltpu.VMEM((2 * rows, rows), LOW),
             pltpu.VMEM((rows, part), LOW),
         ],
     )
-    up_kept, up_sent = outer_parts(at, up_kept, up_got, digits)
-    d_in_own, d_in_sent, *qkv_grads = call(
-        functools.partial(projection_back_kernel, small_rows),
-        [wide_of(padded, width), low_of(padded, width)]
-        + gradient_outs(width, cols + PAIR, dp_count),
-        at, layer_in, d_projected, proj_sums, sums_one, sums_two, up_sums, wqkv, d_attn_in,
+    up_kept, up_sent = far_parts(at, up_kept, up_got, digits)
+    qkv_grads = call(
+        functools.partial(projection_gradient_kernel, small_rows),
+        gradient_outs(width, cols + PAIR, dp_count),
+        at, layer_in, d_projected, proj_sums, sums_one, *sums_two, up_sums, wqkv, d_attn_in,
         scratch=[pltpu.VMEM((PAIR, width), WIDE)],
     )
-    out_got, *qkv_grads = join(out_got, *qkv_grads, *down_got)[: 1 + len(qkv_grads)]
+    out_got, down_got, *qkv_grads = join(out_got, down_got, *qkv_grads)
+    down_kept, down_sent = near_parts(at, down_kept, down_got)
     out_kept, out_sent = halve(at, out_kept, [out_got])
     out_got = rotate(out_sent, x_digit, 1)
-    qkv_kept, qkv_sent = halve(at, *swap_cores(qkv_grads, dp_count, core_digit))
-
-    qkv_sent, *up_sent = join(qkv_sent, *up_sent)
+    qkv_kept, qkv_parts = swap_cores(qkv_grads, dp_count, core_digit)
+    up_sent, *qkv_parts = join(up_sent, *qkv_parts)
+    qkv_kept, qkv_sent = halve(at, qkv_kept, qkv_parts)
+
     qkv_got = rotate(qkv_sent, x_digit, 1)
-    up_got = outer_send(up_sent, digits)
-    qkv_got, d_in_sent, out_got, *up_got = join(qkv_got, d_in_sent, out_got, *up_got)
+    up_got = rotate(up_sent, digits[-3], 2)
+    down_got = swap_near(down_sent, digits[-3])
+    d_in_own, d_in_sent = call(
+        projection_back_kernel, [wide_of(padded, width), low_of(padded, width)],
+        at, tie(d_projected, qkv_sent), wqkv, d_attn_in,
+    )
+    up_kept, up_sent = near_parts(at, up_kept, up_got)
+    qkv_got, d_in_sent, out_got, up_sent, down_got = join(
+        qkv_got, d_in_sent, out_got, up_sent, down_got
+    )
+    up_got = swap_near(up_sent, digits[-3])
     d_in_got = swap_tensor(d_in_sent)
     both_kept, both_sent = outer_parts(
         at, qkv_kept, qkv_got, digits, out_kept, out_got
     )
     both_got = outer_send(both_sent, digits)
-    grad_ffn_down = outer_sum(down_kept, down_got, digits)
-    grad_ffn_up = outer_sum(up_kept, up_got, digits)
+    grad_ffn_down = outer_sum(down_kept, [down_got], digits)
+    grad_ffn_up = outer_sum(up_kept, [up_got], digits)
     (grad_rows,) = call(
         functools.partial(rows_kernel, mem_count), [wide_of(half_rows, width)], at, d_in_own, d_in_got
     )
@@ -943,7 +1005,7 @@
         scratch=[pltpu.VMEM((PAIR, PAIR), WIDE)],
     )
     return (
-        layer_out.reshape(half_rows, 1, width),
+        jnp.concatenate(layer_out, axis=0).reshape(half_rows, 1, width),
         grad_rows.reshape(half_rows, 1, width),
         grad_qkv,
         grad_out_weight,

time: 198 us -> 193 us (0.975)
  waiting for transfers between devices: 70.7 us -> 65.1 us
    ppermute x47 -> x44, starting transfers between devices: 39.4 us -> 33.5 us  [rotate(): return lax.ppermute(value, 'dp', pairs)]
    ppermute x12 -> x14, waiting for transfers between devices: 25.6 us -> 21.6 us  [swap_tensor(): return lax.ppermute(value, 'tensor', [(0, 1), (1, 0)])]
    ppermute x0 -> x2, starting transfers between devices: none -> 2.88 us  [swap_near(): return lax.ppermute(value, 'dp', pairs)]
    ppermute x12 -> x14, starting transfers between devices: 14 us -> 16.2 us  [swap_tensor(): return lax.ppermute(value, 'tensor', [(0, 1), (1, 0)])]
    ppermute x47 -> x44, waiting for transfers between devices: 45.1 us -> 43.5 us  [rotate(): return lax.ppermute(value, 'dp', pairs)]
    pallas_call x29 -> x33, Pallas kernels: 53.6 us -> 53.7 us  [call(): pl.pallas_call(kernel, in_specs=[pl.BlockSpec(memory_space=pltpu.SMEM)] +...]
    unnamed x19 -> x20, local copies, waits for them, and re-layouts: 5.44 us -> 5.45 us
  transfers between devices with their start and end apart: 59 -> 60, of which waited for: 22 -> 24; matrix products, arithmetic and copies ran while one was open for 5% -> 5% of each run, Pallas kernels for 23% -> 26%
where the time goes in v2:
time: 193 us
  waiting for transfers between devices  65.1 us (34%)
  Pallas kernels  53.7 us (28%)
  starting transfers between devices  52.6 us (27%)
  local copies, waits for them, and re-layouts  8.79 us (5%)
  matrix products  7.34 us (4%)
  other arithmetic  2.55 us (1%)
  between operations  2.53 us (1%)
    pallas_call x33, Pallas kernels, call(): pl.pallas_call(kernel, in_specs=[pl.BlockSpec(memory_space=pltpu.SMEM)] +...  53.7 us
    ppermute x44, waiting for transfers between devices, rotate(): return lax.ppermute(value, 'dp', pairs)  43.5 us
    ppermute x44, starting transfers between devices, rotate(): return lax.ppermute(value, 'dp', pairs)  33.5 us
    ppermute x14, waiting for transfers between devices, swap_tensor(): return lax.ppermute(value, 'tensor', [(0, 1), (1, 0)])  21.6 us
    ppermute x14, starting transfers between devices, swap_tensor(): return lax.ppermute(value, 'tensor', [(0, 1), (1, 0)])  16.2 us
    unnamed x20, local copies, waits for them, and re-layouts  5.45 us
  transfers between devices with their start and end apart: 60, of which 24 were waited for; matrix products, arithmetic and copies ran while one was open for 5% of the time, Pallas kernels for 26%

profile of v2, /device:TPU:0, one launch (start us, length us, event | category | flops | bytes accessed | tf_op | source)
XLA Modules:
  0.0 192.6 jit_solution(10496792886369371186)
XLA Ops:
  1.4 0.9 copy-done.2
  4.4 3.0 %collective-permute-start = (bf16[24,1280]{1,0:T(8,128)(2,1)S(1)}, bf16[24,1280]{1,0:T(8,128)(2,1)S(1)}, u32[]{:S(2)}, u32[]{:S(2)}) collective-permute-start(bf16[24,1280]{1,0:T(8,128)(2,1)S(1)} %get-tuple-element.143), channel_id=1, source_target_pairs={{0,1},{1,0},{2,3},{3,2},{4,5},{5,4},{6,7},{7,6},{8,9},{9,8},{10,11... | collective-permute-start | bytes 184328 | tf_op jit(solution)/shard_map/ppermute | solution.py:104
  8.7 1.0 pad.4.own
  11.8 1.2 collective-permute-start.4
  13.0 3.6 %collective-permute-start.3 = (bf16[48,1664]{1,0:T(8,128)(2,1)S(1)}, bf16[48,1664]{1,0:T(8,128)(2,1)S(1)}, u32[]{:S(2)}, u32[]{:S(2)}) collective-permute-start(bf16[48,1664]{1,0:T(8,128)(2,1)S(1)} %shard_map.214), channel_id=1, source_target_pairs={{0,24},{2,26},{4,28},{6,30},{8,0},{10,2},{12,4},{14,6},{16,8},{18,... | collective-permute-start | bytes 479240 | tf_op jit(solution)/shard_map/ppermute | solution.py:100
  16.6 1.0 collective-permute-start.2
  17.6 3.6 %collective-permute-done.3 = bf16[48,1664]{1,0:T(8,128)(2,1)S(1)} collective-permute-done((bf16[48,1664]{1,0:T(8,128)(2,1)S(1)}, bf16[48,1664]{1,0:T(8,128)(2,1)S(1)}, u32[]{:S(2)}, u32[]{:S(2)}) %collective-permute-start.3) | collective-permute-done | bytes 159776 | tf_op jit(solution)/shard_map/ppermute | solution.py:100
  21.2 4.2 %collective-permute-done.1 = bf16[48,1664]{1,0:T(8,128)(2,1)S(1)} collective-permute-done((bf16[48,1664]{1,0:T(8,128)(2,1)S(1)}, bf16[48,1664]{1,0:T(8,128)(2,1)S(1)}, u32[]{:S(2)}, u32[]{:S(2)}) %collective-permute-start.1) | collective-permute-done | bytes 159776 | tf_op jit(solution)/shard_map/ppermute | solution.py:100
  25.5 4.1 %collective-permute-done.2 = bf16[48,1664]{1,0:T(8,128)(2,1)S(1)} collective-permute-done((bf16[48,1664]{1,0:T(8,128)(2,1)S(1)}, bf16[48,1664]{1,0:T(8,128)(2,1)S(1)}, u32[]{:S(2)}, u32[]{:S(2)}) %collective-permute-start.2) | collective-permute-done | bytes 159776 | tf_op jit(solution)/shard_map/ppermute | solution.py:100
  29.7 1.6 collective-permute-start.5
  31.3 2.6 %collective-permute-start.7 = (bf16[48,1536]{1,0:T(8,128)(2,1)S(1)}, bf16[48,1536]{1,0:T(8,128)(2,1)S(1)}, u32[]{:S(2)}, u32[]{:S(2)}) collective-permute-start(bf16[48,1536]{1,0:T(8,128)(2,1)S(1)} %copy-done.7), channel_id=1, source_target_pairs={{0,16},{2,18},{4,20},{6,22},{8,24},{10,26},{12,28},{14,30},{16,0},... | collective-permute-start | bytes 442376 | tf_op jit(solution)/shard_map/ppermute | solution.py:100
  33.9 1.2 collective-permute-start.8
  35.1 4.8 %collective-permute-done.6 = bf16[48,1536]{1,0:T(8,128)(2,1)S(1)} collective-permute-done((bf16[48,1536]{1,0:T(8,128)(2,1)S(1)}, bf16[48,1536]{1,0:T(8,128)(2,1)S(1)}, u32[]{:S(2)}, u32[]{:S(2)}) %collective-permute-start.6) | collective-permute-done | bytes 147488 | tf_op jit(solution)/shard_map/ppermute | solution.py:100
  39.9 4.3 %collective-permute-done.7 = bf16[48,1536]{1,0:T(8,128)(2,1)S(1)} collective-permute-done((bf16[48,1536]{1,0:T(8,128)(2,1)S(1)}, bf16[48,1536]{1,0:T(8,128)(2,1)S(1)}, u32[]{:S(2)}, u32[]{:S(2)}) %collective-permute-start.7) | collective-permute-done | bytes 147488 | tf_op jit(solution)/shard_map/ppermute | solution.py:100
  44.3 0.9 collective-permute-done.5.refs_1_.x_got
  45.7 1.5 collective-permute-start.19
  48.5 1.1 collective-permute-start.15
  49.6 2.1 %collective-permute-start.16 = (bf16[48,1536]{1,0:T(8,128)(2,1)S(1)}, bf16[48,1536]{1,0:T(8,128)(2,1)S(1)}, u32[]{:S(2)}, u32[]{:S(2)}) collective-permute-start(bf16[48,1536]{1,0:T(8,128)(2,1)S(1)} %bitcast.84), channel_id=1, source_target_pairs={{0,16},{2,18},{4,20},{6,22},{8,24},{10,26},{12,28},{14,30},{16,0},... | collective-permute-start | bytes 442376 | tf_op jit(solution)/shard_map/ppermute | solution.py:100
  53.1 7.8 %shard_map.216 = (bf16[544,1152]{1,0:T(8,128)(2,1)S(1)}, bf16[272,384]{1,0:T(8,128)(2,1)S(1)}, bf16[272,384]{1,0:T(8,128)(2,1)S(1)}, f32[544,128]{1,0:T(8,128)S(...) custom-call(s32[15]{0:T(128)S(1)} %concatenate.12.at, bf16[272,768]{1,0:T(8,128)(2,1)S(1)} %pad.4.own, ...), custom_call_target="tpu_custom_call" | custom-call | flops 1 | bytes 1 | tf_op jit(solution)/shard_map/pallas_call | solution.py:60
  61.0 1.4 collective-permute-start.11
  63.1 0.9 collective-permute-start.18
  64.7 2.3 %collective-permute-done.11.got = bf16[272,384]{1,0:T(8,128)(2,1)S(1)} collective-permute-done((bf16[272,384]{1,0:T(8,128)(2,1)S(1)}, bf16[272,384]{1,0:T(8,128)(2,1)S(1)}, u32[]{:S(2)}, u32[]{:S(2)}) %collective-permute-start.11) | collective-permute-done | bytes 208928 | tf_op jit(solution)/shard_map/ppermute | solution.py:104
  67.0 1.3 shard_map.219
  68.3 1.4 collective-permute-start.14
  69.7 1.4 shard_map.220
  71.9 6.9 %collective-permute-done.18.refs_1_ = bf16[4,48,1536]{2,1,0:T(8,128)(2,1)S(1)} collective-permute-done((bf16[4,48,1536]{2,1,0:T(8,128)(2,1)S(1)}, bf16[4,48,1536]{2,1,0:T(8,128)(2,1)S(1)}, u32[]{:S(2)}, u32[]{:S(2)}) %collective-permute-start.18) | collective-permute-done | bytes 589856 | tf_op jit(solution)/shard_map/ppermute | solution.py:100
  79.0 0.9 multiply_convert_fusion.1
  79.9 0.9 collective-permute-done.23.refs_3_
  82.4 0.9 multiply_convert_fusion
  84.1 1.3 collective-permute-start.25
  86.3 5.4 %collective-permute-done.24.got = bf16[144,768]{1,0:T(8,128)(2,1)S(1)} collective-permute-done((bf16[144,768]{1,0:T(8,128)(2,1)S(1)}, bf16[144,768]{1,0:T(8,128)(2,1)S(1)}, u32[]{:S(2)}, u32[]{:S(2)}) %collective-permute-start.24) | collective-permute-done | bytes 221216 | tf_op jit(solution)/shard_map/ppermute | solution.py:104
  91.7 1.0 shard_map.223
  93.6 1.5 collective-permute-done.25.got
  95.1 1.0 shard_map.224
  96.1 1.0 fusion.b_up
  97.9 3.7 %shard_map.225 = (f32[768,1536]{1,0:T(8,128)S(1)}, f32[768,1536]{1,0:T(8,128)S(1)}, f32[1,1536]{1,0:T(1,128)S(1)}) custom-call(s32[15]{0:T(128)S(1)} %concatenate.12.at, bf16[272,768]{1,0:T(8,128)(2,1)S(1)} %constant_dynamic-update-slice_fusion.a_down, bf16[272,1536]{1,0:T(8,128)(2,1)S(1)} %get-tuple-element.286.b_down, ...), custom_call_target="tpu_custom_call" | custom-call | flops 1 | bytes 1 | tf_op jit(solution)/shard_map/pallas_call | solution.py:60
  102.4 2.5 %collective-permute-done.28 = bf16[128,768]{1,0:T(8,128)(2,1)S(1)} collective-permute-done((bf16[128,768]{1,0:T(8,128)(2,1)S(1)}, bf16[128,768]{1,0:T(8,128)(2,1)S(1)}, u32[]{:S(2)}, u32[]{:S(2)}) %collective-permute-start.28) | collective-permute-done | bytes 196640 | tf_op jit(solution)/shard_map/ppermute | solution.py:104
  105.0 1.0 fusion.1.b
  105.9 1.1 convolution_convert_fusion
  107.8 2.2 %shard_map.229 = (bf16[8,48,1536]{2,1,0:T(8,128)(2,1)S(1)}, bf16[8,48,384]{2,1,0:T(8,128)(2,1)S(1)}, bf16[8,48,384]{2,1,0:T(8,128)(2,1)S(1)}, bf16[8,48,384]{2,1,0:T(8,128)(2,1)S(1)}, bf16[8,48,384]{2,1,0:T(8,128)(2,1)S(1)}) custom-call(s32[15]{0:T(128)S(1)} %concatenate.12.at, f32[768,1536]{1,0:T(8,128)S(1)} %get-tuple-element.191.own, ...), custom_call_target="tpu_custom_call" | custom-call | flops 1 | bytes 1 | tf_op jit(solution)/shard_map/pallas_call | solution.py:60
  113.8 1.2 collective-permute-start.42
  115.0 3.6 %shard_map.231 = (f32[4,384]{1,0:T(4,128)S(1)}, bf16[8,48,1536]{2,1,0:T(8,128)(2,1)S(1)}, bf16[8,48,384]{2,1,0:T(8,128)(2,1)S(1)}, bf16[8,48,384]{2,1,0:T(8,128)...) custom-call(s32[15]{0:T(128)S(1)} %concatenate.12.at, ...), custom_call_target="tpu_custom_call" | custom-call | flops 1 | bytes 1 | tf_op jit(solution)/shard_map/pallas_call | solution.py:60
  119.7 1.6 shard_map.226
  121.3 1.2 collective-permute-start.30
  122.5 1.4 shard_map.227
  126.6 2.6 %collective-permute-done.42.got = bf16[4,48,1536]{2,1,0:T(8,128)(2,1)S(1)} collective-permute-done((bf16[4,48,1536]{2,1,0:T(8,128)(2,1)S(1)}, bf16[4,48,1536]{2,1,0:T(8,128)(2,1)S(1)}, u32[]{:S(2)}, u32[]{:S(2)}) %collective-permute-start.42) | collective-permute-done | bytes 589856 | tf_op jit(solution)/shard_map/ppermute | solution.py:100
  129.9 1.4 collective-permute-start.43
  131.3 1.9 %collective-permute-start.44 = (bf16[2,48,1536]{2,1,0:T(8,128)(2,1)S(1)}, bf16[2,48,1536]{2,1,0:T(8,128)(2,1)S(1)}, u32[]{:S(2)}, u32[]{:S(2)}) collective-permute-start(bf16[2,48,1536]{2,1,0:T(8,128)(2,1)S(1)} %get-tuple-element.212), channel_id=1, source_target_pairs={{0,16},{2,18},{4,20},{6,22},{8,24},{10,26},{12,28},{14,30},{16,0},... | collective-permute-start | bytes 884744 | tf_op jit(solution)/shard_map/ppermute | solution.py:100
  133.8 9.6 %shard_map.234 = (bf16[544,1152]{1,0:T(8,128)(2,1)S(1)}, f32[1,1152]{1,0:T(1,128)S(1)}) custom-call(s32[15]{0:T(128)S(1)} %concatenate.12.at, bf16[544,1152]{1,0:T(8,128)(2,1)S(1)} %get-tuple-element.170.qkv, bf16[272,384]{1,0:T(8,128)(2,1)S(1)} %get-tuple-element.179.own, bf16[272,384]{1,0:T(8,128)(2,1)S(1)} %collective-permute-done.30.got, ...), custom_call_target="tpu_custom_call" | custom-call | flops 1 | bytes 1 | tf_op jit(solution)/shard_map/pallas_call | solution.py:60
  143.4 2.9 %shard_map.235 = (bf16[8,48,1280]{2,1,0:T(8,128)(2,1)S(1)}, bf16[8,48,384]{2,1,0:T(8,128)(2,1)S(1)}, bf16[8,48,384]{2,1,0:T(8,128)(2,1)S(1)}, bf16[8,48,384]{2,1,0:T(8,128)(2,1)S(1)}, bf16[8,48,128]{2,1,0:T(8,128)(2,1)S(1)}) custom-call(s32[15]{0:T(128)S(1)} %concatenate.12.at, bf16[544,768]{1,0:T(8,128)(2,1)S(1)} %get-tuple-element.153.layer_in, ...), custom_call_target="tpu_custom_call" | custom-call | flops 1 | bytes 1 | tf_op jit(solution)/shard_map/pallas_call | solution.py:60
  148.2 0.9 collective-permute-done.49.refs_3_
  149.8 1.5 collective-permute-start.50
  151.4 1.0 collective-permute-start.52
  153.0 2.8 %collective-permute-start.53 = (bf16[1,48,1536]{2,1,0:T(8,128)(2,1)S(1)}, bf16[1,48,1536]{2,1,0:T(8,128)(2,1)S(1)}, u32[]{:S(2)}, u32[]{:S(2)}) collective-permute-start(bf16[1,48,1536]{2,1,0:T(8,128)(2,1)S(1)} %get-tuple-element.248), channel_id=1, source_target_pairs={{0,8},{2,10},{4,12},{6,14},{8,0},{10,2},{12,4},{14,6},{16,24},{18,... | collective-permute-start | bytes 442376 | tf_op jit(solution)/shard_map/ppermute | solution.py:402
  157.8 1.8 shard_map.238
  159.6 7.7 %collective-permute-done.52.got = bf16[2,48,1536]{2,1,0:T(8,128)(2,1)S(1)} collective-permute-done((bf16[2,48,1536]{2,1,0:T(8,128)(2,1)S(1)}, bf16[2,48,1536]{2,1,0:T(8,128)(2,1)S(1)}, u32[]{:S(2)}, u32[]{:S(2)}) %collective-permute-start.52) | collective-permute-done | bytes 294944 | tf_op jit(solution)/shard_map/ppermute | solution.py:100
  168.8 2.1 %collective-permute-start.55 = (bf16[1,48,1664]{2,1,0:T(8,128)(2,1)S(1)}, bf16[1,48,1664]{2,1,0:T(8,128)(2,1)S(1)}, u32[]{:S(2)}, u32[]{:S(2)}) collective-permute-start(bf16[1,48,1664]{2,1,0:T(8,128)(2,1)S(1)} %get-tuple-element.254), channel_id=1, source_target_pairs={{0,8},{2,10},{4,12},{6,14},{8,16},{10,18},{12,20},{14,22},{16,24},... | collective-permute-start | bytes 479240 | tf_op jit(solution)/shard_map/ppermute | solution.py:100
  171.3 2.8 %collective-permute-start.57 = (bf16[1,48,1664]{2,1,0:T(8,128)(2,1)S(1)}, bf16[1,48,1664]{2,1,0:T(8,128)(2,1)S(1)}, u32[]{:S(2)}, u32[]{:S(2)}) collective-permute-start(bf16[1,48,1664]{2,1,0:T(8,128)(2,1)S(1)} %get-tuple-element.256), channel_id=1, source_target_pairs={{0,24},{2,26},{4,28},{6,30},{8,0},{10,2},{12,4},{14,6},{16,8},{18,... | collective-permute-start | bytes 479240 | tf_op jit(solution)/shard_map/ppermute | solution.py:100
  174.2 0.9 collective-permute-start.54
  175.8 8.8 %collective-permute-done.54.got = bf16[272,768]{1,0:T(8,128)(2,1)S(1)} collective-permute-done((bf16[272,768]{1,0:T(8,128)(2,1)S(1)}, bf16[272,768]{1,0:T(8,128)(2,1)S(1)}, u32[]{:S(2)}, u32[]{:S(2)}) %collective-permute-start.54) | collective-permute-done | bytes 417824 | tf_op jit(solution)/shard_map/ppermute | solution.py:104
  185.3 1.2 shard_map.244
  188.0 1.7 copy.24
  189.7 1.0 collective-permute-done.58.got
  190.7 1.3 shard_map.245
  (133 shorter events, 36.5 us)
Async XLA Ops:
  4.3 26.9 %copy-start.7 = (bf16[48,1536]{1,0:T(8,128)(2,1)S(1)}, bf16[48,1536]{1,0:T(8,128)(2,1)}, u32[]{:S(2)}) copy-start(bf16[48,1536]{1,0:T(8,128)(2,1)} %param.24) | copy-start | bytes 442372
  4.4 6.1 %collective-permute-start = (bf16[24,1280]{1,0:T(8,128)(2,1)S(1)}, bf16[24,1280]{1,0:T(8,128)(2,1)S(1)}, u32[]{:S(2)}, u32[]{:S(2)}) collective-permute-start(bf16[24,1280]{1,0:T(8,128)(2,1)S(1)} %get-tuple-element.143), channel_id=1, source_target_pairs={{0,1},{1,0},{2,3},{3,2},{4,5},{5,4},{6,7},{7,6},{8,9},{9,8},{10,11... | collective-permute-start | bytes 184328 | tf_op jit(solution)/shard_map/ppermute | solution.py:104
  11.8 17.9 %collective-permute-start.4 = (bf16[272,768]{1,0:T(8,128)(2,1)S(1)}, bf16[272,768]{1,0:T(8,128)(2,1)S(1)}, u32[]{:S(2)}, u32[]{:S(2)}) collective-permute-start(bf16[272,768]{1,0:T(8,128)(2,1)S(1)} %pad.4.own), channel_id=1, source_target_pairs={{0,1},{1,0},{2,3},{3,2},{4,5},{5,4},{6,7},{7,6},{8,9},{9,8},{10,11... | collective-permute-start | bytes 1253384 | tf_op jit(solution)/shard_map/ppermute | solution.py:104
  13.0 8.2 %collective-permute-start.3 = (bf16[48,1664]{1,0:T(8,128)(2,1)S(1)}, bf16[48,1664]{1,0:T(8,128)(2,1)S(1)}, u32[]{:S(2)}, u32[]{:S(2)}) collective-permute-start(bf16[48,1664]{1,0:T(8,128)(2,1)S(1)} %shard_map.214), channel_id=1, source_target_pairs={{0,24},{2,26},{4,28},{6,30},{8,0},{10,2},{12,4},{14,6},{16,8},{18,... | collective-permute-start | bytes 479240 | tf_op jit(solution)/shard_map/ppermute | solution.py:100
  16.6 8.8 %collective-permute-start.1 = (bf16[48,1664]{1,0:T(8,128)(2,1)S(1)}, bf16[48,1664]{1,0:T(8,128)(2,1)S(1)}, u32[]{:S(2)}, u32[]{:S(2)}) collective-permute-start(bf16[48,1664]{1,0:T(8,128)(2,1)S(1)} %shard_map.214), channel_id=1, source_target_pairs={{0,8},{2,10},{4,12},{6,14},{8,16},{10,18},{12,20},{14,22},{16,24},... | collective-permute-start | bytes 479240 | tf_op jit(solution)/shard_map/ppermute | solution.py:100
  16.6 13.0 %collective-permute-start.2 = (bf16[48,1664]{1,0:T(8,128)(2,1)S(1)}, bf16[48,1664]{1,0:T(8,128)(2,1)S(1)}, u32[]{:S(2)}, u32[]{:S(2)}) collective-permute-start(bf16[48,1664]{1,0:T(8,128)(2,1)S(1)} %shard_map.214), channel_id=1, source_target_pairs={{0,16},{2,18},{4,20},{6,22},{8,24},{10,26},{12,28},{14,30},{16,0},... | collective-permute-start | bytes 479240 | tf_op jit(solution)/shard_map/ppermute | solution.py:100
  29.7 18.9 %copy-start.8 = (bf16[1536,48]{0,1:T(8,128)(2,1)S(1)}, bf16[1536,48]{0,1:T(8,128)(2,1)}, u32[]{:S(2)}) copy-start(bf16[1536,48]{0,1:T(8,128)(2,1)} %param.26) | copy-start | bytes 442372
  29.7 15.5 %collective-permute-start.5 = (bf16[4,48,1664]{2,1,0:T(8,128)(2,1)S(1)}, bf16[4,48,1664]{2,1,0:T(8,128)(2,1)S(1)}, u32[]{:S(2)}, u32[]{:S(2)}) collective-permute-start(bf16[4,48,1664]{2,1,0:T(8,128)(2,1)S(1)} %pad_maximum_fusion.refs_0_.mine), channel_id=1, source_target_pairs={{0,4},{2,6},{4,0},{6,2},{8,12},{10,14},{12,8},{14,10},{16,20},{18,... | collective-permute-start | bytes 1916936 | tf_op jit(solution)/shard_map/ppermute | solution.py:100
  31.3 8.6 %collective-permute-start.6 = (bf16[48,1536]{1,0:T(8,128)(2,1)S(1)}, bf16[48,1536]{1,0:T(8,128)(2,1)S(1)}, u32[]{:S(2)}, u32[]{:S(2)}) collective-permute-start(bf16[48,1536]{1,0:T(8,128)(2,1)S(1)} %copy-done.7), channel_id=1, source_target_pairs={{0,8},{2,10},{4,12},{6,14},{8,16},{10,18},{12,20},{14,22},{16,24},... | collective-permute-start | bytes 442376 | tf_op jit(solution)/shard_map/ppermute | solution.py:100
  31.3 12.9 %collective-permute-start.7 = (bf16[48,1536]{1,0:T(8,128)(2,1)S(1)}, bf16[48,1536]{1,0:T(8,128)(2,1)S(1)}, u32[]{:S(2)}, u32[]{:S(2)}) collective-permute-start(bf16[48,1536]{1,0:T(8,128)(2,1)S(1)} %copy-done.7), channel_id=1, source_target_pairs={{0,16},{2,18},{4,20},{6,22},{8,24},{10,26},{12,28},{14,30},{16,0},... | collective-permute-start | bytes 442376 | tf_op jit(solution)/shard_map/ppermute | solution.py:100
  33.9 10.3 %collective-permute-start.8 = (bf16[48,1536]{1,0:T(8,128)(2,1)S(1)}, bf16[48,1536]{1,0:T(8,128)(2,1)S(1)}, u32[]{:S(2)}, u32[]{:S(2)}) collective-permute-start(bf16[48,1536]{1,0:T(8,128)(2,1)S(1)} %copy-done.7), channel_id=1, source_target_pairs={{0,24},{2,26},{4,28},{6,30},{8,0},{10,2},{12,4},{14,6},{16,8},{18,... | collective-permute-start | bytes 442376 | tf_op jit(solution)/shard_map/ppermute | solution.py:100
  45.2 4.4 %collective-permute-start.10 = (bf16[4,48,1664]{2,1,0:T(8,128)(2,1)S(1)}, bf16[4,48,1664]{2,1,0:T(8,128)(2,1)S(1)}, u32[]{:S(2)}, u32[]{:S(2)}) collective-permute-start(bf16[4,48,1664]{2,1,0:T(8,128)(2,1)S(1)} %collective-permute-done.5.refs_1_.x_got), channel_id=1, source_target_pairs={{0,2},{2,0},{4,6},{6,4},{8,10},{10,8},{12,14},{14,12},{16,18},{18,... | collective-permute-start | bytes 1916936 | tf_op jit(solution)/shard_map/ppermute | solution.py:100
  45.2 6.5 %collective-permute-start.9 = (bf16[4,48,1664]{2,1,0:T(8,128)(2,1)S(1)}, bf16[4,48,1664]{2,1,0:T(8,128)(2,1)S(1)}, u32[]{:S(2)}, u32[]{:S(2)}) collective-permute-start(bf16[4,48,1664]{2,1,0:T(8,128)(2,1)S(1)} %pad_maximum_fusion.refs_0_.mine), channel_id=1, source_target_pairs={{0,2},{2,0},{4,6},{6,4},{8,10},{10,8},{12,14},{14,12},{16,18},{18,... | collective-permute-start | bytes 1916936 | tf_op jit(solution)/shard_map/ppermute | solution.py:100
  45.7 16.8 %collective-permute-start.19 = (bf16[4,48,1536]{2,1,0:T(8,128)(2,1)S(1)}, bf16[4,48,1536]{2,1,0:T(8,128)(2,1)S(1)}, u32[]{:S(2)}, u32[]{:S(2)}) collective-permute-start(bf16[4,48,1536]{2,1,0:T(8,128)(2,1)S(1)} %pad_maximum_fusion.1.refs_0_), channel_id=1, source_target_pairs={{0,4},{2,6},{4,0},{6,2},{8,12},{10,14},{12,8},{14,10},{16,20},{18,... | collective-permute-start | bytes 1769480 | tf_op jit(solution)/shard_map/ppermute | solution.py:100
  47.8 13.2 %collective-permute-start.12 = (bf16[8,24,768]{2,1,0:T(8,128)(2,1)S(1)}, bf16[8,24,768]{2,1,0:T(8,128)(2,1)S(1)}, u32[]{:S(2)}, u32[]{:S(2)}) collective-permute-start(bf16[8,24,768]{2,1,0:T(8,128)(2,1)S(1)} %shard_map.217), channel_id=1, source_target_pairs={{0,1},{1,0},{2,3},{3,2},{4,5},{5,4},{6,7},{7,6},{8,9},{9,8},{10,11... | collective-permute-start | bytes 884744 | tf_op jit(solution)/shard_map/ppermute | solution.py:104
  48.5 13.8 %collective-permute-start.15 = (bf16[48,1536]{1,0:T(8,128)(2,1)S(1)}, bf16[48,1536]{1,0:T(8,128)(2,1)S(1)}, u32[]{:S(2)}, u32[]{:S(2)}) collective-permute-start(bf16[48,1536]{1,0:T(8,128)(2,1)S(1)} %bitcast.83), channel_id=1, source_target_pairs={{0,8},{2,10},{4,12},{6,14},{8,16},{10,18},{12,20},{14,22},{16,24},... | collective-permute-start | bytes 442376 | tf_op jit(solution)/shard_map/ppermute | solution.py:100
  49.6 12.7 %collective-permute-start.16 = (bf16[48,1536]{1,0:T(8,128)(2,1)S(1)}, bf16[48,1536]{1,0:T(8,128)(2,1)S(1)}, u32[]{:S(2)}, u32[]{:S(2)}) collective-permute-start(bf16[48,1536]{1,0:T(8,128)(2,1)S(1)} %bitcast.84), channel_id=1, source_target_pairs={{0,16},{2,18},{4,20},{6,22},{8,24},{10,26},{12,28},{14,30},{16,0},... | collective-permute-start | bytes 442376 | tf_op jit(solution)/shard_map/ppermute | solution.py:100
  51.7 10.7 %collective-permute-start.17 = (bf16[48,1536]{1,0:T(8,128)(2,1)S(1)}, bf16[48,1536]{1,0:T(8,128)(2,1)S(1)}, u32[]{:S(2)}, u32[]{:S(2)}) collective-permute-start(bf16[48,1536]{1,0:T(8,128)(2,1)S(1)} %bitcast.85), channel_id=1, source_target_pairs={{0,24},{2,26},{4,28},{6,30},{8,0},{10,2},{12,4},{14,6},{16,8},{18,... | collective-permute-start | bytes 442376 | tf_op jit(solution)/shard_map/ppermute | solution.py:100
  61.0 6.0 %collective-permute-start.11 = (bf16[272,384]{1,0:T(8,128)(2,1)S(1)}, bf16[272,384]{1,0:T(8,128)(2,1)S(1)}, u32[]{:S(2)}, u32[]{:S(2)}) collective-permute-start(bf16[272,384]{1,0:T(8,128)(2,1)S(1)} %get-tuple-element.151), channel_id=1, source_target_pairs={{0,1},{1,0},{2,3},{3,2},{4,5},{5,4},{6,7},{7,6},{8,9},{9,8},{10,11... | collective-permute-start | bytes 626696 | tf_op jit(solution)/shard_map/ppermute | solution.py:104
  62.4 1.7 collective-permute-start.13
  62.5 8.7 %collective-permute-start.21 = (bf16[4,48,1536]{2,1,0:T(8,128)(2,1)S(1)}, bf16[4,48,1536]{2,1,0:T(8,128)(2,1)S(1)}, u32[]{:S(2)}, u32[]{:S(2)}) collective-permute-start(bf16[4,48,1536]{2,1,0:T(8,128)(2,1)S(1)} %collective-permute-done.19.refs_1_), channel_id=1, source_target_pairs={{0,2},{2,0},{4,6},{6,4},{8,10},{10,8},{12,14},{14,12},{16,18},{18,... | collective-permute-start | bytes 1769480 | tf_op jit(solution)/shard_map/ppermute | solution.py:100
  63.0 8.1 %collective-permute-start.20 = (bf16[4,48,1536]{2,1,0:T(8,128)(2,1)S(1)}, bf16[4,48,1536]{2,1,0:T(8,128)(2,1)S(1)}, u32[]{:S(2)}, u32[]{:S(2)}) collective-permute-start(bf16[4,48,1536]{2,1,0:T(8,128)(2,1)S(1)} %pad_maximum_fusion.1.refs_0_), channel_id=1, source_target_pairs={{0,2},{2,0},{4,6},{6,4},{8,10},{10,8},{12,14},{14,12},{16,18},{18,... | collective-permute-start | bytes 1769480 | tf_op jit(solution)/shard_map/ppermute | solution.py:100
  63.1 15.7 %collective-permute-start.18 = (bf16[4,48,1536]{2,1,0:T(8,128)(2,1)S(1)}, bf16[4,48,1536]{2,1,0:T(8,128)(2,1)S(1)}, u32[]{:S(2)}, u32[]{:S(2)}) collective-permute-start(bf16[4,48,1536]{2,1,0:T(8,128)(2,1)S(1)} %pad_maximum_fusion.2.refs_0_), channel_id=1, source_target_pairs={{0,4},{2,6},{4,0},{6,2},{8,12},{10,14},{12,8},{14,10},{16,20},{18,... | collective-permute-start | bytes 1769480 | tf_op jit(solution)/shard_map/ppermute | solution.py:100
  64.7 5.0 %copy-start.1 = (s32[384,2]{1,0:T(8,128)S(1)}, s32[384,2]{1,0:T(8,128)}, u32[]{:S(2)}) copy-start(s32[384,2]{1,0:T(8,128)} %constant.78.clone.target) | copy-start | bytes 9220
  68.3 10.5 %collective-permute-start.14 = (bf16[272,768]{1,0:T(8,128)(2,1)S(1)}, bf16[272,768]{1,0:T(8,128)(2,1)S(1)}, u32[]{:S(2)}, u32[]{:S(2)}) collective-permute-start(bf16[272,768]{1,0:T(8,128)(2,1)S(1)} %get-tuple-element.166.a_up), channel_id=1, source_target_pairs={{0,1},{1,0},{2,3},{3,2},{4,5},{5,4},{6,7},{7,6},{8,9},{9,8},{10,11... | collective-permute-start | bytes 1253384 | tf_op jit(solution)/shard_map/ppermute | solution.py:104
  69.7 10.2 %collective-permute-start.22 = (bf16[4,48,1536]{2,1,0:T(8,128)(2,1)S(1)}, bf16[4,48,1536]{2,1,0:T(8,128)(2,1)S(1)}, u32[]{:S(2)}, u32[]{:S(2)}) collective-permute-start(bf16[4,48,1536]{2,1,0:T(8,128)(2,1)S(1)} %pad_maximum_fusion.2.refs_0_), channel_id=1, source_target_pairs={{0,2},{2,0},{4,6},{6,4},{8,10},{10,8},{12,14},{14,12},{16,18},{18,... | collective-permute-start | bytes 1769480 | tf_op jit(solution)/shard_map/ppermute | solution.py:100
  78.8 2.0 %collective-permute-start.23 = (bf16[4,48,1536]{2,1,0:T(8,128)(2,1)S(1)}, bf16[4,48,1536]{2,1,0:T(8,128)(2,1)S(1)}, u32[]{:S(2)}, u32[]{:S(2)}) collective-permute-start(bf16[4,48,1536]{2,1,0:T(8,128)(2,1)S(1)} %collective-permute-done.18.refs_1_), channel_id=1, source_target_pairs={{0,2},{2,0},{4,6},{6,4},{8,10},{10,8},{12,14},{14,12},{16,18},{18,... | collective-permute-start | bytes 1769480 | tf_op jit(solution)/shard_map/ppermute | solution.py:100
  83.3 8.3 %collective-permute-start.24 = (bf16[144,768]{1,0:T(8,128)(2,1)S(1)}, bf16[144,768]{1,0:T(8,128)(2,1)S(1)}, u32[]{:S(2)}, u32[]{:S(2)}) collective-permute-start(bf16[144,768]{1,0:T(8,128)(2,1)S(1)} %slice.12), channel_id=1, source_target_pairs={{0,1},{1,0},{2,3},{3,2},{4,5},{5,4},{6,7},{7,6},{8,9},{9,8},{10,11... | collective-permute-start | bytes 663560 | tf_op jit(solution)/shard_map/ppermute | solution.py:104
  84.1 11.0 %collective-permute-start.25 = (bf16[128,768]{1,0:T(8,128)(2,1)S(1)}, bf16[128,768]{1,0:T(8,128)(2,1)S(1)}, u32[]{:S(2)}, u32[]{:S(2)}) collective-permute-start(bf16[128,768]{1,0:T(8,128)(2,1)S(1)} %slice.13), channel_id=1, source_target_pairs={{0,1},{1,0},{2,3},{3,2},{4,5},{5,4},{6,7},{7,6},{8,9},{9,8},{10,11... | collective-permute-start | bytes 589832 | tf_op jit(solution)/shard_map/ppermute | solution.py:104
  85.4 6.3 %copy-start = (bf16[266,1,768]{2,0,1:T(8,128)(2,1)S(1)}, bf16[266,1,768]{2,0,1:T(8,128)(2,1)}, u32[]{:S(2)}) copy-start(bf16[266,1,768]{2,0,1:T(8,128)(2,1)} %param.15) | copy-start | bytes 1225732
  92.7 2.4 %collective-permute-start.26 = (bf16[16,128]{1,0:T(8,128)(2,1)S(1)}, bf16[16,128]{1,0:T(8,128)(2,1)S(1)}, u32[]{:S(2)}, u32[]{:S(2)}) collective-permute-start(bf16[16,128]{1,0:T(8,128)(2,1)S(1)} %slice.11), channel_id=1, source_target_pairs={{0,2},{2,0},{4,6},{6,4},{8,10},{10,8},{12,14},{14,12},{16,18},{18,... | collective-permute-start | bytes 12296 | tf_op jit(solution)/shard_map/ppermute | solution.py:100
  92.8 12.1 %collective-permute-start.27 = (bf16[144,768]{1,0:T(8,128)(2,1)S(1)}, bf16[144,768]{1,0:T(8,128)(2,1)S(1)}, u32[]{:S(2)}, u32[]{:S(2)}) collective-permute-start(bf16[144,768]{1,0:T(8,128)(2,1)S(1)} %get-tuple-element.168), channel_id=1, source_target_pairs={{0,1},{1,0},{2,3},{3,2},{4,5},{5,4},{6,7},{7,6},{8,9},{9,8},{10,11... | collective-permute-start | bytes 663560 | tf_op jit(solution)/shard_map/ppermute | solution.py:104
  97.1 7.8 %collective-permute-start.28 = (bf16[128,768]{1,0:T(8,128)(2,1)S(1)}, bf16[128,768]{1,0:T(8,128)(2,1)S(1)}, u32[]{:S(2)}, u32[]{:S(2)}) collective-permute-start(bf16[128,768]{1,0:T(8,128)(2,1)S(1)} %get-tuple-element.173), channel_id=1, source_target_pairs={{0,1},{1,0},{2,3},{3,2},{4,5},{5,4},{6,7},{7,6},{8,9},{9,8},{10,11... | collective-permute-start | bytes 589832 | tf_op jit(solution)/shard_map/ppermute | solution.py:104
  107.0 12.2 %collective-permute-start.29 = (bf16[272,768]{1,0:T(8,128)(2,1)S(1)}, bf16[272,768]{1,0:T(8,128)(2,1)S(1)}, u32[]{:S(2)}, u32[]{:S(2)}) collective-permute-start(bf16[272,768]{1,0:T(8,128)(2,1)S(1)} %convolution_convert_fusion), channel_id=1, source_target_pairs={{0,1},{1,0},{2,3},{3,2},{4,5},{5,4},{6,7},{7,6},{8,9},{9,8},{10,11... | collective-permute-start | bytes 1253384 | tf_op jit(solution)/shard_map/ppermute | solution.py:104
  110.0 1.6 collective-permute-start.34
  110.1 2.0 %collective-permute-start.35 = (bf16[8,48,384]{2,1,0:T(8,128)(2,1)S(1)}, bf16[8,48,384]{2,1,0:T(8,128)(2,1)S(1)}, u32[]{:S(2)}, u32[]{:S(2)}) collective-permute-start(bf16[8,48,384]{2,1,0:T(8,128)(2,1)S(1)} %get-tuple-element.195), channel_id=1, source_target_pairs={{0,2},{2,0},{4,6},{6,4},{8,10},{10,8},{12,14},{14,12},{16,18},{18,... | collective-permute-start | bytes 884744 | tf_op jit(solution)/shard_map/ppermute | solution.py:100
  110.6 1.9 collective-permute-start.36
  110.7 2.3 %collective-permute-start.37 = (bf16[8,48,384]{2,1,0:T(8,128)(2,1)S(1)}, bf16[8,48,384]{2,1,0:T(8,128)(2,1)S(1)}, u32[]{:S(2)}, u32[]{:S(2)}) collective-permute-start(bf16[8,48,384]{2,1,0:T(8,128)(2,1)S(1)} %get-tuple-element.197), channel_id=1, source_target_pairs={{0,2},{2,0},{4,6},{6,4},{8,10},{10,8},{12,14},{14,12},{16,18},{18,... | collective-permute-start | bytes 884744 | tf_op jit(solution)/shard_map/ppermute | solution.py:100
  113.8 15.4 %collective-permute-start.42 = (bf16[4,48,1536]{2,1,0:T(8,128)(2,1)S(1)}, bf16[4,48,1536]{2,1,0:T(8,128)(2,1)S(1)}, u32[]{:S(2)}, u32[]{:S(2)}) collective-permute-start(bf16[4,48,1536]{2,1,0:T(8,128)(2,1)S(1)} %get-tuple-element.198), channel_id=1, source_target_pairs={{0,4},{2,6},{4,0},{6,2},{8,12},{10,14},{12,8},{14,10},{16,20},{18,... | collective-permute-start | bytes 1769480 | tf_op jit(solution)/shard_map/ppermute | solution.py:100
  118.6 2.7 %collective-permute-start.38 = (bf16[8,48,384]{2,1,0:T(8,128)(2,1)S(1)}, bf16[8,48,384]{2,1,0:T(8,128)(2,1)S(1)}, u32[]{:S(2)}, u32[]{:S(2)}) collective-permute-start(bf16[8,48,384]{2,1,0:T(8,128)(2,1)S(1)} %get-tuple-element.201), channel_id=1, source_target_pairs={{0,2},{2,0},{4,6},{6,4},{8,10},{10,8},{12,14},{14,12},{16,18},{18,... | collective-permute-start | bytes 884744 | tf_op jit(solution)/shard_map/ppermute | solution.py:100
  118.6 5.2 %collective-permute-start.39 = (bf16[8,48,384]{2,1,0:T(8,128)(2,1)S(1)}, bf16[8,48,384]{2,1,0:T(8,128)(2,1)S(1)}, u32[]{:S(2)}, u32[]{:S(2)}) collective-permute-start(bf16[8,48,384]{2,1,0:T(8,128)(2,1)S(1)} %get-tuple-element.202), channel_id=1, source_target_pairs={{0,2},{2,0},{4,6},{6,4},{8,10},{10,8},{12,14},{14,12},{16,18},{18,... | collective-permute-start | bytes 884744 | tf_op jit(solution)/shard_map/ppermute | solution.py:100
  119.1 4.8 %collective-permute-start.40 = (bf16[8,48,384]{2,1,0:T(8,128)(2,1)S(1)}, bf16[8,48,384]{2,1,0:T(8,128)(2,1)S(1)}, u32[]{:S(2)}, u32[]{:S(2)}) collective-permute-start(bf16[8,48,384]{2,1,0:T(8,128)(2,1)S(1)} %get-tuple-element.203), channel_id=1, source_target_pairs={{0,2},{2,0},{4,6},{6,4},{8,10},{10,8},{12,14},{14,12},{16,18},{18,... | collective-permute-start | bytes 884744 | tf_op jit(solution)/shard_map/ppermute | solution.py:100
  119.2 5.2 %collective-permute-start.41 = (bf16[8,48,384]{2,1,0:T(8,128)(2,1)S(1)}, bf16[8,48,384]{2,1,0:T(8,128)(2,1)S(1)}, u32[]{:S(2)}, u32[]{:S(2)}) collective-permute-start(bf16[8,48,384]{2,1,0:T(8,128)(2,1)S(1)} %get-tuple-element.204), channel_id=1, source_target_pairs={{0,2},{2,0},{4,6},{6,4},{8,10},{10,8},{12,14},{14,12},{16,18},{18,... | collective-permute-start | bytes 884744 | tf_op jit(solution)/shard_map/ppermute | solution.py:100
  121.3 8.6 %collective-permute-start.30 = (bf16[272,384]{1,0:T(8,128)(2,1)S(1)}, bf16[272,384]{1,0:T(8,128)(2,1)S(1)}, u32[]{:S(2)}, u32[]{:S(2)}) collective-permute-start(bf16[272,384]{1,0:T(8,128)(2,1)S(1)} %get-tuple-element.180), channel_id=1, source_target_pairs={{0,1},{1,0},{2,3},{3,2},{4,5},{5,4},{6,7},{7,6},{8,9},{9,8},{10,11... | collective-permute-start | bytes 626696 | tf_op jit(solution)/shard_map/ppermute | solution.py:104
  123.9 1.5 collective-permute-start.31
  123.9 1.7 collective-permute-start.32
  124.4 1.5 collective-permute-start.33
  129.9 16.5 %collective-permute-start.43 = (bf16[8,24,768]{2,1,0:T(8,128)(2,1)S(1)}, bf16[8,24,768]{2,1,0:T(8,128)(2,1)S(1)}, u32[]{:S(2)}, u32[]{:S(2)}) collective-permute-start(bf16[8,24,768]{2,1,0:T(8,128)(2,1)S(1)} %get-tuple-element.211), channel_id=1, source_target_pairs={{0,1},{1,0},{2,3},{3,2},{4,5},{5,4},{6,7},{7,6},{8,9},{9,8},{10,11... | collective-permute-start | bytes 884744 | tf_op jit(solution)/shard_map/ppermute | solution.py:104
  131.3 15.2 %collective-permute-start.44 = (bf16[2,48,1536]{2,1,0:T(8,128)(2,1)S(1)}, bf16[2,48,1536]{2,1,0:T(8,128)(2,1)S(1)}, u32[]{:S(2)}, u32[]{:S(2)}) collective-permute-start(bf16[2,48,1536]{2,1,0:T(8,128)(2,1)S(1)} %get-tuple-element.212), channel_id=1, source_target_pairs={{0,16},{2,18},{4,20},{6,22},{8,24},{10,26},{12,28},{14,30},{16,0},... | collective-permute-start | bytes 884744 | tf_op jit(solution)/shard_map/ppermute | solution.py:100
  133.2 14.2 %collective-permute-start.45 = (bf16[4,48,1536]{2,1,0:T(8,128)(2,1)S(1)}, bf16[4,48,1536]{2,1,0:T(8,128)(2,1)S(1)}, u32[]{:S(2)}, u32[]{:S(2)}) collective-permute-start(bf16[4,48,1536]{2,1,0:T(8,128)(2,1)S(1)} %get-tuple-element.226), channel_id=1, source_target_pairs={{0,4},{2,6},{4,0},{6,2},{8,12},{10,14},{12,8},{14,10},{16,20},{18,... | collective-permute-start | bytes 1769480 | tf_op jit(solution)/shard_map/ppermute | solution.py:100
  146.4 2.6 %collective-permute-start.46 = (bf16[8,48,384]{2,1,0:T(8,128)(2,1)S(1)}, bf16[8,48,384]{2,1,0:T(8,128)(2,1)S(1)}, u32[]{:S(2)}, u32[]{:S(2)}) collective-permute-start(bf16[8,48,384]{2,1,0:T(8,128)(2,1)S(1)} %get-tuple-element.228), channel_id=1, source_target_pairs={{0,2},{2,0},{4,6},{6,4},{8,10},{10,8},{12,14},{14,12},{16,18},{18,... | collective-permute-start | bytes 884744 | tf_op jit(solution)/shard_map/ppermute | solution.py:100
  146.5 2.6 %collective-permute-start.47 = (bf16[8,48,384]{2,1,0:T(8,128)(2,1)S(1)}, bf16[8,48,384]{2,1,0:T(8,128)(2,1)S(1)}, u32[]{:S(2)}, u32[]{:S(2)}) collective-permute-start(bf16[8,48,384]{2,1,0:T(8,128)(2,1)S(1)} %get-tuple-element.229), channel_id=1, source_target_pairs={{0,2},{2,0},{4,6},{6,4},{8,10},{10,8},{12,14},{14,12},{16,18},{18,... | collective-permute-start | bytes 884744 | tf_op jit(solution)/shard_map/ppermute | solution.py:100
  147.0 2.1 %collective-permute-start.48 = (bf16[8,48,384]{2,1,0:T(8,128)(2,1)S(1)}, bf16[8,48,384]{2,1,0:T(8,128)(2,1)S(1)}, u32[]{:S(2)}, u32[]{:S(2)}) collective-permute-start(bf16[8,48,384]{2,1,0:T(8,128)(2,1)S(1)} %get-tuple-element.230), channel_id=1, source_target_pairs={{0,2},{2,0},{4,6},{6,4},{8,10},{10,8},{12,14},{14,12},{16,18},{18,... | collective-permute-start | bytes 884744 | tf_op jit(solution)/shard_map/ppermute | solution.py:100
  147.0 2.0 %collective-permute-start.49 = (bf16[8,48,128]{2,1,0:T(8,128)(2,1)S(1)}, bf16[8,48,128]{2,1,0:T(8,128)(2,1)S(1)}, u32[]{:S(2)}, u32[]{:S(2)}) collective-permute-start(bf16[8,48,128]{2,1,0:T(8,128)(2,1)S(1)} %get-tuple-element.231), channel_id=1, source_target_pairs={{0,2},{2,0},{4,6},{6,4},{8,10},{10,8},{12,14},{14,12},{16,18},{18,... | collective-permute-start | bytes 294920 | tf_op jit(solution)/shard_map/ppermute | solution.py:100
  149.8 18.1 %collective-permute-start.50 = (bf16[4,48,1280]{2,1,0:T(8,128)(2,1)S(1)}, bf16[4,48,1280]{2,1,0:T(8,128)(2,1)S(1)}, u32[]{:S(2)}, u32[]{:S(2)}) collective-permute-start(bf16[4,48,1280]{2,1,0:T(8,128)(2,1)S(1)} %get-tuple-element.236), channel_id=1, source_target_pairs={{0,4},{2,6},{4,0},{6,2},{8,12},{10,14},{12,8},{14,10},{16,20},{18,... | collective-permute-start | bytes 1474568 | tf_op jit(solution)/shard_map/ppermute | solution.py:100
  151.4 16.0 %collective-permute-start.52 = (bf16[2,48,1536]{2,1,0:T(8,128)(2,1)S(1)}, bf16[2,48,1536]{2,1,0:T(8,128)(2,1)S(1)}, u32[]{:S(2)}, u32[]{:S(2)}) collective-permute-start(bf16[2,48,1536]{2,1,0:T(8,128)(2,1)S(1)} %get-tuple-element.244), channel_id=1, source_target_pairs={{0,16},{2,18},{4,20},{6,22},{8,24},{10,26},{12,28},{14,30},{16,0},... | collective-permute-start | bytes 884744 | tf_op jit(solution)/shard_map/ppermute | solution.py:100
  153.0 15.0 %collective-permute-start.53 = (bf16[1,48,1536]{2,1,0:T(8,128)(2,1)S(1)}, bf16[1,48,1536]{2,1,0:T(8,128)(2,1)S(1)}, u32[]{:S(2)}, u32[]{:S(2)}) collective-permute-start(bf16[1,48,1536]{2,1,0:T(8,128)(2,1)S(1)} %get-tuple-element.248), channel_id=1, source_target_pairs={{0,8},{2,10},{4,12},{6,14},{8,0},{10,2},{12,4},{14,6},{16,24},{18,... | collective-permute-start | bytes 442376 | tf_op jit(solution)/shard_map/ppermute | solution.py:402
  156.4 11.6 %collective-permute-start.51 = (bf16[4,24,768]{2,1,0:T(8,128)(2,1)S(1)}, bf16[4,24,768]{2,1,0:T(8,128)(2,1)S(1)}, u32[]{:S(2)}, u32[]{:S(2)}) collective-permute-start(bf16[4,24,768]{2,1,0:T(8,128)(2,1)S(1)} %get-tuple-element.242), channel_id=1, source_target_pairs={{0,4},{2,6},{4,0},{6,2},{8,12},{10,14},{12,8},{14,10},{16,20},{18,... | collective-permute-start | bytes 442376 | tf_op jit(solution)/shard_map/ppermute | solution.py:100
  168.0 19.2 %collective-permute-start.59 = (bf16[1,48,1536]{2,1,0:T(8,128)(2,1)S(1)}, bf16[1,48,1536]{2,1,0:T(8,128)(2,1)S(1)}, u32[]{:S(2)}, u32[]{:S(2)}) collective-permute-start(bf16[1,48,1536]{2,1,0:T(8,128)(2,1)S(1)} %get-tuple-element.270), channel_id=1, source_target_pairs={{0,8},{2,10},{4,12},{6,14},{8,0},{10,2},{12,4},{14,6},{16,24},{18,... | collective-permute-start | bytes 442376 | tf_op jit(solution)/shard_map/ppermute | solution.py:402
  168.8 16.5 %collective-permute-start.55 = (bf16[1,48,1664]{2,1,0:T(8,128)(2,1)S(1)}, bf16[1,48,1664]{2,1,0:T(8,128)(2,1)S(1)}, u32[]{:S(2)}, u32[]{:S(2)}) collective-permute-start(bf16[1,48,1664]{2,1,0:T(8,128)(2,1)S(1)} %get-tuple-element.254), channel_id=1, source_target_pairs={{0,8},{2,10},{4,12},{6,14},{8,16},{10,18},{12,20},{14,22},{16,24},... | collective-permute-start | bytes 479240 | tf_op jit(solution)/shard_map/ppermute | solution.py:100
  170.8 14.4 %collective-permute-start.56 = (bf16[1,48,1664]{2,1,0:T(8,128)(2,1)S(1)}, bf16[1,48,1664]{2,1,0:T(8,128)(2,1)S(1)}, u32[]{:S(2)}, u32[]{:S(2)}) collective-permute-start(bf16[1,48,1664]{2,1,0:T(8,128)(2,1)S(1)} %get-tuple-element.255), channel_id=1, source_target_pairs={{0,16},{2,18},{4,20},{6,22},{8,24},{10,26},{12,28},{14,30},{16,0},... | collective-permute-start | bytes 479240 | tf_op jit(solution)/shard_map/ppermute | solution.py:100
  171.3 13.9 %collective-permute-start.57 = (bf16[1,48,1664]{2,1,0:T(8,128)(2,1)S(1)}, bf16[1,48,1664]{2,1,0:T(8,128)(2,1)S(1)}, u32[]{:S(2)}, u32[]{:S(2)}) collective-permute-start(bf16[1,48,1664]{2,1,0:T(8,128)(2,1)S(1)} %get-tuple-element.256), channel_id=1, source_target_pairs={{0,24},{2,26},{4,28},{6,30},{8,0},{10,2},{12,4},{14,6},{16,8},{18,... | collective-permute-start | bytes 479240 | tf_op jit(solution)/shard_map/ppermute | solution.py:100
  174.2 10.4 %collective-permute-start.54 = (bf16[272,768]{1,0:T(8,128)(2,1)S(1)}, bf16[272,768]{1,0:T(8,128)(2,1)S(1)}, u32[]{:S(2)}, u32[]{:S(2)}) collective-permute-start(bf16[272,768]{1,0:T(8,128)(2,1)S(1)} %get-tuple-element.249), channel_id=1, source_target_pairs={{0,1},{1,0},{2,3},{3,2},{4,5},{5,4},{6,7},{7,6},{8,9},{9,8},{10,11... | collective-permute-start | bytes 1253384 | tf_op jit(solution)/shard_map/ppermute | solution.py:104
  186.5 4.2 %collective-permute-start.58 = (bf16[24,1280]{1,0:T(8,128)(2,1)S(1)}, bf16[24,1280]{1,0:T(8,128)(2,1)S(1)}, u32[]{:S(2)}, u32[]{:S(2)}) collective-permute-start(bf16[24,1280]{1,0:T(8,128)(2,1)S(1)} %get-tuple-element.263), channel_id=1, source_target_pairs={{0,1},{1,0},{2,3},{3,2},{4,5},{5,4},{6,7},{7,6},{8,9},{9,8},{10,11... | collective-permute-start | bytes 184328 | tf_op jit(solution)/shard_map/ppermute | solution.py:104
  (5 other events, 3.7 us)

commit v3 on v2

--- a/solution.py
+++ b/solution.py
@@ -20,6 +20,7 @@
 OUT_TILE = 256
 ROWS = 16
 PAIR = 2 * HEAD
+UP_AT = 32
 QUICK = pl.CostEstimate(flops=1, bytes_accessed=1, transcendentals=0)
 T, X, CORE, OUTER, DP, FRESH, LENGTH, STARTS = range(8)
 
@@ -104,6 +105,15 @@
     return lax.ppermute(value, "tensor", [(0, 1), (1, 0)])
 
 
+def swap_both(value, digit):
+    stride, _ = digit
+    pairs = []
+    for at in range(lax.axis_size("dp")):
+        other = at + stride if (at // stride) % 2 == 0 else at - stride
+        pairs += [(2 * at + side, 2 * other + 1 - side) for side in range(2)]
+    return lax.ppermute(value, ("dp", "tensor"), pairs)
+
+
 def tie(value, *others):
     return lax.optimization_barrier((value,) + others)[0]
 
@@ -118,7 +128,27 @@
     return value.reshape((-1,) + value.shape[-2:])
 
 
-def placer(sizes, me):
+def swap_near(value, digit):
+    stride, _ = digit
+    pairs = []
+    for at in range(lax.axis_size("dp")):
+        pairs.append((at, at + stride if (at // stride) % 2 == 0 else at - stride))
+    return lax.ppermute(value, "dp", pairs)
+
+
+def spread_near(value, digits):
+    assert digits[-3][1] == 4
+    return jnp.stack([value, swap_near(value, digits[-3])])
+
+
+def spread_far(pair, digits):
+    value = jnp.concatenate([pair, rotate(pair, digits[-3], 2)], axis=0)
+    for digit in reversed(digits[:-3]):
+        value = jnp.stack([value] + [rotate(value, digit, step) for step in range(1, digit[1])])
+    return value.reshape((-1,) + value.shape[-2:])
+
+
+def placer(sizes, me, paired):
     outer, digits = sizes[:-2], []
     for size in reversed(sizes):
         digits.append(lax.rem(me, size))
@@ -131,8 +161,12 @@
             steps.append(slot % size)
             slot //= size
         place = 0
-        for size, digit, step in zip(outer, digits, steps[::-1]):
-            place = place * size + lax.rem(digit + (size - step), size)
+        for n, (size, digit, step) in enumerate(zip(outer, digits, steps[::-1])):
+            if paired and n == len(outer) - 1:
+                at = lax.bitwise_xor(digit, step)
+            else:
+                at = lax.rem(digit + (size - step), size)
+            place = place * size + at
         x, core = digits[-2], digits[-1]
         place = place * 2 + (1 - x if swap_x else x)
         return place * 2 + (1 - core if swap_core else core)
@@ -140,10 +174,10 @@
     return place_of
 
 
-def assemble_kernel(sizes, at, *refs):
+def assemble_kernel(sizes, paired, at, *refs):
     parts, whole = refs[:4], refs[4]
     cols = whole.shape[2]
-    place_of = placer(sizes, at[DP])
+    place_of = placer(sizes, at[DP], paired)
     for swap_core in range(2):
         for swap_x in range(2):
             source = parts[2 * swap_core + swap_x]
@@ -156,68 +190,84 @@
     return [mine, x_got, rotate(mine, core, 1), rotate(x_got, core, 1)]
 
 
-def assemble(at, parts, digits, cols):
+def assemble(at, parts, digits, cols, paired=False):
     slots, rows, _ = parts[0].shape
     sizes = tuple(size for _, size in digits)
     (whole,) = call(
-        functools.partial(assemble_kernel, sizes), [low_of(4 * slots, rows, cols)], at, *parts
+        functools.partial(assemble_kernel, sizes, paired),
+        [low_of(4 * slots, rows, cols)],
+        at,
+        *parts,
     )
     return whole.reshape(4 * slots * rows, cols)
+
+
+def assemble_first_kernel(sizes, at, *refs):
+    parts, whole = refs[:4], refs[4]
+    lines, cols = whole.shape[1] // 2, whole.shape[2]
+    place_of = placer(sizes, at[DP], False)
+    first = at[T] == 0
+    for swap_core in range(2):
+        for swap_x in range(2):
+            source = parts[2 * swap_core + swap_x]
+            far = source.shape[2] - cols
+            for slot in range(source.shape[0]):
+                place = place_of(swap_core, swap_x, slot)
+                a, b = source[slot, :, :cols], source[slot, :, far:]
+                whole[place, :lines] = jnp.where(first, a, b)
+                whole[place, lines:] = jnp.where(first, b, a)
 
 
 def assemble_out_kernel(sizes, cols, at, *refs):
     parts, gots, whole = refs[:4], refs[4:6], refs[6]
-    place_of = placer(sizes, at[DP])
+    place_of = placer(sizes, at[DP], False)
     first = at[T] == 0
-    lines = whole.shape[1] // 2
+    lines, width = whole.shape[1] // 2, whole.shape[2]
     for swap_core in range(2):
         for swap_x in range(2):
             source, got = parts[2 * swap_core + swap_x], gots[swap_core]
             slots = source.shape[0]
             for slot in range(slots):
-                mine = jnp.concatenate(
-                    [source[slot, :lines, cols:], source[slot, lines:, cols:]], axis=1
-                )
-                other = got[swap_x * slots + slot]
+                mine, other = source[slot, :, cols : cols + width], got[swap_x * slots + slot]
                 place = place_of(swap_core, swap_x, slot)
                 whole[place, :lines] = jnp.where(first, mine, other)
                 whole[place, lines:] = jnp.where(first, other, mine)
 
 
-def columns_kernel(part, small_rows, at, weight, vectors, gains, memory, up, kept, sent, turn):
-    lines, width = weight.shape[0], weight.shape[1] // 3
+def columns_kernel(small_rows, at, weight, vectors, gains, memory, up, out, packed, turn):
+    lines, width = weight.shape
+    packed[:, :width] = weight[...]
+    turn[...] = jnp.zeros_like(turn)
+    for source, (low, high) in zip((memory, vectors, gains), small_rows):
+        turn[low:high, :lines] = source[...].astype(WIDE)
+    columns = turn[...].T[:lines]
+    turn[:lines, :] = columns
+    turn[0:1, UP_AT : UP_AT + up.shape[1]] = up[...].astype(WIDE)
+    packed[:, width : width + PAIR] = turn[:lines, :].astype(LOW)
+    packed[:, width + PAIR :] = out[...]
+
+
+def halves_of_heads_kernel(part, at, packed, mine, other):
+    width = 6 * part
     first = at[T] == 0
-    for pair in range(part // PAIR):
-        for kind in range(3):
-            low = kind * width + pair * PAIR
-            a, b = weight[:, low : low + PAIR], weight[:, low + part : low + part + PAIR]
-            here = (3 * pair + kind) * PAIR
-            kept[:, here : here + PAIR] = jnp.where(first, a, b)
-            sent[:, here : here + PAIR] = jnp.where(first, b, a)
-    turn[...] = jnp.zeros_like(turn)
-    for source, (low, high) in zip((memory, vectors, gains, up), small_rows):
-        turn[low:high, :lines] = source[...].astype(WIDE)
-    columns = turn[...].T[:lines].astype(LOW)
-    kept[:, 3 * part :] = columns
-    sent[:, 3 * part :] = columns
-
-
-def pair_kernel(at, kept, got, out, pair):
-    lines, cols = kept.shape
-    fold = out.shape[1] // 2
-    first = at[T] == 0
-    pair[:lines, :cols] = jnp.where(first, kept[...], got[...])
-    pair[lines:, :cols] = jnp.where(first, got[...], kept[...])
-    pair[:lines, cols:] = out[:, :fold]
-    pair[lines:, cols:] = out[:, fold:]
-
-
-def unfold_kernel(cols, at, mine, x_got, out):
-    slots, lines, fold = mine.shape[0], out.shape[1], out.shape[2] // 2
+    for slot in range(packed.shape[0]):
+        for pair in range(part // PAIR):
+            for kind in range(3):
+                low = 2 * kind * part + pair * PAIR
+                a = packed[slot, :, low : low + PAIR]
+                b = packed[slot, :, low + part : low + part + PAIR]
+                here = (3 * pair + kind) * PAIR
+                mine[slot, :, here : here + PAIR] = jnp.where(first, a, b)
+                other[slot, :, here : here + PAIR] = jnp.where(first, b, a)
+        mine[slot, :, 3 * part :] = packed[slot, :, width:]
+        other[slot, :, 3 * part :] = packed[slot, :, width : width + PAIR]
+
+
+def beside_kernel(cols, at, mine, x_got, out):
+    slots = mine.shape[0]
     for n, source in enumerate((mine, x_got)):
         for slot in range(slots):
-            out[n * slots + slot, :, :fold] = source[slot, :lines, cols:]
-            out[n * slots + slot, :, fold:] = source[slot, lines:, cols:]
+            out[n * slots + slot] = source[slot, :, cols : cols + out.shape[2]]
 
 
 def put_blocks(total, kept, sent, core, at):
@@ -291,28 +341,20 @@
     put_gradient(a, b, outs, at[CORE], own=own)
 
 
-def rest_sums_kernel(spots, at, own, own_sums, a, b, target, sums, *outs):
+def rest_sums_kernel(at, own, own_sums, a, b, sums, *outs):
     put_gradient(a, b, outs, at[CORE], own=own)
-    total = (own_sums[...] + jnp.sum(b[...].astype(WIDE), axis=0, keepdims=True)).astype(LOW)
-    total = jnp.broadcast_to(total, (8, total.shape[1]))
-    for spot in range(spots):
-        sums[spot : spot + 1, :] = nt(total, one_hot(target, spot, total.shape[1]))[:1]
-
-
-def one_hot(target, spot, count):
-    at = lax.broadcasted_iota(jnp.int32, (target.shape[0], count), 1)
-    return (at == target[:, :1] + spot * target[0, 1]).astype(WIDE).astype(LOW)
-
-
-def up_row_kernel(first_row, spots, at, small, target, row):
-    part = target.shape[0]
-    total = jnp.zeros((8, row.shape[1]), WIDE)
-    for spot in range(spots):
-        line = small[first_row + spot : first_row + spot + 1, :]
-        line = jnp.where(at[T] == 0, line[:, :part], line[:, part:]).astype(LOW)
-        line = jnp.broadcast_to(line, (8, part))
-        total = total + nn(line, one_hot(target, spot, row.shape[1]))
-    row[...] = jnp.broadcast_to(total[:1], row.shape)
+    sums[...] = own_sums[...] + jnp.sum(b[...].astype(WIDE), axis=0, keepdims=True)
+
+
+def up_row_kernel(lines, at, w, row, line):
+    half, each = w.shape[0] // 2, row.shape[1] * lines * 2 // w.shape[0]
+    low = w.shape[1] - PAIR
+    for n in range(half // lines):
+        a = w[n * lines : n * lines + 1, low:].astype(WIDE)
+        b = w[half + n * lines : half + n * lines + 1, low:].astype(WIDE)
+        value = jnp.where(at[T] == 0, a, b)[:, UP_AT : UP_AT + each]
+        line[:, n * each : (n + 1) * each] = value
+    row[...] = jnp.broadcast_to(line[...], row.shape)
 
 
 def halve_kernel(at, mine, *refs):
@@ -334,30 +376,43 @@
     return call(halve_kernel, [low_of(groups // 2, rows, cols)] * 2, at, mine, *got)
 
 
-def parts_kernel(size, at, mine, got, *refs):
-    folded, outs = refs[: len(refs) - size], refs[len(refs) - size :]
+def quarter_kernel(at, mine, *refs):
+    got, (out_mine, out_got, keep, to_x, to_y, to_both) = refs[:-6], refs[-6:]
+    lines, cols = to_y.shape[1:]
+    first = at[T] == 0
+    for group in range(keep.shape[0]):
+        own, other = 2 * group + at[X], 2 * group + 1 - at[X]
+        for place, same, across in ((own, keep, to_y), (other, to_x, to_both)):
+            low = 0
+            for part in got:
+                high = low + part.shape[2]
+                total = mine[place, :, low:high].astype(WIDE) + part[place].astype(WIDE)
+                a, b = total[:lines], total[lines:]
+                same[group, :, low:high] = jnp.where(first, a, b).astype(LOW)
+                across[group, :, low:high] = jnp.where(first, b, a).astype(LOW)
+                low = high
+            total = out_mine[place].astype(WIDE) + out_got[place].astype(WIDE)
+            same[group, :, cols:] = total.astype(LOW)
+
+
+def parts_kernel(size, at, mine, x_got, y_got, both_got, *outs):
     me = at[OUTER]
     cols = mine.shape[2]
     for group in range(outs[0].shape[0]):
         for step, out in enumerate(outs):
             place = group * size + lax.rem(me + step, size)
-            total = mine[place].astype(WIDE) + got[place].astype(WIDE)
+            total = mine[place].astype(WIDE) + x_got[place].astype(WIDE)
             out[group, :, :cols] = total.astype(out.dtype)
-            if folded:
-                total = folded[0][place].astype(WIDE) + folded[1][place].astype(WIDE)
-                lines, fold = total.shape[0], total.shape[1] // 2
-                out[group, :lines, cols:] = total[:, :fold].astype(out.dtype)
-                out[group, lines:, cols:] = total[:, fold:].astype(out.dtype)
-
-
-def outer_parts(at, mine, got, digits, *folded):
+            total = y_got[place].astype(WIDE) + both_got[place].astype(WIDE)
+            out[group, :, cols:] = total.astype(out.dtype)
+
+
+def outer_parts(at, digits, *parts):
     size = digits[-3][1]
-    blocks, rows, cols = mine.shape
-    if folded:
-        cols += folded[0].shape[2] // 2
-    shape = (blocks // size, rows, cols)
+    blocks, rows, cols = parts[0].shape
+    shape = (blocks // size, rows, cols + parts[2].shape[2])
     outs = [wide_of(*shape)] + [low_of(*shape)] * (size - 1)
-    kept, *sent = call(functools.partial(parts_kernel, size), outs, at, mine, got, *folded)
+    kept, *sent = call(functools.partial(parts_kernel, size), outs, at, *parts)
     return kept, sent
 
 
@@ -392,14 +447,6 @@
     return call(
         near_kernel, [wide_of(blocks // 2, rows, cols), low_of(blocks // 2, rows, cols)], at, mine, got
     )
-
-
-def swap_near(value, digit):
-    stride, _ = digit
-    pairs = []
-    for at in range(lax.axis_size("dp")):
-        pairs.append((at, at + stride if (at // stride) % 2 == 0 else at - stride))
-    return lax.ppermute(value, "dp", pairs)
 
 
 def outer_send(sent, digits):
@@ -550,15 +597,15 @@
 
 
 def projection_gradient_kernel(
-    small_rows, at, layer_in, d_projected, proj_sums, sums_one, two0, two1, up_sums, wqkv, d_attn,
+    small_rows, lines, at, layer_in, d_projected, proj_sums, sums_one, two0, two1, up_sums, wqkv, d_attn,
     *refs,
 ):
-    grads, turn = refs[:-1], refs[-1]
-    part = up_sums.shape[1]
+    grads, (turn, rows) = refs[:-2], refs[-2:]
     cols = d_projected.shape[1]
+    part = cols // 3
     first = at[T] == 0
     turn[...] = jnp.zeros_like(turn)
-    (m0, m1), (v0, _), (g0, _), (u0, _) = small_rows
+    (m0, m1), (v0, _), (g0, _) = small_rows
     count = m1 - m0
     memory = nt(d_projected[:32, :], wqkv[:, :cols])[:count]
     memory = memory + jnp.where(first, d_attn[:count, :], 0.0)
@@ -570,16 +617,22 @@
         )
         for k in (0, 2)
     ]
-    for value, low in zip(sums + [up_sums[...]], (v0, v0 + 1, u0)):
-        high = low + value.shape[0]
-        turn[low:high, :part] = jnp.where(first, value, 0.0)
-        turn[low:high, part:] = jnp.where(first, 0.0, value)
+    for low, value in enumerate(sums, v0):
+        turn[low : low + 1, :part] = jnp.where(first, value, 0.0)
+        turn[low : low + 1, part:] = jnp.where(first, 0.0, value)
     sums_two = two0[...] + two1[...]
     turn[v0 + 2 : v0 + 4, :] = sums_one[0:2, :]
     turn[v0 + 4 : v0 + 6, :] = sums_two[0:2, :]
     turn[g0 : g0 + 1, :] = sums_one[2:3, :]
     turn[g0 + 1 : g0 + 2, :] = sums_two[2:3, :]
-    small = turn[...].T
+    rows[...] = turn[...].T
+    half = rows.shape[0] // 2
+    each = up_sums.shape[1] * lines // half
+    for n in range(half // lines):
+        value = up_sums[:, n * each : (n + 1) * each]
+        for side, low in ((0, n * lines), (1, half + n * lines)):
+            rows[low : low + 1, UP_AT : UP_AT + each] = jnp.where(at[T] == side, value, 0.0)
+    small = rows[...]
     put_gradient(layer_in, d_projected, grads, at[CORE])
     if len(grads) == 1:
         grads[0][:, cols:] = small.astype(LOW)
@@ -594,37 +647,30 @@
     d_sent[...] = nt(half_rows_of(d_projected, 1 - t, padded), wqkv[:, :cols]).astype(LOW)
 
 
-def halves_kernel(count, at, *refs):
-    parts, (mine, give, out) = refs[:count], refs[count:]
-    lines, cols = mine.shape
-    fold = out.shape[1] // 2
+def finish_kernel(
+    part, small_rows, count, at, *refs
+):
+    parts, (qkv, out, memory, vectors, gains, up, turn) = refs[:count], refs[count:]
     total = parts[0][...]
-    for part in parts[1:]:
-        total = total + part[...].astype(WIDE)
-    first = at[T] == 0
-    low, high = total[:lines, :cols], total[lines:, :cols]
-    mine[...] = jnp.where(first, low, high)
-    give[...] = jnp.where(first, high, low).astype(LOW)
-    out[:, :fold] = total[:lines, cols:]
-    out[:, fold:] = total[lines:, cols:]
-
-
-def finish_kernel(part, small_rows, at, mine, got, qkv, memory, vectors, gains, up, turn):
-    lines = mine.shape[0]
+    for value in parts[1:]:
+        total = total + value[...].astype(WIDE)
+    lines = total.shape[0]
     cols, width = 3 * part, 2 * part
+    mine, got = total[:, : cols + PAIR], total[:, cols + PAIR + width :]
     first = at[T] == 0
     for pair in range(part // PAIR):
         for kind in range(3):
             here = (3 * pair + kind) * PAIR
-            a = mine[:, here : here + PAIR]
-            b = got[:, here : here + PAIR].astype(WIDE)
+            a, b = mine[:, here : here + PAIR], got[:, here : here + PAIR]
             low = kind * width + pair * PAIR
             qkv[:, low : low + PAIR] = jnp.where(first, a, b)
             qkv[:, low + part : low + part + PAIR] = jnp.where(first, b, a)
+    out[...] = total[:, cols + PAIR : cols + PAIR + width]
     turn[...] = jnp.zeros_like(turn)
-    turn[:lines, :] = mine[:, cols : cols + PAIR] + got[:, cols : cols + PAIR].astype(WIDE)
+    turn[:lines, :] = mine[:, cols:] + got[:, cols:]
+    up[...] = turn[0:1, UP_AT : UP_AT + up.shape[1]]
     small = turn[...].T
-    for target, (low, high) in zip((memory, vectors, gains, up), small_rows):
+    for target, (low, high) in zip((memory, vectors, gains), small_rows):
         target[...] = small[low:high, :lines]
 
 
@@ -759,16 +805,11 @@
     hidden_mine = ffn_up.shape[1]
     feat = bias_vec.shape[1]
     lines = qkv_weight.shape[0]
-    spots = up_bias.shape[0] // feat
     doc_count = starts.shape[1]
-    counts = (mem_count, bias_vec.shape[0], gains.shape[0], spots)
+    counts = (mem_count, bias_vec.shape[0], gains.shape[0])
     edges = [sum(counts[:n]) for n in range(len(counts) + 1)]
     small_rows = tuple(zip(edges[:-1], edges[1:]))
     bias, gain = edges[1], edges[2]
-    target = np.arange(part)
-    target = (target // feat) * (spots * feat) + target % feat
-    target = np.stack([target, np.full(part, feat)], axis=1).astype(np.int32)
-
     integers = [
         lax.axis_index("tensor"),
         digit_at(x_digit),
@@ -780,35 +821,45 @@
     ]
     at = jnp.concatenate([jnp.stack(integers).astype(jnp.int32), starts[0]])
 
-    kept, sent = call(
-        functools.partial(columns_kernel, part, small_rows),
-        [low_of(lines, cols + PAIR)] * 2,
-        lax.axis_index("tensor").astype(jnp.int32).reshape(1),
-        qkv_weight, bias_vec, gains, mem_init, up_bias.reshape(spots, feat),
+    side = lax.axis_index("tensor").astype(jnp.int32).reshape(1)
+    (packed,) = call(
+        functools.partial(columns_kernel, small_rows),
+        [low_of(lines, 3 * width + PAIR + width)],
+        side, qkv_weight, bias_vec, gains, mem_init, up_bias.reshape(1, -1), out_weight,
         scratch=[pltpu.VMEM((PAIR, PAIR), WIDE)],
-        room=48 << 20,
-    )
-    first_cols = cols + PAIR + part
-    (first_pair,) = call(
-        pair_kernel, [low_of(2 * lines, first_cols)], at, kept, swap_tensor(sent), out_weight
-    )
-    rows_low = jnp.pad(rows_in[:, 0, :], ((0, padded - half_rows), (0, 0)))
-    rows_other = swap_tensor(tie(rows_low, first_pair))
-    first_z = spread_outer(first_pair, digits)
-    first_z, rows_other = join(first_z, rows_other)
-    first_x = rotate(first_z, x_digit, 1)
-    up_z = spread_outer(tie(ffn_up, first_z), digits)
-    down_in = tie(ffn_down.T, up_z)
-    first_z, first_x, up_z = join(first_z, first_x, up_z)
-    first_parts = swap_blocks(first_z, first_x, digits)
-    wqkv = assemble(at, first_parts, digits, cols + PAIR)
+        room=57 << 20,
+    )
+    rows_low = jnp.pad(tie(rows_in, packed)[:, 0, :], ((0, padded - half_rows), (0, 0)))
+    rows_other = swap_tensor(rows_low)
+    up_pair = spread_near(tie(ffn_up, packed), digits)
+    first_z = spread_outer(packed, digits)
+    first_z, rows_other, up_pair = join(first_z, rows_other, up_pair)
+    slots = first_z.shape[0]
+    mine, other = call(
+        functools.partial(halves_of_heads_kernel, part),
+        [low_of(slots, lines, cols + PAIR + width), low_of(slots, lines, cols + PAIR)],
+        at, first_z,
+    )
+    first_parts = [mine, swap_tensor(other), rotate(mine, x_digit, 1), swap_both(other, x_digit)]
+    up_z = spread_far(up_pair, digits)
+    down_pair = spread_near(tie(ffn_down.T, mine), digits)
+    *first_parts, up_z, down_pair = join(*first_parts, up_z, down_pair)
+    first_parts = [jnp.concatenate(first_parts[n : n + 2], axis=2) for n in (0, 2)]
+    core_parts = [rotate(value, core_digit, 1) for value in first_parts]
+    sizes = tuple(size for _, size in digits)
+    (wqkv,) = call(
+        functools.partial(assemble_first_kernel, sizes),
+        [low_of(dp_count, 2 * lines, cols + PAIR)],
+        at, *first_parts, *core_parts,
+    )
+    wqkv = wqkv.reshape(width, cols + PAIR)
     (out_sent,) = call(
-        functools.partial(unfold_kernel, cols + PAIR),
-        [low_of(dp_count // 2, lines, width)], at, first_z, first_x,
+        functools.partial(beside_kernel, cols + PAIR),
+        [low_of(dp_count // 2, lines, width)], at, *first_parts,
     )
     out_got = swap_tensor(out_sent)
     up_x = rotate(up_z, x_digit, 1)
-    down_z = spread_outer(down_in, digits)
+    down_z = spread_far(down_pair, digits)
 
     projected, mix_own, mix_sent, log_total, layer_in, small = call(
         functools.partial(forward_kernel, half_rows, mem_count, doc_count, bias),
@@ -818,7 +869,7 @@
             low_of(padded, part),
             wide_of(rows, PAIR),
             low_of(rows, width),
-            wide_of(edges[-1], width),
+            wide_of(ceil_to(edges[-1], 32), width),
         ],
         at, rows_low, rows_other, wqkv,
         scratch=[
@@ -830,11 +881,9 @@
     mix_got = swap_tensor(mix_sent)
     out_got = tie(out_got, mix_sent)
     (wout,) = call(
-        functools.partial(
-            assemble_out_kernel, tuple(size for _, size in digits), cols + PAIR
-        ),
+        functools.partial(assemble_out_kernel, sizes, cols + PAIR),
         [low_of(dp_count, 2 * lines, width)],
-        at, *first_parts, out_got, rotate(out_got, core_digit, 1),
+        at, *first_parts, *core_parts, out_got, rotate(out_got, core_digit, 1),
     )
     wout = wout.reshape(width, width)
     mixed, unit, scale, normed_own = call(
@@ -846,14 +895,14 @@
 
     normed_got = swap_tensor(normed_own)
     up_x, up_z, down_z = tie(up_x, mix_sent), tie(up_z, mix_sent), tie(down_z, mix_sent)
-    up = assemble(at, swap_blocks(up_z, up_x, digits), digits, hidden_mine)
+    up = assemble(at, swap_blocks(up_z, up_x, digits), digits, hidden_mine, paired=True)
     (up_b,) = call(
-        functools.partial(up_row_kernel, edges[3], spots),
-        [wide_of(ROWS, hidden_mine)], at, small, jnp.asarray(target),
+        functools.partial(up_row_kernel, lines), [wide_of(ROWS, hidden_mine)], at, wqkv,
+        scratch=[pltpu.VMEM((1, hidden_mine), WIDE)],
     )
     down_x = rotate(down_z, x_digit, 1)
     normed_got, down_x, up_b, up = join(normed_got, down_x, up_b, up)
-    down_t = assemble(at, swap_blocks(down_z, down_x, digits), digits, hidden_mine)
+    down_t = assemble(at, swap_blocks(down_z, down_x, digits), digits, hidden_mine, paired=True)
 
     def feed_forward(rows):
         pre_act = nn(rows, up).reshape(-1, *up_b.shape) + up_b
@@ -907,8 +956,8 @@
     down_kept, down_sent = halve(at, *swap_cores(down_grads, dp_count, core_digit))
     down_got = rotate(down_sent, x_digit, 1)
     up_sums, *up_grads = call(
-        functools.partial(rest_sums_kernel, spots), [wide_of(spots, part)] + outs, at,
-        up_own, sums_own, normed_got, tie(d_pre_got, down_sent), jnp.asarray(target),
+        rest_sums_kernel, [wide_of(1, hidden_mine)] + outs,
+        at, up_own, sums_own, normed_got, tie(d_pre_got, down_sent),
     )
     up_kept, up_sent = halve(at, *swap_cores(up_grads, dp_count, core_digit))
 
@@ -952,35 +1001,34 @@
     )
     up_kept, up_sent = far_parts(at, up_kept, up_got, digits)
     qkv_grads = call(
-        functools.partial(projection_gradient_kernel, small_rows),
+        functools.partial(projection_gradient_kernel, small_rows, lines),
         gradient_outs(width, cols + PAIR, dp_count),
         at, layer_in, d_projected, proj_sums, sums_one, *sums_two, up_sums, wqkv, d_attn_in,
-        scratch=[pltpu.VMEM((PAIR, width), WIDE)],
+        scratch=[pltpu.VMEM((PAIR, width), WIDE), pltpu.VMEM((width, PAIR), WIDE)],
     )
     out_got, down_got, *qkv_grads = join(out_got, down_got, *qkv_grads)
     down_kept, down_sent = near_parts(at, down_kept, down_got)
-    out_kept, out_sent = halve(at, out_kept, [out_got])
-    out_got = rotate(out_sent, x_digit, 1)
     qkv_kept, qkv_parts = swap_cores(qkv_grads, dp_count, core_digit)
     up_sent, *qkv_parts = join(up_sent, *qkv_parts)
-    qkv_kept, qkv_sent = halve(at, qkv_kept, qkv_parts)
-
-    qkv_got = rotate(qkv_sent, x_digit, 1)
+    slots = dp_count // 4
+    mine, to_x, to_y, to_both = call(
+        quarter_kernel,
+        [low_of(slots, lines, cols + PAIR + width)] * 2 + [low_of(slots, lines, cols + PAIR)] * 2,
+        at, qkv_kept, *qkv_parts, out_kept, out_got,
+    )
+
+    both_got = [rotate(to_x, x_digit, 1), swap_tensor(to_y), swap_both(to_both, x_digit)]
     up_got = rotate(up_sent, digits[-3], 2)
     down_got = swap_near(down_sent, digits[-3])
     d_in_own, d_in_sent = call(
         projection_back_kernel, [wide_of(padded, width), low_of(padded, width)],
-        at, tie(d_projected, qkv_sent), wqkv, d_attn_in,
+        at, tie(d_projected, to_x), wqkv, d_attn_in,
     )
     up_kept, up_sent = near_parts(at, up_kept, up_got)
-    qkv_got, d_in_sent, out_got, up_sent, down_got = join(
-        qkv_got, d_in_sent, out_got, up_sent, down_got
-    )
+    *both_got, d_in_sent, up_sent, down_got = join(*both_got, d_in_sent, up_sent, down_got)
     up_got = swap_near(up_sent, digits[-3])
     d_in_got = swap_tensor(d_in_sent)
-    both_kept, both_sent = outer_parts(
-        at, qkv_kept, qkv_got, digits, out_kept, out_got
-    )
+    both_kept, both_sent = outer_parts(at, digits, mine, *both_got)
     both_got = outer_send(both_sent, digits)
     grad_ffn_down = outer_sum(down_kept, [down_got], digits)
     grad_ffn_up = outer_sum(up_kept, [up_got], digits)
@@ -993,15 +1041,12 @@
         parts = [both_kept[0], *[part[0] for part in both_got]]
     else:
         parts = [outer_sum(both_kept, both_got, digits)]
-    mine, give, grad_out_weight = call(
-        functools.partial(halves_kernel, len(parts)),
-        [wide_of(lines, cols + PAIR), low_of(lines, cols + PAIR), wide_of(lines, width)],
+    grad_qkv, grad_out_weight, grad_mem, grad_vec, grad_gains, grad_up_bias = call(
+        functools.partial(finish_kernel, part, small_rows, len(parts)),
+        [wide_of(lines, 3 * width), wide_of(lines, width)]
+        + [wide_of(n, feat) for n in counts]
+        + [wide_of(1, up_bias.shape[0])],
         at, *parts,
-    )
-    grad_qkv, grad_mem, grad_vec, grad_gains, grad_up_bias = call(
-        functools.partial(finish_kernel, part, small_rows),
-        [wide_of(lines, 3 * width)] + [wide_of(n, feat) for n in counts],
-        at, mine, swap_tensor(give),
         scratch=[pltpu.VMEM((PAIR, PAIR), WIDE)],
     )
     return (

time: 193 us -> 184 us (0.953)
  local copies, waits for them, and re-layouts: 8.79 us -> 3.88 us
  starting transfers between devices: 52.6 us -> 49.4 us
    ppermute x44 -> x39, starting transfers between devices: 33.5 us -> 24.2 us  [rotate(): return lax.ppermute(value, 'dp', pairs)]
    ppermute x14, waiting for transfers between devices: 21.6 us -> 14.4 us  [swap_tensor(): return lax.ppermute(value, 'tensor', [(0, 1), (1, 0)])]
    unnamed x20 -> x8, local copies, waits for them, and re-layouts: 5.45 us -> 1.81 us
    ppermute x2 -> x4, starting transfers between devices: 2.88 us -> 5.97 us  [swap_near(): return lax.ppermute(value, 'dp', pairs)]
    ppermute x0 -> x2, waiting for transfers between devices: none -> 2.76 us  [swap_both(): return lax.ppermute(value, ('dp', 'tensor'), pairs)]
    ppermute x2 -> x4, waiting for transfers between devices: 0.01 us -> 2.74 us  [swap_near(): return lax.ppermute(value, 'dp', pairs)]
    ppermute x14, starting transfers between devices: 16.2 us -> 18.4 us  [swap_tensor(): return lax.ppermute(value, 'tensor', [(0, 1), (1, 0)])]
    pallas_call x33 -> x31, Pallas kernels: 53.7 us -> 51.9 us  [call(): pl.pallas_call(kernel, in_specs=[pl.BlockSpec(memory_space=pltpu.SMEM)] +...]
  transfers between devices with their start and end apart: 60 -> 59, of which waited for: 24 -> 24; matrix products, arithmetic and copies ran while one was open for 5% -> 5% of each run, Pallas kernels for 26% -> 25%
where the time goes in v3:
time: 184 us
  waiting for transfers between devices  64.5 us (35%)
  Pallas kernels  51.9 us (28%)
  starting transfers between devices  49.4 us (27%)
  matrix products  7.14 us (4%)
  other arithmetic  4.38 us (2%)
  local copies, waits for them, and re-layouts  3.88 us (2%)
  between operations  2.53 us (1%)
    pallas_call x31, Pallas kernels, call(): pl.pallas_call(kernel, in_specs=[pl.BlockSpec(memory_space=pltpu.SMEM)] +...  51.9 us
    ppermute x39, waiting for transfers between devices, rotate(): return lax.ppermute(value, 'dp', pairs)  44.6 us
    ppermute x39, starting transfers between devices, rotate(): return lax.ppermute(value, 'dp', pairs)  24.2 us
    ppermute x14, starting transfers between devices, swap_tensor(): return lax.ppermute(value, 'tensor', [(0, 1), (1, 0)])  18.4 us
    ppermute x14, waiting for transfers between devices, swap_tensor(): return lax.ppermute(value, 'tensor', [(0, 1), (1, 0)])  14.4 us
    ppermute x4, starting transfers between devices, swap_near(): return lax.ppermute(value, 'dp', pairs)  5.97 us
    dot_general x4, matrix products, nn(): lax.dot_general(a, b, (((1,), (0,)), ((), ())), preferred_element_type=WIDE)  3.8 us
  transfers between devices with their start and end apart: 59, of which 24 were waited for; matrix products, arithmetic and copies ran while one was open for 5% of the time, Pallas kernels for 25%

profile of v3, /device:TPU:0, one launch (start us, length us, event | category | flops | bytes accessed | tf_op | source)
XLA Modules:
  0.0 183.8 jit_solution(344914168304466046)
XLA Ops:
  0.6 1.7 shard_map.204
  2.3 3.0 %collective-permute-start.4 = (bf16[48,1536]{1,0:T(8,128)(2,1)}, bf16[48,1536]{1,0:T(8,128)(2,1)S(1)}, u32[]{:S(2)}, u32[]{:S(2)}) collective-permute-start(bf16[48,1536]{1,0:T(8,128)(2,1)} %param.23), channel_id=1, source_target_pairs={{0,8},{2,10},{4,12},{6,14},{8,0},{10,2},{12,4},{14,6},{16,24},{18,... | collective-permute-start | bytes 442376 | tf_op jit(solution)/shard_map/ppermute | solution.py:136
  5.4 2.6 %collective-permute-start.1 = (bf16[24,3200]{1,0:T(8,128)(2,1)}, bf16[24,3200]{1,0:T(8,128)(2,1)S(1)}, u32[]{:S(2)}, u32[]{:S(2)}) collective-permute-start(bf16[24,3200]{1,0:T(8,128)(2,1)} %shard_map.204), channel_id=1, source_target_pairs={{0,16},{2,18},{4,20},{6,22},{8,24},{10,26},{12,28},{14,30},{16,0},... | collective-permute-start | bytes 460808 | tf_op jit(solution)/shard_map/ppermute | solution.py:101
  8.0 2.0 %collective-permute-start = (bf16[24,3200]{1,0:T(8,128)(2,1)}, bf16[24,3200]{1,0:T(8,128)(2,1)S(1)}, u32[]{:S(2)}, u32[]{:S(2)}) collective-permute-start(bf16[24,3200]{1,0:T(8,128)(2,1)} %shard_map.204), channel_id=1, source_target_pairs={{0,8},{2,10},{4,12},{6,14},{8,16},{10,18},{12,20},{14,22},{16,24},... | collective-permute-start | bytes 460808 | tf_op jit(solution)/shard_map/ppermute | solution.py:101
  10.0 1.1 pad.4.own
  11.1 1.6 collective-permute-start.3
  14.7 0.9 pad_maximum_fusion.4
  15.6 1.0 collective-permute-done.1
  16.7 5.0 %collective-permute-done = bf16[24,3200]{1,0:T(8,128)(2,1)S(1)} collective-permute-done((bf16[24,3200]{1,0:T(8,128)(2,1)}, bf16[24,3200]{1,0:T(8,128)(2,1)S(1)}, u32[]{:S(2)}, u32[]{:S(2)}) %collective-permute-start) | collective-permute-done | bytes 153632 | tf_op jit(solution)/shard_map/ppermute | solution.py:101
  21.6 1.0 pad_maximum_fusion.packed
  24.1 1.2 collective-permute-start.8
  25.4 1.5 collective-permute-start.6
  26.9 1.5 collective-permute-start.5
  28.9 2.5 %collective-permute-done.9 = bf16[48,1536]{1,0:T(8,128)(2,1)S(1)} collective-permute-done((bf16[48,1536]{1,0:T(8,128)(2,1)S(1)}, bf16[48,1536]{1,0:T(8,128)(2,1)S(1)}, u32[]{:S(2)}, u32[]{:S(2)}) %collective-permute-start.9) | collective-permute-done | bytes 147488 | tf_op jit(solution)/shard_map/ppermute | solution.py:136
  31.4 7.1 %collective-permute-done.8 = bf16[2,48,1536]{2,1,0:T(8,128)(2,1)S(1)} collective-permute-done((bf16[2,48,1536]{2,1,0:T(8,128)(2,1)S(1)}, bf16[2,48,1536]{2,1,0:T(8,128)(2,1)S(1)}, u32[]{:S(2)}, u32[]{:S(2)}) %collective-permute-start.8) | collective-permute-done | bytes 294944 | tf_op jit(solution)/shard_map/ppermute | solution.py:101
  38.6 2.5 %collective-permute-done.7 = bf16[4,24,1280]{2,1,0:T(8,128)(2,1)S(1)} collective-permute-done((bf16[4,24,1280]{2,1,0:T(8,128)(2,1)S(1)}, bf16[4,24,1280]{2,1,0:T(8,128)(2,1)S(1)}, u32[]{:S(2)}, u32[]{:S(2)}) %collective-permute-start.7) | collective-permute-done | bytes 245792 | tf_op jit(solution)/shard_map/ppermute | solution.py:114
  41.9 1.5 collective-permute-start.18
  44.5 1.1 collective-permute-start.16
  46.4 7.8 %shard_map.207 = (bf16[544,1152]{1,0:T(8,128)(2,1)S(1)}, bf16[272,384]{1,0:T(8,128)(2,1)S(1)}, bf16[272,384]{1,0:T(8,128)(2,1)S(1)}, f32[544,128]{1,0:T(8,128)S(...) custom-call(s32[15]{0:T(128)S(1)} %concatenate.24.at, bf16[272,768]{1,0:T(8,128)(2,1)S(1)} %pad.4.own, ...), custom_call_target="tpu_custom_call" | custom-call | flops 1 | bytes 1 | tf_op jit(solution)/shard_map/pallas_call | solution.py:61
  54.2 1.6 collective-permute-start.12
  55.8 4.4 %collective-permute-done.16 = bf16[2,48,1536]{2,1,0:T(8,128)(2,1)S(1)} collective-permute-done((bf16[2,48,1536]{2,1,0:T(8,128)(2,1)S(1)}, bf16[2,48,1536]{2,1,0:T(8,128)(2,1)S(1)}, u32[]{:S(2)}, u32[]{:S(2)}) %collective-permute-start.16) | collective-permute-done | bytes 294944 | tf_op jit(solution)/shard_map/ppermute | solution.py:101
  62.0 1.3 shard_map.210
  63.3 1.6 collective-permute-start.15
  66.3 9.8 %collective-permute-done.17.refs_1_ = bf16[4,48,1536]{2,1,0:T(8,128)(2,1)S(1)} collective-permute-done((bf16[4,48,1536]{2,1,0:T(8,128)(2,1)S(1)}, bf16[4,48,1536]{2,1,0:T(8,128)(2,1)S(1)}, u32[]{:S(2)}, u32[]{:S(2)}) %collective-permute-start.17) | collective-permute-done | bytes 589856 | tf_op jit(solution)/shard_map/ppermute | solution.py:101
  76.3 0.9 multiply_convert_fusion.1
  77.3 0.9 collective-permute-done.22.refs_3_
  78.8 0.8 convolution_convert_fusion.1
  79.7 0.9 multiply_convert_fusion
  80.6 1.6 collective-permute-start.23
  83.6 5.4 %collective-permute-done.23.got = bf16[144,768]{1,0:T(8,128)(2,1)S(1)} collective-permute-done((bf16[144,768]{1,0:T(8,128)(2,1)S(1)}, bf16[144,768]{1,0:T(8,128)(2,1)S(1)}, u32[]{:S(2)}, u32[]{:S(2)}) %collective-permute-start.23) | collective-permute-done | bytes 221216 | tf_op jit(solution)/shard_map/ppermute | solution.py:105
  89.0 1.0 shard_map.214
  90.1 1.6 collective-permute-start.26
  92.4 1.0 shard_map.215
  93.4 1.0 fusion.b_up
  94.4 1.6 collective-permute-start.27
  96.0 3.7 %shard_map.216 = (f32[768,1536]{1,0:T(8,128)S(1)}, f32[768,1536]{1,0:T(8,128)S(1)}, f32[1,1536]{1,0:T(1,128)S(1)}) custom-call(s32[15]{0:T(128)S(1)} %concatenate.24.at, bf16[272,768]{1,0:T(8,128)(2,1)S(1)} %constant_dynamic-update-slice_fusion.4.a_down, bf16[272,1536]{1,0:T(8,128)(2,1)S(1)} %get-tuple-element.292.b_down, ...), custom_call_target="tpu_custom_call" | custom-call | flops 1 | bytes 1 | tf_op jit(solution)/shard_map/pallas_call | solution.py:61
  100.5 1.7 collective-permute-done.27
  102.3 1.0 fusion.1.b
  103.3 0.8 convolution_convert_fusion
  104.1 1.6 collective-permute-start.28
  105.7 2.4 %shard_map.220 = (bf16[8,48,1536]{2,1,0:T(8,128)(2,1)S(1)}, bf16[8,48,384]{2,1,0:T(8,128)(2,1)S(1)}, bf16[8,48,384]{2,1,0:T(8,128)(2,1)S(1)}, bf16[8,48,384]{2,1,0:T(8,128)(2,1)S(1)}, bf16[8,48,384]{2,1,0:T(8,128)(2,1)S(1)}) custom-call(s32[15]{0:T(128)S(1)} %concatenate.24.at, f32[768,1536]{1,0:T(8,128)S(1)} %get-tuple-element.198.own, ...), custom_call_target="tpu_custom_call" | custom-call | flops 1 | bytes 1 | tf_op jit(solution)/shard_map/pallas_call | solution.py:61
  111.1 0.8 shard_map.221
  112.5 2.4 %shard_map.222 = (f32[1,1536]{1,0:T(1,128)S(1)}, bf16[8,48,1536]{2,1,0:T(8,128)(2,1)S(1)}, bf16[8,48,384]{2,1,0:T(8,128)(2,1)S(1)}, bf16[8,48,384]{2,1,0:T(8,128...) custom-call(s32[15]{0:T(128)S(1)} %concatenate.24.at, ...), custom_call_target="tpu_custom_call" | custom-call | flops 1 | bytes 1 | tf_op jit(solution)/shard_map/pallas_call | solution.py:61
  116.0 1.6 shard_map.217
  117.6 1.0 collective-permute-start.29
  118.7 1.4 shard_map.218
  120.9 0.8 shard_map.223
  122.9 4.5 %collective-permute-done.41.got = bf16[4,48,1536]{2,1,0:T(8,128)(2,1)S(1)} collective-permute-done((bf16[4,48,1536]{2,1,0:T(8,128)(2,1)S(1)}, bf16[4,48,1536]{2,1,0:T(8,128)(2,1)S(1)}, u32[]{:S(2)}, u32[]{:S(2)}) %collective-permute-start.41) | collective-permute-done | bytes 589856 | tf_op jit(solution)/shard_map/ppermute | solution.py:101
  129.1 9.6 %shard_map.225 = (bf16[544,1152]{1,0:T(8,128)(2,1)S(1)}, f32[1,1152]{1,0:T(1,128)S(1)}) custom-call(s32[15]{0:T(128)S(1)} %concatenate.24.at, bf16[544,1152]{1,0:T(8,128)(2,1)S(1)} %get-tuple-element.177.qkv, bf16[272,384]{1,0:T(8,128)(2,1)S(1)} %get-tuple-element.186.own, bf16[272,384]{1,0:T(8,128)(2,1)S(1)} %collective-permute-done.29.got, ...), custom_call_target="tpu_custom_call" | custom-call | flops 1 | bytes 1 | tf_op jit(solution)/shard_map/pallas_call | solution.py:61
  138.8 3.0 %shard_map.226 = (bf16[8,48,1280]{2,1,0:T(8,128)(2,1)S(1)}, bf16[8,48,384]{2,1,0:T(8,128)(2,1)S(1)}, bf16[8,48,384]{2,1,0:T(8,128)(2,1)S(1)}, bf16[8,48,384]{2,1,0:T(8,128)(2,1)S(1)}, bf16[8,48,128]{2,1,0:T(8,128)(2,1)S(1)}) custom-call(s32[15]{0:T(128)S(1)} %concatenate.24.at, bf16[544,768]{1,0:T(8,128)(2,1)S(1)} %get-tuple-element.160.layer_in, ...), custom_call_target="tpu_custom_call" | custom-call | flops 1 | bytes 1 | tf_op jit(solution)/shard_map/pallas_call | solution.py:61
  141.8 1.4 collective-permute-done.43.got
  144.9 0.9 collective-permute-done.48.refs_3_
  145.7 0.9 shard_map.228
  147.3 2.6 %collective-permute-start.52 = (bf16[2,48,1536]{2,1,0:T(8,128)(2,1)S(1)}, bf16[2,48,1536]{2,1,0:T(8,128)(2,1)S(1)}, u32[]{:S(2)}, u32[]{:S(2)}) collective-permute-start(bf16[2,48,1536]{2,1,0:T(8,128)(2,1)S(1)} %get-tuple-element.252), channel_id=1, source_target_pairs={{0,16},{2,18},{4,20},{6,22},{8,24},{10,26},{12,28},{14,30},{16,0},... | collective-permute-start | bytes 884744 | tf_op jit(solution)/shard_map/ppermute | solution.py:101
  149.9 1.5 collective-permute-start.50
  154.0 1.8 shard_map.229
  155.9 7.4 %collective-permute-done.52.got = bf16[2,48,1536]{2,1,0:T(8,128)(2,1)S(1)} collective-permute-done((bf16[2,48,1536]{2,1,0:T(8,128)(2,1)S(1)}, bf16[2,48,1536]{2,1,0:T(8,128)(2,1)S(1)}, u32[]{:S(2)}, u32[]{:S(2)}) %collective-permute-start.52) | collective-permute-done | bytes 294944 | tf_op jit(solution)/shard_map/ppermute | solution.py:101
  164.1 1.3 collective-permute-start.58
  166.9 1.6 collective-permute-start.56
  168.5 1.6 collective-permute-start.57
  170.2 1.5 collective-permute-start.54
  173.4 6.6 %collective-permute-done.54.got = bf16[272,768]{1,0:T(8,128)(2,1)S(1)} collective-permute-done((bf16[272,768]{1,0:T(8,128)(2,1)S(1)}, bf16[272,768]{1,0:T(8,128)(2,1)S(1)}, u32[]{:S(2)}, u32[]{:S(2)}) %collective-permute-start.54) | collective-permute-done | bytes 417824 | tf_op jit(solution)/shard_map/ppermute | solution.py:105
  180.7 1.7 copy.23
  182.4 1.3 shard_map.234
  (119 shorter events, 30.3 us)
Async XLA Ops:
  2.3 12.3 %collective-permute-start.4 = (bf16[48,1536]{1,0:T(8,128)(2,1)}, bf16[48,1536]{1,0:T(8,128)(2,1)S(1)}, u32[]{:S(2)}, u32[]{:S(2)}) collective-permute-start(bf16[48,1536]{1,0:T(8,128)(2,1)} %param.23), channel_id=1, source_target_pairs={{0,8},{2,10},{4,12},{6,14},{8,0},{10,2},{12,4},{14,6},{16,24},{18,... | collective-permute-start | bytes 442376 | tf_op jit(solution)/shard_map/ppermute | solution.py:136
  5.4 11.3 %collective-permute-start.1 = (bf16[24,3200]{1,0:T(8,128)(2,1)}, bf16[24,3200]{1,0:T(8,128)(2,1)S(1)}, u32[]{:S(2)}, u32[]{:S(2)}) collective-permute-start(bf16[24,3200]{1,0:T(8,128)(2,1)} %shard_map.204), channel_id=1, source_target_pairs={{0,16},{2,18},{4,20},{6,22},{8,24},{10,26},{12,28},{14,30},{16,0},... | collective-permute-start | bytes 460808 | tf_op jit(solution)/shard_map/ppermute | solution.py:101
  8.0 8.7 %collective-permute-start.2 = (bf16[24,3200]{1,0:T(8,128)(2,1)}, bf16[24,3200]{1,0:T(8,128)(2,1)S(1)}, u32[]{:S(2)}, u32[]{:S(2)}) collective-permute-start(bf16[24,3200]{1,0:T(8,128)(2,1)} %shard_map.204), channel_id=1, source_target_pairs={{0,24},{2,26},{4,28},{6,30},{8,0},{10,2},{12,4},{14,6},{16,8},{18,... | collective-permute-start | bytes 460808 | tf_op jit(solution)/shard_map/ppermute | solution.py:101
  8.0 13.7 %collective-permute-start = (bf16[24,3200]{1,0:T(8,128)(2,1)}, bf16[24,3200]{1,0:T(8,128)(2,1)S(1)}, u32[]{:S(2)}, u32[]{:S(2)}) collective-permute-start(bf16[24,3200]{1,0:T(8,128)(2,1)} %shard_map.204), channel_id=1, source_target_pairs={{0,8},{2,10},{4,12},{6,14},{8,16},{10,18},{12,20},{14,22},{16,24},... | collective-permute-start | bytes 460808 | tf_op jit(solution)/shard_map/ppermute | solution.py:101
  10.0 13.3 %copy-start.1 = (bf16[1536,48]{0,1:T(8,128)(2,1)S(1)}, bf16[1536,48]{0,1:T(8,128)(2,1)}, u32[]{:S(2)}) copy-start(bf16[1536,48]{0,1:T(8,128)(2,1)} %param.25) | copy-start | bytes 442372
  11.1 11.6 %collective-permute-start.3 = (bf16[272,768]{1,0:T(8,128)(2,1)S(1)}, bf16[272,768]{1,0:T(8,128)(2,1)S(1)}, u32[]{:S(2)}, u32[]{:S(2)}) collective-permute-start(bf16[272,768]{1,0:T(8,128)(2,1)S(1)} %pad.4.own), channel_id=1, source_target_pairs={{0,1},{1,0},{2,3},{3,2},{4,5},{5,4},{6,7},{7,6},{8,9},{9,8},{10,11... | collective-permute-start | bytes 1253384 | tf_op jit(solution)/shard_map/ppermute | solution.py:105
  23.3 8.1 %collective-permute-start.9 = (bf16[48,1536]{1,0:T(8,128)(2,1)S(1)}, bf16[48,1536]{1,0:T(8,128)(2,1)S(1)}, u32[]{:S(2)}, u32[]{:S(2)}) collective-permute-start(bf16[48,1536]{1,0:T(8,128)(2,1)S(1)} %bitcast.82), channel_id=1, source_target_pairs={{0,8},{2,10},{4,12},{6,14},{8,0},{10,2},{12,4},{14,6},{16,24},{18,... | collective-permute-start | bytes 442376 | tf_op jit(solution)/shard_map/ppermute | solution.py:136
  24.1 14.4 %collective-permute-start.8 = (bf16[2,48,1536]{2,1,0:T(8,128)(2,1)S(1)}, bf16[2,48,1536]{2,1,0:T(8,128)(2,1)S(1)}, u32[]{:S(2)}, u32[]{:S(2)}) collective-permute-start(bf16[2,48,1536]{2,1,0:T(8,128)(2,1)S(1)} %pad_maximum_fusion.4), channel_id=1, source_target_pairs={{0,16},{2,18},{4,20},{6,22},{8,24},{10,26},{12,28},{14,30},{16,0},... | collective-permute-start | bytes 884744 | tf_op jit(solution)/shard_map/ppermute | solution.py:101
  25.4 15.8 %collective-permute-start.6 = (bf16[4,24,2048]{2,1,0:T(8,128)(2,1)S(1)}, bf16[4,24,2048]{2,1,0:T(8,128)(2,1)S(1)}, u32[]{:S(2)}, u32[]{:S(2)}) collective-permute-start(bf16[4,24,2048]{2,1,0:T(8,128)(2,1)S(1)} %get-tuple-element.153), channel_id=1, source_target_pairs={{0,4},{2,6},{4,0},{6,2},{8,12},{10,14},{12,8},{14,10},{16,20},{18,... | collective-permute-start | bytes 1179656 | tf_op jit(solution)/shard_map/ppermute | solution.py:101
  26.9 11.7 %collective-permute-start.5 = (bf16[4,24,1280]{2,1,0:T(8,128)(2,1)S(1)}, bf16[4,24,1280]{2,1,0:T(8,128)(2,1)S(1)}, u32[]{:S(2)}, u32[]{:S(2)}) collective-permute-start(bf16[4,24,1280]{2,1,0:T(8,128)(2,1)S(1)} %get-tuple-element.150), channel_id=1, source_target_pairs={{0,1},{1,0},{2,3},{3,2},{4,5},{5,4},{6,7},{7,6},{8,9},{9,8},{10,11... | collective-permute-start | bytes 737288 | tf_op jit(solution)/shard_map/ppermute | solution.py:105
  28.4 12.7 %collective-permute-start.7 = (bf16[4,24,1280]{2,1,0:T(8,128)(2,1)S(1)}, bf16[4,24,1280]{2,1,0:T(8,128)(2,1)S(1)}, u32[]{:S(2)}, u32[]{:S(2)}) collective-permute-start(bf16[4,24,1280]{2,1,0:T(8,128)(2,1)S(1)} %get-tuple-element.150), channel_id=1, source_target_pairs={{0,5},{1,4},{2,7},{3,6},{4,1},{5,0},{6,3},{7,2},{8,13},{9,12},{10,... | collective-permute-start | bytes 737288 | tf_op jit(solution)/shard_map/ppermute | solution.py:114
  41.2 4.5 %collective-permute-start.11 = (bf16[4,24,3328]{2,1,0:T(8,128)(2,1)S(1)}, bf16[4,24,3328]{2,1,0:T(8,128)(2,1)S(1)}, u32[]{:S(2)}, u32[]{:S(2)}) collective-permute-start(bf16[4,24,3328]{2,1,0:T(8,128)(2,1)S(1)} %constant_dynamic-update-slice_fusion.2.refs_1_.x_got), channel_id=1, source_target_pairs={{0,2},{2,0},{4,6},{6,4},{8,10},{10,8},{12,14},{14,12},{16,18},{18,... | collective-permute-start | bytes 1916936 | tf_op jit(solution)/shard_map/ppermute | solution.py:101
  41.3 4.3 %collective-permute-start.10 = (bf16[4,24,3328]{2,1,0:T(8,128)(2,1)S(1)}, bf16[4,24,3328]{2,1,0:T(8,128)(2,1)S(1)}, u32[]{:S(2)}, u32[]{:S(2)}) collective-permute-start(bf16[4,24,3328]{2,1,0:T(8,128)(2,1)S(1)} %constant_dynamic-update-slice_fusion.refs_0_.mine), channel_id=1, source_target_pairs={{0,2},{2,0},{4,6},{6,4},{8,10},{10,8},{12,14},{14,12},{16,18},{18,... | collective-permute-start | bytes 1916936 | tf_op jit(solution)/shard_map/ppermute | solution.py:101
  41.9 18.3 %collective-permute-start.18 = (bf16[4,48,1536]{2,1,0:T(8,128)(2,1)S(1)}, bf16[4,48,1536]{2,1,0:T(8,128)(2,1)S(1)}, u32[]{:S(2)}, u32[]{:S(2)}) collective-permute-start(bf16[4,48,1536]{2,1,0:T(8,128)(2,1)S(1)} %pad_maximum_fusion.1.refs_0_), channel_id=1, source_target_pairs={{0,4},{2,6},{4,0},{6,2},{8,12},{10,14},{12,8},{14,10},{16,20},{18,... | collective-permute-start | bytes 1769480 | tf_op jit(solution)/shard_map/ppermute | solution.py:101
  43.9 11.8 %collective-permute-start.13 = (bf16[8,24,768]{2,1,0:T(8,128)(2,1)S(1)}, bf16[8,24,768]{2,1,0:T(8,128)(2,1)S(1)}, u32[]{:S(2)}, u32[]{:S(2)}) collective-permute-start(bf16[8,24,768]{2,1,0:T(8,128)(2,1)S(1)} %shard_map.208), channel_id=1, source_target_pairs={{0,1},{1,0},{2,3},{3,2},{4,5},{5,4},{6,7},{7,6},{8,9},{9,8},{10,11... | collective-permute-start | bytes 884744 | tf_op jit(solution)/shard_map/ppermute | solution.py:105
  44.5 15.7 %collective-permute-start.16 = (bf16[2,48,1536]{2,1,0:T(8,128)(2,1)S(1)}, bf16[2,48,1536]{2,1,0:T(8,128)(2,1)S(1)}, u32[]{:S(2)}, u32[]{:S(2)}) collective-permute-start(bf16[2,48,1536]{2,1,0:T(8,128)(2,1)S(1)} %pad_maximum_fusion.5), channel_id=1, source_target_pairs={{0,16},{2,18},{4,20},{6,22},{8,24},{10,26},{12,28},{14,30},{16,0},... | collective-permute-start | bytes 884744 | tf_op jit(solution)/shard_map/ppermute | solution.py:101
  54.2 7.8 %collective-permute-start.12 = (bf16[272,384]{1,0:T(8,128)(2,1)S(1)}, bf16[272,384]{1,0:T(8,128)(2,1)S(1)}, u32[]{:S(2)}, u32[]{:S(2)}) collective-permute-start(bf16[272,384]{1,0:T(8,128)(2,1)S(1)} %get-tuple-element.158), channel_id=1, source_target_pairs={{0,1},{1,0},{2,3},{3,2},{4,5},{5,4},{6,7},{7,6},{8,9},{9,8},{10,11... | collective-permute-start | bytes 626696 | tf_op jit(solution)/shard_map/ppermute | solution.py:105
  55.8 5.6 %collective-permute-start.14 = (bf16[8,24,768]{2,1,0:T(8,128)(2,1)S(1)}, bf16[8,24,768]{2,1,0:T(8,128)(2,1)S(1)}, u32[]{:S(2)}, u32[]{:S(2)}) collective-permute-start(bf16[8,24,768]{2,1,0:T(8,128)(2,1)S(1)} %collective-permute-done.13.refs_4_), channel_id=1, source_target_pairs={{0,2},{2,0},{4,6},{6,4},{8,10},{10,8},{12,14},{14,12},{16,18},{18,... | collective-permute-start | bytes 884744 | tf_op jit(solution)/shard_map/ppermute | solution.py:101
  60.2 5.4 %collective-permute-start.20 = (bf16[4,48,1536]{2,1,0:T(8,128)(2,1)S(1)}, bf16[4,48,1536]{2,1,0:T(8,128)(2,1)S(1)}, u32[]{:S(2)}, u32[]{:S(2)}) collective-permute-start(bf16[4,48,1536]{2,1,0:T(8,128)(2,1)S(1)} %collective-permute-done.18.refs_1_), channel_id=1, source_target_pairs={{0,2},{2,0},{4,6},{6,4},{8,10},{10,8},{12,14},{14,12},{16,18},{18,... | collective-permute-start | bytes 1769480 | tf_op jit(solution)/shard_map/ppermute | solution.py:101
  60.3 5.3 %collective-permute-start.19 = (bf16[4,48,1536]{2,1,0:T(8,128)(2,1)S(1)}, bf16[4,48,1536]{2,1,0:T(8,128)(2,1)S(1)}, u32[]{:S(2)}, u32[]{:S(2)}) collective-permute-start(bf16[4,48,1536]{2,1,0:T(8,128)(2,1)S(1)} %pad_maximum_fusion.1.refs_0_), channel_id=1, source_target_pairs={{0,2},{2,0},{4,6},{6,4},{8,10},{10,8},{12,14},{14,12},{16,18},{18,... | collective-permute-start | bytes 1769480 | tf_op jit(solution)/shard_map/ppermute | solution.py:101
  60.8 15.3 %collective-permute-start.17 = (bf16[4,48,1536]{2,1,0:T(8,128)(2,1)S(1)}, bf16[4,48,1536]{2,1,0:T(8,128)(2,1)S(1)}, u32[]{:S(2)}, u32[]{:S(2)}) collective-permute-start(bf16[4,48,1536]{2,1,0:T(8,128)(2,1)S(1)} %pad_maximum_fusion.2.refs_0_), channel_id=1, source_target_pairs={{0,4},{2,6},{4,0},{6,2},{8,12},{10,14},{12,8},{14,10},{16,20},{18,... | collective-permute-start | bytes 1769480 | tf_op jit(solution)/shard_map/ppermute | solution.py:101
  63.3 12.8 %collective-permute-start.15 = (bf16[272,768]{1,0:T(8,128)(2,1)S(1)}, bf16[272,768]{1,0:T(8,128)(2,1)S(1)}, u32[]{:S(2)}, u32[]{:S(2)}) collective-permute-start(bf16[272,768]{1,0:T(8,128)(2,1)S(1)} %get-tuple-element.173.a_up), channel_id=1, source_target_pairs={{0,1},{1,0},{2,3},{3,2},{4,5},{5,4},{6,7},{7,6},{8,9},{9,8},{10,11... | collective-permute-start | bytes 1253384 | tf_op jit(solution)/shard_map/ppermute | solution.py:105
  65.5 11.7 %collective-permute-start.21 = (bf16[4,48,1536]{2,1,0:T(8,128)(2,1)S(1)}, bf16[4,48,1536]{2,1,0:T(8,128)(2,1)S(1)}, u32[]{:S(2)}, u32[]{:S(2)}) collective-permute-start(bf16[4,48,1536]{2,1,0:T(8,128)(2,1)S(1)} %pad_maximum_fusion.2.refs_0_), channel_id=1, source_target_pairs={{0,2},{2,0},{4,6},{6,4},{8,10},{10,8},{12,14},{14,12},{16,18},{18,... | collective-permute-start | bytes 1769480 | tf_op jit(solution)/shard_map/ppermute | solution.py:101
  76.1 2.0 %collective-permute-start.22 = (bf16[4,48,1536]{2,1,0:T(8,128)(2,1)S(1)}, bf16[4,48,1536]{2,1,0:T(8,128)(2,1)S(1)}, u32[]{:S(2)}, u32[]{:S(2)}) collective-permute-start(bf16[4,48,1536]{2,1,0:T(8,128)(2,1)S(1)} %collective-permute-done.17.refs_1_), channel_id=1, source_target_pairs={{0,2},{2,0},{4,6},{6,4},{8,10},{10,8},{12,14},{14,12},{16,18},{18,... | collective-permute-start | bytes 1769480 | tf_op jit(solution)/shard_map/ppermute | solution.py:101
  80.6 8.3 %collective-permute-start.23 = (bf16[144,768]{1,0:T(8,128)(2,1)S(1)}, bf16[144,768]{1,0:T(8,128)(2,1)S(1)}, u32[]{:S(2)}, u32[]{:S(2)}) collective-permute-start(bf16[144,768]{1,0:T(8,128)(2,1)S(1)} %slice.12), channel_id=1, source_target_pairs={{0,1},{1,0},{2,3},{3,2},{4,5},{5,4},{6,7},{7,6},{8,9},{9,8},{10,11... | collective-permute-start | bytes 663560 | tf_op jit(solution)/shard_map/ppermute | solution.py:105
  82.2 10.1 %collective-permute-start.24 = (bf16[128,768]{1,0:T(8,128)(2,1)S(1)}, bf16[128,768]{1,0:T(8,128)(2,1)S(1)}, u32[]{:S(2)}, u32[]{:S(2)}) collective-permute-start(bf16[128,768]{1,0:T(8,128)(2,1)S(1)} %slice.13), channel_id=1, source_target_pairs={{0,1},{1,0},{2,3},{3,2},{4,5},{5,4},{6,7},{7,6},{8,9},{9,8},{10,11... | collective-permute-start | bytes 589832 | tf_op jit(solution)/shard_map/ppermute | solution.py:105
  82.7 6.3 %copy-start = (bf16[266,1,768]{2,0,1:T(8,128)(2,1)S(1)}, bf16[266,1,768]{2,0,1:T(8,128)(2,1)}, u32[]{:S(2)}) copy-start(bf16[266,1,768]{2,0,1:T(8,128)(2,1)} %param.14) | copy-start | bytes 1225732
  90.0 2.4 %collective-permute-start.25 = (bf16[16,128]{1,0:T(8,128)(2,1)S(1)}, bf16[16,128]{1,0:T(8,128)(2,1)S(1)}, u32[]{:S(2)}, u32[]{:S(2)}) collective-permute-start(bf16[16,128]{1,0:T(8,128)(2,1)S(1)} %slice.11), channel_id=1, source_target_pairs={{0,2},{2,0},{4,6},{6,4},{8,10},{10,8},{12,14},{14,12},{16,18},{18,... | collective-permute-start | bytes 12296 | tf_op jit(solution)/shard_map/ppermute | solution.py:101
  90.1 12.1 %collective-permute-start.26 = (bf16[144,768]{1,0:T(8,128)(2,1)S(1)}, bf16[144,768]{1,0:T(8,128)(2,1)S(1)}, u32[]{:S(2)}, u32[]{:S(2)}) collective-permute-start(bf16[144,768]{1,0:T(8,128)(2,1)S(1)} %get-tuple-element.175), channel_id=1, source_target_pairs={{0,1},{1,0},{2,3},{3,2},{4,5},{5,4},{6,7},{7,6},{8,9},{9,8},{10,11... | collective-permute-start | bytes 663560 | tf_op jit(solution)/shard_map/ppermute | solution.py:105
  94.4 7.8 %collective-permute-start.27 = (bf16[128,768]{1,0:T(8,128)(2,1)S(1)}, bf16[128,768]{1,0:T(8,128)(2,1)S(1)}, u32[]{:S(2)}, u32[]{:S(2)}) collective-permute-start(bf16[128,768]{1,0:T(8,128)(2,1)S(1)} %get-tuple-element.180), channel_id=1, source_target_pairs={{0,1},{1,0},{2,3},{3,2},{4,5},{5,4},{6,7},{7,6},{8,9},{9,8},{10,11... | collective-permute-start | bytes 589832 | tf_op jit(solution)/shard_map/ppermute | solution.py:105
  104.1 11.4 %collective-permute-start.28 = (bf16[272,768]{1,0:T(8,128)(2,1)S(1)}, bf16[272,768]{1,0:T(8,128)(2,1)S(1)}, u32[]{:S(2)}, u32[]{:S(2)}) collective-permute-start(bf16[272,768]{1,0:T(8,128)(2,1)S(1)} %convolution_convert_fusion), channel_id=1, source_target_pairs={{0,1},{1,0},{2,3},{3,2},{4,5},{5,4},{6,7},{7,6},{8,9},{9,8},{10,11... | collective-permute-start | bytes 1253384 | tf_op jit(solution)/shard_map/ppermute | solution.py:105
  108.2 1.6 collective-permute-start.33
  108.2 2.0 %collective-permute-start.34 = (bf16[8,48,384]{2,1,0:T(8,128)(2,1)S(1)}, bf16[8,48,384]{2,1,0:T(8,128)(2,1)S(1)}, u32[]{:S(2)}, u32[]{:S(2)}) collective-permute-start(bf16[8,48,384]{2,1,0:T(8,128)(2,1)S(1)} %get-tuple-element.202), channel_id=1, source_target_pairs={{0,2},{2,0},{4,6},{6,4},{8,10},{10,8},{12,14},{14,12},{16,18},{18,... | collective-permute-start | bytes 884744 | tf_op jit(solution)/shard_map/ppermute | solution.py:101
  108.7 1.9 %collective-permute-start.35 = (bf16[8,48,384]{2,1,0:T(8,128)(2,1)S(1)}, bf16[8,48,384]{2,1,0:T(8,128)(2,1)S(1)}, u32[]{:S(2)}, u32[]{:S(2)}) collective-permute-start(bf16[8,48,384]{2,1,0:T(8,128)(2,1)S(1)} %get-tuple-element.203), channel_id=1, source_target_pairs={{0,2},{2,0},{4,6},{6,4},{8,10},{10,8},{12,14},{14,12},{16,18},{18,... | collective-permute-start | bytes 884744 | tf_op jit(solution)/shard_map/ppermute | solution.py:101
  108.8 2.3 %collective-permute-start.36 = (bf16[8,48,384]{2,1,0:T(8,128)(2,1)S(1)}, bf16[8,48,384]{2,1,0:T(8,128)(2,1)S(1)}, u32[]{:S(2)}, u32[]{:S(2)}) collective-permute-start(bf16[8,48,384]{2,1,0:T(8,128)(2,1)S(1)} %get-tuple-element.204), channel_id=1, source_target_pairs={{0,2},{2,0},{4,6},{6,4},{8,10},{10,8},{12,14},{14,12},{16,18},{18,... | collective-permute-start | bytes 884744 | tf_op jit(solution)/shard_map/ppermute | solution.py:101
  111.9 15.4 %collective-permute-start.41 = (bf16[4,48,1536]{2,1,0:T(8,128)(2,1)S(1)}, bf16[4,48,1536]{2,1,0:T(8,128)(2,1)S(1)}, u32[]{:S(2)}, u32[]{:S(2)}) collective-permute-start(bf16[4,48,1536]{2,1,0:T(8,128)(2,1)S(1)} %get-tuple-element.205), channel_id=1, source_target_pairs={{0,4},{2,6},{4,0},{6,2},{8,12},{10,14},{12,8},{14,10},{16,20},{18,... | collective-permute-start | bytes 1769480 | tf_op jit(solution)/shard_map/ppermute | solution.py:101
  114.9 2.7 %collective-permute-start.37 = (bf16[8,48,384]{2,1,0:T(8,128)(2,1)S(1)}, bf16[8,48,384]{2,1,0:T(8,128)(2,1)S(1)}, u32[]{:S(2)}, u32[]{:S(2)}) collective-permute-start(bf16[8,48,384]{2,1,0:T(8,128)(2,1)S(1)} %get-tuple-element.208), channel_id=1, source_target_pairs={{0,2},{2,0},{4,6},{6,4},{8,10},{10,8},{12,14},{14,12},{16,18},{18,... | collective-permute-start | bytes 884744 | tf_op jit(solution)/shard_map/ppermute | solution.py:101
  115.0 5.1 %collective-permute-start.38 = (bf16[8,48,384]{2,1,0:T(8,128)(2,1)S(1)}, bf16[8,48,384]{2,1,0:T(8,128)(2,1)S(1)}, u32[]{:S(2)}, u32[]{:S(2)}) collective-permute-start(bf16[8,48,384]{2,1,0:T(8,128)(2,1)S(1)} %get-tuple-element.209), channel_id=1, source_target_pairs={{0,2},{2,0},{4,6},{6,4},{8,10},{10,8},{12,14},{14,12},{16,18},{18,... | collective-permute-start | bytes 884744 | tf_op jit(solution)/shard_map/ppermute | solution.py:101
  115.5 4.9 %collective-permute-start.39 = (bf16[8,48,384]{2,1,0:T(8,128)(2,1)S(1)}, bf16[8,48,384]{2,1,0:T(8,128)(2,1)S(1)}, u32[]{:S(2)}, u32[]{:S(2)}) collective-permute-start(bf16[8,48,384]{2,1,0:T(8,128)(2,1)S(1)} %get-tuple-element.210), channel_id=1, source_target_pairs={{0,2},{2,0},{4,6},{6,4},{8,10},{10,8},{12,14},{14,12},{16,18},{18,... | collective-permute-start | bytes 884744 | tf_op jit(solution)/shard_map/ppermute | solution.py:101
  115.6 5.1 %collective-permute-start.40 = (bf16[8,48,384]{2,1,0:T(8,128)(2,1)S(1)}, bf16[8,48,384]{2,1,0:T(8,128)(2,1)S(1)}, u32[]{:S(2)}, u32[]{:S(2)}) collective-permute-start(bf16[8,48,384]{2,1,0:T(8,128)(2,1)S(1)} %get-tuple-element.211), channel_id=1, source_target_pairs={{0,2},{2,0},{4,6},{6,4},{8,10},{10,8},{12,14},{14,12},{16,18},{18,... | collective-permute-start | bytes 884744 | tf_op jit(solution)/shard_map/ppermute | solution.py:101
  117.6 10.4 %collective-permute-start.29 = (bf16[272,384]{1,0:T(8,128)(2,1)S(1)}, bf16[272,384]{1,0:T(8,128)(2,1)S(1)}, u32[]{:S(2)}, u32[]{:S(2)}) collective-permute-start(bf16[272,384]{1,0:T(8,128)(2,1)S(1)} %get-tuple-element.187), channel_id=1, source_target_pairs={{0,1},{1,0},{2,3},{3,2},{4,5},{5,4},{6,7},{7,6},{8,9},{9,8},{10,11... | collective-permute-start | bytes 626696 | tf_op jit(solution)/shard_map/ppermute | solution.py:105
  120.1 1.7 collective-permute-start.30
  120.4 1.5 collective-permute-start.31
  120.7 1.5 collective-permute-start.32
  128.0 13.7 %collective-permute-start.42 = (bf16[8,24,768]{2,1,0:T(8,128)(2,1)S(1)}, bf16[8,24,768]{2,1,0:T(8,128)(2,1)S(1)}, u32[]{:S(2)}, u32[]{:S(2)}) collective-permute-start(bf16[8,24,768]{2,1,0:T(8,128)(2,1)S(1)} %get-tuple-element.218), channel_id=1, source_target_pairs={{0,1},{1,0},{2,3},{3,2},{4,5},{5,4},{6,7},{7,6},{8,9},{9,8},{10,11... | collective-permute-start | bytes 884744 | tf_op jit(solution)/shard_map/ppermute | solution.py:105
  128.6 14.6 %collective-permute-start.43 = (bf16[2,48,1536]{2,1,0:T(8,128)(2,1)S(1)}, bf16[2,48,1536]{2,1,0:T(8,128)(2,1)S(1)}, u32[]{:S(2)}, u32[]{:S(2)}) collective-permute-start(bf16[2,48,1536]{2,1,0:T(8,128)(2,1)S(1)} %get-tuple-element.219), channel_id=1, source_target_pairs={{0,16},{2,18},{4,20},{6,22},{8,24},{10,26},{12,28},{14,30},{16,0},... | collective-permute-start | bytes 884744 | tf_op jit(solution)/shard_map/ppermute | solution.py:101
  128.6 15.6 %collective-permute-start.44 = (bf16[4,48,1536]{2,1,0:T(8,128)(2,1)S(1)}, bf16[4,48,1536]{2,1,0:T(8,128)(2,1)S(1)}, u32[]{:S(2)}, u32[]{:S(2)}) collective-permute-start(bf16[4,48,1536]{2,1,0:T(8,128)(2,1)S(1)} %get-tuple-element.233), channel_id=1, source_target_pairs={{0,4},{2,6},{4,0},{6,2},{8,12},{10,14},{12,8},{14,10},{16,20},{18,... | collective-permute-start | bytes 1769480 | tf_op jit(solution)/shard_map/ppermute | solution.py:101
  143.2 2.6 %collective-permute-start.45 = (bf16[8,48,384]{2,1,0:T(8,128)(2,1)S(1)}, bf16[8,48,384]{2,1,0:T(8,128)(2,1)S(1)}, u32[]{:S(2)}, u32[]{:S(2)}) collective-permute-start(bf16[8,48,384]{2,1,0:T(8,128)(2,1)S(1)} %get-tuple-element.235), channel_id=1, source_target_pairs={{0,2},{2,0},{4,6},{6,4},{8,10},{10,8},{12,14},{14,12},{16,18},{18,... | collective-permute-start | bytes 884744 | tf_op jit(solution)/shard_map/ppermute | solution.py:101
  143.2 2.6 %collective-permute-start.46 = (bf16[8,48,384]{2,1,0:T(8,128)(2,1)S(1)}, bf16[8,48,384]{2,1,0:T(8,128)(2,1)S(1)}, u32[]{:S(2)}, u32[]{:S(2)}) collective-permute-start(bf16[8,48,384]{2,1,0:T(8,128)(2,1)S(1)} %get-tuple-element.236), channel_id=1, source_target_pairs={{0,2},{2,0},{4,6},{6,4},{8,10},{10,8},{12,14},{14,12},{16,18},{18,... | collective-permute-start | bytes 884744 | tf_op jit(solution)/shard_map/ppermute | solution.py:101
  143.7 2.1 %collective-permute-start.47 = (bf16[8,48,384]{2,1,0:T(8,128)(2,1)S(1)}, bf16[8,48,384]{2,1,0:T(8,128)(2,1)S(1)}, u32[]{:S(2)}, u32[]{:S(2)}) collective-permute-start(bf16[8,48,384]{2,1,0:T(8,128)(2,1)S(1)} %get-tuple-element.237), channel_id=1, source_target_pairs={{0,2},{2,0},{4,6},{6,4},{8,10},{10,8},{12,14},{14,12},{16,18},{18,... | collective-permute-start | bytes 884744 | tf_op jit(solution)/shard_map/ppermute | solution.py:101
  143.7 2.0 %collective-permute-start.48 = (bf16[8,48,128]{2,1,0:T(8,128)(2,1)S(1)}, bf16[8,48,128]{2,1,0:T(8,128)(2,1)S(1)}, u32[]{:S(2)}, u32[]{:S(2)}) collective-permute-start(bf16[8,48,128]{2,1,0:T(8,128)(2,1)S(1)} %get-tuple-element.238), channel_id=1, source_target_pairs={{0,2},{2,0},{4,6},{6,4},{8,10},{10,8},{12,14},{14,12},{16,18},{18,... | collective-permute-start | bytes 294920 | tf_op jit(solution)/shard_map/ppermute | solution.py:101
  146.7 17.4 %collective-permute-start.49 = (bf16[4,24,2048]{2,1,0:T(8,128)(2,1)S(1)}, bf16[4,24,2048]{2,1,0:T(8,128)(2,1)S(1)}, u32[]{:S(2)}, u32[]{:S(2)}) collective-permute-start(bf16[4,24,2048]{2,1,0:T(8,128)(2,1)S(1)} %get-tuple-element.245), channel_id=1, source_target_pairs={{0,4},{2,6},{4,0},{6,2},{8,12},{10,14},{12,8},{14,10},{16,20},{18,... | collective-permute-start | bytes 1179656 | tf_op jit(solution)/shard_map/ppermute | solution.py:101
  147.3 16.0 %collective-permute-start.52 = (bf16[2,48,1536]{2,1,0:T(8,128)(2,1)S(1)}, bf16[2,48,1536]{2,1,0:T(8,128)(2,1)S(1)}, u32[]{:S(2)}, u32[]{:S(2)}) collective-permute-start(bf16[2,48,1536]{2,1,0:T(8,128)(2,1)S(1)} %get-tuple-element.252), channel_id=1, source_target_pairs={{0,16},{2,18},{4,20},{6,22},{8,24},{10,26},{12,28},{14,30},{16,0},... | collective-permute-start | bytes 884744 | tf_op jit(solution)/shard_map/ppermute | solution.py:101
  149.9 14.0 %collective-permute-start.50 = (bf16[4,24,1280]{2,1,0:T(8,128)(2,1)S(1)}, bf16[4,24,1280]{2,1,0:T(8,128)(2,1)S(1)}, u32[]{:S(2)}, u32[]{:S(2)}) collective-permute-start(bf16[4,24,1280]{2,1,0:T(8,128)(2,1)S(1)} %get-tuple-element.248), channel_id=1, source_target_pairs={{0,1},{1,0},{2,3},{3,2},{4,5},{5,4},{6,7},{7,6},{8,9},{9,8},{10,11... | collective-permute-start | bytes 737288 | tf_op jit(solution)/shard_map/ppermute | solution.py:105
  151.4 12.7 %collective-permute-start.51 = (bf16[4,24,1280]{2,1,0:T(8,128)(2,1)S(1)}, bf16[4,24,1280]{2,1,0:T(8,128)(2,1)S(1)}, u32[]{:S(2)}, u32[]{:S(2)}) collective-permute-start(bf16[4,24,1280]{2,1,0:T(8,128)(2,1)S(1)} %get-tuple-element.249), channel_id=1, source_target_pairs={{0,5},{1,4},{2,7},{3,6},{4,1},{5,0},{6,3},{7,2},{8,13},{9,12},{10,... | collective-permute-start | bytes 737288 | tf_op jit(solution)/shard_map/ppermute | solution.py:114
  152.4 11.4 %collective-permute-start.53 = (bf16[1,48,1536]{2,1,0:T(8,128)(2,1)S(1)}, bf16[1,48,1536]{2,1,0:T(8,128)(2,1)S(1)}, u32[]{:S(2)}, u32[]{:S(2)}) collective-permute-start(bf16[1,48,1536]{2,1,0:T(8,128)(2,1)S(1)} %get-tuple-element.256), channel_id=1, source_target_pairs={{0,8},{2,10},{4,12},{6,14},{8,0},{10,2},{12,4},{14,6},{16,24},{18,... | collective-permute-start | bytes 442376 | tf_op jit(solution)/shard_map/ppermute | solution.py:136
  164.1 8.6 %collective-permute-start.58 = (bf16[1,48,1536]{2,1,0:T(8,128)(2,1)S(1)}, bf16[1,48,1536]{2,1,0:T(8,128)(2,1)S(1)}, u32[]{:S(2)}, u32[]{:S(2)}) collective-permute-start(bf16[1,48,1536]{2,1,0:T(8,128)(2,1)S(1)} %get-tuple-element.276), channel_id=1, source_target_pairs={{0,8},{2,10},{4,12},{6,14},{8,0},{10,2},{12,4},{14,6},{16,24},{18,... | collective-permute-start | bytes 442376 | tf_op jit(solution)/shard_map/ppermute | solution.py:136
  166.1 14.5 %collective-permute-start.55 = (bf16[1,24,3328]{2,1,0:T(8,128)(2,1)S(1)}, bf16[1,24,3328]{2,1,0:T(8,128)(2,1)S(1)}, u32[]{:S(2)}, u32[]{:S(2)}) collective-permute-start(bf16[1,24,3328]{2,1,0:T(8,128)(2,1)S(1)} %get-tuple-element.262), channel_id=1, source_target_pairs={{0,8},{2,10},{4,12},{6,14},{8,16},{10,18},{12,20},{14,22},{16,24},... | collective-permute-start | bytes 479240 | tf_op jit(solution)/shard_map/ppermute | solution.py:101
  166.9 13.8 %collective-permute-start.56 = (bf16[1,24,3328]{2,1,0:T(8,128)(2,1)S(1)}, bf16[1,24,3328]{2,1,0:T(8,128)(2,1)S(1)}, u32[]{:S(2)}, u32[]{:S(2)}) collective-permute-start(bf16[1,24,3328]{2,1,0:T(8,128)(2,1)S(1)} %get-tuple-element.263), channel_id=1, source_target_pairs={{0,16},{2,18},{4,20},{6,22},{8,24},{10,26},{12,28},{14,30},{16,0},... | collective-permute-start | bytes 479240 | tf_op jit(solution)/shard_map/ppermute | solution.py:101
  168.5 12.1 %collective-permute-start.57 = (bf16[1,24,3328]{2,1,0:T(8,128)(2,1)S(1)}, bf16[1,24,3328]{2,1,0:T(8,128)(2,1)S(1)}, u32[]{:S(2)}, u32[]{:S(2)}) collective-permute-start(bf16[1,24,3328]{2,1,0:T(8,128)(2,1)S(1)} %get-tuple-element.264), channel_id=1, source_target_pairs={{0,24},{2,26},{4,28},{6,30},{8,0},{10,2},{12,4},{14,6},{16,8},{18,... | collective-permute-start | bytes 479240 | tf_op jit(solution)/shard_map/ppermute | solution.py:101
  170.2 9.9 %collective-permute-start.54 = (bf16[272,768]{1,0:T(8,128)(2,1)S(1)}, bf16[272,768]{1,0:T(8,128)(2,1)S(1)}, u32[]{:S(2)}, u32[]{:S(2)}) collective-permute-start(bf16[272,768]{1,0:T(8,128)(2,1)S(1)} %get-tuple-element.257), channel_id=1, source_target_pairs={{0,1},{1,0},{2,3},{3,2},{4,5},{5,4},{6,7},{7,6},{8,9},{9,8},{10,11... | collective-permute-start | bytes 1253384 | tf_op jit(solution)/shard_map/ppermute | solution.py:105

commit v4 on v3

--- a/solution.py
+++ b/solution.py
@@ -65,7 +65,7 @@
         out_specs=[pl.BlockSpec(memory_space=pltpu.VMEM)] * len(outs),
         out_shape=list(outs),
         scratch_shapes=list(scratch),
-        compiler_params=pltpu.CompilerParams(vmem_limit_bytes=room + (3 << 20)),
+        compiler_params=pltpu.CompilerParams(vmem_limit_bytes=room + (9 << 20)),
         cost_estimate=QUICK,
     )(at, *arrays)
 
@@ -148,6 +148,15 @@
     return value.reshape((-1,) + value.shape[-2:])
 
 
+def spread_far_pieces(pair, digits):
+    pieces = [pair, rotate(pair, digits[-3], 2)]
+    for digit in reversed(digits[:-3]):
+        for n, value in enumerate(pieces):
+            value = jnp.stack([value] + [rotate(value, digit, step) for step in range(1, digit[1])])
+            pieces[n] = value.reshape((-1,) + value.shape[-2:])
+    return pieces
+
+
 def placer(sizes, me, paired):
     outer, digits = sizes[:-2], []
     for size in reversed(sizes):
@@ -175,14 +184,17 @@
 
 
 def assemble_kernel(sizes, paired, at, *refs):
-    parts, whole = refs[:4], refs[4]
+    *parts, whole = refs
     cols = whole.shape[2]
+    pieces = len(parts) // 4
     place_of = placer(sizes, at[DP], paired)
     for swap_core in range(2):
         for swap_x in range(2):
-            source = parts[2 * swap_core + swap_x]
-            for slot in range(source.shape[0]):
-                whole[place_of(swap_core, swap_x, slot)] = source[slot, :, :cols]
+            for piece in range(pieces):
+                source = parts[pieces * (2 * swap_core + swap_x) + piece]
+                for block in range(source.shape[0]):
+                    slot = 2 * (pieces * (block // 2) + piece) + block % 2
+                    whole[place_of(swap_core, swap_x, slot)] = source[block, :, :cols]
 
 
 def swap_blocks(mine, x_got, digits):
@@ -190,16 +202,22 @@
     return [mine, x_got, rotate(mine, core, 1), rotate(x_got, core, 1)]
 
 
+def swap_pieces(mine, x_got, digits):
+    core = digits[-1]
+    return [*mine, *x_got] + [rotate(piece, core, 1) for piece in (*mine, *x_got)]
+
+
 def assemble(at, parts, digits, cols, paired=False):
-    slots, rows, _ = parts[0].shape
+    rows = parts[0].shape[1]
+    blocks = sum(part.shape[0] for part in parts)
     sizes = tuple(size for _, size in digits)
     (whole,) = call(
         functools.partial(assemble_kernel, sizes, paired),
-        [low_of(4 * slots, rows, cols)],
+        [low_of(blocks, rows, cols)],
         at,
         *parts,
     )
-    return whole.reshape(4 * slots * rows, cols)
+    return whole.reshape(blocks * rows, cols)
 
 
 def assemble_first_kernel(sizes, at, *refs):
@@ -282,8 +300,9 @@
 
 
 def put_gradient(a, b, outs, core, own=None, tile=TILE):
+    whole = tn(a[...], b[...])
     for n, low in enumerate(range(0, b.shape[1], tile)):
-        total = tn(a[...], b[:, low : low + tile])
+        total = whole[:, low : low + tile]
         if own is not None:
             total = total + own[:, low : low + tile]
         if len(outs) == 1:
@@ -326,6 +345,14 @@
             kept[group, :, low:high] = jnp.where(first, a, b).astype(LOW)
             sent[group, :, low:high] = jnp.where(first, b, a).astype(LOW)
             low = high
+
+
+def own_forward_kernel(at, normed, up, up_b, down_t, _, hidden, slope, out):
+    pre_act = nn(normed[...], up[...]).reshape(-1, *up_b.shape) + up_b[...]
+    active, slopes = (value.reshape(hidden.shape) for value in gelu_parts(pre_act))
+    hidden[...] = active.astype(LOW)
+    slope[...] = slopes
+    out[...] = nt(hidden[...], down_t[...])
 
 
 def own_kernel(at, a_down, b_down, a_up, b_up, down, up, sums):
@@ -427,7 +454,8 @@
                 out[2 * group + n] = total.astype(out.dtype)
 
 
-def near_kernel(at, mine, got, kept, sent):
+def near_kernel(at, mine, got, *refs):
+    kept, sent = refs[-2:]
     for group in range(kept.shape[0]):
         kept[group] = mine[2 * group] + got[2 * group].astype(WIDE)
         total = mine[2 * group + 1] + got[2 * group + 1].astype(WIDE)
@@ -442,11 +470,10 @@
     )
 
 
-def near_parts(at, mine, got):
+def near_parts(at, mine, got, *ahead):
     blocks, rows, cols = mine.shape
-    return call(
-        near_kernel, [wide_of(blocks // 2, rows, cols), low_of(blocks // 2, rows, cols)], at, mine, got
-    )
+    outs = [wide_of(blocks // 2, rows, cols), low_of(blocks // 2, rows, cols)]
+    return call(near_kernel, outs, at, mine, got, *ahead)
 
 
 def outer_send(sent, digits):
@@ -766,8 +793,8 @@
     real = out.shape[0]
     row = lax.broadcasted_iota(jnp.int32, (32, 1), 0)
     fresh = (row < mem_count) & (at[FRESH] == 1) & (at[T] == 0)
-    out[:32, :] = jnp.where(fresh, 0.0, own[:32, :] + got[:32, :].astype(WIDE))
-    out[32:, :] = own[32:real, :] + got[32:real, :].astype(WIDE)
+    out[:32, 0, :] = jnp.where(fresh, 0.0, own[:32, :] + got[:32, :].astype(WIDE))
+    out[32:, 0, :] = own[32:real, :] + got[32:real, :].astype(WIDE)
 
 
 def gelu_parts(pre):
@@ -843,7 +870,8 @@
     first_parts = [mine, swap_tensor(other), rotate(mine, x_digit, 1), swap_both(other, x_digit)]
     up_z = spread_far(up_pair, digits)
     down_pair = spread_near(tie(ffn_down.T, mine), digits)
-    *first_parts, up_z, down_pair = join(*first_parts, up_z, down_pair)
+    up_z, down_in = join(up_z, down_pair)
+    *first_parts, up_z = join(*first_parts, up_z)
     first_parts = [jnp.concatenate(first_parts[n : n + 2], axis=2) for n in (0, 2)]
     core_parts = [rotate(value, core_digit, 1) for value in first_parts]
     sizes = tuple(size for _, size in digits)
@@ -859,7 +887,8 @@
     )
     out_got = swap_tensor(out_sent)
     up_x = rotate(up_z, x_digit, 1)
-    down_z = spread_far(down_pair, digits)
+    down_pieces = spread_far_pieces(down_in, digits)
+    down_x = [rotate(down_pieces[0], x_digit, 1)]
 
     projected, mix_own, mix_sent, log_total, layer_in, small = call(
         functools.partial(forward_kernel, half_rows, mem_count, doc_count, bias),
@@ -886,6 +915,7 @@
         at, *first_parts, *core_parts, out_got, rotate(out_got, core_digit, 1),
     )
     wout = wout.reshape(width, width)
+    mix_got, *down_pieces = join(mix_got, *down_pieces)
     mixed, unit, scale, normed_own = call(
         functools.partial(first_norm_kernel, bias, gain),
         [low_of(padded, width), wide_of(padded, width), wide_of(padded, PAIR), low_of(padded, width)],
@@ -894,15 +924,18 @@
     )
 
     normed_got = swap_tensor(normed_own)
-    up_x, up_z, down_z = tie(up_x, mix_sent), tie(up_z, mix_sent), tie(down_z, mix_sent)
+    up_x, up_z = tie(up_x, mix_sent), tie(up_z, mix_sent)
+    down_pieces = [tie(piece, mix_sent) for piece in down_pieces]
+    down_x = [tie(down_x[0], mix_sent)]
     up = assemble(at, swap_blocks(up_z, up_x, digits), digits, hidden_mine, paired=True)
     (up_b,) = call(
         functools.partial(up_row_kernel, lines), [wide_of(ROWS, hidden_mine)], at, wqkv,
         scratch=[pltpu.VMEM((1, hidden_mine), WIDE)],
     )
-    down_x = rotate(down_z, x_digit, 1)
-    normed_got, down_x, up_b, up = join(normed_got, down_x, up_b, up)
-    down_t = assemble(at, swap_blocks(down_z, down_x, digits), digits, hidden_mine, paired=True)
+    down_pieces[1], down_x[0] = join(down_pieces[1], down_x[0])
+    down_x.append(rotate(down_pieces[1], x_digit, 1))
+    normed_got, up_b, up = join(normed_got, up_b, up)
+    down_t = assemble(at, swap_pieces(down_pieces, down_x, digits), digits, hidden_mine, paired=True)
 
     def feed_forward(rows):
         pre_act = nn(rows, up).reshape(-1, *up_b.shape) + up_b
@@ -914,8 +947,14 @@
     pieces = ((0, cut), (cut, padded))
     hidden_got, slope_got, ffn_sent = feed_forward(normed_got)
     ffn_sent = ffn_sent.astype(LOW)
-    ffn_got = [swap_tensor(ffn_sent[low:high]) for low, high in pieces]
-    hidden_own, slope_own, ffn_own = feed_forward(tie(normed_own, ffn_sent))
+    (_, first_cut), (_, end) = pieces
+    ffn_got = [swap_tensor(ffn_sent[:first_cut])]
+    hidden_own, slope_own, ffn_own = call(
+        own_forward_kernel,
+        [low_of(padded, hidden_mine), wide_of(padded, hidden_mine), wide_of(padded, width)],
+        at, normed_own, up, up_b, down_t, rotate(ffn_sent[:ROWS, :PAIR], core_digit, 1),
+    )
+    ffn_got.append(swap_tensor(tie(ffn_sent, ffn_own)[first_cut:end]))
     d_out_rows = d_out.reshape(half_rows, width)
     second, ahead = [], small
     for (low, high), got in zip(pieces, ffn_got):
@@ -1024,16 +1063,17 @@
         projection_back_kernel, [wide_of(padded, width), low_of(padded, width)],
         at, tie(d_projected, to_x), wqkv, d_attn_in,
     )
-    up_kept, up_sent = near_parts(at, up_kept, up_got)
-    *both_got, d_in_sent, up_sent, down_got = join(*both_got, d_in_sent, up_sent, down_got)
+    d_in_got = swap_tensor(d_in_sent)
+    ahead = rotate(tie(d_in_sent, up_got)[:ROWS, :PAIR], core_digit, 1)
+    up_kept, up_sent = near_parts(at, up_kept, up_got, ahead)
+    *both_got, up_sent, down_got = join(*both_got, up_sent, down_got)
     up_got = swap_near(up_sent, digits[-3])
-    d_in_got = swap_tensor(d_in_sent)
     both_kept, both_sent = outer_parts(at, digits, mine, *both_got)
     both_got = outer_send(both_sent, digits)
     grad_ffn_down = outer_sum(down_kept, [down_got], digits)
     grad_ffn_up = outer_sum(up_kept, [up_got], digits)
     (grad_rows,) = call(
-        functools.partial(rows_kernel, mem_count), [wide_of(half_rows, width)], at, d_in_own, d_in_got
+        functools.partial(rows_kernel, mem_count), [wide_of(half_rows, 1, width)], at, d_in_own, d_in_got
     )
     grad_rows, *both_got = join(grad_rows, *both_got)
 
@@ -1051,7 +1091,7 @@
     )
     return (
         jnp.concatenate(layer_out, axis=0).reshape(half_rows, 1, width),
-        grad_rows.reshape(half_rows, 1, width),
+        grad_rows,
         grad_qkv,
         grad_out_weight,
         grad_vec,

time: 184 us -> 180 us (0.978)
  waiting for transfers between devices: 64.5 us -> 61.3 us
  Pallas kernels: 51.9 us -> 54.6 us
  matrix products: 7.14 us -> 5.27 us
    ppermute x14, starting transfers between devices: 18.4 us -> 14 us  [swap_tensor(): return lax.ppermute(value, 'tensor', [(0, 1), (1, 0)])]
    pallas_call x31 -> x32, Pallas kernels: 51.9 us -> 54.6 us  [call(): pl.pallas_call(kernel, in_specs=[pl.BlockSpec(memory_space=pltpu.SMEM)] +...]
    ppermute x4, starting transfers between devices: 5.97 us -> 8.14 us  [swap_near(): return lax.ppermute(value, 'dp', pairs)]
    ppermute x39 -> x44, waiting for transfers between devices: 44.6 us -> 42.7 us  [rotate(): return lax.ppermute(value, 'dp', pairs)]
    dot_general x4 -> x3, matrix products: 3.8 us -> 2.75 us  [nn(): lax.dot_general(a, b, (((1,), (0,)), ((), ())), preferred_element_type=WIDE)]
    ppermute x39 -> x44, starting transfers between devices: 24.2 us -> 25.2 us  [rotate(): return lax.ppermute(value, 'dp', pairs)]
  transfers between devices with their start and end apart: 59 -> 64, of which waited for: 24 -> 28; matrix products, arithmetic and copies ran while one was open for 5% -> 5% of each run, Pallas kernels for 25% -> 28%
where the time goes in v4:
time: 180 us; the launch traced here: 179 us
  waiting for transfers between devices  61.3 us (34%)
  Pallas kernels  54.6 us (30%)
  starting transfers between devices  49.3 us (27%)
  matrix products  5.27 us (3%)
  other arithmetic  4.32 us (2%)
  between operations  2.51 us (1%)
  local copies, waits for them, and re-layouts  2.15 us (1%)
    pallas_call x32, Pallas kernels, call(): pl.pallas_call(kernel, in_specs=[pl.BlockSpec(memory_space=pltpu.SMEM)] +...  54.6 us
    ppermute x44, waiting for transfers between devices, rotate(): return lax.ppermute(value, 'dp', pairs)  42.7 us
    ppermute x44, starting transfers between devices, rotate(): return lax.ppermute(value, 'dp', pairs)  25.2 us
    ppermute x14, starting transfers between devices, swap_tensor(): return lax.ppermute(value, 'tensor', [(0, 1), (1, 0)])  14 us
    ppermute x14, waiting for transfers between devices, swap_tensor(): return lax.ppermute(value, 'tensor', [(0, 1), (1, 0)])  13.5 us
    ppermute x4, starting transfers between devices, swap_near(): return lax.ppermute(value, 'dp', pairs)  8.14 us
  transfers between devices with their start and end apart: 64, of which 28 were waited for; matrix products, arithmetic and copies ran while one was open for 5% of the time, Pallas kernels for 28%

profile of v4, /device:TPU:0, one launch (start us, length us, event | category | flops | bytes accessed | tf_op | source)
XLA Modules:
  0.0 179.5 jit_solution(604784989584520478)
XLA Ops:
  0.6 1.7 shard_map.204
  2.3 3.0 %collective-permute-start.4 = (bf16[48,1536]{1,0:T(8,128)(2,1)}, bf16[48,1536]{1,0:T(8,128)(2,1)S(1)}, u32[]{:S(2)}, u32[]{:S(2)}) collective-permute-start(bf16[48,1536]{1,0:T(8,128)(2,1)} %param.23), channel_id=1, source_target_pairs={{0,8},{2,10},{4,12},{6,14},{8,0},{10,2},{12,4},{14,6},{16,24},{18,... | collective-permute-start | bytes 442376 | tf_op jit(solution)/shard_map/ppermute | solution.py:136
  5.4 2.6 %collective-permute-start.1 = (bf16[24,3200]{1,0:T(8,128)(2,1)}, bf16[24,3200]{1,0:T(8,128)(2,1)S(1)}, u32[]{:S(2)}, u32[]{:S(2)}) collective-permute-start(bf16[24,3200]{1,0:T(8,128)(2,1)} %shard_map.204), channel_id=1, source_target_pairs={{0,16},{2,18},{4,20},{6,22},{8,24},{10,26},{12,28},{14,30},{16,0},... | collective-permute-start | bytes 460808 | tf_op jit(solution)/shard_map/ppermute | solution.py:101
  8.0 2.0 %collective-permute-start = (bf16[24,3200]{1,0:T(8,128)(2,1)}, bf16[24,3200]{1,0:T(8,128)(2,1)S(1)}, u32[]{:S(2)}, u32[]{:S(2)}) collective-permute-start(bf16[24,3200]{1,0:T(8,128)(2,1)} %shard_map.204), channel_id=1, source_target_pairs={{0,8},{2,10},{4,12},{6,14},{8,16},{10,18},{12,20},{14,22},{16,24},... | collective-permute-start | bytes 460808 | tf_op jit(solution)/shard_map/ppermute | solution.py:101
  10.0 1.1 pad.4.own
  11.1 1.6 collective-permute-start.3
  14.7 0.9 pad_maximum_fusion.3
  15.6 1.0 collective-permute-done.1
  16.7 5.0 %collective-permute-done = bf16[24,3200]{1,0:T(8,128)(2,1)S(1)} collective-permute-done((bf16[24,3200]{1,0:T(8,128)(2,1)}, bf16[24,3200]{1,0:T(8,128)(2,1)S(1)}, u32[]{:S(2)}, u32[]{:S(2)}) %collective-permute-start) | collective-permute-done | bytes 153632 | tf_op jit(solution)/shard_map/ppermute | solution.py:101
  21.6 1.0 pad_maximum_fusion.packed
  24.1 1.2 collective-permute-start.8
  25.4 1.5 collective-permute-start.6
  26.9 1.5 collective-permute-start.5
  28.9 2.5 %collective-permute-done.9 = bf16[48,1536]{1,0:T(8,128)(2,1)S(1)} collective-permute-done((bf16[48,1536]{1,0:T(8,128)(2,1)S(1)}, bf16[48,1536]{1,0:T(8,128)(2,1)S(1)}, u32[]{:S(2)}, u32[]{:S(2)}) %collective-permute-start.9) | collective-permute-done | bytes 147488 | tf_op jit(solution)/shard_map/ppermute | solution.py:136
  31.4 7.1 %collective-permute-done.8 = bf16[2,48,1536]{2,1,0:T(8,128)(2,1)S(1)} collective-permute-done((bf16[2,48,1536]{2,1,0:T(8,128)(2,1)S(1)}, bf16[2,48,1536]{2,1,0:T(8,128)(2,1)S(1)}, u32[]{:S(2)}, u32[]{:S(2)}) %collective-permute-start.8) | collective-permute-done | bytes 294944 | tf_op jit(solution)/shard_map/ppermute | solution.py:101
  38.6 2.5 %collective-permute-done.7 = bf16[4,24,1280]{2,1,0:T(8,128)(2,1)S(1)} collective-permute-done((bf16[4,24,1280]{2,1,0:T(8,128)(2,1)S(1)}, bf16[4,24,1280]{2,1,0:T(8,128)(2,1)S(1)}, u32[]{:S(2)}, u32[]{:S(2)}) %collective-permute-start.7) | collective-permute-done | bytes 245792 | tf_op jit(solution)/shard_map/ppermute | solution.py:114
  41.9 1.5 collective-permute-start.17
  44.5 1.1 collective-permute-start.13
  46.4 7.8 %shard_map.207 = (bf16[544,1152]{1,0:T(8,128)(2,1)S(1)}, bf16[272,384]{1,0:T(8,128)(2,1)S(1)}, bf16[272,384]{1,0:T(8,128)(2,1)S(1)}, f32[544,128]{1,0:T(8,128)S(...) custom-call(s32[15]{0:T(128)S(1)} %concatenate.21.at, bf16[272,768]{1,0:T(8,128)(2,1)S(1)} %pad.4.own, ...), custom_call_target="tpu_custom_call" | custom-call | flops 1 | bytes 1 | tf_op jit(solution)/shard_map/pallas_call | solution.py:61
  54.3 1.6 collective-permute-start.12
  57.2 3.0 %collective-permute-done.13.refs_1_ = bf16[2,48,1536]{2,1,0:T(8,128)(2,1)S(1)} collective-permute-done((bf16[2,48,1536]{2,1,0:T(8,128)(2,1)S(1)}, bf16[2,48,1536]{2,1,0:T(8,128)(2,1)S(1)}, u32[]{:S(2)}, u32[]{:S(2)}) %collective-permute-start.13) | collective-permute-done | bytes 294944 | tf_op jit(solution)/shard_map/ppermute | solution.py:101
  60.2 1.7 collective-permute-done.12.got
  62.5 1.3 shard_map.210
  63.8 1.6 collective-permute-start.16
  66.7 7.0 %collective-permute-done.21.refs_3_ = bf16[2,48,1536]{2,1,0:T(8,128)(2,1)S(1)} collective-permute-done((bf16[2,48,1536]{2,1,0:T(8,128)(2,1)S(1)}, bf16[2,48,1536]{2,1,0:T(8,128)(2,1)S(1)}, u32[]{:S(2)}, u32[]{:S(2)}) %collective-permute-start.21) | collective-permute-done | bytes 294944 | tf_op jit(solution)/shard_map/ppermute | solution.py:101
  75.3 0.9 multiply_convert_fusion
  77.0 0.8 convolution_convert_fusion.1
  77.9 1.6 collective-permute-start.27
  79.5 1.2 collective-permute-done.26._
  80.6 2.4 %shard_map.214 = (bf16[272,1536]{1,0:T(8,128)(2,1)S(1)}, f32[272,1536]{1,0:T(8,128)S(1)}, f32[272,768]{1,0:T(8,128)S(1)}) custom-call(s32[15]{0:T(128)S(1)} %concatenate.21.at, bf16[272,768]{1,0:T(8,128)(2,1)S(1)} %get-tuple-element.176.normed.a_up, bf16[768,1536]{1,0:T(8,128)(2,1)S(1)} %bitcast.57, f32[16,1536]{1,0:T(8,128)S(1)} %shard_map.211.up_b, ...), custom_call_target="tpu_custom_call" | custom-call | flops 1 | bytes 1 | tf_op jit(solution)/shard_map/pallas_call | solution.py:61
  83.7 2.0 %collective-permute-done.27.got = bf16[144,768]{1,0:T(8,128)(2,1)S(1)} collective-permute-done((bf16[144,768]{1,0:T(8,128)(2,1)S(1)}, bf16[144,768]{1,0:T(8,128)(2,1)S(1)}, u32[]{:S(2)}, u32[]{:S(2)}) %collective-permute-start.27) | collective-permute-done | bytes 221216 | tf_op jit(solution)/shard_map/ppermute | solution.py:105
  85.6 1.0 shard_map.215
  87.3 2.9 %collective-permute-done.28.got = bf16[128,768]{1,0:T(8,128)(2,1)S(1)} collective-permute-done((bf16[128,768]{1,0:T(8,128)(2,1)S(1)}, bf16[128,768]{1,0:T(8,128)(2,1)S(1)}, u32[]{:S(2)}, u32[]{:S(2)}) %collective-permute-start.28) | collective-permute-done | bytes 196640 | tf_op jit(solution)/shard_map/ppermute | solution.py:105
  90.3 1.0 shard_map.216
  91.9 0.8 fusion.b_up
  92.7 3.7 %shard_map.217 = (f32[768,1536]{1,0:T(8,128)S(1)}, f32[768,1536]{1,0:T(8,128)S(1)}, f32[1,1536]{1,0:T(1,128)S(1)}) custom-call(s32[15]{0:T(128)S(1)} %concatenate.21.at, bf16[272,768]{1,0:T(8,128)(2,1)S(1)} %constant_dynamic-update-slice_fusion.4.a_down, bf16[272,1536]{1,0:T(8,128)(2,1)S(1)} %get-tuple-element.200.b_down, ...), custom_call_target="tpu_custom_call" | custom-call | flops 1 | bytes 1 | tf_op jit(solution)/shard_map/pallas_call | solution.py:61
  97.3 1.8 %collective-permute-done.31 = bf16[128,768]{1,0:T(8,128)(2,1)S(1)} collective-permute-done((bf16[128,768]{1,0:T(8,128)(2,1)S(1)}, bf16[128,768]{1,0:T(8,128)(2,1)S(1)}, u32[]{:S(2)}, u32[]{:S(2)}) %collective-permute-start.31) | collective-permute-done | bytes 196640 | tf_op jit(solution)/shard_map/ppermute | solution.py:105
  99.1 1.0 fusion.1.b
  101.5 2.2 %shard_map.221 = (bf16[8,48,1536]{2,1,0:T(8,128)(2,1)S(1)}, bf16[8,48,384]{2,1,0:T(8,128)(2,1)S(1)}, bf16[8,48,384]{2,1,0:T(8,128)(2,1)S(1)}, bf16[8,48,384]{2,1,0:T(8,128)(2,1)S(1)}, bf16[8,48,384]{2,1,0:T(8,128)(2,1)S(1)}) custom-call(s32[15]{0:T(128)S(1)} %concatenate.21.at, f32[768,1536]{1,0:T(8,128)S(1)} %get-tuple-element.218.own, ...), custom_call_target="tpu_custom_call" | custom-call | flops 1 | bytes 1 | tf_op jit(solution)/shard_map/pallas_call | solution.py:61
  106.7 0.8 shard_map.222
  108.1 2.1 %shard_map.223 = (f32[1,1536]{1,0:T(1,128)S(1)}, bf16[8,48,1536]{2,1,0:T(8,128)(2,1)S(1)}, bf16[8,48,384]{2,1,0:T(8,128)(2,1)S(1)}, bf16[8,48,384]{2,1,0:T(8,128...) custom-call(s32[15]{0:T(128)S(1)} %concatenate.21.at, ...), custom_call_target="tpu_custom_call" | custom-call | flops 1 | bytes 1 | tf_op jit(solution)/shard_map/pallas_call | solution.py:61
  110.9 1.5 collective-permute-done.32.got
  112.4 1.6 shard_map.218
  114.7 1.4 shard_map.219
  116.9 0.8 shard_map.224
  118.8 4.1 %collective-permute-done.45.got = bf16[4,48,1536]{2,1,0:T(8,128)(2,1)S(1)} collective-permute-done((bf16[4,48,1536]{2,1,0:T(8,128)(2,1)S(1)}, bf16[4,48,1536]{2,1,0:T(8,128)(2,1)S(1)}, u32[]{:S(2)}, u32[]{:S(2)}) %collective-permute-start.45) | collective-permute-done | bytes 589856 | tf_op jit(solution)/shard_map/ppermute | solution.py:101
  123.6 1.6 collective-permute-start.46
  125.2 1.8 collective-permute-start.47
  127.5 9.6 %shard_map.226 = (bf16[544,1152]{1,0:T(8,128)(2,1)S(1)}, f32[1,1152]{1,0:T(1,128)S(1)}) custom-call(s32[15]{0:T(128)S(1)} %concatenate.21.at, bf16[544,1152]{1,0:T(8,128)(2,1)S(1)} %get-tuple-element.195.qkv, bf16[272,384]{1,0:T(8,128)(2,1)S(1)} %get-tuple-element.206.own, bf16[272,384]{1,0:T(8,128)(2,1)S(1)} %collective-permute-done.33.got, ...), custom_call_target="tpu_custom_call" | custom-call | flops 1 | bytes 1 | tf_op jit(solution)/shard_map/pallas_call | solution.py:61
  137.2 2.7 %shard_map.227 = (bf16[8,48,1280]{2,1,0:T(8,128)(2,1)S(1)}, bf16[8,48,384]{2,1,0:T(8,128)(2,1)S(1)}, bf16[8,48,384]{2,1,0:T(8,128)(2,1)S(1)}, bf16[8,48,384]{2,1,0:T(8,128)(2,1)S(1)}, bf16[8,48,128]{2,1,0:T(8,128)(2,1)S(1)}) custom-call(s32[15]{0:T(128)S(1)} %concatenate.21.at, bf16[544,768]{1,0:T(8,128)(2,1)S(1)} %get-tuple-element.173.layer_in, ...), custom_call_target="tpu_custom_call" | custom-call | flops 1 | bytes 1 | tf_op jit(solution)/shard_map/pallas_call | solution.py:61
  142.1 0.9 collective-permute-done.52.refs_3_
  143.8 0.9 shard_map.229
  144.7 1.6 collective-permute-start.54
  146.8 1.5 collective-permute-start.56
  148.9 2.6 %collective-permute-start.59 = (bf16[1,48,1536]{2,1,0:T(8,128)(2,1)S(1)}, bf16[1,48,1536]{2,1,0:T(8,128)(2,1)S(1)}, u32[]{:S(2)}, u32[]{:S(2)}) collective-permute-start(bf16[1,48,1536]{2,1,0:T(8,128)(2,1)S(1)} %get-tuple-element.278), channel_id=1, source_target_pairs={{0,8},{2,10},{4,12},{6,14},{8,0},{10,2},{12,4},{14,6},{16,24},{18,... | collective-permute-start | bytes 442376 | tf_op jit(solution)/shard_map/ppermute | solution.py:136
  151.4 1.8 %shard_map.230 = (f32[272,768]{1,0:T(8,128)S(1)}, bf16[272,768]{1,0:T(8,128)(2,1)S(1)}) custom-call(s32[15]{0:T(128)S(1)} %concatenate.21.at, bf16[544,1152]{1,0:T(8,128)(2,1)S(1)} %get-tuple-element.266.d_projected, bf16[768,1280]{1,0:T(8,128)(2,1)S(1)} %bitcast.51, f32[272,768]{1,0:T(8,128)S(1)} %get-tuple-element.245.d_attn), custom_call_target="tpu_custom_call" | custom-call | flops 1 | bytes 1 | tf_op jit(solution)/shard_map/pallas_call | solution.py:61
  153.3 6.1 %collective-permute-done.57.got = bf16[2,48,1536]{2,1,0:T(8,128)(2,1)S(1)} collective-permute-done((bf16[2,48,1536]{2,1,0:T(8,128)(2,1)S(1)}, bf16[2,48,1536]{2,1,0:T(8,128)(2,1)S(1)}, u32[]{:S(2)}, u32[]{:S(2)}) %collective-permute-start.57) | collective-permute-done | bytes 294944 | tf_op jit(solution)/shard_map/ppermute | solution.py:101
  161.7 1.7 collective-permute-start.63
  164.6 1.2 collective-permute-start.61
  165.8 2.2 %collective-permute-start.62 = (bf16[1,24,3328]{2,1,0:T(8,128)(2,1)S(1)}, bf16[1,24,3328]{2,1,0:T(8,128)(2,1)S(1)}, u32[]{:S(2)}, u32[]{:S(2)}) collective-permute-start(bf16[1,24,3328]{2,1,0:T(8,128)(2,1)S(1)} %get-tuple-element.284), channel_id=1, source_target_pairs={{0,24},{2,26},{4,28},{6,30},{8,0},{10,2},{12,4},{14,6},{16,8},{18,... | collective-permute-start | bytes 479240 | tf_op jit(solution)/shard_map/ppermute | solution.py:101
  168.8 3.5 %collective-permute-done.53.got = bf16[272,768]{1,0:T(8,128)(2,1)S(1)} collective-permute-done((bf16[272,768]{1,0:T(8,128)(2,1)S(1)}, bf16[272,768]{1,0:T(8,128)(2,1)S(1)}, u32[]{:S(2)}, u32[]{:S(2)}) %collective-permute-start.53) | collective-permute-done | bytes 417824 | tf_op jit(solution)/shard_map/ppermute | solution.py:105
  172.3 1.6 shard_map.231
  174.7 3.4 %collective-permute-done.61 = bf16[1,24,3328]{2,1,0:T(8,128)(2,1)S(1)} collective-permute-done((bf16[1,24,3328]{2,1,0:T(8,128)(2,1)S(1)}, bf16[1,24,3328]{2,1,0:T(8,128)(2,1)S(1)}, u32[]{:S(2)}, u32[]{:S(2)}) %collective-permute-start.61) | collective-permute-done | bytes 159776 | tf_op jit(solution)/shard_map/ppermute | solution.py:101
  178.1 1.3 shard_map.235
  (128 shorter events, 32.0 us)
Async XLA Ops:
  2.3 12.3 %collective-permute-start.4 = (bf16[48,1536]{1,0:T(8,128)(2,1)}, bf16[48,1536]{1,0:T(8,128)(2,1)S(1)}, u32[]{:S(2)}, u32[]{:S(2)}) collective-permute-start(bf16[48,1536]{1,0:T(8,128)(2,1)} %param.23), channel_id=1, source_target_pairs={{0,8},{2,10},{4,12},{6,14},{8,0},{10,2},{12,4},{14,6},{16,24},{18,... | collective-permute-start | bytes 442376 | tf_op jit(solution)/shard_map/ppermute | solution.py:136
  5.4 11.3 %collective-permute-start.1 = (bf16[24,3200]{1,0:T(8,128)(2,1)}, bf16[24,3200]{1,0:T(8,128)(2,1)S(1)}, u32[]{:S(2)}, u32[]{:S(2)}) collective-permute-start(bf16[24,3200]{1,0:T(8,128)(2,1)} %shard_map.204), channel_id=1, source_target_pairs={{0,16},{2,18},{4,20},{6,22},{8,24},{10,26},{12,28},{14,30},{16,0},... | collective-permute-start | bytes 460808 | tf_op jit(solution)/shard_map/ppermute | solution.py:101
  8.0 8.7 %collective-permute-start.2 = (bf16[24,3200]{1,0:T(8,128)(2,1)}, bf16[24,3200]{1,0:T(8,128)(2,1)S(1)}, u32[]{:S(2)}, u32[]{:S(2)}) collective-permute-start(bf16[24,3200]{1,0:T(8,128)(2,1)} %shard_map.204), channel_id=1, source_target_pairs={{0,24},{2,26},{4,28},{6,30},{8,0},{10,2},{12,4},{14,6},{16,8},{18,... | collective-permute-start | bytes 460808 | tf_op jit(solution)/shard_map/ppermute | solution.py:101
  8.0 13.7 %collective-permute-start = (bf16[24,3200]{1,0:T(8,128)(2,1)}, bf16[24,3200]{1,0:T(8,128)(2,1)S(1)}, u32[]{:S(2)}, u32[]{:S(2)}) collective-permute-start(bf16[24,3200]{1,0:T(8,128)(2,1)} %shard_map.204), channel_id=1, source_target_pairs={{0,8},{2,10},{4,12},{6,14},{8,16},{10,18},{12,20},{14,22},{16,24},... | collective-permute-start | bytes 460808 | tf_op jit(solution)/shard_map/ppermute | solution.py:101
  11.1 11.6 %collective-permute-start.3 = (bf16[272,768]{1,0:T(8,128)(2,1)S(1)}, bf16[272,768]{1,0:T(8,128)(2,1)S(1)}, u32[]{:S(2)}, u32[]{:S(2)}) collective-permute-start(bf16[272,768]{1,0:T(8,128)(2,1)S(1)} %pad.4.own), channel_id=1, source_target_pairs={{0,1},{1,0},{2,3},{3,2},{4,5},{5,4},{6,7},{7,6},{8,9},{9,8},{10,11... | collective-permute-start | bytes 1253384 | tf_op jit(solution)/shard_map/ppermute | solution.py:105
  23.3 8.1 %collective-permute-start.9 = (bf16[48,1536]{1,0:T(8,128)(2,1)S(1)}, bf16[48,1536]{1,0:T(8,128)(2,1)S(1)}, u32[]{:S(2)}, u32[]{:S(2)}) collective-permute-start(bf16[48,1536]{1,0:T(8,128)(2,1)S(1)} %bitcast.75), channel_id=1, source_target_pairs={{0,8},{2,10},{4,12},{6,14},{8,0},{10,2},{12,4},{14,6},{16,24},{18,... | collective-permute-start | bytes 442376 | tf_op jit(solution)/shard_map/ppermute | solution.py:136
  24.1 14.4 %collective-permute-start.8 = (bf16[2,48,1536]{2,1,0:T(8,128)(2,1)S(1)}, bf16[2,48,1536]{2,1,0:T(8,128)(2,1)S(1)}, u32[]{:S(2)}, u32[]{:S(2)}) collective-permute-start(bf16[2,48,1536]{2,1,0:T(8,128)(2,1)S(1)} %pad_maximum_fusion.3), channel_id=1, source_target_pairs={{0,16},{2,18},{4,20},{6,22},{8,24},{10,26},{12,28},{14,30},{16,0},... | collective-permute-start | bytes 884744 | tf_op jit(solution)/shard_map/ppermute | solution.py:101
  25.4 15.8 %collective-permute-start.6 = (bf16[4,24,2048]{2,1,0:T(8,128)(2,1)S(1)}, bf16[4,24,2048]{2,1,0:T(8,128)(2,1)S(1)}, u32[]{:S(2)}, u32[]{:S(2)}) collective-permute-start(bf16[4,24,2048]{2,1,0:T(8,128)(2,1)S(1)} %get-tuple-element.164), channel_id=1, source_target_pairs={{0,4},{2,6},{4,0},{6,2},{8,12},{10,14},{12,8},{14,10},{16,20},{18,... | collective-permute-start | bytes 1179656 | tf_op jit(solution)/shard_map/ppermute | solution.py:101
  26.9 11.7 %collective-permute-start.5 = (bf16[4,24,1280]{2,1,0:T(8,128)(2,1)S(1)}, bf16[4,24,1280]{2,1,0:T(8,128)(2,1)S(1)}, u32[]{:S(2)}, u32[]{:S(2)}) collective-permute-start(bf16[4,24,1280]{2,1,0:T(8,128)(2,1)S(1)} %get-tuple-element.160), channel_id=1, source_target_pairs={{0,1},{1,0},{2,3},{3,2},{4,5},{5,4},{6,7},{7,6},{8,9},{9,8},{10,11... | collective-permute-start | bytes 737288 | tf_op jit(solution)/shard_map/ppermute | solution.py:105
  28.4 12.7 %collective-permute-start.7 = (bf16[4,24,1280]{2,1,0:T(8,128)(2,1)S(1)}, bf16[4,24,1280]{2,1,0:T(8,128)(2,1)S(1)}, u32[]{:S(2)}, u32[]{:S(2)}) collective-permute-start(bf16[4,24,1280]{2,1,0:T(8,128)(2,1)S(1)} %get-tuple-element.160), channel_id=1, source_target_pairs={{0,5},{1,4},{2,7},{3,6},{4,1},{5,0},{6,3},{7,2},{8,13},{9,12},{10,... | collective-permute-start | bytes 737288 | tf_op jit(solution)/shard_map/ppermute | solution.py:114
  41.2 4.5 %collective-permute-start.11 = (bf16[4,24,3328]{2,1,0:T(8,128)(2,1)S(1)}, bf16[4,24,3328]{2,1,0:T(8,128)(2,1)S(1)}, u32[]{:S(2)}, u32[]{:S(2)}) collective-permute-start(bf16[4,24,3328]{2,1,0:T(8,128)(2,1)S(1)} %constant_dynamic-update-slice_fusion.2.refs_1_.x_got), channel_id=1, source_target_pairs={{0,2},{2,0},{4,6},{6,4},{8,10},{10,8},{12,14},{14,12},{16,18},{18,... | collective-permute-start | bytes 1916936 | tf_op jit(solution)/shard_map/ppermute | solution.py:101
  41.3 4.3 %collective-permute-start.10 = (bf16[4,24,3328]{2,1,0:T(8,128)(2,1)S(1)}, bf16[4,24,3328]{2,1,0:T(8,128)(2,1)S(1)}, u32[]{:S(2)}, u32[]{:S(2)}) collective-permute-start(bf16[4,24,3328]{2,1,0:T(8,128)(2,1)S(1)} %constant_dynamic-update-slice_fusion.refs_0_.mine), channel_id=1, source_target_pairs={{0,2},{2,0},{4,6},{6,4},{8,10},{10,8},{12,14},{14,12},{16,18},{18,... | collective-permute-start | bytes 1916936 | tf_op jit(solution)/shard_map/ppermute | solution.py:101
  41.9 15.3 %collective-permute-start.17 = (bf16[4,48,1536]{2,1,0:T(8,128)(2,1)S(1)}, bf16[4,48,1536]{2,1,0:T(8,128)(2,1)S(1)}, u32[]{:S(2)}, u32[]{:S(2)}) collective-permute-start(bf16[4,48,1536]{2,1,0:T(8,128)(2,1)S(1)} %pad_maximum_fusion.1.refs_0_), channel_id=1, source_target_pairs={{0,4},{2,6},{4,0},{6,2},{8,12},{10,14},{12,8},{14,10},{16,20},{18,... | collective-permute-start | bytes 1769480 | tf_op jit(solution)/shard_map/ppermute | solution.py:101
  43.9 10.3 %collective-permute-start.14 = (bf16[8,24,768]{2,1,0:T(8,128)(2,1)S(1)}, bf16[8,24,768]{2,1,0:T(8,128)(2,1)S(1)}, u32[]{:S(2)}, u32[]{:S(2)}) collective-permute-start(bf16[8,24,768]{2,1,0:T(8,128)(2,1)S(1)} %shard_map.208), channel_id=1, source_target_pairs={{0,1},{1,0},{2,3},{3,2},{4,5},{5,4},{6,7},{7,6},{8,9},{9,8},{10,11... | collective-permute-start | bytes 884744 | tf_op jit(solution)/shard_map/ppermute | solution.py:105
  44.5 15.7 %collective-permute-start.13 = (bf16[2,48,1536]{2,1,0:T(8,128)(2,1)S(1)}, bf16[2,48,1536]{2,1,0:T(8,128)(2,1)S(1)}, u32[]{:S(2)}, u32[]{:S(2)}) collective-permute-start(bf16[2,48,1536]{2,1,0:T(8,128)(2,1)S(1)} %pad_maximum_fusion.4.refs_0_), channel_id=1, source_target_pairs={{0,16},{2,18},{4,20},{6,22},{8,24},{10,26},{12,28},{14,30},{16,0},... | collective-permute-start | bytes 884744 | tf_op jit(solution)/shard_map/ppermute | solution.py:101
  54.2 7.7 %collective-permute-start.15 = (bf16[8,24,768]{2,1,0:T(8,128)(2,1)S(1)}, bf16[8,24,768]{2,1,0:T(8,128)(2,1)S(1)}, u32[]{:S(2)}, u32[]{:S(2)}) collective-permute-start(bf16[8,24,768]{2,1,0:T(8,128)(2,1)S(1)} %collective-permute-done.14.refs_4_), channel_id=1, source_target_pairs={{0,2},{2,0},{4,6},{6,4},{8,10},{10,8},{12,14},{14,12},{16,18},{18,... | collective-permute-start | bytes 884744 | tf_op jit(solution)/shard_map/ppermute | solution.py:101
  54.3 7.6 %collective-permute-start.12 = (bf16[272,384]{1,0:T(8,128)(2,1)S(1)}, bf16[272,384]{1,0:T(8,128)(2,1)S(1)}, u32[]{:S(2)}, u32[]{:S(2)}) collective-permute-start(bf16[272,384]{1,0:T(8,128)(2,1)S(1)} %get-tuple-element.169), channel_id=1, source_target_pairs={{0,1},{1,0},{2,3},{3,2},{4,5},{5,4},{6,7},{7,6},{8,9},{9,8},{10,11... | collective-permute-start | bytes 626696 | tf_op jit(solution)/shard_map/ppermute | solution.py:105
  55.9 9.6 %collective-permute-start.20 = (bf16[2,48,1536]{2,1,0:T(8,128)(2,1)S(1)}, bf16[2,48,1536]{2,1,0:T(8,128)(2,1)S(1)}, u32[]{:S(2)}, u32[]{:S(2)}) collective-permute-start(bf16[2,48,1536]{2,1,0:T(8,128)(2,1)S(1)} %pad_maximum_fusion.4.refs_0_), channel_id=1, source_target_pairs={{0,4},{2,6},{4,0},{6,2},{8,12},{10,14},{12,8},{14,10},{16,20},{18,... | collective-permute-start | bytes 884744 | tf_op jit(solution)/shard_map/ppermute | solution.py:101
  57.2 16.5 %collective-permute-start.19 = (bf16[4,48,1536]{2,1,0:T(8,128)(2,1)S(1)}, bf16[4,48,1536]{2,1,0:T(8,128)(2,1)S(1)}, u32[]{:S(2)}, u32[]{:S(2)}) collective-permute-start(bf16[4,48,1536]{2,1,0:T(8,128)(2,1)S(1)} %collective-permute-done.17.refs_1_), channel_id=1, source_target_pairs={{0,2},{2,0},{4,6},{6,4},{8,10},{10,8},{12,14},{14,12},{16,18},{18,... | collective-permute-start | bytes 1769480 | tf_op jit(solution)/shard_map/ppermute | solution.py:101
  60.2 14.1 %collective-permute-start.18 = (bf16[4,48,1536]{2,1,0:T(8,128)(2,1)S(1)}, bf16[4,48,1536]{2,1,0:T(8,128)(2,1)S(1)}, u32[]{:S(2)}, u32[]{:S(2)}) collective-permute-start(bf16[4,48,1536]{2,1,0:T(8,128)(2,1)S(1)} %pad_maximum_fusion.1.refs_0_), channel_id=1, source_target_pairs={{0,2},{2,0},{4,6},{6,4},{8,10},{10,8},{12,14},{14,12},{16,18},{18,... | collective-permute-start | bytes 1769480 | tf_op jit(solution)/shard_map/ppermute | solution.py:101
  63.8 11.3 %collective-permute-start.16 = (bf16[272,768]{1,0:T(8,128)(2,1)S(1)}, bf16[272,768]{1,0:T(8,128)(2,1)S(1)}, u32[]{:S(2)}, u32[]{:S(2)}) collective-permute-start(bf16[272,768]{1,0:T(8,128)(2,1)S(1)} %get-tuple-element.176.normed.a_up), channel_id=1, source_target_pairs={{0,1},{1,0},{2,3},{3,2},{4,5},{5,4},{6,7},{7,6},{8,9},{9,8},{10,11... | collective-permute-start | bytes 1253384 | tf_op jit(solution)/shard_map/ppermute | solution.py:105
  65.4 8.3 %collective-permute-start.21 = (bf16[2,48,1536]{2,1,0:T(8,128)(2,1)S(1)}, bf16[2,48,1536]{2,1,0:T(8,128)(2,1)S(1)}, u32[]{:S(2)}, u32[]{:S(2)}) collective-permute-start(bf16[2,48,1536]{2,1,0:T(8,128)(2,1)S(1)} %collective-permute-done.13.refs_1_), channel_id=1, source_target_pairs={{0,4},{2,6},{4,0},{6,2},{8,12},{10,14},{12,8},{14,10},{16,20},{18,... | collective-permute-start | bytes 884744 | tf_op jit(solution)/shard_map/ppermute | solution.py:101
  66.6 9.6 %collective-permute-start.23 = (bf16[2,48,1536]{2,1,0:T(8,128)(2,1)S(1)}, bf16[2,48,1536]{2,1,0:T(8,128)(2,1)S(1)}, u32[]{:S(2)}, u32[]{:S(2)}) collective-permute-start(bf16[2,48,1536]{2,1,0:T(8,128)(2,1)S(1)} %collective-permute-done.13.refs_1_), channel_id=1, source_target_pairs={{0,2},{2,0},{4,6},{6,4},{8,10},{10,8},{12,14},{14,12},{16,18},{18,... | collective-permute-start | bytes 884744 | tf_op jit(solution)/shard_map/ppermute | solution.py:101
  73.7 2.5 %collective-permute-start.24 = (bf16[2,48,1536]{2,1,0:T(8,128)(2,1)S(1)}, bf16[2,48,1536]{2,1,0:T(8,128)(2,1)S(1)}, u32[]{:S(2)}, u32[]{:S(2)}) collective-permute-start(bf16[2,48,1536]{2,1,0:T(8,128)(2,1)S(1)} %collective-permute-done.20.refs_2_), channel_id=1, source_target_pairs={{0,2},{2,0},{4,6},{6,4},{8,10},{10,8},{12,14},{14,12},{16,18},{18,... | collective-permute-start | bytes 884744 | tf_op jit(solution)/shard_map/ppermute | solution.py:101
  73.7 2.5 %collective-permute-start.22 = (bf16[2,48,1536]{2,1,0:T(8,128)(2,1)S(1)}, bf16[2,48,1536]{2,1,0:T(8,128)(2,1)S(1)}, u32[]{:S(2)}, u32[]{:S(2)}) collective-permute-start(bf16[2,48,1536]{2,1,0:T(8,128)(2,1)S(1)} %pad_maximum_fusion.4.refs_0_), channel_id=1, source_target_pairs={{0,2},{2,0},{4,6},{6,4},{8,10},{10,8},{12,14},{14,12},{16,18},{18,... | collective-permute-start | bytes 884744 | tf_op jit(solution)/shard_map/ppermute | solution.py:101
  74.2 2.0 %collective-permute-start.25 = (bf16[2,48,1536]{2,1,0:T(8,128)(2,1)S(1)}, bf16[2,48,1536]{2,1,0:T(8,128)(2,1)S(1)}, u32[]{:S(2)}, u32[]{:S(2)}) collective-permute-start(bf16[2,48,1536]{2,1,0:T(8,128)(2,1)S(1)} %collective-permute-done.21.refs_3_), channel_id=1, source_target_pairs={{0,2},{2,0},{4,6},{6,4},{8,10},{10,8},{12,14},{14,12},{16,18},{18,... | collective-permute-start | bytes 884744 | tf_op jit(solution)/shard_map/ppermute | solution.py:101
  77.9 7.8 %collective-permute-start.27 = (bf16[144,768]{1,0:T(8,128)(2,1)S(1)}, bf16[144,768]{1,0:T(8,128)(2,1)S(1)}, u32[]{:S(2)}, u32[]{:S(2)}) collective-permute-start(bf16[144,768]{1,0:T(8,128)(2,1)S(1)} %slice.21), channel_id=1, source_target_pairs={{0,1},{1,0},{2,3},{3,2},{4,5},{5,4},{6,7},{7,6},{8,9},{9,8},{10,11... | collective-permute-start | bytes 663560 | tf_op jit(solution)/shard_map/ppermute | solution.py:105
  79.5 1.2 collective-permute-start.26
  83.1 7.2 %collective-permute-start.28 = (bf16[128,768]{1,0:T(8,128)(2,1)S(1)}, bf16[128,768]{1,0:T(8,128)(2,1)S(1)}, u32[]{:S(2)}, u32[]{:S(2)}) collective-permute-start(bf16[128,768]{1,0:T(8,128)(2,1)S(1)} %slice.17), channel_id=1, source_target_pairs={{0,1},{1,0},{2,3},{3,2},{4,5},{5,4},{6,7},{7,6},{8,9},{9,8},{10,11... | collective-permute-start | bytes 589832 | tf_op jit(solution)/shard_map/ppermute | solution.py:105
  86.7 3.6 %collective-permute-start.29 = (bf16[16,128]{1,0:T(8,128)(2,1)S(1)}, bf16[16,128]{1,0:T(8,128)(2,1)S(1)}, u32[]{:S(2)}, u32[]{:S(2)}) collective-permute-start(bf16[16,128]{1,0:T(8,128)(2,1)S(1)} %slice.18), channel_id=1, source_target_pairs={{0,2},{2,0},{4,6},{6,4},{8,10},{10,8},{12,14},{14,12},{16,18},{18,... | collective-permute-start | bytes 12296 | tf_op jit(solution)/shard_map/ppermute | solution.py:101
  86.8 12.3 %collective-permute-start.30 = (bf16[144,768]{1,0:T(8,128)(2,1)S(1)}, bf16[144,768]{1,0:T(8,128)(2,1)S(1)}, u32[]{:S(2)}, u32[]{:S(2)}) collective-permute-start(bf16[144,768]{1,0:T(8,128)(2,1)S(1)} %get-tuple-element.193), channel_id=1, source_target_pairs={{0,1},{1,0},{2,3},{3,2},{4,5},{5,4},{6,7},{7,6},{8,9},{9,8},{10,11... | collective-permute-start | bytes 663560 | tf_op jit(solution)/shard_map/ppermute | solution.py:105
  91.3 7.8 %collective-permute-start.31 = (bf16[128,768]{1,0:T(8,128)(2,1)S(1)}, bf16[128,768]{1,0:T(8,128)(2,1)S(1)}, u32[]{:S(2)}, u32[]{:S(2)}) collective-permute-start(bf16[128,768]{1,0:T(8,128)(2,1)S(1)} %get-tuple-element.198), channel_id=1, source_target_pairs={{0,1},{1,0},{2,3},{3,2},{4,5},{5,4},{6,7},{7,6},{8,9},{9,8},{10,11... | collective-permute-start | bytes 589832 | tf_op jit(solution)/shard_map/ppermute | solution.py:105
  101.0 11.4 %collective-permute-start.32 = (bf16[272,768]{1,0:T(8,128)(2,1)S(1)}, bf16[272,768]{1,0:T(8,128)(2,1)S(1)}, u32[]{:S(2)}, u32[]{:S(2)}) collective-permute-start(bf16[272,768]{1,0:T(8,128)(2,1)S(1)} %convolution_convert_fusion), channel_id=1, source_target_pairs={{0,1},{1,0},{2,3},{3,2},{4,5},{5,4},{6,7},{7,6},{8,9},{9,8},{10,11... | collective-permute-start | bytes 1253384 | tf_op jit(solution)/shard_map/ppermute | solution.py:105
  103.7 1.6 collective-permute-start.37
  103.8 2.0 %collective-permute-start.38 = (bf16[8,48,384]{2,1,0:T(8,128)(2,1)S(1)}, bf16[8,48,384]{2,1,0:T(8,128)(2,1)S(1)}, u32[]{:S(2)}, u32[]{:S(2)}) collective-permute-start(bf16[8,48,384]{2,1,0:T(8,128)(2,1)S(1)} %get-tuple-element.222), channel_id=1, source_target_pairs={{0,2},{2,0},{4,6},{6,4},{8,10},{10,8},{12,14},{14,12},{16,18},{18,... | collective-permute-start | bytes 884744 | tf_op jit(solution)/shard_map/ppermute | solution.py:101
  104.3 1.9 %collective-permute-start.39 = (bf16[8,48,384]{2,1,0:T(8,128)(2,1)S(1)}, bf16[8,48,384]{2,1,0:T(8,128)(2,1)S(1)}, u32[]{:S(2)}, u32[]{:S(2)}) collective-permute-start(bf16[8,48,384]{2,1,0:T(8,128)(2,1)S(1)} %get-tuple-element.223), channel_id=1, source_target_pairs={{0,2},{2,0},{4,6},{6,4},{8,10},{10,8},{12,14},{14,12},{16,18},{18,... | collective-permute-start | bytes 884744 | tf_op jit(solution)/shard_map/ppermute | solution.py:101
  104.4 2.3 %collective-permute-start.40 = (bf16[8,48,384]{2,1,0:T(8,128)(2,1)S(1)}, bf16[8,48,384]{2,1,0:T(8,128)(2,1)S(1)}, u32[]{:S(2)}, u32[]{:S(2)}) collective-permute-start(bf16[8,48,384]{2,1,0:T(8,128)(2,1)S(1)} %get-tuple-element.224), channel_id=1, source_target_pairs={{0,2},{2,0},{4,6},{6,4},{8,10},{10,8},{12,14},{14,12},{16,18},{18,... | collective-permute-start | bytes 884744 | tf_op jit(solution)/shard_map/ppermute | solution.py:101
  107.5 15.4 %collective-permute-start.45 = (bf16[4,48,1536]{2,1,0:T(8,128)(2,1)S(1)}, bf16[4,48,1536]{2,1,0:T(8,128)(2,1)S(1)}, u32[]{:S(2)}, u32[]{:S(2)}) collective-permute-start(bf16[4,48,1536]{2,1,0:T(8,128)(2,1)S(1)} %get-tuple-element.225), channel_id=1, source_target_pairs={{0,4},{2,6},{4,0},{6,2},{8,12},{10,14},{12,8},{14,10},{16,20},{18,... | collective-permute-start | bytes 1769480 | tf_op jit(solution)/shard_map/ppermute | solution.py:101
  110.2 3.8 %collective-permute-start.41 = (bf16[8,48,384]{2,1,0:T(8,128)(2,1)S(1)}, bf16[8,48,384]{2,1,0:T(8,128)(2,1)S(1)}, u32[]{:S(2)}, u32[]{:S(2)}) collective-permute-start(bf16[8,48,384]{2,1,0:T(8,128)(2,1)S(1)} %get-tuple-element.228), channel_id=1, source_target_pairs={{0,2},{2,0},{4,6},{6,4},{8,10},{10,8},{12,14},{14,12},{16,18},{18,... | collective-permute-start | bytes 884744 | tf_op jit(solution)/shard_map/ppermute | solution.py:101
  110.3 5.7 %collective-permute-start.42 = (bf16[8,48,384]{2,1,0:T(8,128)(2,1)S(1)}, bf16[8,48,384]{2,1,0:T(8,128)(2,1)S(1)}, u32[]{:S(2)}, u32[]{:S(2)}) collective-permute-start(bf16[8,48,384]{2,1,0:T(8,128)(2,1)S(1)} %get-tuple-element.229), channel_id=1, source_target_pairs={{0,2},{2,0},{4,6},{6,4},{8,10},{10,8},{12,14},{14,12},{16,18},{18,... | collective-permute-start | bytes 884744 | tf_op jit(solution)/shard_map/ppermute | solution.py:101
  110.8 5.6 %collective-permute-start.43 = (bf16[8,48,384]{2,1,0:T(8,128)(2,1)S(1)}, bf16[8,48,384]{2,1,0:T(8,128)(2,1)S(1)}, u32[]{:S(2)}, u32[]{:S(2)}) collective-permute-start(bf16[8,48,384]{2,1,0:T(8,128)(2,1)S(1)} %get-tuple-element.230), channel_id=1, source_target_pairs={{0,2},{2,0},{4,6},{6,4},{8,10},{10,8},{12,14},{14,12},{16,18},{18,... | collective-permute-start | bytes 884744 | tf_op jit(solution)/shard_map/ppermute | solution.py:101
  112.4 4.2 %collective-permute-start.44 = (bf16[8,48,384]{2,1,0:T(8,128)(2,1)S(1)}, bf16[8,48,384]{2,1,0:T(8,128)(2,1)S(1)}, u32[]{:S(2)}, u32[]{:S(2)}) collective-permute-start(bf16[8,48,384]{2,1,0:T(8,128)(2,1)S(1)} %get-tuple-element.231), channel_id=1, source_target_pairs={{0,2},{2,0},{4,6},{6,4},{8,10},{10,8},{12,14},{14,12},{16,18},{18,... | collective-permute-start | bytes 884744 | tf_op jit(solution)/shard_map/ppermute | solution.py:101
  114.1 9.6 %collective-permute-start.33 = (bf16[272,384]{1,0:T(8,128)(2,1)S(1)}, bf16[272,384]{1,0:T(8,128)(2,1)S(1)}, u32[]{:S(2)}, u32[]{:S(2)}) collective-permute-start(bf16[272,384]{1,0:T(8,128)(2,1)S(1)} %get-tuple-element.207), channel_id=1, source_target_pairs={{0,1},{1,0},{2,3},{3,2},{4,5},{5,4},{6,7},{7,6},{8,9},{9,8},{10,11... | collective-permute-start | bytes 626696 | tf_op jit(solution)/shard_map/ppermute | solution.py:105
  116.1 1.7 collective-permute-start.34
  116.3 1.5 collective-permute-start.35
  116.6 1.5 collective-permute-start.36
  123.6 16.3 %collective-permute-start.46 = (bf16[8,24,768]{2,1,0:T(8,128)(2,1)S(1)}, bf16[8,24,768]{2,1,0:T(8,128)(2,1)S(1)}, u32[]{:S(2)}, u32[]{:S(2)}) collective-permute-start(bf16[8,24,768]{2,1,0:T(8,128)(2,1)S(1)} %get-tuple-element.238), channel_id=1, source_target_pairs={{0,1},{1,0},{2,3},{3,2},{4,5},{5,4},{6,7},{7,6},{8,9},{9,8},{10,11... | collective-permute-start | bytes 884744 | tf_op jit(solution)/shard_map/ppermute | solution.py:105
  125.2 15.2 %collective-permute-start.47 = (bf16[2,48,1536]{2,1,0:T(8,128)(2,1)S(1)}, bf16[2,48,1536]{2,1,0:T(8,128)(2,1)S(1)}, u32[]{:S(2)}, u32[]{:S(2)}) collective-permute-start(bf16[2,48,1536]{2,1,0:T(8,128)(2,1)S(1)} %get-tuple-element.239), channel_id=1, source_target_pairs={{0,16},{2,18},{4,20},{6,22},{8,24},{10,26},{12,28},{14,30},{16,0},... | collective-permute-start | bytes 884744 | tf_op jit(solution)/shard_map/ppermute | solution.py:101
  127.0 14.4 %collective-permute-start.48 = (bf16[4,48,1536]{2,1,0:T(8,128)(2,1)S(1)}, bf16[4,48,1536]{2,1,0:T(8,128)(2,1)S(1)}, u32[]{:S(2)}, u32[]{:S(2)}) collective-permute-start(bf16[4,48,1536]{2,1,0:T(8,128)(2,1)S(1)} %get-tuple-element.253), channel_id=1, source_target_pairs={{0,4},{2,6},{4,0},{6,2},{8,12},{10,14},{12,8},{14,10},{16,20},{18,... | collective-permute-start | bytes 1769480 | tf_op jit(solution)/shard_map/ppermute | solution.py:101
  140.4 2.6 %collective-permute-start.49 = (bf16[8,48,384]{2,1,0:T(8,128)(2,1)S(1)}, bf16[8,48,384]{2,1,0:T(8,128)(2,1)S(1)}, u32[]{:S(2)}, u32[]{:S(2)}) collective-permute-start(bf16[8,48,384]{2,1,0:T(8,128)(2,1)S(1)} %get-tuple-element.255), channel_id=1, source_target_pairs={{0,2},{2,0},{4,6},{6,4},{8,10},{10,8},{12,14},{14,12},{16,18},{18,... | collective-permute-start | bytes 884744 | tf_op jit(solution)/shard_map/ppermute | solution.py:101
  140.4 2.6 %collective-permute-start.50 = (bf16[8,48,384]{2,1,0:T(8,128)(2,1)S(1)}, bf16[8,48,384]{2,1,0:T(8,128)(2,1)S(1)}, u32[]{:S(2)}, u32[]{:S(2)}) collective-permute-start(bf16[8,48,384]{2,1,0:T(8,128)(2,1)S(1)} %get-tuple-element.256), channel_id=1, source_target_pairs={{0,2},{2,0},{4,6},{6,4},{8,10},{10,8},{12,14},{14,12},{16,18},{18,... | collective-permute-start | bytes 884744 | tf_op jit(solution)/shard_map/ppermute | solution.py:101
  140.9 2.1 %collective-permute-start.51 = (bf16[8,48,384]{2,1,0:T(8,128)(2,1)S(1)}, bf16[8,48,384]{2,1,0:T(8,128)(2,1)S(1)}, u32[]{:S(2)}, u32[]{:S(2)}) collective-permute-start(bf16[8,48,384]{2,1,0:T(8,128)(2,1)S(1)} %get-tuple-element.257), channel_id=1, source_target_pairs={{0,2},{2,0},{4,6},{6,4},{8,10},{10,8},{12,14},{14,12},{16,18},{18,... | collective-permute-start | bytes 884744 | tf_op jit(solution)/shard_map/ppermute | solution.py:101
  140.9 2.1 %collective-permute-start.52 = (bf16[8,48,128]{2,1,0:T(8,128)(2,1)S(1)}, bf16[8,48,128]{2,1,0:T(8,128)(2,1)S(1)}, u32[]{:S(2)}, u32[]{:S(2)}) collective-permute-start(bf16[8,48,128]{2,1,0:T(8,128)(2,1)S(1)} %get-tuple-element.258), channel_id=1, source_target_pairs={{0,2},{2,0},{4,6},{6,4},{8,10},{10,8},{12,14},{14,12},{16,18},{18,... | collective-permute-start | bytes 294920 | tf_op jit(solution)/shard_map/ppermute | solution.py:101
  143.0 16.4 %collective-permute-start.57 = (bf16[2,48,1536]{2,1,0:T(8,128)(2,1)S(1)}, bf16[2,48,1536]{2,1,0:T(8,128)(2,1)S(1)}, u32[]{:S(2)}, u32[]{:S(2)}) collective-permute-start(bf16[2,48,1536]{2,1,0:T(8,128)(2,1)S(1)} %get-tuple-element.273), channel_id=1, source_target_pairs={{0,16},{2,18},{4,20},{6,22},{8,24},{10,26},{12,28},{14,30},{16,0},... | collective-permute-start | bytes 884744 | tf_op jit(solution)/shard_map/ppermute | solution.py:101
  144.7 17.0 %collective-permute-start.54 = (bf16[4,24,2048]{2,1,0:T(8,128)(2,1)S(1)}, bf16[4,24,2048]{2,1,0:T(8,128)(2,1)S(1)}, u32[]{:S(2)}, u32[]{:S(2)}) collective-permute-start(bf16[4,24,2048]{2,1,0:T(8,128)(2,1)S(1)} %get-tuple-element.265), channel_id=1, source_target_pairs={{0,4},{2,6},{4,0},{6,2},{8,12},{10,14},{12,8},{14,10},{16,20},{18,... | collective-permute-start | bytes 1179656 | tf_op jit(solution)/shard_map/ppermute | solution.py:101
  146.3 15.4 %collective-permute-start.55 = (bf16[4,24,1280]{2,1,0:T(8,128)(2,1)S(1)}, bf16[4,24,1280]{2,1,0:T(8,128)(2,1)S(1)}, u32[]{:S(2)}, u32[]{:S(2)}) collective-permute-start(bf16[4,24,1280]{2,1,0:T(8,128)(2,1)S(1)} %get-tuple-element.270), channel_id=1, source_target_pairs={{0,1},{1,0},{2,3},{3,2},{4,5},{5,4},{6,7},{7,6},{8,9},{9,8},{10,11... | collective-permute-start | bytes 737288 | tf_op jit(solution)/shard_map/ppermute | solution.py:105
  146.8 14.9 %collective-permute-start.56 = (bf16[4,24,1280]{2,1,0:T(8,128)(2,1)S(1)}, bf16[4,24,1280]{2,1,0:T(8,128)(2,1)S(1)}, u32[]{:S(2)}, u32[]{:S(2)}) collective-permute-start(bf16[4,24,1280]{2,1,0:T(8,128)(2,1)S(1)} %get-tuple-element.271), channel_id=1, source_target_pairs={{0,5},{1,4},{2,7},{3,6},{4,1},{5,0},{6,3},{7,2},{8,13},{9,12},{10,... | collective-permute-start | bytes 737288 | tf_op jit(solution)/shard_map/ppermute | solution.py:114
  148.9 12.8 %collective-permute-start.59 = (bf16[1,48,1536]{2,1,0:T(8,128)(2,1)S(1)}, bf16[1,48,1536]{2,1,0:T(8,128)(2,1)S(1)}, u32[]{:S(2)}, u32[]{:S(2)}) collective-permute-start(bf16[1,48,1536]{2,1,0:T(8,128)(2,1)S(1)} %get-tuple-element.278), channel_id=1, source_target_pairs={{0,8},{2,10},{4,12},{6,14},{8,0},{10,2},{12,4},{14,6},{16,24},{18,... | collective-permute-start | bytes 442376 | tf_op jit(solution)/shard_map/ppermute | solution.py:136
  159.4 1.2 collective-permute-start.58
  160.6 11.7 %collective-permute-start.53 = (bf16[272,768]{1,0:T(8,128)(2,1)S(1)}, bf16[272,768]{1,0:T(8,128)(2,1)S(1)}, u32[]{:S(2)}, u32[]{:S(2)}) collective-permute-start(bf16[272,768]{1,0:T(8,128)(2,1)S(1)} %get-tuple-element.274), channel_id=1, source_target_pairs={{0,1},{1,0},{2,3},{3,2},{4,5},{5,4},{6,7},{7,6},{8,9},{9,8},{10,11... | collective-permute-start | bytes 1253384 | tf_op jit(solution)/shard_map/ppermute | solution.py:105
  161.7 12.2 %collective-permute-start.63 = (bf16[1,48,1536]{2,1,0:T(8,128)(2,1)S(1)}, bf16[1,48,1536]{2,1,0:T(8,128)(2,1)S(1)}, u32[]{:S(2)}, u32[]{:S(2)}) collective-permute-start(bf16[1,48,1536]{2,1,0:T(8,128)(2,1)S(1)} %get-tuple-element.296), channel_id=1, source_target_pairs={{0,8},{2,10},{4,12},{6,14},{8,0},{10,2},{12,4},{14,6},{16,24},{18,... | collective-permute-start | bytes 442376 | tf_op jit(solution)/shard_map/ppermute | solution.py:136
  164.1 10.5 %collective-permute-start.60 = (bf16[1,24,3328]{2,1,0:T(8,128)(2,1)S(1)}, bf16[1,24,3328]{2,1,0:T(8,128)(2,1)S(1)}, u32[]{:S(2)}, u32[]{:S(2)}) collective-permute-start(bf16[1,24,3328]{2,1,0:T(8,128)(2,1)S(1)} %get-tuple-element.282), channel_id=1, source_target_pairs={{0,8},{2,10},{4,12},{6,14},{8,16},{10,18},{12,20},{14,22},{16,24},... | collective-permute-start | bytes 479240 | tf_op jit(solution)/shard_map/ppermute | solution.py:101
  164.6 13.5 %collective-permute-start.61 = (bf16[1,24,3328]{2,1,0:T(8,128)(2,1)S(1)}, bf16[1,24,3328]{2,1,0:T(8,128)(2,1)S(1)}, u32[]{:S(2)}, u32[]{:S(2)}) collective-permute-start(bf16[1,24,3328]{2,1,0:T(8,128)(2,1)S(1)} %get-tuple-element.283), channel_id=1, source_target_pairs={{0,16},{2,18},{4,20},{6,22},{8,24},{10,26},{12,28},{14,30},{16,0},... | collective-permute-start | bytes 479240 | tf_op jit(solution)/shard_map/ppermute | solution.py:101
  165.8 12.3 %collective-permute-start.62 = (bf16[1,24,3328]{2,1,0:T(8,128)(2,1)S(1)}, bf16[1,24,3328]{2,1,0:T(8,128)(2,1)S(1)}, u32[]{:S(2)}, u32[]{:S(2)}) collective-permute-start(bf16[1,24,3328]{2,1,0:T(8,128)(2,1)S(1)} %get-tuple-element.284), channel_id=1, source_target_pairs={{0,24},{2,26},{4,28},{6,30},{8,0},{10,2},{12,4},{14,6},{16,8},{18,... | collective-permute-start | bytes 479240 | tf_op jit(solution)/shard_map/ppermute | solution.py:101
  (2 other events, 19.5 us)

commit v5 on v4

--- a/solution.py
+++ b/solution.py
@@ -860,7 +860,7 @@
     rows_other = swap_tensor(rows_low)
     up_pair = spread_near(tie(ffn_up, packed), digits)
     first_z = spread_outer(packed, digits)
-    first_z, rows_other, up_pair = join(first_z, rows_other, up_pair)
+    rows_other, up_pair = join(rows_other, tie(up_pair, first_z))
     slots = first_z.shape[0]
     mine, other = call(
         functools.partial(halves_of_heads_kernel, part),
@@ -870,8 +870,7 @@
     first_parts = [mine, swap_tensor(other), rotate(mine, x_digit, 1), swap_both(other, x_digit)]
     up_z = spread_far(up_pair, digits)
     down_pair = spread_near(tie(ffn_down.T, mine), digits)
-    up_z, down_in = join(up_z, down_pair)
-    *first_parts, up_z = join(*first_parts, up_z)
+    *first_parts, up_z, down_in = join(*first_parts, up_z, down_pair)
     first_parts = [jnp.concatenate(first_parts[n : n + 2], axis=2) for n in (0, 2)]
     core_parts = [rotate(value, core_digit, 1) for value in first_parts]
     sizes = tuple(size for _, size in digits)

time: 180 us -> 180 us (level)
    ppermute x44, starting transfers between devices: 25.2 us -> 29.1 us  [rotate(): return lax.ppermute(value, 'dp', pairs)]
    ppermute x4, starting transfers between devices: 8.14 us -> 4.94 us  [swap_near(): return lax.ppermute(value, 'dp', pairs)]
    ppermute x4, waiting for transfers between devices: 2.53 us -> 0.01 us  [swap_near(): return lax.ppermute(value, 'dp', pairs)]
    ppermute x44, waiting for transfers between devices: 42.7 us -> 44.7 us  [rotate(): return lax.ppermute(value, 'dp', pairs)]
  transfers between devices with their start and end apart: 64 -> 64, of which waited for: 28 -> 27; matrix products, arithmetic and copies ran while one was open for 5% -> 4% of each run, Pallas kernels for 28% -> 28%
where the time goes in v5:
time: 180 us; the launch traced here: 179 us
  waiting for transfers between devices  61.5 us (34%)
  Pallas kernels  54.6 us (30%)
  starting transfers between devices  49.9 us (28%)
  matrix products  5.27 us (3%)
  other arithmetic  3.41 us (2%)
  between operations  2.5 us (1%)
  local copies, waits for them, and re-layouts  2.12 us (1%)
    pallas_call x32, Pallas kernels, call(): pl.pallas_call(kernel, in_specs=[pl.BlockSpec(memory_space=pltpu.SMEM)] +...  54.6 us
    ppermute x44, waiting for transfers between devices, rotate(): return lax.ppermute(value, 'dp', pairs)  44.7 us
    ppermute x44, starting transfers between devices, rotate(): return lax.ppermute(value, 'dp', pairs)  29.1 us
    ppermute x14, waiting for transfers between devices, swap_tensor(): return lax.ppermute(value, 'tensor', [(0, 1), (1, 0)])  14.6 us
    ppermute x14, starting transfers between devices, swap_tensor(): return lax.ppermute(value, 'tensor', [(0, 1), (1, 0)])  13.9 us
    ppermute x4, starting transfers between devices, swap_near(): return lax.ppermute(value, 'dp', pairs)  4.94 us
  transfers between devices with their start and end apart: 64, of which 27 were waited for; matrix products, arithmetic and copies ran while one was open for 4% of the time, Pallas kernels for 28%

profile of v5, /device:TPU:0, one launch (start us, length us, event | category | flops | bytes accessed | tf_op | source)
XLA Modules:
  0.0 179.4 jit_solution(10886787596148198688)
XLA Ops:
  0.6 1.7 shard_map.204
  2.3 3.0 %collective-permute-start.2 = (bf16[24,3200]{1,0:T(8,128)(2,1)}, bf16[24,3200]{1,0:T(8,128)(2,1)S(1)}, u32[]{:S(2)}, u32[]{:S(2)}) collective-permute-start(bf16[24,3200]{1,0:T(8,128)(2,1)} %shard_map.204), channel_id=1, source_target_pairs={{0,8},{2,10},{4,12},{6,14},{8,16},{10,18},{12,20},{14,22},{16,24},... | collective-permute-start | bytes 460808 | tf_op jit(solution)/shard_map/ppermute | solution.py:101
  5.4 2.6 %collective-permute-start.3 = (bf16[24,3200]{1,0:T(8,128)(2,1)}, bf16[24,3200]{1,0:T(8,128)(2,1)S(1)}, u32[]{:S(2)}, u32[]{:S(2)}) collective-permute-start(bf16[24,3200]{1,0:T(8,128)(2,1)} %shard_map.204), channel_id=1, source_target_pairs={{0,16},{2,18},{4,20},{6,22},{8,24},{10,26},{12,28},{14,30},{16,0},... | collective-permute-start | bytes 460808 | tf_op jit(solution)/shard_map/ppermute | solution.py:101
  8.0 1.3 collective-permute-start.4
  10.0 1.0 pad.4.own
  11.0 1.6 collective-permute-start
  14.7 3.6 %collective-permute-done.3 = bf16[24,3200]{1,0:T(8,128)(2,1)S(1)} collective-permute-done((bf16[24,3200]{1,0:T(8,128)(2,1)}, bf16[24,3200]{1,0:T(8,128)(2,1)S(1)}, u32[]{:S(2)}, u32[]{:S(2)}) %collective-permute-start.3) | collective-permute-done | bytes 153632 | tf_op jit(solution)/shard_map/ppermute | solution.py:101
  18.7 1.0 pad_maximum_fusion.packed
  20.3 3.5 %collective-permute-start.9 = (bf16[48,1536]{1,0:T(8,128)(2,1)S(1)}, bf16[48,1536]{1,0:T(8,128)(2,1)S(1)}, u32[]{:S(2)}, u32[]{:S(2)}) collective-permute-start(bf16[48,1536]{1,0:T(8,128)(2,1)S(1)} %bitcast.75), channel_id=1, source_target_pairs={{0,8},{2,10},{4,12},{6,14},{8,0},{10,2},{12,4},{14,6},{16,24},{18,... | collective-permute-start | bytes 442376 | tf_op jit(solution)/shard_map/ppermute | solution.py:136
  23.8 1.7 collective-permute-start.8
  25.5 1.5 collective-permute-start.6
  27.0 1.5 collective-permute-start.5
  29.1 10.5 %collective-permute-done.8 = bf16[2,48,1536]{2,1,0:T(8,128)(2,1)S(1)} collective-permute-done((bf16[2,48,1536]{2,1,0:T(8,128)(2,1)S(1)}, bf16[2,48,1536]{2,1,0:T(8,128)(2,1)S(1)}, u32[]{:S(2)}, u32[]{:S(2)}) %collective-permute-start.8) | collective-permute-done | bytes 294944 | tf_op jit(solution)/shard_map/ppermute | solution.py:101
  39.7 1.5 collective-permute-done.7
  41.9 1.5 collective-permute-start.17
  44.6 2.3 %collective-permute-start.13 = (bf16[2,48,1536]{2,1,0:T(8,128)(2,1)S(1)}, bf16[2,48,1536]{2,1,0:T(8,128)(2,1)S(1)}, u32[]{:S(2)}, u32[]{:S(2)}) collective-permute-start(bf16[2,48,1536]{2,1,0:T(8,128)(2,1)S(1)} %pad_maximum_fusion.4.refs_0_), channel_id=1, source_target_pairs={{0,16},{2,18},{4,20},{6,22},{8,24},{10,26},{12,28},{14,30},{16,0},... | collective-permute-start | bytes 884744 | tf_op jit(solution)/shard_map/ppermute | solution.py:101
  47.6 7.8 %shard_map.207 = (bf16[544,1152]{1,0:T(8,128)(2,1)S(1)}, bf16[272,384]{1,0:T(8,128)(2,1)S(1)}, bf16[272,384]{1,0:T(8,128)(2,1)S(1)}, f32[544,128]{1,0:T(8,128)S(...) custom-call(s32[15]{0:T(128)S(1)} %concatenate.21.at, bf16[272,768]{1,0:T(8,128)(2,1)S(1)} %pad.4.own, ...), custom_call_target="tpu_custom_call" | custom-call | flops 1 | bytes 1 | tf_op jit(solution)/shard_map/pallas_call | solution.py:61
  55.6 1.6 collective-permute-start.12
  57.7 2.5 %collective-permute-done.13.refs_1_ = bf16[2,48,1536]{2,1,0:T(8,128)(2,1)S(1)} collective-permute-done((bf16[2,48,1536]{2,1,0:T(8,128)(2,1)S(1)}, bf16[2,48,1536]{2,1,0:T(8,128)(2,1)S(1)}, u32[]{:S(2)}, u32[]{:S(2)}) %collective-permute-start.13) | collective-permute-done | bytes 294944 | tf_op jit(solution)/shard_map/ppermute | solution.py:101
  60.2 2.9 %collective-permute-done.12.got = bf16[272,384]{1,0:T(8,128)(2,1)S(1)} collective-permute-done((bf16[272,384]{1,0:T(8,128)(2,1)S(1)}, bf16[272,384]{1,0:T(8,128)(2,1)S(1)}, u32[]{:S(2)}, u32[]{:S(2)}) %collective-permute-start.12) | collective-permute-done | bytes 208928 | tf_op jit(solution)/shard_map/ppermute | solution.py:105
  63.8 1.3 shard_map.210
  65.1 1.6 collective-permute-start.16
  68.0 7.0 %collective-permute-done.21.refs_3_ = bf16[2,48,1536]{2,1,0:T(8,128)(2,1)S(1)} collective-permute-done((bf16[2,48,1536]{2,1,0:T(8,128)(2,1)S(1)}, bf16[2,48,1536]{2,1,0:T(8,128)(2,1)S(1)}, u32[]{:S(2)}, u32[]{:S(2)}) %collective-permute-start.21) | collective-permute-done | bytes 294944 | tf_op jit(solution)/shard_map/ppermute | solution.py:101
  76.6 0.9 multiply_convert_fusion
  78.3 0.8 convolution_convert_fusion.1
  79.1 1.6 collective-permute-start.27
  80.7 1.2 collective-permute-done.26._
  81.9 2.4 %shard_map.214 = (bf16[272,1536]{1,0:T(8,128)(2,1)S(1)}, f32[272,1536]{1,0:T(8,128)S(1)}, f32[272,768]{1,0:T(8,128)S(1)}) custom-call(s32[15]{0:T(128)S(1)} %concatenate.21.at, bf16[272,768]{1,0:T(8,128)(2,1)S(1)} %get-tuple-element.174.normed.a_up, bf16[768,1536]{1,0:T(8,128)(2,1)S(1)} %bitcast.57, f32[16,1536]{1,0:T(8,128)S(1)} %shard_map.211.up_b, ...), custom_call_target="tpu_custom_call" | custom-call | flops 1 | bytes 1 | tf_op jit(solution)/shard_map/pallas_call | solution.py:61
  85.0 2.0 %collective-permute-done.27.got = bf16[144,768]{1,0:T(8,128)(2,1)S(1)} collective-permute-done((bf16[144,768]{1,0:T(8,128)(2,1)S(1)}, bf16[144,768]{1,0:T(8,128)(2,1)S(1)}, u32[]{:S(2)}, u32[]{:S(2)}) %collective-permute-start.27) | collective-permute-done | bytes 221216 | tf_op jit(solution)/shard_map/ppermute | solution.py:105
  86.9 1.0 shard_map.215
  88.6 2.9 %collective-permute-done.28.got = bf16[128,768]{1,0:T(8,128)(2,1)S(1)} collective-permute-done((bf16[128,768]{1,0:T(8,128)(2,1)S(1)}, bf16[128,768]{1,0:T(8,128)(2,1)S(1)}, u32[]{:S(2)}, u32[]{:S(2)}) %collective-permute-start.28) | collective-permute-done | bytes 196640 | tf_op jit(solution)/shard_map/ppermute | solution.py:105
  91.5 1.0 shard_map.216
  93.2 0.8 fusion.b_up
  94.0 3.7 %shard_map.217 = (f32[768,1536]{1,0:T(8,128)S(1)}, f32[768,1536]{1,0:T(8,128)S(1)}, f32[1,1536]{1,0:T(1,128)S(1)}) custom-call(s32[15]{0:T(128)S(1)} %concatenate.21.at, bf16[272,768]{1,0:T(8,128)(2,1)S(1)} %constant_dynamic-update-slice_fusion.4.a_down, bf16[272,1536]{1,0:T(8,128)(2,1)S(1)} %get-tuple-element.198.b_down, ...), custom_call_target="tpu_custom_call" | custom-call | flops 1 | bytes 1 | tf_op jit(solution)/shard_map/pallas_call | solution.py:61
  97.7 0.8 fusion.6.own
  98.5 1.8 %collective-permute-done.31 = bf16[128,768]{1,0:T(8,128)(2,1)S(1)} collective-permute-done((bf16[128,768]{1,0:T(8,128)(2,1)S(1)}, bf16[128,768]{1,0:T(8,128)(2,1)S(1)}, u32[]{:S(2)}, u32[]{:S(2)}) %collective-permute-start.31) | collective-permute-done | bytes 196640 | tf_op jit(solution)/shard_map/ppermute | solution.py:105
  100.4 1.0 fusion.1.b
  101.4 0.8 convolution_convert_fusion
  102.8 2.2 %shard_map.221 = (bf16[8,48,1536]{2,1,0:T(8,128)(2,1)S(1)}, bf16[8,48,384]{2,1,0:T(8,128)(2,1)S(1)}, bf16[8,48,384]{2,1,0:T(8,128)(2,1)S(1)}, bf16[8,48,384]{2,1,0:T(8,128)(2,1)S(1)}, bf16[8,48,384]{2,1,0:T(8,128)(2,1)S(1)}) custom-call(s32[15]{0:T(128)S(1)} %concatenate.21.at, f32[768,1536]{1,0:T(8,128)S(1)} %get-tuple-element.216.own, ...), custom_call_target="tpu_custom_call" | custom-call | flops 1 | bytes 1 | tf_op jit(solution)/shard_map/pallas_call | solution.py:61
  107.9 0.8 shard_map.222
  109.4 2.1 %shard_map.223 = (f32[1,1536]{1,0:T(1,128)S(1)}, bf16[8,48,1536]{2,1,0:T(8,128)(2,1)S(1)}, bf16[8,48,384]{2,1,0:T(8,128)(2,1)S(1)}, bf16[8,48,384]{2,1,0:T(8,128...) custom-call(s32[15]{0:T(128)S(1)} %concatenate.21.at, ...), custom_call_target="tpu_custom_call" | custom-call | flops 1 | bytes 1 | tf_op jit(solution)/shard_map/pallas_call | solution.py:61
  112.2 1.5 collective-permute-done.32.got
  113.7 1.6 shard_map.218
  115.9 1.4 shard_map.219
  118.1 0.8 shard_map.224
  120.1 4.1 %collective-permute-done.45.got = bf16[4,48,1536]{2,1,0:T(8,128)(2,1)S(1)} collective-permute-done((bf16[4,48,1536]{2,1,0:T(8,128)(2,1)S(1)}, bf16[4,48,1536]{2,1,0:T(8,128)(2,1)S(1)}, u32[]{:S(2)}, u32[]{:S(2)}) %collective-permute-start.45) | collective-permute-done | bytes 589856 | tf_op jit(solution)/shard_map/ppermute | solution.py:101
  124.9 1.6 collective-permute-start.46
  127.6 9.6 %shard_map.226 = (bf16[544,1152]{1,0:T(8,128)(2,1)S(1)}, f32[1,1152]{1,0:T(1,128)S(1)}) custom-call(s32[15]{0:T(128)S(1)} %concatenate.21.at, bf16[544,1152]{1,0:T(8,128)(2,1)S(1)} %get-tuple-element.193.qkv, bf16[272,384]{1,0:T(8,128)(2,1)S(1)} %get-tuple-element.204.own, bf16[272,384]{1,0:T(8,128)(2,1)S(1)} %collective-permute-done.33.got, ...), custom_call_target="tpu_custom_call" | custom-call | flops 1 | bytes 1 | tf_op jit(solution)/shard_map/pallas_call | solution.py:61
  137.3 2.7 %shard_map.227 = (bf16[8,48,1280]{2,1,0:T(8,128)(2,1)S(1)}, bf16[8,48,384]{2,1,0:T(8,128)(2,1)S(1)}, bf16[8,48,384]{2,1,0:T(8,128)(2,1)S(1)}, bf16[8,48,384]{2,1,0:T(8,128)(2,1)S(1)}, bf16[8,48,128]{2,1,0:T(8,128)(2,1)S(1)}) custom-call(s32[15]{0:T(128)S(1)} %concatenate.21.at, bf16[544,768]{1,0:T(8,128)(2,1)S(1)} %get-tuple-element.171.layer_in, ...), custom_call_target="tpu_custom_call" | custom-call | flops 1 | bytes 1 | tf_op jit(solution)/shard_map/pallas_call | solution.py:61
  140.0 1.4 collective-permute-done.47.got
  143.1 0.9 collective-permute-done.52.refs_3_
  144.0 1.1 collective-permute-start.57
  145.1 0.9 shard_map.229
  146.0 1.6 collective-permute-start.54
  148.0 1.5 collective-permute-start.56
  150.6 1.8 %shard_map.230 = (f32[272,768]{1,0:T(8,128)S(1)}, bf16[272,768]{1,0:T(8,128)(2,1)S(1)}) custom-call(s32[15]{0:T(128)S(1)} %concatenate.21.at, bf16[544,1152]{1,0:T(8,128)(2,1)S(1)} %get-tuple-element.264.d_projected, bf16[768,1280]{1,0:T(8,128)(2,1)S(1)} %bitcast.51, f32[272,768]{1,0:T(8,128)S(1)} %get-tuple-element.243.d_attn), custom_call_target="tpu_custom_call" | custom-call | flops 1 | bytes 1 | tf_op jit(solution)/shard_map/pallas_call | solution.py:61
  152.4 6.6 %collective-permute-done.57.got = bf16[2,48,1536]{2,1,0:T(8,128)(2,1)S(1)} collective-permute-done((bf16[2,48,1536]{2,1,0:T(8,128)(2,1)S(1)}, bf16[2,48,1536]{2,1,0:T(8,128)(2,1)S(1)}, u32[]{:S(2)}, u32[]{:S(2)}) %collective-permute-start.57) | collective-permute-done | bytes 294944 | tf_op jit(solution)/shard_map/ppermute | solution.py:101
  163.2 1.7 collective-permute-start.60
  164.9 2.0 %collective-permute-start.61 = (bf16[1,24,3328]{2,1,0:T(8,128)(2,1)S(1)}, bf16[1,24,3328]{2,1,0:T(8,128)(2,1)S(1)}, u32[]{:S(2)}, u32[]{:S(2)}) collective-permute-start(bf16[1,24,3328]{2,1,0:T(8,128)(2,1)S(1)} %get-tuple-element.281), channel_id=1, source_target_pairs={{0,16},{2,18},{4,20},{6,22},{8,24},{10,26},{12,28},{14,30},{16,0},... | collective-permute-start | bytes 479240 | tf_op jit(solution)/shard_map/ppermute | solution.py:101
  166.9 0.9 collective-permute-start.62
  168.6 3.3 %collective-permute-done.53.got = bf16[272,768]{1,0:T(8,128)(2,1)S(1)} collective-permute-done((bf16[272,768]{1,0:T(8,128)(2,1)S(1)}, bf16[272,768]{1,0:T(8,128)(2,1)S(1)}, u32[]{:S(2)}, u32[]{:S(2)}) %collective-permute-start.53) | collective-permute-done | bytes 417824 | tf_op jit(solution)/shard_map/ppermute | solution.py:105
  171.9 1.6 shard_map.231
  174.3 3.7 %collective-permute-done.61 = bf16[1,24,3328]{2,1,0:T(8,128)(2,1)S(1)} collective-permute-done((bf16[1,24,3328]{2,1,0:T(8,128)(2,1)S(1)}, bf16[1,24,3328]{2,1,0:T(8,128)(2,1)S(1)}, u32[]{:S(2)}, u32[]{:S(2)}) %collective-permute-start.61) | collective-permute-done | bytes 159776 | tf_op jit(solution)/shard_map/ppermute | solution.py:101
  178.1 1.3 shard_map.235
  (130 shorter events, 30.3 us)
Async XLA Ops:
  2.3 12.3 %collective-permute-start.2 = (bf16[24,3200]{1,0:T(8,128)(2,1)}, bf16[24,3200]{1,0:T(8,128)(2,1)S(1)}, u32[]{:S(2)}, u32[]{:S(2)}) collective-permute-start(bf16[24,3200]{1,0:T(8,128)(2,1)} %shard_map.204), channel_id=1, source_target_pairs={{0,8},{2,10},{4,12},{6,14},{8,16},{10,18},{12,20},{14,22},{16,24},... | collective-permute-start | bytes 460808 | tf_op jit(solution)/shard_map/ppermute | solution.py:101
  5.4 12.9 %collective-permute-start.3 = (bf16[24,3200]{1,0:T(8,128)(2,1)}, bf16[24,3200]{1,0:T(8,128)(2,1)S(1)}, u32[]{:S(2)}, u32[]{:S(2)}) collective-permute-start(bf16[24,3200]{1,0:T(8,128)(2,1)} %shard_map.204), channel_id=1, source_target_pairs={{0,16},{2,18},{4,20},{6,22},{8,24},{10,26},{12,28},{14,30},{16,0},... | collective-permute-start | bytes 460808 | tf_op jit(solution)/shard_map/ppermute | solution.py:101
  8.0 10.7 %collective-permute-start.4 = (bf16[24,3200]{1,0:T(8,128)(2,1)}, bf16[24,3200]{1,0:T(8,128)(2,1)S(1)}, u32[]{:S(2)}, u32[]{:S(2)}) collective-permute-start(bf16[24,3200]{1,0:T(8,128)(2,1)} %shard_map.204), channel_id=1, source_target_pairs={{0,24},{2,26},{4,28},{6,30},{8,0},{10,2},{12,4},{14,6},{16,8},{18,... | collective-permute-start | bytes 460808 | tf_op jit(solution)/shard_map/ppermute | solution.py:101
  9.3 14.5 %collective-permute-start.1 = (bf16[48,1536]{1,0:T(8,128)(2,1)}, bf16[48,1536]{1,0:T(8,128)(2,1)S(1)}, u32[]{:S(2)}, u32[]{:S(2)}) collective-permute-start(bf16[48,1536]{1,0:T(8,128)(2,1)} %param.23), channel_id=1, source_target_pairs={{0,8},{2,10},{4,12},{6,14},{8,0},{10,2},{12,4},{14,6},{16,24},{18,... | collective-permute-start | bytes 442376 | tf_op jit(solution)/shard_map/ppermute | solution.py:136
  11.0 12.8 %collective-permute-start = (bf16[272,768]{1,0:T(8,128)(2,1)S(1)}, bf16[272,768]{1,0:T(8,128)(2,1)S(1)}, u32[]{:S(2)}, u32[]{:S(2)}) collective-permute-start(bf16[272,768]{1,0:T(8,128)(2,1)S(1)} %pad.4.own), channel_id=1, source_target_pairs={{0,1},{1,0},{2,3},{3,2},{4,5},{5,4},{6,7},{7,6},{8,9},{9,8},{10,11... | collective-permute-start | bytes 1253384 | tf_op jit(solution)/shard_map/ppermute | solution.py:105
  20.3 8.7 %collective-permute-start.9 = (bf16[48,1536]{1,0:T(8,128)(2,1)S(1)}, bf16[48,1536]{1,0:T(8,128)(2,1)S(1)}, u32[]{:S(2)}, u32[]{:S(2)}) collective-permute-start(bf16[48,1536]{1,0:T(8,128)(2,1)S(1)} %bitcast.75), channel_id=1, source_target_pairs={{0,8},{2,10},{4,12},{6,14},{8,0},{10,2},{12,4},{14,6},{16,24},{18,... | collective-permute-start | bytes 442376 | tf_op jit(solution)/shard_map/ppermute | solution.py:136
  23.8 15.8 %collective-permute-start.8 = (bf16[2,48,1536]{2,1,0:T(8,128)(2,1)S(1)}, bf16[2,48,1536]{2,1,0:T(8,128)(2,1)S(1)}, u32[]{:S(2)}, u32[]{:S(2)}) collective-permute-start(bf16[2,48,1536]{2,1,0:T(8,128)(2,1)S(1)} %pad_maximum_fusion.3), channel_id=1, source_target_pairs={{0,16},{2,18},{4,20},{6,22},{8,24},{10,26},{12,28},{14,30},{16,0},... | collective-permute-start | bytes 884744 | tf_op jit(solution)/shard_map/ppermute | solution.py:101
  25.5 15.6 %collective-permute-start.6 = (bf16[4,24,2048]{2,1,0:T(8,128)(2,1)S(1)}, bf16[4,24,2048]{2,1,0:T(8,128)(2,1)S(1)}, u32[]{:S(2)}, u32[]{:S(2)}) collective-permute-start(bf16[4,24,2048]{2,1,0:T(8,128)(2,1)S(1)} %get-tuple-element.162), channel_id=1, source_target_pairs={{0,4},{2,6},{4,0},{6,2},{8,12},{10,14},{12,8},{14,10},{16,20},{18,... | collective-permute-start | bytes 1179656 | tf_op jit(solution)/shard_map/ppermute | solution.py:101
  27.0 12.6 %collective-permute-start.5 = (bf16[4,24,1280]{2,1,0:T(8,128)(2,1)S(1)}, bf16[4,24,1280]{2,1,0:T(8,128)(2,1)S(1)}, u32[]{:S(2)}, u32[]{:S(2)}) collective-permute-start(bf16[4,24,1280]{2,1,0:T(8,128)(2,1)S(1)} %get-tuple-element.159), channel_id=1, source_target_pairs={{0,1},{1,0},{2,3},{3,2},{4,5},{5,4},{6,7},{7,6},{8,9},{9,8},{10,11... | collective-permute-start | bytes 737288 | tf_op jit(solution)/shard_map/ppermute | solution.py:105
  28.6 12.6 %collective-permute-start.7 = (bf16[4,24,1280]{2,1,0:T(8,128)(2,1)S(1)}, bf16[4,24,1280]{2,1,0:T(8,128)(2,1)S(1)}, u32[]{:S(2)}, u32[]{:S(2)}) collective-permute-start(bf16[4,24,1280]{2,1,0:T(8,128)(2,1)S(1)} %get-tuple-element.159), channel_id=1, source_target_pairs={{0,5},{1,4},{2,7},{3,6},{4,1},{5,0},{6,3},{7,2},{8,13},{9,12},{10,... | collective-permute-start | bytes 737288 | tf_op jit(solution)/shard_map/ppermute | solution.py:114
  41.2 5.7 %collective-permute-start.11 = (bf16[4,24,3328]{2,1,0:T(8,128)(2,1)S(1)}, bf16[4,24,3328]{2,1,0:T(8,128)(2,1)S(1)}, u32[]{:S(2)}, u32[]{:S(2)}) collective-permute-start(bf16[4,24,3328]{2,1,0:T(8,128)(2,1)S(1)} %constant_dynamic-update-slice_fusion.2.refs_1_.x_got), channel_id=1, source_target_pairs={{0,2},{2,0},{4,6},{6,4},{8,10},{10,8},{12,14},{14,12},{16,18},{18,... | collective-permute-start | bytes 1916936 | tf_op jit(solution)/shard_map/ppermute | solution.py:101
  41.4 5.5 %collective-permute-start.10 = (bf16[4,24,3328]{2,1,0:T(8,128)(2,1)S(1)}, bf16[4,24,3328]{2,1,0:T(8,128)(2,1)S(1)}, u32[]{:S(2)}, u32[]{:S(2)}) collective-permute-start(bf16[4,24,3328]{2,1,0:T(8,128)(2,1)S(1)} %constant_dynamic-update-slice_fusion.refs_0_.mine), channel_id=1, source_target_pairs={{0,2},{2,0},{4,6},{6,4},{8,10},{10,8},{12,14},{14,12},{16,18},{18,... | collective-permute-start | bytes 1916936 | tf_op jit(solution)/shard_map/ppermute | solution.py:101
  41.9 15.7 %collective-permute-start.17 = (bf16[4,48,1536]{2,1,0:T(8,128)(2,1)S(1)}, bf16[4,48,1536]{2,1,0:T(8,128)(2,1)S(1)}, u32[]{:S(2)}, u32[]{:S(2)}) collective-permute-start(bf16[4,48,1536]{2,1,0:T(8,128)(2,1)S(1)} %pad_maximum_fusion.1.refs_0_), channel_id=1, source_target_pairs={{0,4},{2,6},{4,0},{6,2},{8,12},{10,14},{12,8},{14,10},{16,20},{18,... | collective-permute-start | bytes 1769480 | tf_op jit(solution)/shard_map/ppermute | solution.py:101
  44.0 11.5 %collective-permute-start.14 = (bf16[8,24,768]{2,1,0:T(8,128)(2,1)S(1)}, bf16[8,24,768]{2,1,0:T(8,128)(2,1)S(1)}, u32[]{:S(2)}, u32[]{:S(2)}) collective-permute-start(bf16[8,24,768]{2,1,0:T(8,128)(2,1)S(1)} %shard_map.208), channel_id=1, source_target_pairs={{0,1},{1,0},{2,3},{3,2},{4,5},{5,4},{6,7},{7,6},{8,9},{9,8},{10,11... | collective-permute-start | bytes 884744 | tf_op jit(solution)/shard_map/ppermute | solution.py:105
  44.6 15.6 %collective-permute-start.13 = (bf16[2,48,1536]{2,1,0:T(8,128)(2,1)S(1)}, bf16[2,48,1536]{2,1,0:T(8,128)(2,1)S(1)}, u32[]{:S(2)}, u32[]{:S(2)}) collective-permute-start(bf16[2,48,1536]{2,1,0:T(8,128)(2,1)S(1)} %pad_maximum_fusion.4.refs_0_), channel_id=1, source_target_pairs={{0,16},{2,18},{4,20},{6,22},{8,24},{10,26},{12,28},{14,30},{16,0},... | collective-permute-start | bytes 884744 | tf_op jit(solution)/shard_map/ppermute | solution.py:101
  55.5 7.7 %collective-permute-start.15 = (bf16[8,24,768]{2,1,0:T(8,128)(2,1)S(1)}, bf16[8,24,768]{2,1,0:T(8,128)(2,1)S(1)}, u32[]{:S(2)}, u32[]{:S(2)}) collective-permute-start(bf16[8,24,768]{2,1,0:T(8,128)(2,1)S(1)} %collective-permute-done.14.refs_4_), channel_id=1, source_target_pairs={{0,2},{2,0},{4,6},{6,4},{8,10},{10,8},{12,14},{14,12},{16,18},{18,... | collective-permute-start | bytes 884744 | tf_op jit(solution)/shard_map/ppermute | solution.py:101
  55.6 7.6 %collective-permute-start.12 = (bf16[272,384]{1,0:T(8,128)(2,1)S(1)}, bf16[272,384]{1,0:T(8,128)(2,1)S(1)}, u32[]{:S(2)}, u32[]{:S(2)}) collective-permute-start(bf16[272,384]{1,0:T(8,128)(2,1)S(1)} %get-tuple-element.167), channel_id=1, source_target_pairs={{0,1},{1,0},{2,3},{3,2},{4,5},{5,4},{6,7},{7,6},{8,9},{9,8},{10,11... | collective-permute-start | bytes 626696 | tf_op jit(solution)/shard_map/ppermute | solution.py:105
  57.2 9.6 %collective-permute-start.20 = (bf16[2,48,1536]{2,1,0:T(8,128)(2,1)S(1)}, bf16[2,48,1536]{2,1,0:T(8,128)(2,1)S(1)}, u32[]{:S(2)}, u32[]{:S(2)}) collective-permute-start(bf16[2,48,1536]{2,1,0:T(8,128)(2,1)S(1)} %pad_maximum_fusion.4.refs_0_), channel_id=1, source_target_pairs={{0,4},{2,6},{4,0},{6,2},{8,12},{10,14},{12,8},{14,10},{16,20},{18,... | collective-permute-start | bytes 884744 | tf_op jit(solution)/shard_map/ppermute | solution.py:101
  57.7 17.3 %collective-permute-start.19 = (bf16[4,48,1536]{2,1,0:T(8,128)(2,1)S(1)}, bf16[4,48,1536]{2,1,0:T(8,128)(2,1)S(1)}, u32[]{:S(2)}, u32[]{:S(2)}) collective-permute-start(bf16[4,48,1536]{2,1,0:T(8,128)(2,1)S(1)} %collective-permute-done.17.refs_1_), channel_id=1, source_target_pairs={{0,2},{2,0},{4,6},{6,4},{8,10},{10,8},{12,14},{14,12},{16,18},{18,... | collective-permute-start | bytes 1769480 | tf_op jit(solution)/shard_map/ppermute | solution.py:101
  60.2 15.3 %collective-permute-start.18 = (bf16[4,48,1536]{2,1,0:T(8,128)(2,1)S(1)}, bf16[4,48,1536]{2,1,0:T(8,128)(2,1)S(1)}, u32[]{:S(2)}, u32[]{:S(2)}) collective-permute-start(bf16[4,48,1536]{2,1,0:T(8,128)(2,1)S(1)} %pad_maximum_fusion.1.refs_0_), channel_id=1, source_target_pairs={{0,2},{2,0},{4,6},{6,4},{8,10},{10,8},{12,14},{14,12},{16,18},{18,... | collective-permute-start | bytes 1769480 | tf_op jit(solution)/shard_map/ppermute | solution.py:101
  65.1 11.3 %collective-permute-start.16 = (bf16[272,768]{1,0:T(8,128)(2,1)S(1)}, bf16[272,768]{1,0:T(8,128)(2,1)S(1)}, u32[]{:S(2)}, u32[]{:S(2)}) collective-permute-start(bf16[272,768]{1,0:T(8,128)(2,1)S(1)} %get-tuple-element.174.normed.a_up), channel_id=1, source_target_pairs={{0,1},{1,0},{2,3},{3,2},{4,5},{5,4},{6,7},{7,6},{8,9},{9,8},{10,11... | collective-permute-start | bytes 1253384 | tf_op jit(solution)/shard_map/ppermute | solution.py:105
  66.7 8.3 %collective-permute-start.21 = (bf16[2,48,1536]{2,1,0:T(8,128)(2,1)S(1)}, bf16[2,48,1536]{2,1,0:T(8,128)(2,1)S(1)}, u32[]{:S(2)}, u32[]{:S(2)}) collective-permute-start(bf16[2,48,1536]{2,1,0:T(8,128)(2,1)S(1)} %collective-permute-done.13.refs_1_), channel_id=1, source_target_pairs={{0,4},{2,6},{4,0},{6,2},{8,12},{10,14},{12,8},{14,10},{16,20},{18,... | collective-permute-start | bytes 884744 | tf_op jit(solution)/shard_map/ppermute | solution.py:101
  67.9 9.6 %collective-permute-start.23 = (bf16[2,48,1536]{2,1,0:T(8,128)(2,1)S(1)}, bf16[2,48,1536]{2,1,0:T(8,128)(2,1)S(1)}, u32[]{:S(2)}, u32[]{:S(2)}) collective-permute-start(bf16[2,48,1536]{2,1,0:T(8,128)(2,1)S(1)} %collective-permute-done.13.refs_1_), channel_id=1, source_target_pairs={{0,2},{2,0},{4,6},{6,4},{8,10},{10,8},{12,14},{14,12},{16,18},{18,... | collective-permute-start | bytes 884744 | tf_op jit(solution)/shard_map/ppermute | solution.py:101
  75.0 2.5 %collective-permute-start.24 = (bf16[2,48,1536]{2,1,0:T(8,128)(2,1)S(1)}, bf16[2,48,1536]{2,1,0:T(8,128)(2,1)S(1)}, u32[]{:S(2)}, u32[]{:S(2)}) collective-permute-start(bf16[2,48,1536]{2,1,0:T(8,128)(2,1)S(1)} %collective-permute-done.20.refs_2_), channel_id=1, source_target_pairs={{0,2},{2,0},{4,6},{6,4},{8,10},{10,8},{12,14},{14,12},{16,18},{18,... | collective-permute-start | bytes 884744 | tf_op jit(solution)/shard_map/ppermute | solution.py:101
  75.0 2.5 %collective-permute-start.22 = (bf16[2,48,1536]{2,1,0:T(8,128)(2,1)S(1)}, bf16[2,48,1536]{2,1,0:T(8,128)(2,1)S(1)}, u32[]{:S(2)}, u32[]{:S(2)}) collective-permute-start(bf16[2,48,1536]{2,1,0:T(8,128)(2,1)S(1)} %pad_maximum_fusion.4.refs_0_), channel_id=1, source_target_pairs={{0,2},{2,0},{4,6},{6,4},{8,10},{10,8},{12,14},{14,12},{16,18},{18,... | collective-permute-start | bytes 884744 | tf_op jit(solution)/shard_map/ppermute | solution.py:101
  75.5 2.0 %collective-permute-start.25 = (bf16[2,48,1536]{2,1,0:T(8,128)(2,1)S(1)}, bf16[2,48,1536]{2,1,0:T(8,128)(2,1)S(1)}, u32[]{:S(2)}, u32[]{:S(2)}) collective-permute-start(bf16[2,48,1536]{2,1,0:T(8,128)(2,1)S(1)} %collective-permute-done.21.refs_3_), channel_id=1, source_target_pairs={{0,2},{2,0},{4,6},{6,4},{8,10},{10,8},{12,14},{14,12},{16,18},{18,... | collective-permute-start | bytes 884744 | tf_op jit(solution)/shard_map/ppermute | solution.py:101
  79.1 7.8 %collective-permute-start.27 = (bf16[144,768]{1,0:T(8,128)(2,1)S(1)}, bf16[144,768]{1,0:T(8,128)(2,1)S(1)}, u32[]{:S(2)}, u32[]{:S(2)}) collective-permute-start(bf16[144,768]{1,0:T(8,128)(2,1)S(1)} %slice.21), channel_id=1, source_target_pairs={{0,1},{1,0},{2,3},{3,2},{4,5},{5,4},{6,7},{7,6},{8,9},{9,8},{10,11... | collective-permute-start | bytes 663560 | tf_op jit(solution)/shard_map/ppermute | solution.py:105
  80.7 1.2 collective-permute-start.26
  84.4 7.2 %collective-permute-start.28 = (bf16[128,768]{1,0:T(8,128)(2,1)S(1)}, bf16[128,768]{1,0:T(8,128)(2,1)S(1)}, u32[]{:S(2)}, u32[]{:S(2)}) collective-permute-start(bf16[128,768]{1,0:T(8,128)(2,1)S(1)} %slice.17), channel_id=1, source_target_pairs={{0,1},{1,0},{2,3},{3,2},{4,5},{5,4},{6,7},{7,6},{8,9},{9,8},{10,11... | collective-permute-start | bytes 589832 | tf_op jit(solution)/shard_map/ppermute | solution.py:105
  88.0 3.6 %collective-permute-start.29 = (bf16[16,128]{1,0:T(8,128)(2,1)S(1)}, bf16[16,128]{1,0:T(8,128)(2,1)S(1)}, u32[]{:S(2)}, u32[]{:S(2)}) collective-permute-start(bf16[16,128]{1,0:T(8,128)(2,1)S(1)} %slice.18), channel_id=1, source_target_pairs={{0,2},{2,0},{4,6},{6,4},{8,10},{10,8},{12,14},{14,12},{16,18},{18,... | collective-permute-start | bytes 12296 | tf_op jit(solution)/shard_map/ppermute | solution.py:101
  88.1 12.3 %collective-permute-start.30 = (bf16[144,768]{1,0:T(8,128)(2,1)S(1)}, bf16[144,768]{1,0:T(8,128)(2,1)S(1)}, u32[]{:S(2)}, u32[]{:S(2)}) collective-permute-start(bf16[144,768]{1,0:T(8,128)(2,1)S(1)} %get-tuple-element.191), channel_id=1, source_target_pairs={{0,1},{1,0},{2,3},{3,2},{4,5},{5,4},{6,7},{7,6},{8,9},{9,8},{10,11... | collective-permute-start | bytes 663560 | tf_op jit(solution)/shard_map/ppermute | solution.py:105
  92.5 7.8 %collective-permute-start.31 = (bf16[128,768]{1,0:T(8,128)(2,1)S(1)}, bf16[128,768]{1,0:T(8,128)(2,1)S(1)}, u32[]{:S(2)}, u32[]{:S(2)}) collective-permute-start(bf16[128,768]{1,0:T(8,128)(2,1)S(1)} %get-tuple-element.196), channel_id=1, source_target_pairs={{0,1},{1,0},{2,3},{3,2},{4,5},{5,4},{6,7},{7,6},{8,9},{9,8},{10,11... | collective-permute-start | bytes 589832 | tf_op jit(solution)/shard_map/ppermute | solution.py:105
  102.2 11.4 %collective-permute-start.32 = (bf16[272,768]{1,0:T(8,128)(2,1)S(1)}, bf16[272,768]{1,0:T(8,128)(2,1)S(1)}, u32[]{:S(2)}, u32[]{:S(2)}) collective-permute-start(bf16[272,768]{1,0:T(8,128)(2,1)S(1)} %convolution_convert_fusion), channel_id=1, source_target_pairs={{0,1},{1,0},{2,3},{3,2},{4,5},{5,4},{6,7},{7,6},{8,9},{9,8},{10,11... | collective-permute-start | bytes 1253384 | tf_op jit(solution)/shard_map/ppermute | solution.py:105
  105.0 1.6 collective-permute-start.37
  105.1 2.0 %collective-permute-start.38 = (bf16[8,48,384]{2,1,0:T(8,128)(2,1)S(1)}, bf16[8,48,384]{2,1,0:T(8,128)(2,1)S(1)}, u32[]{:S(2)}, u32[]{:S(2)}) collective-permute-start(bf16[8,48,384]{2,1,0:T(8,128)(2,1)S(1)} %get-tuple-element.220), channel_id=1, source_target_pairs={{0,2},{2,0},{4,6},{6,4},{8,10},{10,8},{12,14},{14,12},{16,18},{18,... | collective-permute-start | bytes 884744 | tf_op jit(solution)/shard_map/ppermute | solution.py:101
  105.6 1.9 %collective-permute-start.39 = (bf16[8,48,384]{2,1,0:T(8,128)(2,1)S(1)}, bf16[8,48,384]{2,1,0:T(8,128)(2,1)S(1)}, u32[]{:S(2)}, u32[]{:S(2)}) collective-permute-start(bf16[8,48,384]{2,1,0:T(8,128)(2,1)S(1)} %get-tuple-element.221), channel_id=1, source_target_pairs={{0,2},{2,0},{4,6},{6,4},{8,10},{10,8},{12,14},{14,12},{16,18},{18,... | collective-permute-start | bytes 884744 | tf_op jit(solution)/shard_map/ppermute | solution.py:101
  105.7 2.3 %collective-permute-start.40 = (bf16[8,48,384]{2,1,0:T(8,128)(2,1)S(1)}, bf16[8,48,384]{2,1,0:T(8,128)(2,1)S(1)}, u32[]{:S(2)}, u32[]{:S(2)}) collective-permute-start(bf16[8,48,384]{2,1,0:T(8,128)(2,1)S(1)} %get-tuple-element.222), channel_id=1, source_target_pairs={{0,2},{2,0},{4,6},{6,4},{8,10},{10,8},{12,14},{14,12},{16,18},{18,... | collective-permute-start | bytes 884744 | tf_op jit(solution)/shard_map/ppermute | solution.py:101
  108.8 15.4 %collective-permute-start.45 = (bf16[4,48,1536]{2,1,0:T(8,128)(2,1)S(1)}, bf16[4,48,1536]{2,1,0:T(8,128)(2,1)S(1)}, u32[]{:S(2)}, u32[]{:S(2)}) collective-permute-start(bf16[4,48,1536]{2,1,0:T(8,128)(2,1)S(1)} %get-tuple-element.223), channel_id=1, source_target_pairs={{0,4},{2,6},{4,0},{6,2},{8,12},{10,14},{12,8},{14,10},{16,20},{18,... | collective-permute-start | bytes 1769480 | tf_op jit(solution)/shard_map/ppermute | solution.py:101
  111.5 3.8 %collective-permute-start.41 = (bf16[8,48,384]{2,1,0:T(8,128)(2,1)S(1)}, bf16[8,48,384]{2,1,0:T(8,128)(2,1)S(1)}, u32[]{:S(2)}, u32[]{:S(2)}) collective-permute-start(bf16[8,48,384]{2,1,0:T(8,128)(2,1)S(1)} %get-tuple-element.226), channel_id=1, source_target_pairs={{0,2},{2,0},{4,6},{6,4},{8,10},{10,8},{12,14},{14,12},{16,18},{18,... | collective-permute-start | bytes 884744 | tf_op jit(solution)/shard_map/ppermute | solution.py:101
  111.6 5.7 %collective-permute-start.42 = (bf16[8,48,384]{2,1,0:T(8,128)(2,1)S(1)}, bf16[8,48,384]{2,1,0:T(8,128)(2,1)S(1)}, u32[]{:S(2)}, u32[]{:S(2)}) collective-permute-start(bf16[8,48,384]{2,1,0:T(8,128)(2,1)S(1)} %get-tuple-element.227), channel_id=1, source_target_pairs={{0,2},{2,0},{4,6},{6,4},{8,10},{10,8},{12,14},{14,12},{16,18},{18,... | collective-permute-start | bytes 884744 | tf_op jit(solution)/shard_map/ppermute | solution.py:101
  112.1 5.5 %collective-permute-start.43 = (bf16[8,48,384]{2,1,0:T(8,128)(2,1)S(1)}, bf16[8,48,384]{2,1,0:T(8,128)(2,1)S(1)}, u32[]{:S(2)}, u32[]{:S(2)}) collective-permute-start(bf16[8,48,384]{2,1,0:T(8,128)(2,1)S(1)} %get-tuple-element.228), channel_id=1, source_target_pairs={{0,2},{2,0},{4,6},{6,4},{8,10},{10,8},{12,14},{14,12},{16,18},{18,... | collective-permute-start | bytes 884744 | tf_op jit(solution)/shard_map/ppermute | solution.py:101
  113.7 4.2 %collective-permute-start.44 = (bf16[8,48,384]{2,1,0:T(8,128)(2,1)S(1)}, bf16[8,48,384]{2,1,0:T(8,128)(2,1)S(1)}, u32[]{:S(2)}, u32[]{:S(2)}) collective-permute-start(bf16[8,48,384]{2,1,0:T(8,128)(2,1)S(1)} %get-tuple-element.229), channel_id=1, source_target_pairs={{0,2},{2,0},{4,6},{6,4},{8,10},{10,8},{12,14},{14,12},{16,18},{18,... | collective-permute-start | bytes 884744 | tf_op jit(solution)/shard_map/ppermute | solution.py:101
  115.3 9.6 %collective-permute-start.33 = (bf16[272,384]{1,0:T(8,128)(2,1)S(1)}, bf16[272,384]{1,0:T(8,128)(2,1)S(1)}, u32[]{:S(2)}, u32[]{:S(2)}) collective-permute-start(bf16[272,384]{1,0:T(8,128)(2,1)S(1)} %get-tuple-element.205), channel_id=1, source_target_pairs={{0,1},{1,0},{2,3},{3,2},{4,5},{5,4},{6,7},{7,6},{8,9},{9,8},{10,11... | collective-permute-start | bytes 626696 | tf_op jit(solution)/shard_map/ppermute | solution.py:105
  117.3 1.7 collective-permute-start.34
  117.6 1.5 collective-permute-start.35
  117.9 1.5 collective-permute-start.36
  124.9 15.1 %collective-permute-start.46 = (bf16[8,24,768]{2,1,0:T(8,128)(2,1)S(1)}, bf16[8,24,768]{2,1,0:T(8,128)(2,1)S(1)}, u32[]{:S(2)}, u32[]{:S(2)}) collective-permute-start(bf16[8,24,768]{2,1,0:T(8,128)(2,1)S(1)} %get-tuple-element.236), channel_id=1, source_target_pairs={{0,1},{1,0},{2,3},{3,2},{4,5},{5,4},{6,7},{7,6},{8,9},{9,8},{10,11... | collective-permute-start | bytes 884744 | tf_op jit(solution)/shard_map/ppermute | solution.py:105
  126.5 14.9 %collective-permute-start.47 = (bf16[2,48,1536]{2,1,0:T(8,128)(2,1)S(1)}, bf16[2,48,1536]{2,1,0:T(8,128)(2,1)S(1)}, u32[]{:S(2)}, u32[]{:S(2)}) collective-permute-start(bf16[2,48,1536]{2,1,0:T(8,128)(2,1)S(1)} %get-tuple-element.237), channel_id=1, source_target_pairs={{0,16},{2,18},{4,20},{6,22},{8,24},{10,26},{12,28},{14,30},{16,0},... | collective-permute-start | bytes 884744 | tf_op jit(solution)/shard_map/ppermute | solution.py:101
  127.1 15.4 %collective-permute-start.48 = (bf16[4,48,1536]{2,1,0:T(8,128)(2,1)S(1)}, bf16[4,48,1536]{2,1,0:T(8,128)(2,1)S(1)}, u32[]{:S(2)}, u32[]{:S(2)}) collective-permute-start(bf16[4,48,1536]{2,1,0:T(8,128)(2,1)S(1)} %get-tuple-element.251), channel_id=1, source_target_pairs={{0,4},{2,6},{4,0},{6,2},{8,12},{10,14},{12,8},{14,10},{16,20},{18,... | collective-permute-start | bytes 1769480 | tf_op jit(solution)/shard_map/ppermute | solution.py:101
  141.4 2.6 %collective-permute-start.49 = (bf16[8,48,384]{2,1,0:T(8,128)(2,1)S(1)}, bf16[8,48,384]{2,1,0:T(8,128)(2,1)S(1)}, u32[]{:S(2)}, u32[]{:S(2)}) collective-permute-start(bf16[8,48,384]{2,1,0:T(8,128)(2,1)S(1)} %get-tuple-element.253), channel_id=1, source_target_pairs={{0,2},{2,0},{4,6},{6,4},{8,10},{10,8},{12,14},{14,12},{16,18},{18,... | collective-permute-start | bytes 884744 | tf_op jit(solution)/shard_map/ppermute | solution.py:101
  141.4 2.6 %collective-permute-start.50 = (bf16[8,48,384]{2,1,0:T(8,128)(2,1)S(1)}, bf16[8,48,384]{2,1,0:T(8,128)(2,1)S(1)}, u32[]{:S(2)}, u32[]{:S(2)}) collective-permute-start(bf16[8,48,384]{2,1,0:T(8,128)(2,1)S(1)} %get-tuple-element.254), channel_id=1, source_target_pairs={{0,2},{2,0},{4,6},{6,4},{8,10},{10,8},{12,14},{14,12},{16,18},{18,... | collective-permute-start | bytes 884744 | tf_op jit(solution)/shard_map/ppermute | solution.py:101
  141.9 2.1 %collective-permute-start.51 = (bf16[8,48,384]{2,1,0:T(8,128)(2,1)S(1)}, bf16[8,48,384]{2,1,0:T(8,128)(2,1)S(1)}, u32[]{:S(2)}, u32[]{:S(2)}) collective-permute-start(bf16[8,48,384]{2,1,0:T(8,128)(2,1)S(1)} %get-tuple-element.255), channel_id=1, source_target_pairs={{0,2},{2,0},{4,6},{6,4},{8,10},{10,8},{12,14},{14,12},{16,18},{18,... | collective-permute-start | bytes 884744 | tf_op jit(solution)/shard_map/ppermute | solution.py:101
  141.9 2.0 %collective-permute-start.52 = (bf16[8,48,128]{2,1,0:T(8,128)(2,1)S(1)}, bf16[8,48,128]{2,1,0:T(8,128)(2,1)S(1)}, u32[]{:S(2)}, u32[]{:S(2)}) collective-permute-start(bf16[8,48,128]{2,1,0:T(8,128)(2,1)S(1)} %get-tuple-element.256), channel_id=1, source_target_pairs={{0,2},{2,0},{4,6},{6,4},{8,10},{10,8},{12,14},{14,12},{16,18},{18,... | collective-permute-start | bytes 294920 | tf_op jit(solution)/shard_map/ppermute | solution.py:101
  144.0 15.1 %collective-permute-start.57 = (bf16[2,48,1536]{2,1,0:T(8,128)(2,1)S(1)}, bf16[2,48,1536]{2,1,0:T(8,128)(2,1)S(1)}, u32[]{:S(2)}, u32[]{:S(2)}) collective-permute-start(bf16[2,48,1536]{2,1,0:T(8,128)(2,1)S(1)} %get-tuple-element.271), channel_id=1, source_target_pairs={{0,16},{2,18},{4,20},{6,22},{8,24},{10,26},{12,28},{14,30},{16,0},... | collective-permute-start | bytes 884744 | tf_op jit(solution)/shard_map/ppermute | solution.py:101
  146.0 16.1 %collective-permute-start.54 = (bf16[4,24,2048]{2,1,0:T(8,128)(2,1)S(1)}, bf16[4,24,2048]{2,1,0:T(8,128)(2,1)S(1)}, u32[]{:S(2)}, u32[]{:S(2)}) collective-permute-start(bf16[4,24,2048]{2,1,0:T(8,128)(2,1)S(1)} %get-tuple-element.263), channel_id=1, source_target_pairs={{0,4},{2,6},{4,0},{6,2},{8,12},{10,14},{12,8},{14,10},{16,20},{18,... | collective-permute-start | bytes 1179656 | tf_op jit(solution)/shard_map/ppermute | solution.py:101
  147.5 13.8 %collective-permute-start.55 = (bf16[4,24,1280]{2,1,0:T(8,128)(2,1)S(1)}, bf16[4,24,1280]{2,1,0:T(8,128)(2,1)S(1)}, u32[]{:S(2)}, u32[]{:S(2)}) collective-permute-start(bf16[4,24,1280]{2,1,0:T(8,128)(2,1)S(1)} %get-tuple-element.268), channel_id=1, source_target_pairs={{0,1},{1,0},{2,3},{3,2},{4,5},{5,4},{6,7},{7,6},{8,9},{9,8},{10,11... | collective-permute-start | bytes 737288 | tf_op jit(solution)/shard_map/ppermute | solution.py:105
  148.0 14.1 %collective-permute-start.56 = (bf16[4,24,1280]{2,1,0:T(8,128)(2,1)S(1)}, bf16[4,24,1280]{2,1,0:T(8,128)(2,1)S(1)}, u32[]{:S(2)}, u32[]{:S(2)}) collective-permute-start(bf16[4,24,1280]{2,1,0:T(8,128)(2,1)S(1)} %get-tuple-element.269), channel_id=1, source_target_pairs={{0,5},{1,4},{2,7},{3,6},{4,1},{5,0},{6,3},{7,2},{8,13},{9,12},{10,... | collective-permute-start | bytes 737288 | tf_op jit(solution)/shard_map/ppermute | solution.py:114
  150.2 11.2 %collective-permute-start.59 = (bf16[1,48,1536]{2,1,0:T(8,128)(2,1)S(1)}, bf16[1,48,1536]{2,1,0:T(8,128)(2,1)S(1)}, u32[]{:S(2)}, u32[]{:S(2)}) collective-permute-start(bf16[1,48,1536]{2,1,0:T(8,128)(2,1)S(1)} %get-tuple-element.276), channel_id=1, source_target_pairs={{0,8},{2,10},{4,12},{6,14},{8,0},{10,2},{12,4},{14,6},{16,24},{18,... | collective-permute-start | bytes 442376 | tf_op jit(solution)/shard_map/ppermute | solution.py:136
  159.1 1.2 collective-permute-start.58
  160.2 11.7 %collective-permute-start.53 = (bf16[272,768]{1,0:T(8,128)(2,1)S(1)}, bf16[272,768]{1,0:T(8,128)(2,1)S(1)}, u32[]{:S(2)}, u32[]{:S(2)}) collective-permute-start(bf16[272,768]{1,0:T(8,128)(2,1)S(1)} %get-tuple-element.272), channel_id=1, source_target_pairs={{0,1},{1,0},{2,3},{3,2},{4,5},{5,4},{6,7},{7,6},{8,9},{9,8},{10,11... | collective-permute-start | bytes 1253384 | tf_op jit(solution)/shard_map/ppermute | solution.py:105
  162.1 11.5 %collective-permute-start.63 = (bf16[1,48,1536]{2,1,0:T(8,128)(2,1)S(1)}, bf16[1,48,1536]{2,1,0:T(8,128)(2,1)S(1)}, u32[]{:S(2)}, u32[]{:S(2)}) collective-permute-start(bf16[1,48,1536]{2,1,0:T(8,128)(2,1)S(1)} %get-tuple-element.294), channel_id=1, source_target_pairs={{0,8},{2,10},{4,12},{6,14},{8,0},{10,2},{12,4},{14,6},{16,24},{18,... | collective-permute-start | bytes 442376 | tf_op jit(solution)/shard_map/ppermute | solution.py:136
  163.2 11.1 %collective-permute-start.60 = (bf16[1,24,3328]{2,1,0:T(8,128)(2,1)S(1)}, bf16[1,24,3328]{2,1,0:T(8,128)(2,1)S(1)}, u32[]{:S(2)}, u32[]{:S(2)}) collective-permute-start(bf16[1,24,3328]{2,1,0:T(8,128)(2,1)S(1)} %get-tuple-element.280), channel_id=1, source_target_pairs={{0,8},{2,10},{4,12},{6,14},{8,16},{10,18},{12,20},{14,22},{16,24},... | collective-permute-start | bytes 479240 | tf_op jit(solution)/shard_map/ppermute | solution.py:101
  164.9 13.1 %collective-permute-start.61 = (bf16[1,24,3328]{2,1,0:T(8,128)(2,1)S(1)}, bf16[1,24,3328]{2,1,0:T(8,128)(2,1)S(1)}, u32[]{:S(2)}, u32[]{:S(2)}) collective-permute-start(bf16[1,24,3328]{2,1,0:T(8,128)(2,1)S(1)} %get-tuple-element.281), channel_id=1, source_target_pairs={{0,16},{2,18},{4,20},{6,22},{8,24},{10,26},{12,28},{14,30},{16,0},... | collective-permute-start | bytes 479240 | tf_op jit(solution)/shard_map/ppermute | solution.py:101
  166.9 11.1 %collective-permute-start.62 = (bf16[1,24,3328]{2,1,0:T(8,128)(2,1)S(1)}, bf16[1,24,3328]{2,1,0:T(8,128)(2,1)S(1)}, u32[]{:S(2)}, u32[]{:S(2)}) collective-permute-start(bf16[1,24,3328]{2,1,0:T(8,128)(2,1)S(1)} %get-tuple-element.282), channel_id=1, source_target_pairs={{0,24},{2,26},{4,28},{6,30},{8,0},{10,2},{12,4},{14,6},{16,8},{18,... | collective-permute-start | bytes 479240 | tf_op jit(solution)/shard_map/ppermute | solution.py:101
  (3 other events, 45.6 us)

commit v6 on v5

--- a/solution.py
+++ b/solution.py
@@ -858,7 +858,7 @@
     )
     rows_low = jnp.pad(tie(rows_in, packed)[:, 0, :], ((0, padded - half_rows), (0, 0)))
     rows_other = swap_tensor(rows_low)
-    up_pair = spread_near(tie(ffn_up, packed), digits)
+    up_pair = spread_near(ffn_up, digits)
     first_z = spread_outer(packed, digits)
     rows_other, up_pair = join(rows_other, tie(up_pair, first_z))
     slots = first_z.shape[0]

time: 180 us -> 180 us (level)
  no operation moved by 1% of the time
where the time goes in v6:
time: 180 us; the launch traced here: 179 us
  waiting for transfers between devices  61.5 us (34%)
  Pallas kernels  54.6 us (30%)
  starting transfers between devices  49.9 us (28%)
  matrix products  5.27 us (3%)
  other arithmetic  3.41 us (2%)
  between operations  2.5 us (1%)
  local copies, waits for them, and re-layouts  2.12 us (1%)
    pallas_call x32, Pallas kernels, call(): pl.pallas_call(kernel, in_specs=[pl.BlockSpec(memory_space=pltpu.SMEM)] +...  54.6 us
    ppermute x44, waiting for transfers between devices, rotate(): return lax.ppermute(value, 'dp', pairs)  44.7 us
    ppermute x44, starting transfers between devices, rotate(): return lax.ppermute(value, 'dp', pairs)  29.1 us
    ppermute x14, waiting for transfers between devices, swap_tensor(): return lax.ppermute(value, 'tensor', [(0, 1), (1, 0)])  14.6 us
    ppermute x14, starting transfers between devices, swap_tensor(): return lax.ppermute(value, 'tensor', [(0, 1), (1, 0)])  13.9 us
    ppermute x4, starting transfers between devices, swap_near(): return lax.ppermute(value, 'dp', pairs)  4.94 us
  transfers between devices with their start and end apart: 64, of which 27 were waited for; matrix products, arithmetic and copies ran while one was open for 4% of the time, Pallas kernels for 28%

profile of v6, /device:TPU:0, one launch (start us, length us, event | category | flops | bytes accessed | tf_op | source)
XLA Modules:
  0.0 179.4 jit_solution(10886787596148198688)
XLA Ops:
  0.6 1.7 shard_map.204
  2.3 3.0 %collective-permute-start.2 = (bf16[24,3200]{1,0:T(8,128)(2,1)}, bf16[24,3200]{1,0:T(8,128)(2,1)S(1)}, u32[]{:S(2)}, u32[]{:S(2)}) collective-permute-start(bf16[24,3200]{1,0:T(8,128)(2,1)} %shard_map.204), channel_id=1, source_target_pairs={{0,8},{2,10},{4,12},{6,14},{8,16},{10,18},{12,20},{14,22},{16,24},... | collective-permute-start | bytes 460808 | tf_op jit(solution)/shard_map/ppermute | solution.py:101
  5.4 2.6 %collective-permute-start.3 = (bf16[24,3200]{1,0:T(8,128)(2,1)}, bf16[24,3200]{1,0:T(8,128)(2,1)S(1)}, u32[]{:S(2)}, u32[]{:S(2)}) collective-permute-start(bf16[24,3200]{1,0:T(8,128)(2,1)} %shard_map.204), channel_id=1, source_target_pairs={{0,16},{2,18},{4,20},{6,22},{8,24},{10,26},{12,28},{14,30},{16,0},... | collective-permute-start | bytes 460808 | tf_op jit(solution)/shard_map/ppermute | solution.py:101
  8.0 1.3 collective-permute-start.4
  10.0 1.0 pad.4.own
  11.0 1.6 collective-permute-start
  14.7 3.6 %collective-permute-done.3 = bf16[24,3200]{1,0:T(8,128)(2,1)S(1)} collective-permute-done((bf16[24,3200]{1,0:T(8,128)(2,1)}, bf16[24,3200]{1,0:T(8,128)(2,1)S(1)}, u32[]{:S(2)}, u32[]{:S(2)}) %collective-permute-start.3) | collective-permute-done | bytes 153632 | tf_op jit(solution)/shard_map/ppermute | solution.py:101
  18.7 1.0 pad_maximum_fusion.packed
  20.3 3.5 %collective-permute-start.9 = (bf16[48,1536]{1,0:T(8,128)(2,1)S(1)}, bf16[48,1536]{1,0:T(8,128)(2,1)S(1)}, u32[]{:S(2)}, u32[]{:S(2)}) collective-permute-start(bf16[48,1536]{1,0:T(8,128)(2,1)S(1)} %bitcast.75), channel_id=1, source_target_pairs={{0,8},{2,10},{4,12},{6,14},{8,0},{10,2},{12,4},{14,6},{16,24},{18,... | collective-permute-start | bytes 442376 | tf_op jit(solution)/shard_map/ppermute | solution.py:136
  23.8 1.7 collective-permute-start.8
  25.5 1.5 collective-permute-start.6
  27.0 1.5 collective-permute-start.5
  29.1 10.5 %collective-permute-done.8 = bf16[2,48,1536]{2,1,0:T(8,128)(2,1)S(1)} collective-permute-done((bf16[2,48,1536]{2,1,0:T(8,128)(2,1)S(1)}, bf16[2,48,1536]{2,1,0:T(8,128)(2,1)S(1)}, u32[]{:S(2)}, u32[]{:S(2)}) %collective-permute-start.8) | collective-permute-done | bytes 294944 | tf_op jit(solution)/shard_map/ppermute | solution.py:101
  39.7 1.5 collective-permute-done.7
  41.9 1.5 collective-permute-start.17
  44.6 2.3 %collective-permute-start.13 = (bf16[2,48,1536]{2,1,0:T(8,128)(2,1)S(1)}, bf16[2,48,1536]{2,1,0:T(8,128)(2,1)S(1)}, u32[]{:S(2)}, u32[]{:S(2)}) collective-permute-start(bf16[2,48,1536]{2,1,0:T(8,128)(2,1)S(1)} %pad_maximum_fusion.4.refs_0_), channel_id=1, source_target_pairs={{0,16},{2,18},{4,20},{6,22},{8,24},{10,26},{12,28},{14,30},{16,0},... | collective-permute-start | bytes 884744 | tf_op jit(solution)/shard_map/ppermute | solution.py:101
  47.6 7.8 %shard_map.207 = (bf16[544,1152]{1,0:T(8,128)(2,1)S(1)}, bf16[272,384]{1,0:T(8,128)(2,1)S(1)}, bf16[272,384]{1,0:T(8,128)(2,1)S(1)}, f32[544,128]{1,0:T(8,128)S(...) custom-call(s32[15]{0:T(128)S(1)} %concatenate.21.at, bf16[272,768]{1,0:T(8,128)(2,1)S(1)} %pad.4.own, ...), custom_call_target="tpu_custom_call" | custom-call | flops 1 | bytes 1 | tf_op jit(solution)/shard_map/pallas_call | solution.py:61
  55.6 1.6 collective-permute-start.12
  57.7 2.5 %collective-permute-done.13.refs_1_ = bf16[2,48,1536]{2,1,0:T(8,128)(2,1)S(1)} collective-permute-done((bf16[2,48,1536]{2,1,0:T(8,128)(2,1)S(1)}, bf16[2,48,1536]{2,1,0:T(8,128)(2,1)S(1)}, u32[]{:S(2)}, u32[]{:S(2)}) %collective-permute-start.13) | collective-permute-done | bytes 294944 | tf_op jit(solution)/shard_map/ppermute | solution.py:101
  60.2 2.9 %collective-permute-done.12.got = bf16[272,384]{1,0:T(8,128)(2,1)S(1)} collective-permute-done((bf16[272,384]{1,0:T(8,128)(2,1)S(1)}, bf16[272,384]{1,0:T(8,128)(2,1)S(1)}, u32[]{:S(2)}, u32[]{:S(2)}) %collective-permute-start.12) | collective-permute-done | bytes 208928 | tf_op jit(solution)/shard_map/ppermute | solution.py:105
  63.8 1.3 shard_map.210
  65.1 1.6 collective-permute-start.16
  68.0 7.0 %collective-permute-done.21.refs_3_ = bf16[2,48,1536]{2,1,0:T(8,128)(2,1)S(1)} collective-permute-done((bf16[2,48,1536]{2,1,0:T(8,128)(2,1)S(1)}, bf16[2,48,1536]{2,1,0:T(8,128)(2,1)S(1)}, u32[]{:S(2)}, u32[]{:S(2)}) %collective-permute-start.21) | collective-permute-done | bytes 294944 | tf_op jit(solution)/shard_map/ppermute | solution.py:101
  76.6 0.9 multiply_convert_fusion
  78.3 0.8 convolution_convert_fusion.1
  79.1 1.6 collective-permute-start.27
  80.7 1.2 collective-permute-done.26._
  81.9 2.4 %shard_map.214 = (bf16[272,1536]{1,0:T(8,128)(2,1)S(1)}, f32[272,1536]{1,0:T(8,128)S(1)}, f32[272,768]{1,0:T(8,128)S(1)}) custom-call(s32[15]{0:T(128)S(1)} %concatenate.21.at, bf16[272,768]{1,0:T(8,128)(2,1)S(1)} %get-tuple-element.172.normed.a_up, bf16[768,1536]{1,0:T(8,128)(2,1)S(1)} %bitcast.57, f32[16,1536]{1,0:T(8,128)S(1)} %shard_map.211.up_b, ...), custom_call_target="tpu_custom_call" | custom-call | flops 1 | bytes 1 | tf_op jit(solution)/shard_map/pallas_call | solution.py:61
  85.0 2.0 %collective-permute-done.27.got = bf16[144,768]{1,0:T(8,128)(2,1)S(1)} collective-permute-done((bf16[144,768]{1,0:T(8,128)(2,1)S(1)}, bf16[144,768]{1,0:T(8,128)(2,1)S(1)}, u32[]{:S(2)}, u32[]{:S(2)}) %collective-permute-start.27) | collective-permute-done | bytes 221216 | tf_op jit(solution)/shard_map/ppermute | solution.py:105
  86.9 1.0 shard_map.215
  88.6 2.9 %collective-permute-done.28.got = bf16[128,768]{1,0:T(8,128)(2,1)S(1)} collective-permute-done((bf16[128,768]{1,0:T(8,128)(2,1)S(1)}, bf16[128,768]{1,0:T(8,128)(2,1)S(1)}, u32[]{:S(2)}, u32[]{:S(2)}) %collective-permute-start.28) | collective-permute-done | bytes 196640 | tf_op jit(solution)/shard_map/ppermute | solution.py:105
  91.5 1.0 shard_map.216
  93.2 0.8 fusion.b_up
  94.0 3.7 %shard_map.217 = (f32[768,1536]{1,0:T(8,128)S(1)}, f32[768,1536]{1,0:T(8,128)S(1)}, f32[1,1536]{1,0:T(1,128)S(1)}) custom-call(s32[15]{0:T(128)S(1)} %concatenate.21.at, bf16[272,768]{1,0:T(8,128)(2,1)S(1)} %constant_dynamic-update-slice_fusion.4.a_down, bf16[272,1536]{1,0:T(8,128)(2,1)S(1)} %get-tuple-element.196.b_down, ...), custom_call_target="tpu_custom_call" | custom-call | flops 1 | bytes 1 | tf_op jit(solution)/shard_map/pallas_call | solution.py:61
  97.7 0.8 fusion.6.own
  98.5 1.8 %collective-permute-done.31 = bf16[128,768]{1,0:T(8,128)(2,1)S(1)} collective-permute-done((bf16[128,768]{1,0:T(8,128)(2,1)S(1)}, bf16[128,768]{1,0:T(8,128)(2,1)S(1)}, u32[]{:S(2)}, u32[]{:S(2)}) %collective-permute-start.31) | collective-permute-done | bytes 196640 | tf_op jit(solution)/shard_map/ppermute | solution.py:105
  100.4 1.0 fusion.1.b
  101.4 0.8 convolution_convert_fusion
  102.8 2.2 %shard_map.221 = (bf16[8,48,1536]{2,1,0:T(8,128)(2,1)S(1)}, bf16[8,48,384]{2,1,0:T(8,128)(2,1)S(1)}, bf16[8,48,384]{2,1,0:T(8,128)(2,1)S(1)}, bf16[8,48,384]{2,1,0:T(8,128)(2,1)S(1)}, bf16[8,48,384]{2,1,0:T(8,128)(2,1)S(1)}) custom-call(s32[15]{0:T(128)S(1)} %concatenate.21.at, f32[768,1536]{1,0:T(8,128)S(1)} %get-tuple-element.214.own, ...), custom_call_target="tpu_custom_call" | custom-call | flops 1 | bytes 1 | tf_op jit(solution)/shard_map/pallas_call | solution.py:61
  107.9 0.8 shard_map.222
  109.4 2.1 %shard_map.223 = (f32[1,1536]{1,0:T(1,128)S(1)}, bf16[8,48,1536]{2,1,0:T(8,128)(2,1)S(1)}, bf16[8,48,384]{2,1,0:T(8,128)(2,1)S(1)}, bf16[8,48,384]{2,1,0:T(8,128...) custom-call(s32[15]{0:T(128)S(1)} %concatenate.21.at, ...), custom_call_target="tpu_custom_call" | custom-call | flops 1 | bytes 1 | tf_op jit(solution)/shard_map/pallas_call | solution.py:61
  112.2 1.5 collective-permute-done.32.got
  113.7 1.6 shard_map.218
  115.9 1.4 shard_map.219
  118.1 0.8 shard_map.224
  120.1 4.1 %collective-permute-done.45.got = bf16[4,48,1536]{2,1,0:T(8,128)(2,1)S(1)} collective-permute-done((bf16[4,48,1536]{2,1,0:T(8,128)(2,1)S(1)}, bf16[4,48,1536]{2,1,0:T(8,128)(2,1)S(1)}, u32[]{:S(2)}, u32[]{:S(2)}) %collective-permute-start.45) | collective-permute-done | bytes 589856 | tf_op jit(solution)/shard_map/ppermute | solution.py:101
  124.9 1.6 collective-permute-start.46
  127.6 9.6 %shard_map.226 = (bf16[544,1152]{1,0:T(8,128)(2,1)S(1)}, f32[1,1152]{1,0:T(1,128)S(1)}) custom-call(s32[15]{0:T(128)S(1)} %concatenate.21.at, bf16[544,1152]{1,0:T(8,128)(2,1)S(1)} %get-tuple-element.191.qkv, bf16[272,384]{1,0:T(8,128)(2,1)S(1)} %get-tuple-element.202.own, bf16[272,384]{1,0:T(8,128)(2,1)S(1)} %collective-permute-done.33.got, ...), custom_call_target="tpu_custom_call" | custom-call | flops 1 | bytes 1 | tf_op jit(solution)/shard_map/pallas_call | solution.py:61
  137.3 2.7 %shard_map.227 = (bf16[8,48,1280]{2,1,0:T(8,128)(2,1)S(1)}, bf16[8,48,384]{2,1,0:T(8,128)(2,1)S(1)}, bf16[8,48,384]{2,1,0:T(8,128)(2,1)S(1)}, bf16[8,48,384]{2,1,0:T(8,128)(2,1)S(1)}, bf16[8,48,128]{2,1,0:T(8,128)(2,1)S(1)}) custom-call(s32[15]{0:T(128)S(1)} %concatenate.21.at, bf16[544,768]{1,0:T(8,128)(2,1)S(1)} %get-tuple-element.169.layer_in, ...), custom_call_target="tpu_custom_call" | custom-call | flops 1 | bytes 1 | tf_op jit(solution)/shard_map/pallas_call | solution.py:61
  140.0 1.4 collective-permute-done.47.got
  143.1 0.9 collective-permute-done.52.refs_3_
  144.0 1.1 collective-permute-start.57
  145.1 0.9 shard_map.229
  146.0 1.6 collective-permute-start.54
  148.0 1.5 collective-permute-start.56
  150.6 1.8 %shard_map.230 = (f32[272,768]{1,0:T(8,128)S(1)}, bf16[272,768]{1,0:T(8,128)(2,1)S(1)}) custom-call(s32[15]{0:T(128)S(1)} %concatenate.21.at, bf16[544,1152]{1,0:T(8,128)(2,1)S(1)} %get-tuple-element.262.d_projected, bf16[768,1280]{1,0:T(8,128)(2,1)S(1)} %bitcast.51, f32[272,768]{1,0:T(8,128)S(1)} %get-tuple-element.241.d_attn), custom_call_target="tpu_custom_call" | custom-call | flops 1 | bytes 1 | tf_op jit(solution)/shard_map/pallas_call | solution.py:61
  152.4 6.6 %collective-permute-done.57.got = bf16[2,48,1536]{2,1,0:T(8,128)(2,1)S(1)} collective-permute-done((bf16[2,48,1536]{2,1,0:T(8,128)(2,1)S(1)}, bf16[2,48,1536]{2,1,0:T(8,128)(2,1)S(1)}, u32[]{:S(2)}, u32[]{:S(2)}) %collective-permute-start.57) | collective-permute-done | bytes 294944 | tf_op jit(solution)/shard_map/ppermute | solution.py:101
  163.2 1.7 collective-permute-start.60
  164.9 2.0 %collective-permute-start.61 = (bf16[1,24,3328]{2,1,0:T(8,128)(2,1)S(1)}, bf16[1,24,3328]{2,1,0:T(8,128)(2,1)S(1)}, u32[]{:S(2)}, u32[]{:S(2)}) collective-permute-start(bf16[1,24,3328]{2,1,0:T(8,128)(2,1)S(1)} %get-tuple-element.279), channel_id=1, source_target_pairs={{0,16},{2,18},{4,20},{6,22},{8,24},{10,26},{12,28},{14,30},{16,0},... | collective-permute-start | bytes 479240 | tf_op jit(solution)/shard_map/ppermute | solution.py:101
  166.9 0.9 collective-permute-start.62
  168.6 3.3 %collective-permute-done.53.got = bf16[272,768]{1,0:T(8,128)(2,1)S(1)} collective-permute-done((bf16[272,768]{1,0:T(8,128)(2,1)S(1)}, bf16[272,768]{1,0:T(8,128)(2,1)S(1)}, u32[]{:S(2)}, u32[]{:S(2)}) %collective-permute-start.53) | collective-permute-done | bytes 417824 | tf_op jit(solution)/shard_map/ppermute | solution.py:105
  171.9 1.6 shard_map.231
  174.3 3.7 %collective-permute-done.61 = bf16[1,24,3328]{2,1,0:T(8,128)(2,1)S(1)} collective-permute-done((bf16[1,24,3328]{2,1,0:T(8,128)(2,1)S(1)}, bf16[1,24,3328]{2,1,0:T(8,128)(2,1)S(1)}, u32[]{:S(2)}, u32[]{:S(2)}) %collective-permute-start.61) | collective-permute-done | bytes 159776 | tf_op jit(solution)/shard_map/ppermute | solution.py:101
  178.1 1.3 shard_map.235
  (130 shorter events, 30.3 us)
Async XLA Ops:
  2.3 12.3 %collective-permute-start.2 = (bf16[24,3200]{1,0:T(8,128)(2,1)}, bf16[24,3200]{1,0:T(8,128)(2,1)S(1)}, u32[]{:S(2)}, u32[]{:S(2)}) collective-permute-start(bf16[24,3200]{1,0:T(8,128)(2,1)} %shard_map.204), channel_id=1, source_target_pairs={{0,8},{2,10},{4,12},{6,14},{8,16},{10,18},{12,20},{14,22},{16,24},... | collective-permute-start | bytes 460808 | tf_op jit(solution)/shard_map/ppermute | solution.py:101
  5.4 12.9 %collective-permute-start.3 = (bf16[24,3200]{1,0:T(8,128)(2,1)}, bf16[24,3200]{1,0:T(8,128)(2,1)S(1)}, u32[]{:S(2)}, u32[]{:S(2)}) collective-permute-start(bf16[24,3200]{1,0:T(8,128)(2,1)} %shard_map.204), channel_id=1, source_target_pairs={{0,16},{2,18},{4,20},{6,22},{8,24},{10,26},{12,28},{14,30},{16,0},... | collective-permute-start | bytes 460808 | tf_op jit(solution)/shard_map/ppermute | solution.py:101
  8.0 10.7 %collective-permute-start.4 = (bf16[24,3200]{1,0:T(8,128)(2,1)}, bf16[24,3200]{1,0:T(8,128)(2,1)S(1)}, u32[]{:S(2)}, u32[]{:S(2)}) collective-permute-start(bf16[24,3200]{1,0:T(8,128)(2,1)} %shard_map.204), channel_id=1, source_target_pairs={{0,24},{2,26},{4,28},{6,30},{8,0},{10,2},{12,4},{14,6},{16,8},{18,... | collective-permute-start | bytes 460808 | tf_op jit(solution)/shard_map/ppermute | solution.py:101
  9.3 14.5 %collective-permute-start.1 = (bf16[48,1536]{1,0:T(8,128)(2,1)}, bf16[48,1536]{1,0:T(8,128)(2,1)S(1)}, u32[]{:S(2)}, u32[]{:S(2)}) collective-permute-start(bf16[48,1536]{1,0:T(8,128)(2,1)} %param.23), channel_id=1, source_target_pairs={{0,8},{2,10},{4,12},{6,14},{8,0},{10,2},{12,4},{14,6},{16,24},{18,... | collective-permute-start | bytes 442376 | tf_op jit(solution)/shard_map/ppermute | solution.py:136
  11.0 12.8 %collective-permute-start = (bf16[272,768]{1,0:T(8,128)(2,1)S(1)}, bf16[272,768]{1,0:T(8,128)(2,1)S(1)}, u32[]{:S(2)}, u32[]{:S(2)}) collective-permute-start(bf16[272,768]{1,0:T(8,128)(2,1)S(1)} %pad.4.own), channel_id=1, source_target_pairs={{0,1},{1,0},{2,3},{3,2},{4,5},{5,4},{6,7},{7,6},{8,9},{9,8},{10,11... | collective-permute-start | bytes 1253384 | tf_op jit(solution)/shard_map/ppermute | solution.py:105
  20.3 8.7 %collective-permute-start.9 = (bf16[48,1536]{1,0:T(8,128)(2,1)S(1)}, bf16[48,1536]{1,0:T(8,128)(2,1)S(1)}, u32[]{:S(2)}, u32[]{:S(2)}) collective-permute-start(bf16[48,1536]{1,0:T(8,128)(2,1)S(1)} %bitcast.75), channel_id=1, source_target_pairs={{0,8},{2,10},{4,12},{6,14},{8,0},{10,2},{12,4},{14,6},{16,24},{18,... | collective-permute-start | bytes 442376 | tf_op jit(solution)/shard_map/ppermute | solution.py:136
  23.8 15.8 %collective-permute-start.8 = (bf16[2,48,1536]{2,1,0:T(8,128)(2,1)S(1)}, bf16[2,48,1536]{2,1,0:T(8,128)(2,1)S(1)}, u32[]{:S(2)}, u32[]{:S(2)}) collective-permute-start(bf16[2,48,1536]{2,1,0:T(8,128)(2,1)S(1)} %pad_maximum_fusion.3), channel_id=1, source_target_pairs={{0,16},{2,18},{4,20},{6,22},{8,24},{10,26},{12,28},{14,30},{16,0},... | collective-permute-start | bytes 884744 | tf_op jit(solution)/shard_map/ppermute | solution.py:101
  25.5 15.6 %collective-permute-start.6 = (bf16[4,24,2048]{2,1,0:T(8,128)(2,1)S(1)}, bf16[4,24,2048]{2,1,0:T(8,128)(2,1)S(1)}, u32[]{:S(2)}, u32[]{:S(2)}) collective-permute-start(bf16[4,24,2048]{2,1,0:T(8,128)(2,1)S(1)} %get-tuple-element.160), channel_id=1, source_target_pairs={{0,4},{2,6},{4,0},{6,2},{8,12},{10,14},{12,8},{14,10},{16,20},{18,... | collective-permute-start | bytes 1179656 | tf_op jit(solution)/shard_map/ppermute | solution.py:101
  27.0 12.6 %collective-permute-start.5 = (bf16[4,24,1280]{2,1,0:T(8,128)(2,1)S(1)}, bf16[4,24,1280]{2,1,0:T(8,128)(2,1)S(1)}, u32[]{:S(2)}, u32[]{:S(2)}) collective-permute-start(bf16[4,24,1280]{2,1,0:T(8,128)(2,1)S(1)} %get-tuple-element.157), channel_id=1, source_target_pairs={{0,1},{1,0},{2,3},{3,2},{4,5},{5,4},{6,7},{7,6},{8,9},{9,8},{10,11... | collective-permute-start | bytes 737288 | tf_op jit(solution)/shard_map/ppermute | solution.py:105
  28.6 12.6 %collective-permute-start.7 = (bf16[4,24,1280]{2,1,0:T(8,128)(2,1)S(1)}, bf16[4,24,1280]{2,1,0:T(8,128)(2,1)S(1)}, u32[]{:S(2)}, u32[]{:S(2)}) collective-permute-start(bf16[4,24,1280]{2,1,0:T(8,128)(2,1)S(1)} %get-tuple-element.157), channel_id=1, source_target_pairs={{0,5},{1,4},{2,7},{3,6},{4,1},{5,0},{6,3},{7,2},{8,13},{9,12},{10,... | collective-permute-start | bytes 737288 | tf_op jit(solution)/shard_map/ppermute | solution.py:114
  41.2 5.7 %collective-permute-start.11 = (bf16[4,24,3328]{2,1,0:T(8,128)(2,1)S(1)}, bf16[4,24,3328]{2,1,0:T(8,128)(2,1)S(1)}, u32[]{:S(2)}, u32[]{:S(2)}) collective-permute-start(bf16[4,24,3328]{2,1,0:T(8,128)(2,1)S(1)} %constant_dynamic-update-slice_fusion.2.refs_1_.x_got), channel_id=1, source_target_pairs={{0,2},{2,0},{4,6},{6,4},{8,10},{10,8},{12,14},{14,12},{16,18},{18,... | collective-permute-start | bytes 1916936 | tf_op jit(solution)/shard_map/ppermute | solution.py:101
  41.4 5.5 %collective-permute-start.10 = (bf16[4,24,3328]{2,1,0:T(8,128)(2,1)S(1)}, bf16[4,24,3328]{2,1,0:T(8,128)(2,1)S(1)}, u32[]{:S(2)}, u32[]{:S(2)}) collective-permute-start(bf16[4,24,3328]{2,1,0:T(8,128)(2,1)S(1)} %constant_dynamic-update-slice_fusion.refs_0_.mine), channel_id=1, source_target_pairs={{0,2},{2,0},{4,6},{6,4},{8,10},{10,8},{12,14},{14,12},{16,18},{18,... | collective-permute-start | bytes 1916936 | tf_op jit(solution)/shard_map/ppermute | solution.py:101
  41.9 15.7 %collective-permute-start.17 = (bf16[4,48,1536]{2,1,0:T(8,128)(2,1)S(1)}, bf16[4,48,1536]{2,1,0:T(8,128)(2,1)S(1)}, u32[]{:S(2)}, u32[]{:S(2)}) collective-permute-start(bf16[4,48,1536]{2,1,0:T(8,128)(2,1)S(1)} %pad_maximum_fusion.1.refs_0_), channel_id=1, source_target_pairs={{0,4},{2,6},{4,0},{6,2},{8,12},{10,14},{12,8},{14,10},{16,20},{18,... | collective-permute-start | bytes 1769480 | tf_op jit(solution)/shard_map/ppermute | solution.py:101
  44.0 11.5 %collective-permute-start.14 = (bf16[8,24,768]{2,1,0:T(8,128)(2,1)S(1)}, bf16[8,24,768]{2,1,0:T(8,128)(2,1)S(1)}, u32[]{:S(2)}, u32[]{:S(2)}) collective-permute-start(bf16[8,24,768]{2,1,0:T(8,128)(2,1)S(1)} %shard_map.208), channel_id=1, source_target_pairs={{0,1},{1,0},{2,3},{3,2},{4,5},{5,4},{6,7},{7,6},{8,9},{9,8},{10,11... | collective-permute-start | bytes 884744 | tf_op jit(solution)/shard_map/ppermute | solution.py:105
  44.6 15.6 %collective-permute-start.13 = (bf16[2,48,1536]{2,1,0:T(8,128)(2,1)S(1)}, bf16[2,48,1536]{2,1,0:T(8,128)(2,1)S(1)}, u32[]{:S(2)}, u32[]{:S(2)}) collective-permute-start(bf16[2,48,1536]{2,1,0:T(8,128)(2,1)S(1)} %pad_maximum_fusion.4.refs_0_), channel_id=1, source_target_pairs={{0,16},{2,18},{4,20},{6,22},{8,24},{10,26},{12,28},{14,30},{16,0},... | collective-permute-start | bytes 884744 | tf_op jit(solution)/shard_map/ppermute | solution.py:101
  55.5 7.7 %collective-permute-start.15 = (bf16[8,24,768]{2,1,0:T(8,128)(2,1)S(1)}, bf16[8,24,768]{2,1,0:T(8,128)(2,1)S(1)}, u32[]{:S(2)}, u32[]{:S(2)}) collective-permute-start(bf16[8,24,768]{2,1,0:T(8,128)(2,1)S(1)} %collective-permute-done.14.refs_4_), channel_id=1, source_target_pairs={{0,2},{2,0},{4,6},{6,4},{8,10},{10,8},{12,14},{14,12},{16,18},{18,... | collective-permute-start | bytes 884744 | tf_op jit(solution)/shard_map/ppermute | solution.py:101
  55.6 7.6 %collective-permute-start.12 = (bf16[272,384]{1,0:T(8,128)(2,1)S(1)}, bf16[272,384]{1,0:T(8,128)(2,1)S(1)}, u32[]{:S(2)}, u32[]{:S(2)}) collective-permute-start(bf16[272,384]{1,0:T(8,128)(2,1)S(1)} %get-tuple-element.165), channel_id=1, source_target_pairs={{0,1},{1,0},{2,3},{3,2},{4,5},{5,4},{6,7},{7,6},{8,9},{9,8},{10,11... | collective-permute-start | bytes 626696 | tf_op jit(solution)/shard_map/ppermute | solution.py:105
  57.2 9.6 %collective-permute-start.20 = (bf16[2,48,1536]{2,1,0:T(8,128)(2,1)S(1)}, bf16[2,48,1536]{2,1,0:T(8,128)(2,1)S(1)}, u32[]{:S(2)}, u32[]{:S(2)}) collective-permute-start(bf16[2,48,1536]{2,1,0:T(8,128)(2,1)S(1)} %pad_maximum_fusion.4.refs_0_), channel_id=1, source_target_pairs={{0,4},{2,6},{4,0},{6,2},{8,12},{10,14},{12,8},{14,10},{16,20},{18,... | collective-permute-start | bytes 884744 | tf_op jit(solution)/shard_map/ppermute | solution.py:101
  57.7 17.3 %collective-permute-start.19 = (bf16[4,48,1536]{2,1,0:T(8,128)(2,1)S(1)}, bf16[4,48,1536]{2,1,0:T(8,128)(2,1)S(1)}, u32[]{:S(2)}, u32[]{:S(2)}) collective-permute-start(bf16[4,48,1536]{2,1,0:T(8,128)(2,1)S(1)} %collective-permute-done.17.refs_1_), channel_id=1, source_target_pairs={{0,2},{2,0},{4,6},{6,4},{8,10},{10,8},{12,14},{14,12},{16,18},{18,... | collective-permute-start | bytes 1769480 | tf_op jit(solution)/shard_map/ppermute | solution.py:101
  60.2 15.3 %collective-permute-start.18 = (bf16[4,48,1536]{2,1,0:T(8,128)(2,1)S(1)}, bf16[4,48,1536]{2,1,0:T(8,128)(2,1)S(1)}, u32[]{:S(2)}, u32[]{:S(2)}) collective-permute-start(bf16[4,48,1536]{2,1,0:T(8,128)(2,1)S(1)} %pad_maximum_fusion.1.refs_0_), channel_id=1, source_target_pairs={{0,2},{2,0},{4,6},{6,4},{8,10},{10,8},{12,14},{14,12},{16,18},{18,... | collective-permute-start | bytes 1769480 | tf_op jit(solution)/shard_map/ppermute | solution.py:101
  65.1 11.3 %collective-permute-start.16 = (bf16[272,768]{1,0:T(8,128)(2,1)S(1)}, bf16[272,768]{1,0:T(8,128)(2,1)S(1)}, u32[]{:S(2)}, u32[]{:S(2)}) collective-permute-start(bf16[272,768]{1,0:T(8,128)(2,1)S(1)} %get-tuple-element.172.normed.a_up), channel_id=1, source_target_pairs={{0,1},{1,0},{2,3},{3,2},{4,5},{5,4},{6,7},{7,6},{8,9},{9,8},{10,11... | collective-permute-start | bytes 1253384 | tf_op jit(solution)/shard_map/ppermute | solution.py:105
  66.7 8.3 %collective-permute-start.21 = (bf16[2,48,1536]{2,1,0:T(8,128)(2,1)S(1)}, bf16[2,48,1536]{2,1,0:T(8,128)(2,1)S(1)}, u32[]{:S(2)}, u32[]{:S(2)}) collective-permute-start(bf16[2,48,1536]{2,1,0:T(8,128)(2,1)S(1)} %collective-permute-done.13.refs_1_), channel_id=1, source_target_pairs={{0,4},{2,6},{4,0},{6,2},{8,12},{10,14},{12,8},{14,10},{16,20},{18,... | collective-permute-start | bytes 884744 | tf_op jit(solution)/shard_map/ppermute | solution.py:101
  67.9 9.6 %collective-permute-start.23 = (bf16[2,48,1536]{2,1,0:T(8,128)(2,1)S(1)}, bf16[2,48,1536]{2,1,0:T(8,128)(2,1)S(1)}, u32[]{:S(2)}, u32[]{:S(2)}) collective-permute-start(bf16[2,48,1536]{2,1,0:T(8,128)(2,1)S(1)} %collective-permute-done.13.refs_1_), channel_id=1, source_target_pairs={{0,2},{2,0},{4,6},{6,4},{8,10},{10,8},{12,14},{14,12},{16,18},{18,... | collective-permute-start | bytes 884744 | tf_op jit(solution)/shard_map/ppermute | solution.py:101
  75.0 2.5 %collective-permute-start.24 = (bf16[2,48,1536]{2,1,0:T(8,128)(2,1)S(1)}, bf16[2,48,1536]{2,1,0:T(8,128)(2,1)S(1)}, u32[]{:S(2)}, u32[]{:S(2)}) collective-permute-start(bf16[2,48,1536]{2,1,0:T(8,128)(2,1)S(1)} %collective-permute-done.20.refs_2_), channel_id=1, source_target_pairs={{0,2},{2,0},{4,6},{6,4},{8,10},{10,8},{12,14},{14,12},{16,18},{18,... | collective-permute-start | bytes 884744 | tf_op jit(solution)/shard_map/ppermute | solution.py:101
  75.0 2.5 %collective-permute-start.22 = (bf16[2,48,1536]{2,1,0:T(8,128)(2,1)S(1)}, bf16[2,48,1536]{2,1,0:T(8,128)(2,1)S(1)}, u32[]{:S(2)}, u32[]{:S(2)}) collective-permute-start(bf16[2,48,1536]{2,1,0:T(8,128)(2,1)S(1)} %pad_maximum_fusion.4.refs_0_), channel_id=1, source_target_pairs={{0,2},{2,0},{4,6},{6,4},{8,10},{10,8},{12,14},{14,12},{16,18},{18,... | collective-permute-start | bytes 884744 | tf_op jit(solution)/shard_map/ppermute | solution.py:101
  75.5 2.0 %collective-permute-start.25 = (bf16[2,48,1536]{2,1,0:T(8,128)(2,1)S(1)}, bf16[2,48,1536]{2,1,0:T(8,128)(2,1)S(1)}, u32[]{:S(2)}, u32[]{:S(2)}) collective-permute-start(bf16[2,48,1536]{2,1,0:T(8,128)(2,1)S(1)} %collective-permute-done.21.refs_3_), channel_id=1, source_target_pairs={{0,2},{2,0},{4,6},{6,4},{8,10},{10,8},{12,14},{14,12},{16,18},{18,... | collective-permute-start | bytes 884744 | tf_op jit(solution)/shard_map/ppermute | solution.py:101
  79.1 7.8 %collective-permute-start.27 = (bf16[144,768]{1,0:T(8,128)(2,1)S(1)}, bf16[144,768]{1,0:T(8,128)(2,1)S(1)}, u32[]{:S(2)}, u32[]{:S(2)}) collective-permute-start(bf16[144,768]{1,0:T(8,128)(2,1)S(1)} %slice.21), channel_id=1, source_target_pairs={{0,1},{1,0},{2,3},{3,2},{4,5},{5,4},{6,7},{7,6},{8,9},{9,8},{10,11... | collective-permute-start | bytes 663560 | tf_op jit(solution)/shard_map/ppermute | solution.py:105
  80.7 1.2 collective-permute-start.26
  84.4 7.2 %collective-permute-start.28 = (bf16[128,768]{1,0:T(8,128)(2,1)S(1)}, bf16[128,768]{1,0:T(8,128)(2,1)S(1)}, u32[]{:S(2)}, u32[]{:S(2)}) collective-permute-start(bf16[128,768]{1,0:T(8,128)(2,1)S(1)} %slice.17), channel_id=1, source_target_pairs={{0,1},{1,0},{2,3},{3,2},{4,5},{5,4},{6,7},{7,6},{8,9},{9,8},{10,11... | collective-permute-start | bytes 589832 | tf_op jit(solution)/shard_map/ppermute | solution.py:105
  88.0 3.6 %collective-permute-start.29 = (bf16[16,128]{1,0:T(8,128)(2,1)S(1)}, bf16[16,128]{1,0:T(8,128)(2,1)S(1)}, u32[]{:S(2)}, u32[]{:S(2)}) collective-permute-start(bf16[16,128]{1,0:T(8,128)(2,1)S(1)} %slice.18), channel_id=1, source_target_pairs={{0,2},{2,0},{4,6},{6,4},{8,10},{10,8},{12,14},{14,12},{16,18},{18,... | collective-permute-start | bytes 12296 | tf_op jit(solution)/shard_map/ppermute | solution.py:101
  88.1 12.3 %collective-permute-start.30 = (bf16[144,768]{1,0:T(8,128)(2,1)S(1)}, bf16[144,768]{1,0:T(8,128)(2,1)S(1)}, u32[]{:S(2)}, u32[]{:S(2)}) collective-permute-start(bf16[144,768]{1,0:T(8,128)(2,1)S(1)} %get-tuple-element.189), channel_id=1, source_target_pairs={{0,1},{1,0},{2,3},{3,2},{4,5},{5,4},{6,7},{7,6},{8,9},{9,8},{10,11... | collective-permute-start | bytes 663560 | tf_op jit(solution)/shard_map/ppermute | solution.py:105
  92.5 7.8 %collective-permute-start.31 = (bf16[128,768]{1,0:T(8,128)(2,1)S(1)}, bf16[128,768]{1,0:T(8,128)(2,1)S(1)}, u32[]{:S(2)}, u32[]{:S(2)}) collective-permute-start(bf16[128,768]{1,0:T(8,128)(2,1)S(1)} %get-tuple-element.194), channel_id=1, source_target_pairs={{0,1},{1,0},{2,3},{3,2},{4,5},{5,4},{6,7},{7,6},{8,9},{9,8},{10,11... | collective-permute-start | bytes 589832 | tf_op jit(solution)/shard_map/ppermute | solution.py:105
  102.2 11.4 %collective-permute-start.32 = (bf16[272,768]{1,0:T(8,128)(2,1)S(1)}, bf16[272,768]{1,0:T(8,128)(2,1)S(1)}, u32[]{:S(2)}, u32[]{:S(2)}) collective-permute-start(bf16[272,768]{1,0:T(8,128)(2,1)S(1)} %convolution_convert_fusion), channel_id=1, source_target_pairs={{0,1},{1,0},{2,3},{3,2},{4,5},{5,4},{6,7},{7,6},{8,9},{9,8},{10,11... | collective-permute-start | bytes 1253384 | tf_op jit(solution)/shard_map/ppermute | solution.py:105
  105.0 1.6 collective-permute-start.37
  105.1 2.0 %collective-permute-start.38 = (bf16[8,48,384]{2,1,0:T(8,128)(2,1)S(1)}, bf16[8,48,384]{2,1,0:T(8,128)(2,1)S(1)}, u32[]{:S(2)}, u32[]{:S(2)}) collective-permute-start(bf16[8,48,384]{2,1,0:T(8,128)(2,1)S(1)} %get-tuple-element.218), channel_id=1, source_target_pairs={{0,2},{2,0},{4,6},{6,4},{8,10},{10,8},{12,14},{14,12},{16,18},{18,... | collective-permute-start | bytes 884744 | tf_op jit(solution)/shard_map/ppermute | solution.py:101
  105.6 1.9 %collective-permute-start.39 = (bf16[8,48,384]{2,1,0:T(8,128)(2,1)S(1)}, bf16[8,48,384]{2,1,0:T(8,128)(2,1)S(1)}, u32[]{:S(2)}, u32[]{:S(2)}) collective-permute-start(bf16[8,48,384]{2,1,0:T(8,128)(2,1)S(1)} %get-tuple-element.219), channel_id=1, source_target_pairs={{0,2},{2,0},{4,6},{6,4},{8,10},{10,8},{12,14},{14,12},{16,18},{18,... | collective-permute-start | bytes 884744 | tf_op jit(solution)/shard_map/ppermute | solution.py:101
  105.7 2.3 %collective-permute-start.40 = (bf16[8,48,384]{2,1,0:T(8,128)(2,1)S(1)}, bf16[8,48,384]{2,1,0:T(8,128)(2,1)S(1)}, u32[]{:S(2)}, u32[]{:S(2)}) collective-permute-start(bf16[8,48,384]{2,1,0:T(8,128)(2,1)S(1)} %get-tuple-element.220), channel_id=1, source_target_pairs={{0,2},{2,0},{4,6},{6,4},{8,10},{10,8},{12,14},{14,12},{16,18},{18,... | collective-permute-start | bytes 884744 | tf_op jit(solution)/shard_map/ppermute | solution.py:101
  108.8 15.4 %collective-permute-start.45 = (bf16[4,48,1536]{2,1,0:T(8,128)(2,1)S(1)}, bf16[4,48,1536]{2,1,0:T(8,128)(2,1)S(1)}, u32[]{:S(2)}, u32[]{:S(2)}) collective-permute-start(bf16[4,48,1536]{2,1,0:T(8,128)(2,1)S(1)} %get-tuple-element.221), channel_id=1, source_target_pairs={{0,4},{2,6},{4,0},{6,2},{8,12},{10,14},{12,8},{14,10},{16,20},{18,... | collective-permute-start | bytes 1769480 | tf_op jit(solution)/shard_map/ppermute | solution.py:101
  111.5 3.8 %collective-permute-start.41 = (bf16[8,48,384]{2,1,0:T(8,128)(2,1)S(1)}, bf16[8,48,384]{2,1,0:T(8,128)(2,1)S(1)}, u32[]{:S(2)}, u32[]{:S(2)}) collective-permute-start(bf16[8,48,384]{2,1,0:T(8,128)(2,1)S(1)} %get-tuple-element.224), channel_id=1, source_target_pairs={{0,2},{2,0},{4,6},{6,4},{8,10},{10,8},{12,14},{14,12},{16,18},{18,... | collective-permute-start | bytes 884744 | tf_op jit(solution)/shard_map/ppermute | solution.py:101
  111.6 5.7 %collective-permute-start.42 = (bf16[8,48,384]{2,1,0:T(8,128)(2,1)S(1)}, bf16[8,48,384]{2,1,0:T(8,128)(2,1)S(1)}, u32[]{:S(2)}, u32[]{:S(2)}) collective-permute-start(bf16[8,48,384]{2,1,0:T(8,128)(2,1)S(1)} %get-tuple-element.225), channel_id=1, source_target_pairs={{0,2},{2,0},{4,6},{6,4},{8,10},{10,8},{12,14},{14,12},{16,18},{18,... | collective-permute-start | bytes 884744 | tf_op jit(solution)/shard_map/ppermute | solution.py:101
  112.1 5.5 %collective-permute-start.43 = (bf16[8,48,384]{2,1,0:T(8,128)(2,1)S(1)}, bf16[8,48,384]{2,1,0:T(8,128)(2,1)S(1)}, u32[]{:S(2)}, u32[]{:S(2)}) collective-permute-start(bf16[8,48,384]{2,1,0:T(8,128)(2,1)S(1)} %get-tuple-element.226), channel_id=1, source_target_pairs={{0,2},{2,0},{4,6},{6,4},{8,10},{10,8},{12,14},{14,12},{16,18},{18,... | collective-permute-start | bytes 884744 | tf_op jit(solution)/shard_map/ppermute | solution.py:101
  113.7 4.2 %collective-permute-start.44 = (bf16[8,48,384]{2,1,0:T(8,128)(2,1)S(1)}, bf16[8,48,384]{2,1,0:T(8,128)(2,1)S(1)}, u32[]{:S(2)}, u32[]{:S(2)}) collective-permute-start(bf16[8,48,384]{2,1,0:T(8,128)(2,1)S(1)} %get-tuple-element.227), channel_id=1, source_target_pairs={{0,2},{2,0},{4,6},{6,4},{8,10},{10,8},{12,14},{14,12},{16,18},{18,... | collective-permute-start | bytes 884744 | tf_op jit(solution)/shard_map/ppermute | solution.py:101
  115.3 9.6 %collective-permute-start.33 = (bf16[272,384]{1,0:T(8,128)(2,1)S(1)}, bf16[272,384]{1,0:T(8,128)(2,1)S(1)}, u32[]{:S(2)}, u32[]{:S(2)}) collective-permute-start(bf16[272,384]{1,0:T(8,128)(2,1)S(1)} %get-tuple-element.203), channel_id=1, source_target_pairs={{0,1},{1,0},{2,3},{3,2},{4,5},{5,4},{6,7},{7,6},{8,9},{9,8},{10,11... | collective-permute-start | bytes 626696 | tf_op jit(solution)/shard_map/ppermute | solution.py:105
  117.3 1.7 collective-permute-start.34
  117.6 1.5 collective-permute-start.35
  117.9 1.5 collective-permute-start.36
  124.9 15.1 %collective-permute-start.46 = (bf16[8,24,768]{2,1,0:T(8,128)(2,1)S(1)}, bf16[8,24,768]{2,1,0:T(8,128)(2,1)S(1)}, u32[]{:S(2)}, u32[]{:S(2)}) collective-permute-start(bf16[8,24,768]{2,1,0:T(8,128)(2,1)S(1)} %get-tuple-element.234), channel_id=1, source_target_pairs={{0,1},{1,0},{2,3},{3,2},{4,5},{5,4},{6,7},{7,6},{8,9},{9,8},{10,11... | collective-permute-start | bytes 884744 | tf_op jit(solution)/shard_map/ppermute | solution.py:105
  126.5 14.9 %collective-permute-start.47 = (bf16[2,48,1536]{2,1,0:T(8,128)(2,1)S(1)}, bf16[2,48,1536]{2,1,0:T(8,128)(2,1)S(1)}, u32[]{:S(2)}, u32[]{:S(2)}) collective-permute-start(bf16[2,48,1536]{2,1,0:T(8,128)(2,1)S(1)} %get-tuple-element.235), channel_id=1, source_target_pairs={{0,16},{2,18},{4,20},{6,22},{8,24},{10,26},{12,28},{14,30},{16,0},... | collective-permute-start | bytes 884744 | tf_op jit(solution)/shard_map/ppermute | solution.py:101
  127.1 15.4 %collective-permute-start.48 = (bf16[4,48,1536]{2,1,0:T(8,128)(2,1)S(1)}, bf16[4,48,1536]{2,1,0:T(8,128)(2,1)S(1)}, u32[]{:S(2)}, u32[]{:S(2)}) collective-permute-start(bf16[4,48,1536]{2,1,0:T(8,128)(2,1)S(1)} %get-tuple-element.249), channel_id=1, source_target_pairs={{0,4},{2,6},{4,0},{6,2},{8,12},{10,14},{12,8},{14,10},{16,20},{18,... | collective-permute-start | bytes 1769480 | tf_op jit(solution)/shard_map/ppermute | solution.py:101
  141.4 2.6 %collective-permute-start.49 = (bf16[8,48,384]{2,1,0:T(8,128)(2,1)S(1)}, bf16[8,48,384]{2,1,0:T(8,128)(2,1)S(1)}, u32[]{:S(2)}, u32[]{:S(2)}) collective-permute-start(bf16[8,48,384]{2,1,0:T(8,128)(2,1)S(1)} %get-tuple-element.251), channel_id=1, source_target_pairs={{0,2},{2,0},{4,6},{6,4},{8,10},{10,8},{12,14},{14,12},{16,18},{18,... | collective-permute-start | bytes 884744 | tf_op jit(solution)/shard_map/ppermute | solution.py:101
  141.4 2.6 %collective-permute-start.50 = (bf16[8,48,384]{2,1,0:T(8,128)(2,1)S(1)}, bf16[8,48,384]{2,1,0:T(8,128)(2,1)S(1)}, u32[]{:S(2)}, u32[]{:S(2)}) collective-permute-start(bf16[8,48,384]{2,1,0:T(8,128)(2,1)S(1)} %get-tuple-element.252), channel_id=1, source_target_pairs={{0,2},{2,0},{4,6},{6,4},{8,10},{10,8},{12,14},{14,12},{16,18},{18,... | collective-permute-start | bytes 884744 | tf_op jit(solution)/shard_map/ppermute | solution.py:101
  141.9 2.1 %collective-permute-start.51 = (bf16[8,48,384]{2,1,0:T(8,128)(2,1)S(1)}, bf16[8,48,384]{2,1,0:T(8,128)(2,1)S(1)}, u32[]{:S(2)}, u32[]{:S(2)}) collective-permute-start(bf16[8,48,384]{2,1,0:T(8,128)(2,1)S(1)} %get-tuple-element.253), channel_id=1, source_target_pairs={{0,2},{2,0},{4,6},{6,4},{8,10},{10,8},{12,14},{14,12},{16,18},{18,... | collective-permute-start | bytes 884744 | tf_op jit(solution)/shard_map/ppermute | solution.py:101
  141.9 2.0 %collective-permute-start.52 = (bf16[8,48,128]{2,1,0:T(8,128)(2,1)S(1)}, bf16[8,48,128]{2,1,0:T(8,128)(2,1)S(1)}, u32[]{:S(2)}, u32[]{:S(2)}) collective-permute-start(bf16[8,48,128]{2,1,0:T(8,128)(2,1)S(1)} %get-tuple-element.254), channel_id=1, source_target_pairs={{0,2},{2,0},{4,6},{6,4},{8,10},{10,8},{12,14},{14,12},{16,18},{18,... | collective-permute-start | bytes 294920 | tf_op jit(solution)/shard_map/ppermute | solution.py:101
  144.0 15.1 %collective-permute-start.57 = (bf16[2,48,1536]{2,1,0:T(8,128)(2,1)S(1)}, bf16[2,48,1536]{2,1,0:T(8,128)(2,1)S(1)}, u32[]{:S(2)}, u32[]{:S(2)}) collective-permute-start(bf16[2,48,1536]{2,1,0:T(8,128)(2,1)S(1)} %get-tuple-element.269), channel_id=1, source_target_pairs={{0,16},{2,18},{4,20},{6,22},{8,24},{10,26},{12,28},{14,30},{16,0},... | collective-permute-start | bytes 884744 | tf_op jit(solution)/shard_map/ppermute | solution.py:101
  146.0 16.1 %collective-permute-start.54 = (bf16[4,24,2048]{2,1,0:T(8,128)(2,1)S(1)}, bf16[4,24,2048]{2,1,0:T(8,128)(2,1)S(1)}, u32[]{:S(2)}, u32[]{:S(2)}) collective-permute-start(bf16[4,24,2048]{2,1,0:T(8,128)(2,1)S(1)} %get-tuple-element.261), channel_id=1, source_target_pairs={{0,4},{2,6},{4,0},{6,2},{8,12},{10,14},{12,8},{14,10},{16,20},{18,... | collective-permute-start | bytes 1179656 | tf_op jit(solution)/shard_map/ppermute | solution.py:101
  147.5 13.8 %collective-permute-start.55 = (bf16[4,24,1280]{2,1,0:T(8,128)(2,1)S(1)}, bf16[4,24,1280]{2,1,0:T(8,128)(2,1)S(1)}, u32[]{:S(2)}, u32[]{:S(2)}) collective-permute-start(bf16[4,24,1280]{2,1,0:T(8,128)(2,1)S(1)} %get-tuple-element.266), channel_id=1, source_target_pairs={{0,1},{1,0},{2,3},{3,2},{4,5},{5,4},{6,7},{7,6},{8,9},{9,8},{10,11... | collective-permute-start | bytes 737288 | tf_op jit(solution)/shard_map/ppermute | solution.py:105
  148.0 14.1 %collective-permute-start.56 = (bf16[4,24,1280]{2,1,0:T(8,128)(2,1)S(1)}, bf16[4,24,1280]{2,1,0:T(8,128)(2,1)S(1)}, u32[]{:S(2)}, u32[]{:S(2)}) collective-permute-start(bf16[4,24,1280]{2,1,0:T(8,128)(2,1)S(1)} %get-tuple-element.267), channel_id=1, source_target_pairs={{0,5},{1,4},{2,7},{3,6},{4,1},{5,0},{6,3},{7,2},{8,13},{9,12},{10,... | collective-permute-start | bytes 737288 | tf_op jit(solution)/shard_map/ppermute | solution.py:114
  150.2 11.2 %collective-permute-start.59 = (bf16[1,48,1536]{2,1,0:T(8,128)(2,1)S(1)}, bf16[1,48,1536]{2,1,0:T(8,128)(2,1)S(1)}, u32[]{:S(2)}, u32[]{:S(2)}) collective-permute-start(bf16[1,48,1536]{2,1,0:T(8,128)(2,1)S(1)} %get-tuple-element.274), channel_id=1, source_target_pairs={{0,8},{2,10},{4,12},{6,14},{8,0},{10,2},{12,4},{14,6},{16,24},{18,... | collective-permute-start | bytes 442376 | tf_op jit(solution)/shard_map/ppermute | solution.py:136
  159.1 1.2 collective-permute-start.58
  160.2 11.7 %collective-permute-start.53 = (bf16[272,768]{1,0:T(8,128)(2,1)S(1)}, bf16[272,768]{1,0:T(8,128)(2,1)S(1)}, u32[]{:S(2)}, u32[]{:S(2)}) collective-permute-start(bf16[272,768]{1,0:T(8,128)(2,1)S(1)} %get-tuple-element.270), channel_id=1, source_target_pairs={{0,1},{1,0},{2,3},{3,2},{4,5},{5,4},{6,7},{7,6},{8,9},{9,8},{10,11... | collective-permute-start | bytes 1253384 | tf_op jit(solution)/shard_map/ppermute | solution.py:105
  162.1 11.5 %collective-permute-start.63 = (bf16[1,48,1536]{2,1,0:T(8,128)(2,1)S(1)}, bf16[1,48,1536]{2,1,0:T(8,128)(2,1)S(1)}, u32[]{:S(2)}, u32[]{:S(2)}) collective-permute-start(bf16[1,48,1536]{2,1,0:T(8,128)(2,1)S(1)} %get-tuple-element.292), channel_id=1, source_target_pairs={{0,8},{2,10},{4,12},{6,14},{8,0},{10,2},{12,4},{14,6},{16,24},{18,... | collective-permute-start | bytes 442376 | tf_op jit(solution)/shard_map/ppermute | solution.py:136
  163.2 11.1 %collective-permute-start.60 = (bf16[1,24,3328]{2,1,0:T(8,128)(2,1)S(1)}, bf16[1,24,3328]{2,1,0:T(8,128)(2,1)S(1)}, u32[]{:S(2)}, u32[]{:S(2)}) collective-permute-start(bf16[1,24,3328]{2,1,0:T(8,128)(2,1)S(1)} %get-tuple-element.278), channel_id=1, source_target_pairs={{0,8},{2,10},{4,12},{6,14},{8,16},{10,18},{12,20},{14,22},{16,24},... | collective-permute-start | bytes 479240 | tf_op jit(solution)/shard_map/ppermute | solution.py:101
  164.9 13.1 %collective-permute-start.61 = (bf16[1,24,3328]{2,1,0:T(8,128)(2,1)S(1)}, bf16[1,24,3328]{2,1,0:T(8,128)(2,1)S(1)}, u32[]{:S(2)}, u32[]{:S(2)}) collective-permute-start(bf16[1,24,3328]{2,1,0:T(8,128)(2,1)S(1)} %get-tuple-element.279), channel_id=1, source_target_pairs={{0,16},{2,18},{4,20},{6,22},{8,24},{10,26},{12,28},{14,30},{16,0},... | collective-permute-start | bytes 479240 | tf_op jit(solution)/shard_map/ppermute | solution.py:101
  166.9 11.1 %collective-permute-start.62 = (bf16[1,24,3328]{2,1,0:T(8,128)(2,1)S(1)}, bf16[1,24,3328]{2,1,0:T(8,128)(2,1)S(1)}, u32[]{:S(2)}, u32[]{:S(2)}) collective-permute-start(bf16[1,24,3328]{2,1,0:T(8,128)(2,1)S(1)} %get-tuple-element.280), channel_id=1, source_target_pairs={{0,24},{2,26},{4,28},{6,30},{8,0},{10,2},{12,4},{14,6},{16,8},{18,... | collective-permute-start | bytes 479240 | tf_op jit(solution)/shard_map/ppermute | solution.py:101
  (3 other events, 45.6 us)
